TPU v7x, 32 devices: a whole 2x2x4 slice. The times are simulated.
32 devices in a mesh: mset: 8 (over y, x, core), band: 4 (over z).
Axes of the slice: x: 2, y: 2, z: 4, core: 2. Of those that a mesh axis runs over, the one named last changes fastest.
Arguments:
- coeffs: bfloat16 [2, 704, 30720], P(None, 'band', 'mset'), may hold values from -6 to 6
- legendre: bfloat16 [320, 704, 512], P('mset', None, 'band'), may hold values from -0.3125 to 0.3125
- wavenumber: int32 [320], P('mset'), may hold values from 0 to 639, as said below
- band_rows: int32 [4], P('band'), may hold values from 16 to 128, as said below
Outputs:
- fourier: bfloat16 [96, 640, 512], P('mset', None, 'band')
Inputs may be any that keep to these rules, and one draw needn't show every extreme that they name: All entries differ; pair q stands for wavenumbers wavenumber[q] and 1279 - wavenumber[q]. Both ends of the range occur. `band_rows`: entries 2 j and 2 j + 1 are equal (a band and its mirror image); some band holds 128.
All inputs are finite; a program needn't handle non-finite values.
Results may differ from a plain program's by a relative error of at most 0.0051.
Values may be sent and summed in bfloat16 or wider, within the bound.
No kernel may reach another device: no remote copies, remote signals or barrier semaphores. Data moves between devices by JAX's collectives and lax.ppermute only.
A program may use at most 128 MiB of HBM per device.

v0:
```python
import functools

import jax
import jax.numpy as jnp
from jax import lax
from jax.experimental import pallas as pl
from jax.experimental.pallas import tpu as pltpu
from jax.sharding import PartitionSpec as P

TRUNC = 1279
CHUNK = 8


def owner_limits(wavenumber, parity):
    first = jnp.maximum((TRUNC - wavenumber - parity) // 2 + 1, 0)
    second = jnp.maximum((wavenumber - parity) // 2 + 1, 0)
    return first, first + second


def sums_kernel(rows, fields, start, pairs, order, first, total, *refs):
    blocks, (legendre, out, gathered, flipped, values, sums, arrived) = refs[:-7], refs[-7:]
    _, depth, lats = legendre.shape
    copies = [
        pltpu.make_async_copy(legendre.at[start + pair], values.at[pair], arrived.at[pair]) for pair in range(pairs)
    ]
    for copy in copies:
        copy.start()
    if len(blocks) == 1:
        gathered[...] = blocks[0][...]
    else:
        for step, block in enumerate(blocks):
            offset = pl.multiple_of(order[step] * rows, 16)
            gathered[pl.ds(offset, rows), :] = block[...]
    flipped[...] = gathered[...].T
    row = lax.broadcasted_iota(jnp.int32, (depth, lats), 0)
    for pair in range(pairs):
        copies[pair].wait()
        here = values[pair].astype(jnp.float32)
        in_first = row < first[start + pair]
        in_any = row < total[start + pair]
        part_first = jnp.where(in_first, here, 0.0)
        part_second = jnp.where(in_any, here - part_first, 0.0)
        both = jnp.concatenate([part_first, part_second], axis=1).astype(jnp.bfloat16)
        product = jnp.dot(
            flipped[pair * fields : (pair + 1) * fields, :], both, preferred_element_type=jnp.float32
        )
        sums[:, 2 * pair, :] = product[:, :lats]
        sums[:, 2 * pair + 1, :] = product[:, lats:]
    out[...] = sums[...].astype(out.dtype)


def parity_sums(blocks, order, first, total, legendre, start, pairs, fields):
    rows, columns = blocks[0].shape
    _, depth, lats = legendre.shape
    vmem = pl.BlockSpec(memory_space=pltpu.VMEM)
    scalar = pl.BlockSpec(memory_space=pltpu.SMEM)
    return pl.pallas_call(
        functools.partial(sums_kernel, rows, fields, start, pairs),
        in_specs=[scalar] * 3 + [vmem] * len(blocks) + [pl.BlockSpec(memory_space=pltpu.HBM)],
        out_specs=vmem,
        scratch_shapes=[
            pltpu.VMEM((depth, columns), jnp.bfloat16),
            pltpu.VMEM((columns, depth), jnp.bfloat16),
            pltpu.VMEM((pairs, depth, lats), jnp.bfloat16),
            pltpu.VMEM((fields, 2 * pairs, lats), jnp.float32),
            pltpu.SemaphoreType.DMA((pairs,)),
        ],
        out_shape=jax.ShapeDtypeStruct((fields, 2 * pairs, lats), jnp.bfloat16),
        compiler_params=pltpu.CompilerParams(vmem_limit_bytes=56 * 2**20),
        cost_estimate=pl.CostEstimate(
            flops=4 * pairs * depth * fields * lats,
            bytes_accessed=2 * (depth * columns + pairs * depth * lats + 2 * pairs * fields * lats),
            transcendentals=0,
        ),
        name="parity_sums",
    )(order, first, total, *blocks, legendre)


def shards(coeffs, legendre, wavenumber, band_rows):
    bands = lax.axis_size("band")
    sets = lax.axis_size("mset")
    me = lax.axis_index("band")
    parity = me % 2
    pair_count, depth, lats = legendre.shape
    rows = coeffs.shape[1]
    fields = coeffs.shape[2] // pair_count
    first, total = owner_limits(wavenumber, parity)
    order = me ^ jnp.arange(bands, dtype=jnp.int32)
    valid_lat = jnp.arange(lats, dtype=jnp.int32) < band_rows[0]
    mine = lax.dynamic_index_in_dim(coeffs, parity, 0, keepdims=False)
    other = lax.dynamic_index_in_dim(coeffs, 1 - parity, 0, keepdims=False)
    chunks = pair_count // CHUNK
    steps = list(range(1, bands))

    def swap(value, step):
        return lax.ppermute(value, "band", [(band, band ^ step) for band in range(bands)])

    def columns_of(value, chunk):
        return value[:, chunk * CHUNK * fields : (chunk + 1) * CHUNK * fields]

    def combine(own, partner):
        own = own.astype(jnp.float32)
        partner = jnp.concatenate(partner).astype(jnp.float32)
        grid = jnp.where(parity == 0, own + partner, partner - own)
        return jnp.where(valid_lat, grid, 0.0).astype(jnp.bfloat16)

    def redistribute(grid):
        piece = lax.all_to_all(grid, "mset", split_axis=0, concat_axis=1, tiled=True)
        return piece.reshape(fields // sets, sets, 2 * CHUNK, lats)

    def start_sends(payloads):
        return [swap(payloads[step % 2], step) for step in steps]

    def payloads_of(chunk):
        return [columns_of(mine, chunk), columns_of(other, chunk)]

    blocks = start_sends(payloads_of(0))
    pieces = []
    halves = None
    for chunk in range(chunks):
        if chunk + 1 < chunks:
            blocks, later = lax.optimization_barrier((blocks, payloads_of(chunk + 1)))
            following = start_sends(later)
        if chunk >= 3:
            blocks, pieces[chunk - 3] = lax.optimization_barrier((blocks, pieces[chunk - 3]))
        blocks = [columns_of(mine, chunk)] + blocks
        if rows % 16:
            stacked = jnp.take(jnp.stack(blocks), me ^ jnp.arange(bands), axis=0)
            blocks = [stacked.reshape(bands * rows, -1)]
        own = parity_sums(blocks, order, first, total, legendre, chunk * CHUNK, CHUNK, fields)
        if halves is not None:
            own, halves = lax.optimization_barrier((own, halves))
            pieces.append(redistribute(combine(*halves)))
        middle = fields // 2
        halves = (own, [swap(own[:middle], 1), swap(own[middle:], 1)])
        blocks = following
    pieces.append(redistribute(combine(*halves)))
    return jnp.concatenate(pieces, axis=2).reshape(fields // sets, sets * 2 * pair_count, lats)


def solution(mesh):
    in_specs = (P(None, "band", "mset"), P("mset", None, "band"), P("mset"), P("band"))
    out_specs = P("mset", None, "band")
    return jax.shard_map(shards, mesh=mesh, in_specs=in_specs, out_specs=out_specs, check_vma=False)
```

profile of v0, /device:TPU:0, one launch (start us, length us, event | category | flops | bytes accessed | tf_op | source)
XLA Modules:
  0.0 192.4 jit_solution(11303304817674651914)
XLA Ops:
  2.0 5.1 %collective-permute-start.2 = (bf16[176,768]{1,0:T(8,128)(2,1)S(1)}, bf16[176,768]{1,0:T(8,128)(2,1)S(1)}, u32[]{:S(2)}, u32[]{:S(2)}) collective-permute-start(bf16[176,768]{1,0:T(8,128)(2,1)S(1)} %get-tuple-element.101), channel_id=1, source_target_pairs={{0,3},{1,2},{2,1},{3,0},{4,7},{5,6},{6,5},{7,4},{8,11},{9,10},{10,... | collective-permute-start | bytes 811016 | tf_op jit(solution)/shard_map/ppermute | solution.py:96
  9.1 21.0 %collective-permute-done.1.refs_2_ = bf16[176,768]{1,0:T(8,128)(2,1)S(1)} collective-permute-done((bf16[176,768]{1,0:T(8,128)(2,1)S(1)}, bf16[176,768]{1,0:T(8,128)(2,1)S(1)}, u32[]{:S(2)}, u32[]{:S(2)}) %collective-permute-start.1) | collective-permute-done | bytes 270368 | tf_op jit(solution)/shard_map/ppermute | solution.py:96
  30.2 2.7 %collective-permute-start.5 = (bf16[176,768]{1,0:T(8,128)(2,1)S(1)}, bf16[176,768]{1,0:T(8,128)(2,1)S(1)}, u32[]{:S(2)}, u32[]{:S(2)}) collective-permute-start(bf16[176,768]{1,0:T(8,128)(2,1)S(1)} %get-tuple-element.49), channel_id=1, source_target_pairs={{0,3},{1,2},{2,1},{3,0},{4,7},{5,6},{6,5},{7,4},{8,11},{9,10},{10,... | collective-permute-start | bytes 811016 | tf_op jit(solution)/shard_map/ppermute | solution.py:96
  34.6 5.2 %parity_sums.6 = bf16[96,16,128]{2,1,0:T(8,128)(2,1)} custom-call(s32[4]{0:T(128)} %iota_xor_fusion.order, s32[40]{0:T(128)} %get-tuple-element.94.first, s32[40]{0:T(128)} %get-tuple-element.93.total, bf16[176,768]{1,0:T(8,128)(2,1)} %copy-done.8, bf16[176,768]{1,0:T(8,128)(2,1)} %copy-done.22, bf16[176,768]{1,0:T(8,128)(2,1)} %copy-done.23, ...), custom_call_target="tpu_custom_call" | custom-call | flops 276824064 | bytes 2916352 | tf_op jit(solution)/shard_map/parity_sums/pallas_call | solution.py:57
  43.0 12.4 %collective-permute-done.4.refs_2_ = bf16[176,768]{1,0:T(8,128)(2,1)S(1)} collective-permute-done((bf16[176,768]{1,0:T(8,128)(2,1)S(1)}, bf16[176,768]{1,0:T(8,128)(2,1)S(1)}, u32[]{:S(2)}, u32[]{:S(2)}) %collective-permute-start.4) | collective-permute-done | bytes 270368 | tf_op jit(solution)/shard_map/ppermute | solution.py:96
  56.7 3.2 %collective-permute-start.7 = (bf16[176,768]{1,0:T(8,128)(2,1)S(1)}, bf16[176,768]{1,0:T(8,128)(2,1)S(1)}, u32[]{:S(2)}, u32[]{:S(2)}) collective-permute-start(bf16[176,768]{1,0:T(8,128)(2,1)S(1)} %get-tuple-element.52.refs_0_), channel_id=1, source_target_pairs={{0,2},{1,3},{2,0},{3,1},{4,6},{5,7},{6,4},{7,5},{8,10},{9,11},{10,... | collective-permute-start | bytes 811016 | tf_op jit(solution)/shard_map/ppermute | solution.py:96
  59.9 5.2 %parity_sums.5 = bf16[96,16,128]{2,1,0:T(8,128)(2,1)} custom-call(s32[4]{0:T(128)} %iota_xor_fusion.order, s32[40]{0:T(128)} %get-tuple-element.94.first, s32[40]{0:T(128)} %get-tuple-element.93.total, bf16[176,768]{1,0:T(8,128)(2,1)} %copy-done.7, bf16[176,768]{1,0:T(8,128)(2,1)} %copy-done.19, bf16[176,768]{1,0:T(8,128)(2,1)} %copy-done.21, ...), custom_call_target="tpu_custom_call" | custom-call | flops 276824064 | bytes 2916352 | tf_op jit(solution)/shard_map/parity_sums/pallas_call | solution.py:57
  65.1 3.3 %collective-permute-done.12 = bf16[48,16,128]{2,1,0:T(8,128)(2,1)S(1)} collective-permute-done((bf16[48,16,128]{2,1,0:T(8,128)(2,1)S(1)}, bf16[48,16,128]{2,1,0:T(8,128)(2,1)S(1)}, u32[]{:S(2)}, u32[]{:S(2)}) %collective-permute-start.12) | collective-permute-done | bytes 196640 | tf_op jit(solution)/shard_map/ppermute | solution.py:96
  70.2 2.0 %collective-permute-start.17 = (bf16[48,16,128]{2,1,0:T(8,128)(2,1)}, bf16[48,16,128]{2,1,0:T(8,128)(2,1)}, u32[]{:S(2)}, u32[]{:S(2)}) collective-permute-start(bf16[48,16,128]{2,1,0:T(8,128)(2,1)} %get-tuple-element.114), channel_id=1, source_target_pairs={{0,1},{1,0},{2,3},{3,2},{4,5},{5,4},{6,7},{7,6},{8,9},{9,8},{10,11... | collective-permute-start | bytes 589832 | tf_op jit(solution)/shard_map/ppermute | solution.py:96
  72.9 4.3 %collective-permute-done.7.refs_2_ = bf16[176,768]{1,0:T(8,128)(2,1)S(1)} collective-permute-done((bf16[176,768]{1,0:T(8,128)(2,1)S(1)}, bf16[176,768]{1,0:T(8,128)(2,1)S(1)}, u32[]{:S(2)}, u32[]{:S(2)}) %collective-permute-start.7) | collective-permute-done | bytes 270368 | tf_op jit(solution)/shard_map/ppermute | solution.py:96
  77.3 2.2 %collective-permute-start.11 = (bf16[176,768]{1,0:T(8,128)(2,1)S(1)}, bf16[176,768]{1,0:T(8,128)(2,1)S(1)}, u32[]{:S(2)}, u32[]{:S(2)}) collective-permute-start(bf16[176,768]{1,0:T(8,128)(2,1)S(1)} %get-tuple-element.53), channel_id=1, source_target_pairs={{0,3},{1,2},{2,1},{3,0},{4,7},{5,6},{6,5},{7,4},{8,11},{9,10},{10,... | collective-permute-start | bytes 811016 | tf_op jit(solution)/shard_map/ppermute | solution.py:96
  81.8 5.2 %parity_sums.7 = bf16[96,16,128]{2,1,0:T(8,128)(2,1)} custom-call(s32[4]{0:T(128)} %iota_xor_fusion.order, s32[40]{0:T(128)} %get-tuple-element.94.first, s32[40]{0:T(128)} %get-tuple-element.93.total, bf16[176,768]{1,0:T(8,128)(2,1)} %copy-done.6, bf16[176,768]{1,0:T(8,128)(2,1)} %copy-done.15, bf16[176,768]{1,0:T(8,128)(2,1)} %copy-done.17, ...), custom_call_target="tpu_custom_call" | custom-call | flops 276824064 | bytes 2916352 | tf_op jit(solution)/shard_map/parity_sums/pallas_call | solution.py:57
  87.0 10.2 %collective-permute-done.17 = bf16[48,16,128]{2,1,0:T(8,128)(2,1)} collective-permute-done((bf16[48,16,128]{2,1,0:T(8,128)(2,1)}, bf16[48,16,128]{2,1,0:T(8,128)(2,1)}, u32[]{:S(2)}, u32[]{:S(2)}) %collective-permute-start.17) | collective-permute-done | bytes 196640 | tf_op jit(solution)/shard_map/ppermute | solution.py:96
  97.2 2.3 %fusion.5 = (bf16[96,16,128]{2,1,0:T(8,128)(2,1)}, bf16[96,16,128]{2,1,0:T(8,128)(2,1)}) fusion(bf16[96,16,128]{2,1,0:T(8,128)(2,1)S(1)} %copy-done.3, bf16[48,16,128]{2,1,0:T(8,128)(2,1)} %collective-permute-done.18, bf16[48,16,128]{2,1,0:T(8,128)(2,1)} %collective-permute-done.17, pred[]{:T(512)S(6)} %eq.4, pred[128]{0:T(512)(128)(4,1)S(1)} %iota_compare_fusion, ...), kind=kLoop, calls=%fused_computation.17 | loop fusion | flops 3145728 | bytes 2359425 | tf_op jit(solution)/shard_map/convert_element_type | solution.py:105
  99.5 3.7 %all-to-all-start = ((bf16[96,16,128]{2,1,0:T(8,128)(2,1)}), bf16[96,16,128]{2,1,0:T(8,128)(2,1)S(1)}, u32[]{:S(2)}, u32[]{:S(2)}) async-start(bf16[96,16,128]{2,1,0:T(8,128)(2,1)} %get-tuple-element.121), calls=%async_computation | async-start | bytes 786432 | tf_op jit(solution)/shard_map/all_to_all | solution.py:108
  103.9 2.0 %collective-permute-start.19 = (bf16[48,16,128]{2,1,0:T(8,128)(2,1)S(1)}, bf16[48,16,128]{2,1,0:T(8,128)(2,1)}, u32[]{:S(2)}, u32[]{:S(2)}) collective-permute-start(bf16[48,16,128]{2,1,0:T(8,128)(2,1)S(1)} %get-tuple-element.112), channel_id=1, source_target_pairs={{0,1},{1,0},{2,3},{3,2},{4,5},{5,4},{6,7},{7,6},{8,9},{9,8},{10,11... | collective-permute-start | bytes 589832 | tf_op jit(solution)/shard_map/ppermute | solution.py:96
  107.7 2.8 %collective-permute-start.15 = (bf16[176,768]{1,0:T(8,128)(2,1)S(1)}, bf16[176,768]{1,0:T(8,128)(2,1)S(1)}, u32[]{:S(2)}, u32[]{:S(2)}) collective-permute-start(bf16[176,768]{1,0:T(8,128)(2,1)S(1)} %get-tuple-element.69.refs_0_), channel_id=1, source_target_pairs={{0,2},{1,3},{2,0},{3,1},{4,6},{5,7},{6,4},{7,5},{8,10},{9,11},{10,... | collective-permute-start | bytes 811016 | tf_op jit(solution)/shard_map/ppermute | solution.py:96
  111.5 3.6 %all-to-all-start.1 = ((bf16[96,16,128]{2,1,0:T(8,128)(2,1)}), bf16[96,16,128]{2,1,0:T(8,128)(2,1)S(1)}, u32[]{:S(2)}, u32[]{:S(2)}) async-start(bf16[96,16,128]{2,1,0:T(8,128)(2,1)} %get-tuple-element.120), calls=%async_computation.1 | async-start | bytes 786432 | tf_op jit(solution)/shard_map/all_to_all | solution.py:108
  115.2 5.2 %parity_sums.8 = bf16[96,16,128]{2,1,0:T(8,128)(2,1)} custom-call(s32[4]{0:T(128)} %iota_xor_fusion.order, s32[40]{0:T(128)} %get-tuple-element.94.first, s32[40]{0:T(128)} %get-tuple-element.93.total, bf16[176,768]{1,0:T(8,128)(2,1)} %copy-done.5, bf16[176,768]{1,0:T(8,128)(2,1)} %copy-done.10, bf16[176,768]{1,0:T(8,128)(2,1)} %copy-done.11, ...), custom_call_target="tpu_custom_call" | custom-call | flops 276824064 | bytes 2916352 | tf_op jit(solution)/shard_map/parity_sums/pallas_call | solution.py:57
  120.4 7.3 %collective-permute-done.19 = bf16[48,16,128]{2,1,0:T(8,128)(2,1)} collective-permute-done((bf16[48,16,128]{2,1,0:T(8,128)(2,1)S(1)}, bf16[48,16,128]{2,1,0:T(8,128)(2,1)}, u32[]{:S(2)}, u32[]{:S(2)}) %collective-permute-start.19) | collective-permute-done | bytes 196640 | tf_op jit(solution)/shard_map/ppermute | solution.py:96
  128.9 2.0 %collective-permute-start.21 = (bf16[48,16,128]{2,1,0:T(8,128)(2,1)S(1)}, bf16[48,16,128]{2,1,0:T(8,128)(2,1)S(1)}, u32[]{:S(2)}, u32[]{:S(2)}) collective-permute-start(bf16[48,16,128]{2,1,0:T(8,128)(2,1)S(1)} %get-tuple-element.110), channel_id=1, source_target_pairs={{0,1},{1,0},{2,3},{3,2},{4,5},{5,4},{6,7},{7,6},{8,9},{9,8},{10,11... | collective-permute-start | bytes 589832 | tf_op jit(solution)/shard_map/ppermute | solution.py:96
  131.1 2.3 %collective-permute-done.14.refs_1_ = bf16[176,768]{1,0:T(8,128)(2,1)S(1)} collective-permute-done((bf16[176,768]{1,0:T(8,128)(2,1)S(1)}, bf16[176,768]{1,0:T(8,128)(2,1)S(1)}, u32[]{:S(2)}, u32[]{:S(2)}) %collective-permute-start.14) | collective-permute-done | bytes 270368 | tf_op jit(solution)/shard_map/ppermute | solution.py:96
  134.1 5.2 %parity_sums.9 = bf16[96,16,128]{2,1,0:T(8,128)(2,1)} custom-call(s32[4]{0:T(128)} %iota_xor_fusion.order, s32[40]{0:T(128)} %get-tuple-element.94.first, s32[40]{0:T(128)} %get-tuple-element.93.total, bf16[176,768]{1,0:T(8,128)(2,1)} %copy-done.4, bf16[176,768]{1,0:T(8,128)(2,1)} %copy-done.14, bf16[176,768]{1,0:T(8,128)(2,1)} %copy-done.16, ...), custom_call_target="tpu_custom_call" | custom-call | flops 276824064 | bytes 2916352 | tf_op jit(solution)/shard_map/parity_sums/pallas_call | solution.py:57
  139.4 2.1 %collective-permute-done.21 = bf16[48,16,128]{2,1,0:T(8,128)(2,1)S(1)} collective-permute-done((bf16[48,16,128]{2,1,0:T(8,128)(2,1)S(1)}, bf16[48,16,128]{2,1,0:T(8,128)(2,1)S(1)}, u32[]{:S(2)}, u32[]{:S(2)}) %collective-permute-start.21) | collective-permute-done | bytes 196640 | tf_op jit(solution)/shard_map/ppermute | solution.py:96
  144.6 5.8 %collective-permute-done.23 = bf16[48,16,128]{2,1,0:T(8,128)(2,1)S(1)} collective-permute-done((bf16[48,16,128]{2,1,0:T(8,128)(2,1)S(1)}, bf16[48,16,128]{2,1,0:T(8,128)(2,1)S(1)}, u32[]{:S(2)}, u32[]{:S(2)}) %collective-permute-start.23) | collective-permute-done | bytes 196640 | tf_op jit(solution)/shard_map/ppermute | solution.py:96
  150.4 2.9 %collective-permute-done.24 = bf16[48,16,128]{2,1,0:T(8,128)(2,1)S(1)} collective-permute-done((bf16[48,16,128]{2,1,0:T(8,128)(2,1)S(1)}, bf16[48,16,128]{2,1,0:T(8,128)(2,1)S(1)}, u32[]{:S(2)}, u32[]{:S(2)}) %collective-permute-start.24) | collective-permute-done | bytes 196640 | tf_op jit(solution)/shard_map/ppermute | solution.py:96
  153.3 2.6 %fusion.14 = (bf16[96,16,128]{2,1,0:T(8,128)(2,1)}, bf16[96,16,128]{2,1,0:T(8,128)(2,1)S(1)}, bf16[96,16,128]{2,1,0:T(8,128)(2,1)}) fusion(bf16[96,16,128]{2,1,0:T(8,128)(2,1)} %parity_sums.9, bf16[48,16,128]{2,1,0:T(8,128)(2,1)S(1)} %collective-permute-done.24, bf16[48,16,128]{2,1,0:T(8,128)(2,1)S(1)} %collective-permute-done.23, pred[]{:T(512)S(6)} %eq.4, ...), kind=kLoop, calls=%fused_computation.26 | loop fusion | flops 4718592 | bytes 3539073 | tf_op jit(solution)/shard_map/convert_element_type | solution.py:105
  155.9 11.6 %all_to_all.75 = bf16[96,16,128]{2,1,0:T(8,128)(2,1)S(1)} all-to-all(bf16[96,16,128]{2,1,0:T(8,128)(2,1)S(1)} %get-tuple-element.118), channel_id=1, replica_groups=mesh['mset'=8,'band'=4] {'mset'}, dimensions={0} | all-to-all | bytes 786432 | tf_op jit(solution)/shard_map/all_to_all | solution.py:108
  167.4 3.5 %all-to-all-start.3 = ((bf16[96,16,128]{2,1,0:T(8,128)(2,1)}), bf16[96,16,128]{2,1,0:T(8,128)(2,1)S(1)}, u32[]{:S(2)}, u32[]{:S(2)}) async-start(bf16[96,16,128]{2,1,0:T(8,128)(2,1)} %get-tuple-element.119), calls=%async_computation.3 | async-start | bytes 786432 | tf_op jit(solution)/shard_map/all_to_all | solution.py:108
  170.9 8.2 %all-to-all-done.3 = bf16[96,16,128]{2,1,0:T(8,128)(2,1)S(1)} async-done(((bf16[96,16,128]{2,1,0:T(8,128)(2,1)}), bf16[96,16,128]{2,1,0:T(8,128)(2,1)S(1)}, u32[]{:S(2)}, u32[]{:S(2)}) %all-to-all-start.3) | async-done | bytes 393248 | tf_op jit(solution)/shard_map/all_to_all | solution.py:108
  179.2 3.5 %all-to-all-start.4 = ((bf16[96,16,128]{2,1,0:T(8,128)(2,1)}), bf16[96,16,128]{2,1,0:T(8,128)(2,1)S(1)}, u32[]{:S(2)}, u32[]{:S(2)}) async-start(bf16[96,16,128]{2,1,0:T(8,128)(2,1)} %get-tuple-element.117), calls=%async_computation.4 | async-start | bytes 786432 | tf_op jit(solution)/shard_map/all_to_all | solution.py:108
  182.8 8.1 %all-to-all-done.4 = bf16[96,16,128]{2,1,0:T(8,128)(2,1)S(1)} async-done(((bf16[96,16,128]{2,1,0:T(8,128)(2,1)}), bf16[96,16,128]{2,1,0:T(8,128)(2,1)S(1)}, u32[]{:S(2)}, u32[]{:S(2)}) %all-to-all-start.4) | async-done | bytes 393248 | tf_op jit(solution)/shard_map/all_to_all | solution.py:108
  (105 shorter events, 24.7 us)
Async XLA Ops:
  2.0 28.1 %collective-permute-start.2 = (bf16[176,768]{1,0:T(8,128)(2,1)S(1)}, bf16[176,768]{1,0:T(8,128)(2,1)S(1)}, u32[]{:S(2)}, u32[]{:S(2)}) collective-permute-start(bf16[176,768]{1,0:T(8,128)(2,1)S(1)} %get-tuple-element.101), channel_id=1, source_target_pairs={{0,3},{1,2},{2,1},{3,0},{4,7},{5,6},{6,5},{7,4},{8,11},{9,10},{10,... | collective-permute-start | bytes 811016 | tf_op jit(solution)/shard_map/ppermute | solution.py:96
  7.1 23.0 %collective-permute-start = (bf16[176,768]{1,0:T(8,128)(2,1)S(1)}, bf16[176,768]{1,0:T(8,128)(2,1)S(1)}, u32[]{:S(2)}, u32[]{:S(2)}) collective-permute-start(bf16[176,768]{1,0:T(8,128)(2,1)S(1)} %get-tuple-element.101), channel_id=1, source_target_pairs={{0,1},{1,0},{2,3},{3,2},{4,5},{5,4},{6,7},{7,6},{8,9},{9,8},{10,11... | collective-permute-start | bytes 811016 | tf_op jit(solution)/shard_map/ppermute | solution.py:96
  7.3 49.4 %copy-start.6 = (bf16[176,768]{1,0:T(8,128)(2,1)}, bf16[176,768]{1,0:T(8,128)(2,1)S(1)}, u32[]{:S(2)}) copy-start(bf16[176,768]{1,0:T(8,128)(2,1)S(1)} %get-tuple-element.52.refs_0_) | copy-start | bytes 811012
  7.3 74.1 %copy-start.5 = (bf16[176,768]{1,0:T(8,128)(2,1)}, bf16[176,768]{1,0:T(8,128)(2,1)S(1)}, u32[]{:S(2)}) copy-start(bf16[176,768]{1,0:T(8,128)(2,1)S(1)} %get-tuple-element.54.refs_0_) | copy-start | bytes 811012
  7.3 100.4 %copy-start.4 = (bf16[176,768]{1,0:T(8,128)(2,1)}, bf16[176,768]{1,0:T(8,128)(2,1)S(1)}, u32[]{:S(2)}) copy-start(bf16[176,768]{1,0:T(8,128)(2,1)S(1)} %get-tuple-element.69.refs_0_) | copy-start | bytes 811012
  7.3 22.9 %collective-permute-start.1 = (bf16[176,768]{1,0:T(8,128)(2,1)S(1)}, bf16[176,768]{1,0:T(8,128)(2,1)S(1)}, u32[]{:S(2)}, u32[]{:S(2)}) collective-permute-start(bf16[176,768]{1,0:T(8,128)(2,1)S(1)} %get-tuple-element.106.refs_0_), channel_id=1, source_target_pairs={{0,2},{1,3},{2,0},{3,1},{4,6},{5,7},{6,4},{7,5},{8,10},{9,11},{10,... | collective-permute-start | bytes 811016 | tf_op jit(solution)/shard_map/ppermute | solution.py:96
  30.2 25.2 %collective-permute-start.5 = (bf16[176,768]{1,0:T(8,128)(2,1)S(1)}, bf16[176,768]{1,0:T(8,128)(2,1)S(1)}, u32[]{:S(2)}, u32[]{:S(2)}) collective-permute-start(bf16[176,768]{1,0:T(8,128)(2,1)S(1)} %get-tuple-element.49), channel_id=1, source_target_pairs={{0,3},{1,2},{2,1},{3,0},{4,7},{5,6},{6,5},{7,4},{8,11},{9,10},{10,... | collective-permute-start | bytes 811016 | tf_op jit(solution)/shard_map/ppermute | solution.py:96
  32.8 22.5 %collective-permute-start.3 = (bf16[176,768]{1,0:T(8,128)(2,1)S(1)}, bf16[176,768]{1,0:T(8,128)(2,1)S(1)}, u32[]{:S(2)}, u32[]{:S(2)}) collective-permute-start(bf16[176,768]{1,0:T(8,128)(2,1)S(1)} %get-tuple-element.49), channel_id=1, source_target_pairs={{0,1},{1,0},{2,3},{3,2},{4,5},{5,4},{6,7},{7,6},{8,9},{9,8},{10,11... | collective-permute-start | bytes 811016 | tf_op jit(solution)/shard_map/ppermute | solution.py:96
  32.9 22.5 %collective-permute-start.4 = (bf16[176,768]{1,0:T(8,128)(2,1)S(1)}, bf16[176,768]{1,0:T(8,128)(2,1)S(1)}, u32[]{:S(2)}, u32[]{:S(2)}) collective-permute-start(bf16[176,768]{1,0:T(8,128)(2,1)S(1)} %get-tuple-element.50.refs_0_), channel_id=1, source_target_pairs={{0,2},{1,3},{2,0},{3,1},{4,6},{5,7},{6,4},{7,5},{8,10},{9,11},{10,... | collective-permute-start | bytes 811016 | tf_op jit(solution)/shard_map/ppermute | solution.py:96
  40.9 24.1 %collective-permute-start.13 = (bf16[48,16,128]{2,1,0:T(8,128)(2,1)S(1)}, bf16[48,16,128]{2,1,0:T(8,128)(2,1)S(1)}, u32[]{:S(2)}, u32[]{:S(2)}) collective-permute-start(bf16[48,16,128]{2,1,0:T(8,128)(2,1)S(1)} %get-tuple-element.115), channel_id=1, source_target_pairs={{0,1},{1,0},{2,3},{3,2},{4,5},{5,4},{6,7},{7,6},{8,9},{9,8},{10,11... | collective-permute-start | bytes 589832 | tf_op jit(solution)/shard_map/ppermute | solution.py:96
  41.3 27.1 %collective-permute-start.12 = (bf16[48,16,128]{2,1,0:T(8,128)(2,1)S(1)}, bf16[48,16,128]{2,1,0:T(8,128)(2,1)S(1)}, u32[]{:S(2)}, u32[]{:S(2)}) collective-permute-start(bf16[48,16,128]{2,1,0:T(8,128)(2,1)S(1)} %get-tuple-element.116), channel_id=1, source_target_pairs={{0,1},{1,0},{2,3},{3,2},{4,5},{5,4},{6,7},{7,6},{8,9},{9,8},{10,11... | collective-permute-start | bytes 589832 | tf_op jit(solution)/shard_map/ppermute | solution.py:96
  55.4 21.9 %collective-permute-start.8 = (bf16[176,768]{1,0:T(8,128)(2,1)S(1)}, bf16[176,768]{1,0:T(8,128)(2,1)S(1)}, u32[]{:S(2)}, u32[]{:S(2)}) collective-permute-start(bf16[176,768]{1,0:T(8,128)(2,1)S(1)} %get-tuple-element.51), channel_id=1, source_target_pairs={{0,3},{1,2},{2,1},{3,0},{4,7},{5,6},{6,5},{7,4},{8,11},{9,10},{10,... | collective-permute-start | bytes 811016 | tf_op jit(solution)/shard_map/ppermute | solution.py:96
  56.7 20.6 %collective-permute-start.6 = (bf16[176,768]{1,0:T(8,128)(2,1)S(1)}, bf16[176,768]{1,0:T(8,128)(2,1)S(1)}, u32[]{:S(2)}, u32[]{:S(2)}) collective-permute-start(bf16[176,768]{1,0:T(8,128)(2,1)S(1)} %get-tuple-element.51), channel_id=1, source_target_pairs={{0,1},{1,0},{2,3},{3,2},{4,5},{5,4},{6,7},{7,6},{8,9},{9,8},{10,11... | collective-permute-start | bytes 811016 | tf_op jit(solution)/shard_map/ppermute | solution.py:96
  56.7 20.6 %collective-permute-start.7 = (bf16[176,768]{1,0:T(8,128)(2,1)S(1)}, bf16[176,768]{1,0:T(8,128)(2,1)S(1)}, u32[]{:S(2)}, u32[]{:S(2)}) collective-permute-start(bf16[176,768]{1,0:T(8,128)(2,1)S(1)} %get-tuple-element.52.refs_0_), channel_id=1, source_target_pairs={{0,2},{1,3},{2,0},{3,1},{4,6},{5,7},{6,4},{7,5},{8,10},{9,11},{10,... | collective-permute-start | bytes 811016 | tf_op jit(solution)/shard_map/ppermute | solution.py:96
  70.2 16.8 %collective-permute-start.18 = (bf16[48,16,128]{2,1,0:T(8,128)(2,1)}, bf16[48,16,128]{2,1,0:T(8,128)(2,1)}, u32[]{:S(2)}, u32[]{:S(2)}) collective-permute-start(bf16[48,16,128]{2,1,0:T(8,128)(2,1)} %get-tuple-element.113), channel_id=1, source_target_pairs={{0,1},{1,0},{2,3},{3,2},{4,5},{5,4},{6,7},{7,6},{8,9},{9,8},{10,11... | collective-permute-start | bytes 589832 | tf_op jit(solution)/shard_map/ppermute | solution.py:96
  70.2 27.0 %collective-permute-start.17 = (bf16[48,16,128]{2,1,0:T(8,128)(2,1)}, bf16[48,16,128]{2,1,0:T(8,128)(2,1)}, u32[]{:S(2)}, u32[]{:S(2)}) collective-permute-start(bf16[48,16,128]{2,1,0:T(8,128)(2,1)} %get-tuple-element.114), channel_id=1, source_target_pairs={{0,1},{1,0},{2,3},{3,2},{4,5},{5,4},{6,7},{7,6},{8,9},{9,8},{10,11... | collective-permute-start | bytes 589832 | tf_op jit(solution)/shard_map/ppermute | solution.py:96
  77.3 28.6 %collective-permute-start.11 = (bf16[176,768]{1,0:T(8,128)(2,1)S(1)}, bf16[176,768]{1,0:T(8,128)(2,1)S(1)}, u32[]{:S(2)}, u32[]{:S(2)}) collective-permute-start(bf16[176,768]{1,0:T(8,128)(2,1)S(1)} %get-tuple-element.53), channel_id=1, source_target_pairs={{0,3},{1,2},{2,1},{3,0},{4,7},{5,6},{6,5},{7,4},{8,11},{9,10},{10,... | collective-permute-start | bytes 811016 | tf_op jit(solution)/shard_map/ppermute | solution.py:96
  79.6 26.4 %collective-permute-start.9 = (bf16[176,768]{1,0:T(8,128)(2,1)S(1)}, bf16[176,768]{1,0:T(8,128)(2,1)S(1)}, u32[]{:S(2)}, u32[]{:S(2)}) collective-permute-start(bf16[176,768]{1,0:T(8,128)(2,1)S(1)} %get-tuple-element.53), channel_id=1, source_target_pairs={{0,1},{1,0},{2,3},{3,2},{4,5},{5,4},{6,7},{7,6},{8,9},{9,8},{10,11... | collective-permute-start | bytes 811016 | tf_op jit(solution)/shard_map/ppermute | solution.py:96
  81.3 24.6 %collective-permute-start.10 = (bf16[176,768]{1,0:T(8,128)(2,1)S(1)}, bf16[176,768]{1,0:T(8,128)(2,1)S(1)}, u32[]{:S(2)}, u32[]{:S(2)}) collective-permute-start(bf16[176,768]{1,0:T(8,128)(2,1)S(1)} %get-tuple-element.54.refs_0_), channel_id=1, source_target_pairs={{0,2},{1,3},{2,0},{3,1},{4,6},{5,7},{6,4},{7,5},{8,10},{9,11},{10,... | collective-permute-start | bytes 811016 | tf_op jit(solution)/shard_map/ppermute | solution.py:96
  99.5 12.1 %all-to-all-start = ((bf16[96,16,128]{2,1,0:T(8,128)(2,1)}), bf16[96,16,128]{2,1,0:T(8,128)(2,1)S(1)}, u32[]{:S(2)}, u32[]{:S(2)}) async-start(bf16[96,16,128]{2,1,0:T(8,128)(2,1)} %get-tuple-element.121), calls=%async_computation | async-start | bytes 786432 | tf_op jit(solution)/shard_map/all_to_all | solution.py:108
  103.9 16.5 %collective-permute-start.20 = (bf16[48,16,128]{2,1,0:T(8,128)(2,1)}, bf16[48,16,128]{2,1,0:T(8,128)(2,1)}, u32[]{:S(2)}, u32[]{:S(2)}) collective-permute-start(bf16[48,16,128]{2,1,0:T(8,128)(2,1)} %get-tuple-element.111), channel_id=1, source_target_pairs={{0,1},{1,0},{2,3},{3,2},{4,5},{5,4},{6,7},{7,6},{8,9},{9,8},{10,11... | collective-permute-start | bytes 589832 | tf_op jit(solution)/shard_map/ppermute | solution.py:96
  103.9 23.8 %collective-permute-start.19 = (bf16[48,16,128]{2,1,0:T(8,128)(2,1)S(1)}, bf16[48,16,128]{2,1,0:T(8,128)(2,1)}, u32[]{:S(2)}, u32[]{:S(2)}) collective-permute-start(bf16[48,16,128]{2,1,0:T(8,128)(2,1)S(1)} %get-tuple-element.112), channel_id=1, source_target_pairs={{0,1},{1,0},{2,3},{3,2},{4,5},{5,4},{6,7},{7,6},{8,9},{9,8},{10,11... | collective-permute-start | bytes 589832 | tf_op jit(solution)/shard_map/ppermute | solution.py:96
  106.0 25.1 %collective-permute-start.16 = (bf16[176,768]{1,0:T(8,128)(2,1)S(1)}, bf16[176,768]{1,0:T(8,128)(2,1)S(1)}, u32[]{:S(2)}, u32[]{:S(2)}) collective-permute-start(bf16[176,768]{1,0:T(8,128)(2,1)S(1)} %get-tuple-element.68), channel_id=1, source_target_pairs={{0,3},{1,2},{2,1},{3,0},{4,7},{5,6},{6,5},{7,4},{8,11},{9,10},{10,... | collective-permute-start | bytes 811016 | tf_op jit(solution)/shard_map/ppermute | solution.py:96
  107.6 25.8 %collective-permute-start.14 = (bf16[176,768]{1,0:T(8,128)(2,1)S(1)}, bf16[176,768]{1,0:T(8,128)(2,1)S(1)}, u32[]{:S(2)}, u32[]{:S(2)}) collective-permute-start(bf16[176,768]{1,0:T(8,128)(2,1)S(1)} %get-tuple-element.68), channel_id=1, source_target_pairs={{0,1},{1,0},{2,3},{3,2},{4,5},{5,4},{6,7},{7,6},{8,9},{9,8},{10,11... | collective-permute-start | bytes 811016 | tf_op jit(solution)/shard_map/ppermute | solution.py:96
  107.7 23.4 %collective-permute-start.15 = (bf16[176,768]{1,0:T(8,128)(2,1)S(1)}, bf16[176,768]{1,0:T(8,128)(2,1)S(1)}, u32[]{:S(2)}, u32[]{:S(2)}) collective-permute-start(bf16[176,768]{1,0:T(8,128)(2,1)S(1)} %get-tuple-element.69.refs_0_), channel_id=1, source_target_pairs={{0,2},{1,3},{2,0},{3,1},{4,6},{5,7},{6,4},{7,5},{8,10},{9,11},{10,... | collective-permute-start | bytes 811016 | tf_op jit(solution)/shard_map/ppermute | solution.py:96
  111.5 19.3 %all-to-all-start.1 = ((bf16[96,16,128]{2,1,0:T(8,128)(2,1)}), bf16[96,16,128]{2,1,0:T(8,128)(2,1)S(1)}, u32[]{:S(2)}, u32[]{:S(2)}) async-start(bf16[96,16,128]{2,1,0:T(8,128)(2,1)} %get-tuple-element.120), calls=%async_computation.1 | async-start | bytes 786432 | tf_op jit(solution)/shard_map/all_to_all | solution.py:108
  128.8 10.6 %collective-permute-start.22 = (bf16[48,16,128]{2,1,0:T(8,128)(2,1)S(1)}, bf16[48,16,128]{2,1,0:T(8,128)(2,1)S(1)}, u32[]{:S(2)}, u32[]{:S(2)}) collective-permute-start(bf16[48,16,128]{2,1,0:T(8,128)(2,1)S(1)} %get-tuple-element.109), channel_id=1, source_target_pairs={{0,1},{1,0},{2,3},{3,2},{4,5},{5,4},{6,7},{7,6},{8,9},{9,8},{10,11... | collective-permute-start | bytes 589832 | tf_op jit(solution)/shard_map/ppermute | solution.py:96
  128.9 12.6 %collective-permute-start.21 = (bf16[48,16,128]{2,1,0:T(8,128)(2,1)S(1)}, bf16[48,16,128]{2,1,0:T(8,128)(2,1)S(1)}, u32[]{:S(2)}, u32[]{:S(2)}) collective-permute-start(bf16[48,16,128]{2,1,0:T(8,128)(2,1)S(1)} %get-tuple-element.110), channel_id=1, source_target_pairs={{0,1},{1,0},{2,3},{3,2},{4,5},{5,4},{6,7},{7,6},{8,9},{9,8},{10,11... | collective-permute-start | bytes 589832 | tf_op jit(solution)/shard_map/ppermute | solution.py:96
  142.5 7.9 %collective-permute-start.23 = (bf16[48,16,128]{2,1,0:T(8,128)(2,1)S(1)}, bf16[48,16,128]{2,1,0:T(8,128)(2,1)S(1)}, u32[]{:S(2)}, u32[]{:S(2)}) collective-permute-start(bf16[48,16,128]{2,1,0:T(8,128)(2,1)S(1)} %get-tuple-element.107), channel_id=1, source_target_pairs={{0,1},{1,0},{2,3},{3,2},{4,5},{5,4},{6,7},{7,6},{8,9},{9,8},{10,11... | collective-permute-start | bytes 589832 | tf_op jit(solution)/shard_map/ppermute | solution.py:96
  142.9 10.4 %collective-permute-start.24 = (bf16[48,16,128]{2,1,0:T(8,128)(2,1)S(1)}, bf16[48,16,128]{2,1,0:T(8,128)(2,1)S(1)}, u32[]{:S(2)}, u32[]{:S(2)}) collective-permute-start(bf16[48,16,128]{2,1,0:T(8,128)(2,1)S(1)} %get-tuple-element.108), channel_id=1, source_target_pairs={{0,1},{1,0},{2,3},{3,2},{4,5},{5,4},{6,7},{7,6},{8,9},{9,8},{10,11... | collective-permute-start | bytes 589832 | tf_op jit(solution)/shard_map/ppermute | solution.py:96
  167.4 11.7 %all-to-all-start.3 = ((bf16[96,16,128]{2,1,0:T(8,128)(2,1)}), bf16[96,16,128]{2,1,0:T(8,128)(2,1)S(1)}, u32[]{:S(2)}, u32[]{:S(2)}) async-start(bf16[96,16,128]{2,1,0:T(8,128)(2,1)} %get-tuple-element.119), calls=%async_computation.3 | async-start | bytes 786432 | tf_op jit(solution)/shard_map/all_to_all | solution.py:108
  179.2 11.7 %all-to-all-start.4 = ((bf16[96,16,128]{2,1,0:T(8,128)(2,1)}), bf16[96,16,128]{2,1,0:T(8,128)(2,1)S(1)}, u32[]{:S(2)}, u32[]{:S(2)}) async-start(bf16[96,16,128]{2,1,0:T(8,128)(2,1)} %get-tuple-element.117), calls=%async_computation.4 | async-start | bytes 786432 | tf_op jit(solution)/shard_map/all_to_all | solution.py:108
  (24 other events, 241.9 us)
where the time goes:
time: 193 us; the launch traced here: 192 us
  waiting for transfers between devices  89.3 us (46%)
  starting transfers between devices  48.2 us (25%)
  Pallas kernels  26 us (13%)
  blocking collectives  11.6 us (6%)
  local copies, waits for them, and re-layouts  10.3 us (5%)
  other arithmetic  6 us (3%)
    ppermute x25, waiting for transfers between devices, swap(): lax.ppermute(value, 'band', [(band, band ^ step) for band in range(bands)])  71.8 us
    ppermute x25, starting transfers between devices, swap(): lax.ppermute(value, 'band', [(band, band ^ step) for band in range(bands)])  33.9 us
    pallas_call x5, Pallas kernels, parity_sums(): pl.pallas_call(functools.partial(sums_kernel, rows, fields, start, pairs)...  26 us
    all_to_all x4, waiting for transfers between devices, redistribute(): lax.all_to_all(grid, 'mset', split_axis=0, concat_axis=1, tiled=True)  17.4 us
    all_to_all x4, starting transfers between devices, redistribute(): lax.all_to_all(grid, 'mset', split_axis=0, concat_axis=1, tiled=True)  14.3 us
    all_to_all x1, blocking collectives, redistribute(): lax.all_to_all(grid, 'mset', split_axis=0, concat_axis=1, tiled=True)  11.6 us
    slice x5, local copies, waits for them, and re-layouts, shards(): halves = (own, [swap(own[:middle], 1), swap(own[middle:], 1)])  5.72 us
    convert_element_type x2, other arithmetic, combine(): return jnp.where(valid_lat, grid, 0.0).astype(jnp.bfloat16)  4.84 us
  transfers between devices with their start and end apart: 29, of which 14 were waited for; matrix products, arithmetic and copies ran while one was open for 4% of the time, Pallas kernels for 14%

commit v1 on v0

v1 whole, which is shorter than its diff:
```python
import functools

import jax
import jax.numpy as jnp
from jax import lax
from jax.experimental import pallas as pl
from jax.experimental.pallas import tpu as pltpu
from jax.sharding import PartitionSpec as P

TRUNC = 1279
CHUNKS = (8, 8, 8, 8, 4, 4)
GROUPS = ((0, 1), (2,), (3, 4, 5))


def owner_limits(wavenumber, parity):
    first = jnp.maximum((TRUNC - wavenumber - parity) // 2 + 1, 0)
    second = jnp.maximum((wavenumber - parity) // 2 + 1, 0)
    return first, first + second


def sums_kernel(rows, fields, start, order, first, total, *refs):
    blocks, (legendre, out, gathered, flipped, sums) = refs[:-5], refs[-5:]
    pairs, depth, lats = legendre.shape
    step = 0
    for part in blocks:
        for row in range(0, part.shape[0], rows):
            place = pl.ds(pl.multiple_of(order[step] * rows, 16), rows)
            gathered[place, :] = part[pl.ds(row, rows), :]
            step += 1
    flipped[...] = gathered[...].T
    row = lax.broadcasted_iota(jnp.int32, (depth, lats), 0)
    for pair in range(pairs):
        here = legendre[pair].astype(jnp.float32)
        in_first = row < first[start + pair]
        in_any = row < total[start + pair]
        part_first = jnp.where(in_first, here, 0.0)
        part_second = jnp.where(in_any, here - part_first, 0.0)
        both = jnp.concatenate([part_first, part_second], axis=1).astype(jnp.bfloat16)
        product = jnp.dot(
            flipped[pair * fields : (pair + 1) * fields, :], both, preferred_element_type=jnp.float32
        )
        sums[:, 2 * pair, :] = product[:, :lats]
        sums[:, 2 * pair + 1, :] = product[:, lats:]
    out[...] = sums[...].astype(out.dtype)


def parity_sums(blocks, rows, order, first, total, legendre, start, pairs, fields):
    columns = blocks[0].shape[1]
    _, depth, lats = legendre.shape
    legendre = legendre[start : start + pairs]
    vmem = pl.BlockSpec(memory_space=pltpu.VMEM)
    scalar = pl.BlockSpec(memory_space=pltpu.SMEM)
    return pl.pallas_call(
        functools.partial(sums_kernel, rows, fields, start),
        in_specs=[scalar] * 3 + [vmem] * (len(blocks) + 1),
        out_specs=vmem,
        scratch_shapes=[
            pltpu.VMEM((depth, columns), jnp.bfloat16),
            pltpu.VMEM((columns, depth), jnp.bfloat16),
            pltpu.VMEM((fields, 2 * pairs, lats), jnp.float32),
        ],
        out_shape=jax.ShapeDtypeStruct((fields, 2 * pairs, lats), jnp.bfloat16),
        compiler_params=pltpu.CompilerParams(vmem_limit_bytes=24 * 2**20),
        cost_estimate=pl.CostEstimate(flops=pairs * 10**11, bytes_accessed=pairs * 100 * 2**20, transcendentals=0),
        name="parity_sums",
    )(order, first, total, *blocks, legendre)


def shards(coeffs, legendre, wavenumber, band_rows):
    bands = lax.axis_size("band")
    sets = lax.axis_size("mset")
    me = lax.axis_index("band")
    parity = me % 2
    pair_count, depth, lats = legendre.shape
    rows = coeffs.shape[1]
    fields = coeffs.shape[2] // pair_count
    first, total = owner_limits(wavenumber, parity)
    order = (me if rows % 16 == 0 else 0) ^ jnp.arange(bands, dtype=jnp.int32)
    valid_lat = jnp.arange(lats, dtype=jnp.int32) < band_rows[0]
    assert sum(CHUNKS) == pair_count
    plan = [(sum(CHUNKS[:chunk]), pairs) for chunk, pairs in enumerate(CHUNKS)]
    def swap(value, step):
        return lax.ppermute(value, "band", [(band, band ^ step) for band in range(bands)])

    def payloads_of(chunk):
        start, pairs = plan[chunk]
        place, shape = (0, start * fields), (1, rows, pairs * fields)
        return [lax.dynamic_slice(coeffs, (which, *place), shape)[0] for which in (parity, 1 - parity)]

    def combine(own, partner):
        own, partner = own.astype(jnp.float32), partner.astype(jnp.float32)
        grid = jnp.where(parity == 0, own + partner, partner - own)
        return jnp.where(valid_lat, grid, 0.0).astype(jnp.bfloat16)

    def redistribute(grid):
        piece = lax.all_to_all(grid, "mset", split_axis=0, concat_axis=1, tiled=True)
        return piece.reshape(fields // sets, sets, -1, lats)

    def spread(mine, near):
        held = [mine, near]
        for bit in [2**power for power in range(1, bands.bit_length() - 1)]:
            held.append(swap(jnp.concatenate(held), bit))
        return held

    near, far, own_rows = {}, {}, {}

    def send_direct(payload):
        far[0] = [payload[0]] + [swap(payload[step % 2], step) for step in range(1, bands)]
        near[0] = far[0][1]

    def send_near(chunk):
        payload = payloads_of(chunk)
        if chunk >= 2:
            earlier = far[chunk - 3] if chunk >= 3 else near[chunk - 1]
            payload, earlier = lax.optimization_barrier((payload, earlier))
            if chunk >= 3:
                far[chunk - 3] = earlier
            else:
                near[chunk - 1] = earlier
        own_rows[chunk] = payload[0]
        near[chunk] = swap(payload[1], 1)

    def send_far(chunk):
        parts = [own_rows[chunk], near[chunk]]
        if chunk >= 2:
            parts, far[chunk - 2] = lax.optimization_barrier((parts, far[chunk - 2]))
        far[chunk] = spread(*parts)

    first_rows = payloads_of(0)
    coeffs, first_rows = lax.optimization_barrier((coeffs, first_rows))
    send_direct(first_rows)
    send_near(1)
    send_near(2)
    send_far(1)
    pieces, ready = [], []
    for chunk, (start, pairs) in enumerate(plan):
        if chunk + 2 < len(plan):
            send_far(chunk + 2)
        if 3 <= chunk + 3 < len(plan):
            send_near(chunk + 3)
        blocks = far[chunk]
        if rows % 16:
            stacked = jnp.concatenate(blocks).reshape(bands, rows, -1)
            blocks = [jnp.take(stacked, me ^ jnp.arange(bands), axis=0).reshape(bands * rows, -1)]
        own = parity_sums(
            blocks, rows if rows % 16 == 0 else depth, order, first, total, legendre, start, pairs, fields
        )
        ready.append((own, swap(own, 1)))
        if chunk == GROUPS[len(pieces)][-1]:
            ready, pieces[-1:] = lax.optimization_barrier((ready, pieces[-1:]))
            pieces.append(redistribute(jnp.concatenate([combine(*part) for part in ready], axis=1)))
            ready = []
    return jnp.concatenate(pieces, axis=2).reshape(fields // sets, sets * 2 * pair_count, lats)


def solution(mesh):
    in_specs = (P(None, "band", "mset"), P("mset", None, "band"), P("mset"), P("band"))
    out_specs = P("mset", None, "band")
    return jax.shard_map(shards, mesh=mesh, in_specs=in_specs, out_specs=out_specs, check_vma=False)
```

time: 193 us -> 166 us (0.86)
  waiting for transfers between devices: 89.3 us -> 63.2 us
  starting transfers between devices: 48.2 us -> 34.9 us
  other arithmetic: 6 us -> 17.1 us
  Pallas kernels: 26 us -> 17.5 us
  local copies, waits for them, and re-layouts: 10.3 us -> 15.1 us
  blocking collectives: 11.6 us -> 16.1 us
    all_to_all x4 -> x2, waiting for transfers between devices: 17.4 us -> 0.01 us  [redistribute(): lax.all_to_all(grid, 'mset', split_axis=0, concat_axis=1, tiled=True)]
    concatenate x0 -> x8, other arithmetic: none -> 10.3 us  [the longest x5 7.8 us: spread(): held.append(swap(jnp.concatenate(held), bit))]
    ppermute x25 -> x19, waiting for transfers between devices: 71.8 us -> 63.2 us  [swap(): lax.ppermute(value, 'band', [(band, band ^ step) for band in range(bands)])]
    pallas_call x5 -> x6, Pallas kernels: 26 us -> 17.5 us  [parity_sums(): pl.pallas_call(functools.partial(sums_kernel, rows, fields, start), in_sp...]
    ppermute x25 -> x19, starting transfers between devices: 33.9 us -> 26.6 us  [swap(): lax.ppermute(value, 'band', [(band, band ^ step) for band in range(bands)])]
    all_to_all x4 -> x2, starting transfers between devices: 14.3 us -> 8.31 us  [redistribute(): lax.all_to_all(grid, 'mset', split_axis=0, concat_axis=1, tiled=True)]
    all_to_all x1, blocking collectives: 11.6 us -> 16.1 us  [redistribute(): lax.all_to_all(grid, 'mset', split_axis=0, concat_axis=1, tiled=True)]
    squeeze x1 -> x3, local copies, waits for them, and re-layouts: 1.91 us -> 6.19 us  [payloads_of(): lax.dynamic_slice(coeffs, (which, *place), shape)[0]]
  transfers between devices with their start and end apart: 29 -> 21, of which waited for: 14 -> 9; matrix products, arithmetic and copies ran while one was open for 4% -> 15% of each run, Pallas kernels for 14% -> 11%
where the time goes in v1:
time: 166 us; the launch traced here: 165 us
  waiting for transfers between devices  63.2 us (38%)
  starting transfers between devices  34.9 us (21%)
  Pallas kernels  17.5 us (11%)
  other arithmetic  17.1 us (10%)
  blocking collectives  16.1 us (10%)
  local copies, waits for them, and re-layouts  15.1 us (9%)
    ppermute x19, waiting for transfers between devices, swap(): lax.ppermute(value, 'band', [(band, band ^ step) for band in range(bands)])  63.2 us
    ppermute x19, starting transfers between devices, swap(): lax.ppermute(value, 'band', [(band, band ^ step) for band in range(bands)])  26.6 us
    pallas_call x6, Pallas kernels, parity_sums(): pl.pallas_call(functools.partial(sums_kernel, rows, fields, start), in_sp...  17.5 us
    all_to_all x1, blocking collectives, redistribute(): lax.all_to_all(grid, 'mset', split_axis=0, concat_axis=1, tiled=True)  16.1 us
    all_to_all x2, starting transfers between devices, redistribute(): lax.all_to_all(grid, 'mset', split_axis=0, concat_axis=1, tiled=True)  8.31 us
    concatenate x5, other arithmetic, spread(): held.append(swap(jnp.concatenate(held), bit))  7.8 us
    slice x2, local copies, waits for them, and re-layouts, parity_sums(): legendre = legendre[start:start + pairs]  7.36 us
    convert_element_type x4, other arithmetic, combine(): return jnp.where(valid_lat, grid, 0.0).astype(jnp.bfloat16)  6.32 us
  transfers between devices with their start and end apart: 21, of which 9 were waited for; matrix products, arithmetic and copies ran while one was open for 15% of the time, Pallas kernels for 11%

profile of v1, /device:TPU:0, one launch (start us, length us, event | category | flops | bytes accessed | tf_op | source)
XLA Modules:
  0.0 164.8 jit_solution(11693254110141877634)
XLA Ops:
  1.8 3.0 %collective-permute-start.2 = (bf16[176,768]{1,0:T(8,128)(2,1)}, bf16[176,768]{1,0:T(8,128)(2,1)}, u32[]{:S(2)}, u32[]{:S(2)}) collective-permute-start(bf16[176,768]{1,0:T(8,128)(2,1)} %get-tuple-element.66), channel_id=1, source_target_pairs={{0,1},{1,0},{2,3},{3,2},{4,5},{5,4},{6,7},{7,6},{8,9},{9,8},{10,11... | collective-permute-start | bytes 811016 | tf_op jit(solution)/shard_map/ppermute | solution.py:83
  4.8 2.5 %collective-permute-start.4 = (bf16[176,768]{1,0:T(8,128)(2,1)}, bf16[176,768]{1,0:T(8,128)(2,1)}, u32[]{:S(2)}, u32[]{:S(2)}) collective-permute-start(bf16[176,768]{1,0:T(8,128)(2,1)} %get-tuple-element.66), channel_id=1, source_target_pairs={{0,3},{1,2},{2,1},{3,0},{4,7},{5,6},{6,5},{7,4},{8,11},{9,10},{10,... | collective-permute-start | bytes 811016 | tf_op jit(solution)/shard_map/ppermute | solution.py:83
  7.3 2.4 %dynamic-slice_bitcast_fusion = (bf16[176,768]{1,0:T(8,128)(2,1)S(1)}, bf16[176,768]{1,0:T(8,128)(2,1)S(1)}, bf16[176,768]{1,0:T(8,128)(2,1)}, bf16[176,768]{1,0...) fusion(bf16[2,176,3840]{2,1,0:T(8,128)(2,1)} %param.4, s32[]{:T(128)S(6)} %select_n.86, s32[]{:T(128)S(6)} %select_n.87), kind=kLoop, calls=%fused_computation.38 | loop fusion | bytes 3244040 | tf_op jit(solution)/shard_map/squeeze | solution.py:88
  11.6 4.8 %fusion.18 = (bf16[8,704,128]{2,1,0:T(8,128)(2,1)}, bf16[8,704,128]{2,1,0:T(8,128)(2,1)S(1)}, bf16[8,704,128]{2,1,0:T(8,128)(2,1)}, bf16[8,704,128]{2,1,0:T(8,128)(2,1)S(1)}) fusion(bf16[40,704,128]{2,1,0:T(8,128)(2,1)} %param.5), kind=kLoop, calls=%fused_computation.62 | loop fusion | bytes 11534336 | tf_op jit(solution)/shard_map/slice | solution.py:50
  17.0 2.6 %fusion.19 = (bf16[4,704,128]{2,1,0:T(8,128)(2,1)}, bf16[4,704,128]{2,1,0:T(8,128)(2,1)}) fusion(bf16[40,704,128]{2,1,0:T(8,128)(2,1)} %param.5), kind=kLoop, calls=%fused_computation.63 | loop fusion | bytes 2883584 | tf_op jit(solution)/shard_map/slice | solution.py:50
  19.6 9.4 %collective-permute-done.refs_1_ = bf16[176,768]{1,0:T(8,128)(2,1)} collective-permute-done((bf16[176,768]{1,0:T(8,128)(2,1)S(1)}, bf16[176,768]{1,0:T(8,128)(2,1)}, u32[]{:S(2)}, u32[]{:S(2)}) %collective-permute-start) | collective-permute-done | bytes 270368 | tf_op jit(solution)/shard_map/ppermute | solution.py:83
  29.5 2.0 %dynamic-slice_bitcast_fusion.8 = (bf16[176,384]{1,0:T(8,128)(2,1)}, bf16[176,384]{1,0:T(8,128)(2,1)}, bf16[176,384]{1,0:T(8,128)(2,1)}, bf16[176,384]{1,0:T(8,128)(2,1)}) fusion(bf16[2,176,3840]{2,1,0:T(8,128)(2,1)} %param.4, s32[]{:T(128)S(6)} %select_n.87, s32[]{:T(128)S(6)} %select_n.86), kind=kLoop, calls=%fused_computation.46 | loop fusion | bytes 1081352 | tf_op jit(solution)/shard_map/squeeze | solution.py:88
  31.6 1.8 %pad_maximum_fusion.3 = bf16[352,768]{1,0:T(8,128)(2,1)} fusion(bf16[176,768]{1,0:T(8,128)(2,1)} %collective-permute-done.refs_1_, bf16[176,768]{1,0:T(8,128)(2,1)S(1)} %get-tuple-element.91.refs_0_), kind=kLoop, calls=%fused_computation.23 | loop fusion | flops 1081344 | bytes 1081344 | tf_op jit(solution)/shard_map/concatenate | solution.py:102
  33.4 3.0 %collective-permute-start.6 = (bf16[352,768]{1,0:T(8,128)(2,1)}, bf16[352,768]{1,0:T(8,128)(2,1)}, u32[]{:S(2)}, u32[]{:S(2)}) collective-permute-start(bf16[352,768]{1,0:T(8,128)(2,1)} %pad_maximum_fusion.3), channel_id=1, source_target_pairs={{0,2},{1,3},{2,0},{3,1},{4,6},{5,7},{6,4},{7,5},{8,10},{9,11},{10,... | collective-permute-start | bytes 1622024 | tf_op jit(solution)/shard_map/ppermute | solution.py:83
  37.5 3.4 %parity_sums.7 = bf16[96,16,128]{2,1,0:T(8,128)(2,1)} custom-call(s32[4]{0:T(128)S(1)} %iota_xor_fusion.order, s32[40]{0:T(128)S(1)} %get-tuple-element.120.first, s32[40]{0:T(128)S(1)} %get-tuple-element.119.total, bf16[176,768]{1,0:T(8,128)(2,1)S(1)} %get-tuple-element.87.refs_0_, bf16[176,768]{1,0:T(8,128)(2,1)} %collective-permute-done.2.refs_1_, ...), custom_call_target="tpu_custom_call" | custom-call | flops 799999983616 | bytes 838860800 | tf_op jit(solution)/shard_map/parity_sums/pallas_call | solution.py:53
  40.9 2.0 %collective-permute-start.10 = (bf16[96,16,128]{2,1,0:T(8,128)(2,1)}, bf16[96,16,128]{2,1,0:T(8,128)(2,1)}, u32[]{:S(2)}, u32[]{:S(2)}) collective-permute-start(bf16[96,16,128]{2,1,0:T(8,128)(2,1)} %parity_sums.7), channel_id=1, source_target_pairs={{0,1},{1,0},{2,3},{3,2},{4,5},{5,4},{6,7},{7,6},{8,9},{9,8},{10,11... | collective-permute-start | bytes 1179656 | tf_op jit(solution)/shard_map/ppermute | solution.py:83
  44.7 2.0 %collective-permute-start.8 = (bf16[352,768]{1,0:T(8,128)(2,1)}, bf16[352,768]{1,0:T(8,128)(2,1)}, u32[]{:S(2)}, u32[]{:S(2)}) collective-permute-start(bf16[352,768]{1,0:T(8,128)(2,1)} %pad_maximum_fusion.4), channel_id=1, source_target_pairs={{0,2},{1,3},{2,0},{3,1},{4,6},{5,7},{6,4},{7,5},{8,10},{9,11},{10,... | collective-permute-start | bytes 1622024 | tf_op jit(solution)/shard_map/ppermute | solution.py:83
  46.7 14.1 %collective-permute-done.6.refs_2_ = bf16[352,768]{1,0:T(8,128)(2,1)} collective-permute-done((bf16[352,768]{1,0:T(8,128)(2,1)}, bf16[352,768]{1,0:T(8,128)(2,1)}, u32[]{:S(2)}, u32[]{:S(2)}) %collective-permute-start.6) | collective-permute-done | bytes 540704 | tf_op jit(solution)/shard_map/ppermute | solution.py:83
  60.9 3.3 %parity_sums.8 = bf16[96,16,128]{2,1,0:T(8,128)(2,1)} custom-call(s32[4]{0:T(128)S(1)} %iota_xor_fusion.order, s32[40]{0:T(128)S(1)} %get-tuple-element.120.first, s32[40]{0:T(128)S(1)} %get-tuple-element.119.total, bf16[176,768]{1,0:T(8,128)(2,1)S(1)} %get-tuple-element.91.refs_0_, bf16[176,768]{1,0:T(8,128)(2,1)} %collective-permute-done.refs_1_, ...), custom_call_target="tpu_custom_call" | custom-call | flops 799999983616 | bytes 838860800 | tf_op jit(solution)/shard_map/parity_sums/pallas_call | solution.py:53
  64.2 2.0 %collective-permute-start.11 = (bf16[96,16,128]{2,1,0:T(8,128)(2,1)}, bf16[96,16,128]{2,1,0:T(8,128)(2,1)}, u32[]{:S(2)}, u32[]{:S(2)}) collective-permute-start(bf16[96,16,128]{2,1,0:T(8,128)(2,1)} %parity_sums.8), channel_id=1, source_target_pairs={{0,1},{1,0},{2,3},{3,2},{4,5},{5,4},{6,7},{7,6},{8,9},{9,8},{10,11... | collective-permute-start | bytes 1179656 | tf_op jit(solution)/shard_map/ppermute | solution.py:83
  66.2 1.8 %pad_maximum_fusion.5 = bf16[352,768]{1,0:T(8,128)(2,1)} fusion(bf16[176,768]{1,0:T(8,128)(2,1)} %collective-permute-done.5.refs_1_, bf16[176,768]{1,0:T(8,128)(2,1)S(1)} %copy-done.2), kind=kLoop, calls=%fused_computation.25 | loop fusion | flops 1081344 | bytes 1081344 | tf_op jit(solution)/shard_map/concatenate | solution.py:102
  69.0 9.3 %collective-permute-done.7.refs_1_ = bf16[176,384]{1,0:T(8,128)(2,1)} collective-permute-done((bf16[176,384]{1,0:T(8,128)(2,1)}, bf16[176,384]{1,0:T(8,128)(2,1)}, u32[]{:S(2)}, u32[]{:S(2)}) %collective-permute-start.7) | collective-permute-done | bytes 135200 | tf_op jit(solution)/shard_map/ppermute | solution.py:83
  78.3 5.8 %collective-permute-done.8.refs_2_ = bf16[352,768]{1,0:T(8,128)(2,1)} collective-permute-done((bf16[352,768]{1,0:T(8,128)(2,1)}, bf16[352,768]{1,0:T(8,128)(2,1)}, u32[]{:S(2)}, u32[]{:S(2)}) %collective-permute-start.8) | collective-permute-done | bytes 540704 | tf_op jit(solution)/shard_map/ppermute | solution.py:83
  84.1 3.3 %parity_sums.6 = bf16[96,16,128]{2,1,0:T(8,128)(2,1)} custom-call(s32[4]{0:T(128)S(1)} %iota_xor_fusion.order, s32[40]{0:T(128)S(1)} %get-tuple-element.120.first, s32[40]{0:T(128)S(1)} %get-tuple-element.119.total, bf16[176,768]{1,0:T(8,128)(2,1)S(1)} %copy-done.4, bf16[176,768]{1,0:T(8,128)(2,1)} %collective-permute-done.1.refs_1_, ...), custom_call_target="tpu_custom_call" | custom-call | flops 799999983616 | bytes 838860800 | tf_op jit(solution)/shard_map/parity_sums/pallas_call | solution.py:53
  87.4 2.0 %collective-permute-start.12 = (bf16[176,384]{1,0:T(8,128)(2,1)S(1)}, bf16[176,384]{1,0:T(8,128)(2,1)S(1)}, u32[]{:S(2)}, u32[]{:S(2)}) collective-permute-start(bf16[176,384]{1,0:T(8,128)(2,1)S(1)} %copy-done.10), channel_id=1, source_target_pairs={{0,1},{1,0},{2,3},{3,2},{4,5},{5,4},{6,7},{7,6},{8,9},{9,8},{10,11... | collective-permute-start | bytes 405512 | tf_op jit(solution)/shard_map/ppermute | solution.py:83
  94.8 4.2 %all-to-all-start = ((bf16[96,32,128]{2,1,0:T(8,128)(2,1)}), bf16[96,32,128]{2,1,0:T(8,128)(2,1)}, u32[]{:S(2)}, u32[]{:S(2)}) async-start(bf16[96,32,128]{2,1,0:T(8,128)(2,1)} %pad_maximum_fusion.1), calls=%async_computation | async-start | bytes 1572864 | tf_op jit(solution)/shard_map/all_to_all | solution.py:96
  99.0 13.0 %collective-permute-done.12.refs_1_ = bf16[176,384]{1,0:T(8,128)(2,1)S(1)} collective-permute-done((bf16[176,384]{1,0:T(8,128)(2,1)S(1)}, bf16[176,384]{1,0:T(8,128)(2,1)S(1)}, u32[]{:S(2)}, u32[]{:S(2)}) %collective-permute-start.12) | collective-permute-done | bytes 135200 | tf_op jit(solution)/shard_map/ppermute | solution.py:83
  114.2 3.3 %parity_sums.9 = bf16[96,16,128]{2,1,0:T(8,128)(2,1)} custom-call(s32[4]{0:T(128)S(1)} %iota_xor_fusion.order, s32[40]{0:T(128)S(1)} %get-tuple-element.120.first, s32[40]{0:T(128)S(1)} %get-tuple-element.119.total, bf16[176,768]{1,0:T(8,128)(2,1)S(1)} %copy-done.3, bf16[176,768]{1,0:T(8,128)(2,1)} %collective-permute-done.5.refs_1_, ...), custom_call_target="tpu_custom_call" | custom-call | flops 799999983616 | bytes 838860800 | tf_op jit(solution)/shard_map/parity_sums/pallas_call | solution.py:53
  117.6 2.5 %collective-permute-start.14 = (bf16[96,16,128]{2,1,0:T(8,128)(2,1)}, bf16[96,16,128]{2,1,0:T(8,128)(2,1)}, u32[]{:S(2)}, u32[]{:S(2)}) collective-permute-start(bf16[96,16,128]{2,1,0:T(8,128)(2,1)} %parity_sums.9), channel_id=1, source_target_pairs={{0,1},{1,0},{2,3},{3,2},{4,5},{5,4},{6,7},{7,6},{8,9},{9,8},{10,11... | collective-permute-start | bytes 1179656 | tf_op jit(solution)/shard_map/ppermute | solution.py:83
  120.1 4.6 %collective-permute-done.15.refs_2_ = bf16[352,384]{1,0:T(8,128)(2,1)} collective-permute-done((bf16[352,384]{1,0:T(8,128)(2,1)}, bf16[352,384]{1,0:T(8,128)(2,1)}, u32[]{:S(2)}, u32[]{:S(2)}) %collective-permute-start.15) | collective-permute-done | bytes 270368 | tf_op jit(solution)/shard_map/ppermute | solution.py:83
  124.7 2.5 %parity_sums.10 = bf16[96,8,128]{2,1,0:T(8,128)(2,1)} custom-call(s32[4]{0:T(128)S(1)} %iota_xor_fusion.order, s32[40]{0:T(128)S(1)} %get-tuple-element.120.first, s32[40]{0:T(128)S(1)} %get-tuple-element.119.total, bf16[176,384]{1,0:T(8,128)(2,1)S(1)} %copy-done.9, bf16[176,384]{1,0:T(8,128)(2,1)} %collective-permute-done.7.refs_1_, ...), custom_call_target="tpu_custom_call" | custom-call | flops 399999991808 | bytes 419430400 | tf_op jit(solution)/shard_map/parity_sums/pallas_call | solution.py:53
  127.2 2.1 %fusion.8 = bf16[96,16,128]{2,1,0:T(8,128)(2,1)} fusion(bf16[96,16,128]{2,1,0:T(8,128)(2,1)} %collective-permute-done.9, bf16[96,16,128]{2,1,0:T(8,128)(2,1)} %parity_sums.6, pred[]{:T(512)S(6)} %eq.4, pred[128]{0:T(512)(128)(4,1)S(1)} %copy-done.12), kind=kLoop, calls=%fused_computation.17 | loop fusion | flops 1376256 | bytes 1179777 | tf_op jit(solution)/shard_map/convert_element_type | solution.py:93
  129.3 4.1 %all-to-all-start.1 = ((bf16[96,16,128]{2,1,0:T(8,128)(2,1)}), bf16[96,16,128]{2,1,0:T(8,128)(2,1)}, u32[]{:S(2)}, u32[]{:S(2)}) async-start(bf16[96,16,128]{2,1,0:T(8,128)(2,1)} %fusion.8), calls=%async_computation.1 | async-start | bytes 786432 | tf_op jit(solution)/shard_map/all_to_all | solution.py:96
  135.2 2.0 %collective-permute-start.18 = (bf16[96,8,128]{2,1,0:T(8,128)(2,1)S(1)}, bf16[96,8,128]{2,1,0:T(8,128)(2,1)S(1)}, u32[]{:S(2)}, u32[]{:S(2)}) collective-permute-start(bf16[96,8,128]{2,1,0:T(8,128)(2,1)S(1)} %parity_sums.11), channel_id=1, source_target_pairs={{0,1},{1,0},{2,3},{3,2},{4,5},{5,4},{6,7},{7,6},{8,9},{9,8},{10,11... | collective-permute-start | bytes 589832 | tf_op jit(solution)/shard_map/ppermute | solution.py:83
  137.2 2.4 %collective-permute-done.16 = bf16[96,8,128]{2,1,0:T(8,128)(2,1)} collective-permute-done((bf16[96,8,128]{2,1,0:T(8,128)(2,1)}, bf16[96,8,128]{2,1,0:T(8,128)(2,1)}, u32[]{:S(2)}, u32[]{:S(2)}) %collective-permute-start.16) | collective-permute-done | bytes 196640 | tf_op jit(solution)/shard_map/ppermute | solution.py:83
  139.6 3.6 %collective-permute-done.18 = bf16[96,8,128]{2,1,0:T(8,128)(2,1)S(1)} collective-permute-done((bf16[96,8,128]{2,1,0:T(8,128)(2,1)S(1)}, bf16[96,8,128]{2,1,0:T(8,128)(2,1)S(1)}, u32[]{:S(2)}, u32[]{:S(2)}) %collective-permute-start.18) | collective-permute-done | bytes 196640 | tf_op jit(solution)/shard_map/ppermute | solution.py:83
  145.8 16.1 %all_to_all.45 = bf16[96,32,128]{2,1,0:T(8,128)(2,1)S(1)} all-to-all(bf16[96,32,128]{2,1,0:T(8,128)(2,1)S(1)} %pad_maximum_fusion.2), channel_id=1, replica_groups=mesh['mset'=8,'band'=4] {'mset'}, dimensions={0} | all-to-all | bytes 1572864 | tf_op jit(solution)/shard_map/all_to_all | solution.py:96
  (68 shorter events, 22.9 us)
Async XLA Ops:
  1.8 9.8 %copy-start.14 = (s32[40]{0:T(128)S(1)}, s32[40]{0:T(128)}, u32[]{:S(2)}) copy-start(s32[40]{0:T(128)} %param.6) | copy-start | bytes 484
  1.8 34.7 %collective-permute-start.2 = (bf16[176,768]{1,0:T(8,128)(2,1)}, bf16[176,768]{1,0:T(8,128)(2,1)}, u32[]{:S(2)}, u32[]{:S(2)}) collective-permute-start(bf16[176,768]{1,0:T(8,128)(2,1)} %get-tuple-element.66), channel_id=1, source_target_pairs={{0,1},{1,0},{2,3},{3,2},{4,5},{5,4},{6,7},{7,6},{8,9},{9,8},{10,11... | collective-permute-start | bytes 811016 | tf_op jit(solution)/shard_map/ppermute | solution.py:83
  4.8 31.7 %collective-permute-start.4 = (bf16[176,768]{1,0:T(8,128)(2,1)}, bf16[176,768]{1,0:T(8,128)(2,1)}, u32[]{:S(2)}, u32[]{:S(2)}) collective-permute-start(bf16[176,768]{1,0:T(8,128)(2,1)} %get-tuple-element.66), channel_id=1, source_target_pairs={{0,3},{1,2},{2,1},{3,0},{4,7},{5,6},{6,5},{7,4},{8,11},{9,10},{10,... | collective-permute-start | bytes 811016 | tf_op jit(solution)/shard_map/ppermute | solution.py:83
  9.7 19.3 %collective-permute-start = (bf16[176,768]{1,0:T(8,128)(2,1)S(1)}, bf16[176,768]{1,0:T(8,128)(2,1)}, u32[]{:S(2)}, u32[]{:S(2)}) collective-permute-start(bf16[176,768]{1,0:T(8,128)(2,1)S(1)} %get-tuple-element.128), channel_id=1, source_target_pairs={{0,1},{1,0},{2,3},{3,2},{4,5},{5,4},{6,7},{7,6},{8,9},{9,8},{10,11... | collective-permute-start | bytes 811016 | tf_op jit(solution)/shard_map/ppermute | solution.py:83
  10.3 26.1 %collective-permute-start.3 = (bf16[176,768]{1,0:T(8,128)(2,1)S(1)}, bf16[176,768]{1,0:T(8,128)(2,1)}, u32[]{:S(2)}, u32[]{:S(2)}) collective-permute-start(bf16[176,768]{1,0:T(8,128)(2,1)S(1)} %get-tuple-element.87.refs_0_), channel_id=1, source_target_pairs={{0,2},{1,3},{2,0},{3,1},{4,6},{5,7},{6,4},{7,5},{8,10},{9,11},{10,... | collective-permute-start | bytes 811016 | tf_op jit(solution)/shard_map/ppermute | solution.py:83
  29.0 8.5 %collective-permute-start.1 = (bf16[176,768]{1,0:T(8,128)(2,1)}, bf16[176,768]{1,0:T(8,128)(2,1)}, u32[]{:S(2)}, u32[]{:S(2)}) collective-permute-start(bf16[176,768]{1,0:T(8,128)(2,1)} %get-tuple-element.64), channel_id=1, source_target_pairs={{0,1},{1,0},{2,3},{3,2},{4,5},{5,4},{6,7},{7,6},{8,9},{9,8},{10,11... | collective-permute-start | bytes 811016 | tf_op jit(solution)/shard_map/ppermute | solution.py:83
  29.5 7.9 %copy-start.1 = (bf16[8,704,128]{2,1,0:T(8,128)(2,1)S(1)}, bf16[8,704,128]{2,1,0:T(8,128)(2,1)}, u32[]{:S(2)}) copy-start(bf16[8,704,128]{2,1,0:T(8,128)(2,1)} %get-tuple-element.123.refs_4_) | copy-start | bytes 4325380
  33.4 27.4 %collective-permute-start.6 = (bf16[352,768]{1,0:T(8,128)(2,1)}, bf16[352,768]{1,0:T(8,128)(2,1)}, u32[]{:S(2)}, u32[]{:S(2)}) collective-permute-start(bf16[352,768]{1,0:T(8,128)(2,1)} %pad_maximum_fusion.3), channel_id=1, source_target_pairs={{0,2},{1,3},{2,0},{3,1},{4,6},{5,7},{6,4},{7,5},{8,10},{9,11},{10,... | collective-permute-start | bytes 1622024 | tf_op jit(solution)/shard_map/ppermute | solution.py:83
  37.5 23.4 %collective-permute-start.5 = (bf16[176,768]{1,0:T(8,128)(2,1)}, bf16[176,768]{1,0:T(8,128)(2,1)}, u32[]{:S(2)}, u32[]{:S(2)}) collective-permute-start(bf16[176,768]{1,0:T(8,128)(2,1)} %get-tuple-element.72), channel_id=1, source_target_pairs={{0,1},{1,0},{2,3},{3,2},{4,5},{5,4},{6,7},{7,6},{8,9},{9,8},{10,11... | collective-permute-start | bytes 811016 | tf_op jit(solution)/shard_map/ppermute | solution.py:83
  37.5 5.4 %copy-start.4 = (bf16[176,768]{1,0:T(8,128)(2,1)S(1)}, bf16[176,768]{1,0:T(8,128)(2,1)}, u32[]{:S(2)}) copy-start(bf16[176,768]{1,0:T(8,128)(2,1)} %get-tuple-element.84.refs_0_) | copy-start | bytes 811012
  37.5 23.4 %copy-start = (bf16[8,704,128]{2,1,0:T(8,128)(2,1)S(1)}, bf16[8,704,128]{2,1,0:T(8,128)(2,1)}, u32[]{:S(2)}) copy-start(bf16[8,704,128]{2,1,0:T(8,128)(2,1)} %get-tuple-element.121.refs_3_) | copy-start | bytes 4325380
  40.9 50.2 %collective-permute-start.10 = (bf16[96,16,128]{2,1,0:T(8,128)(2,1)}, bf16[96,16,128]{2,1,0:T(8,128)(2,1)}, u32[]{:S(2)}, u32[]{:S(2)}) collective-permute-start(bf16[96,16,128]{2,1,0:T(8,128)(2,1)} %parity_sums.7), channel_id=1, source_target_pairs={{0,1},{1,0},{2,3},{3,2},{4,5},{5,4},{6,7},{7,6},{8,9},{9,8},{10,11... | collective-permute-start | bytes 1179656 | tf_op jit(solution)/shard_map/ppermute | solution.py:83
  44.7 39.4 %collective-permute-start.8 = (bf16[352,768]{1,0:T(8,128)(2,1)}, bf16[352,768]{1,0:T(8,128)(2,1)}, u32[]{:S(2)}, u32[]{:S(2)}) collective-permute-start(bf16[352,768]{1,0:T(8,128)(2,1)} %pad_maximum_fusion.4), channel_id=1, source_target_pairs={{0,2},{1,3},{2,0},{3,1},{4,6},{5,7},{6,4},{7,5},{8,10},{9,11},{10,... | collective-permute-start | bytes 1622024 | tf_op jit(solution)/shard_map/ppermute | solution.py:83
  60.8 17.4 %collective-permute-start.7 = (bf16[176,384]{1,0:T(8,128)(2,1)}, bf16[176,384]{1,0:T(8,128)(2,1)}, u32[]{:S(2)}, u32[]{:S(2)}) collective-permute-start(bf16[176,384]{1,0:T(8,128)(2,1)} %get-tuple-element.78), channel_id=1, source_target_pairs={{0,1},{1,0},{2,3},{3,2},{4,5},{5,4},{6,7},{7,6},{8,9},{9,8},{10,11... | collective-permute-start | bytes 405512 | tf_op jit(solution)/shard_map/ppermute | solution.py:83
  64.2 28.0 %collective-permute-start.11 = (bf16[96,16,128]{2,1,0:T(8,128)(2,1)}, bf16[96,16,128]{2,1,0:T(8,128)(2,1)}, u32[]{:S(2)}, u32[]{:S(2)}) collective-permute-start(bf16[96,16,128]{2,1,0:T(8,128)(2,1)} %parity_sums.8), channel_id=1, source_target_pairs={{0,1},{1,0},{2,3},{3,2},{4,5},{5,4},{6,7},{7,6},{8,9},{9,8},{10,11... | collective-permute-start | bytes 1179656 | tf_op jit(solution)/shard_map/ppermute | solution.py:83
  68.0 44.0 %collective-permute-start.13 = (bf16[352,768]{1,0:T(8,128)(2,1)}, bf16[352,768]{1,0:T(8,128)(2,1)}, u32[]{:S(2)}, u32[]{:S(2)}) collective-permute-start(bf16[352,768]{1,0:T(8,128)(2,1)} %pad_maximum_fusion.5), channel_id=1, source_target_pairs={{0,2},{1,3},{2,0},{3,1},{4,6},{5,7},{6,4},{7,5},{8,10},{9,11},{10,... | collective-permute-start | bytes 1622024 | tf_op jit(solution)/shard_map/ppermute | solution.py:83
  84.1 8.1 %copy-start.11 = (pred[128]{0:T(512)(128)(4,1)S(1)}, pred[128]{0:T(512)(128)(4,1)}, u32[]{:S(2)}) copy-start(pred[128]{0:T(512)(128)(4,1)} %iota_compare_fusion) | copy-start | bytes 388
  87.4 39.8 %collective-permute-start.9 = (bf16[96,16,128]{2,1,0:T(8,128)(2,1)}, bf16[96,16,128]{2,1,0:T(8,128)(2,1)}, u32[]{:S(2)}, u32[]{:S(2)}) collective-permute-start(bf16[96,16,128]{2,1,0:T(8,128)(2,1)} %parity_sums.6), channel_id=1, source_target_pairs={{0,1},{1,0},{2,3},{3,2},{4,5},{5,4},{6,7},{7,6},{8,9},{9,8},{10,11... | collective-permute-start | bytes 1179656 | tf_op jit(solution)/shard_map/ppermute | solution.py:83
  87.4 24.6 %collective-permute-start.12 = (bf16[176,384]{1,0:T(8,128)(2,1)S(1)}, bf16[176,384]{1,0:T(8,128)(2,1)S(1)}, u32[]{:S(2)}, u32[]{:S(2)}) collective-permute-start(bf16[176,384]{1,0:T(8,128)(2,1)S(1)} %copy-done.10), channel_id=1, source_target_pairs={{0,1},{1,0},{2,3},{3,2},{4,5},{5,4},{6,7},{7,6},{8,9},{9,8},{10,11... | collective-permute-start | bytes 405512 | tf_op jit(solution)/shard_map/ppermute | solution.py:83
  91.1 33.6 %collective-permute-start.15 = (bf16[352,384]{1,0:T(8,128)(2,1)}, bf16[352,384]{1,0:T(8,128)(2,1)}, u32[]{:S(2)}, u32[]{:S(2)}) collective-permute-start(bf16[352,384]{1,0:T(8,128)(2,1)} %pad_maximum_fusion.6), channel_id=1, source_target_pairs={{0,2},{1,3},{2,0},{3,1},{4,6},{5,7},{6,4},{7,5},{8,10},{9,11},{10,... | collective-permute-start | bytes 811016 | tf_op jit(solution)/shard_map/ppermute | solution.py:83
  93.9 18.2 %copy-start.7 = (bf16[176,384]{1,0:T(8,128)(2,1)S(1)}, bf16[176,384]{1,0:T(8,128)(2,1)}, u32[]{:S(2)}) copy-start(bf16[176,384]{1,0:T(8,128)(2,1)} %get-tuple-element.108.refs_0_) | copy-start | bytes 405508
  93.9 20.3 %copy-start.3 = (bf16[176,768]{1,0:T(8,128)(2,1)S(1)}, bf16[176,768]{1,0:T(8,128)(2,1)}, u32[]{:S(2)}) copy-start(bf16[176,768]{1,0:T(8,128)(2,1)} %get-tuple-element.103.refs_0_) | copy-start | bytes 811012
  94.8 32.4 %all-to-all-start = ((bf16[96,32,128]{2,1,0:T(8,128)(2,1)}), bf16[96,32,128]{2,1,0:T(8,128)(2,1)}, u32[]{:S(2)}, u32[]{:S(2)}) async-start(bf16[96,32,128]{2,1,0:T(8,128)(2,1)} %pad_maximum_fusion.1), calls=%async_computation | async-start | bytes 1572864 | tf_op jit(solution)/shard_map/all_to_all | solution.py:96
  112.8 20.7 %collective-permute-start.17 = (bf16[352,384]{1,0:T(8,128)(2,1)}, bf16[352,384]{1,0:T(8,128)(2,1)}, u32[]{:S(2)}, u32[]{:S(2)}) collective-permute-start(bf16[352,384]{1,0:T(8,128)(2,1)} %pad_maximum_fusion.7), channel_id=1, source_target_pairs={{0,2},{1,3},{2,0},{3,1},{4,6},{5,7},{6,4},{7,5},{8,10},{9,11},{10,... | collective-permute-start | bytes 811016 | tf_op jit(solution)/shard_map/ppermute | solution.py:83
  114.2 10.5 %copy-start.6 = (bf16[4,704,128]{2,1,0:T(8,128)(2,1)S(1)}, bf16[4,704,128]{2,1,0:T(8,128)(2,1)}, u32[]{:S(2)}) copy-start(bf16[4,704,128]{2,1,0:T(8,128)(2,1)} %get-tuple-element.126.refs_3_) | copy-start | bytes 2162692
  114.2 10.5 %copy-start.9 = (bf16[176,384]{1,0:T(8,128)(2,1)S(1)}, bf16[176,384]{1,0:T(8,128)(2,1)}, u32[]{:S(2)}) copy-start(bf16[176,384]{1,0:T(8,128)(2,1)} %get-tuple-element.106.refs_0_) | copy-start | bytes 405508
  117.6 22.0 %collective-permute-start.14 = (bf16[96,16,128]{2,1,0:T(8,128)(2,1)}, bf16[96,16,128]{2,1,0:T(8,128)(2,1)}, u32[]{:S(2)}, u32[]{:S(2)}) collective-permute-start(bf16[96,16,128]{2,1,0:T(8,128)(2,1)} %parity_sums.9), channel_id=1, source_target_pairs={{0,1},{1,0},{2,3},{3,2},{4,5},{5,4},{6,7},{7,6},{8,9},{9,8},{10,11... | collective-permute-start | bytes 1179656 | tf_op jit(solution)/shard_map/ppermute | solution.py:83
  127.2 6.3 %copy-start.5 = (bf16[4,704,128]{2,1,0:T(8,128)(2,1)S(1)}, bf16[4,704,128]{2,1,0:T(8,128)(2,1)}, u32[]{:S(2)}) copy-start(bf16[4,704,128]{2,1,0:T(8,128)(2,1)} %get-tuple-element.125.refs_3_) | copy-start | bytes 2162692
  127.2 12.4 %collective-permute-start.16 = (bf16[96,8,128]{2,1,0:T(8,128)(2,1)}, bf16[96,8,128]{2,1,0:T(8,128)(2,1)}, u32[]{:S(2)}, u32[]{:S(2)}) collective-permute-start(bf16[96,8,128]{2,1,0:T(8,128)(2,1)} %parity_sums.10), channel_id=1, source_target_pairs={{0,1},{1,0},{2,3},{3,2},{4,5},{5,4},{6,7},{7,6},{8,9},{9,8},{10,11... | collective-permute-start | bytes 589832 | tf_op jit(solution)/shard_map/ppermute | solution.py:83
  129.3 13.9 %all-to-all-start.1 = ((bf16[96,16,128]{2,1,0:T(8,128)(2,1)}), bf16[96,16,128]{2,1,0:T(8,128)(2,1)}, u32[]{:S(2)}, u32[]{:S(2)}) async-start(bf16[96,16,128]{2,1,0:T(8,128)(2,1)} %fusion.8), calls=%async_computation.1 | async-start | bytes 786432 | tf_op jit(solution)/shard_map/all_to_all | solution.py:96
  133.4 9.8 %copy-start.13 = (pred[128]{0:T(512)(128)(4,1)S(1)}, pred[128]{0:T(512)(128)(4,1)}, u32[]{:S(2)}) copy-start(pred[128]{0:T(512)(128)(4,1)} %iota_compare_fusion) | copy-start | bytes 388
  135.2 8.0 %collective-permute-start.18 = (bf16[96,8,128]{2,1,0:T(8,128)(2,1)S(1)}, bf16[96,8,128]{2,1,0:T(8,128)(2,1)S(1)}, u32[]{:S(2)}, u32[]{:S(2)}) collective-permute-start(bf16[96,8,128]{2,1,0:T(8,128)(2,1)S(1)} %parity_sums.11), channel_id=1, source_target_pairs={{0,1},{1,0},{2,3},{3,2},{4,5},{5,4},{6,7},{7,6},{8,9},{9,8},{10,11... | collective-permute-start | bytes 589832 | tf_op jit(solution)/shard_map/ppermute | solution.py:83
  (4 other events, 16.5 us)

commit v2 on v1

--- a/solution.py
+++ b/solution.py
@@ -8,6 +8,7 @@
 from jax.sharding import PartitionSpec as P
 
 TRUNC = 1279
+VMEM = 24 * 2**20
 CHUNKS = (8, 8, 8, 8, 4, 4)
 GROUPS = ((0, 1), (2,), (3, 4, 5))
 
@@ -60,10 +61,68 @@
             pltpu.VMEM((fields, 2 * pairs, lats), jnp.float32),
         ],
         out_shape=jax.ShapeDtypeStruct((fields, 2 * pairs, lats), jnp.bfloat16),
-        compiler_params=pltpu.CompilerParams(vmem_limit_bytes=24 * 2**20),
+        compiler_params=pltpu.CompilerParams(vmem_limit_bytes=VMEM),
         cost_estimate=pl.CostEstimate(flops=pairs * 10**11, bytes_accessed=pairs * 100 * 2**20, transcendentals=0),
         name="parity_sums",
     )(order, first, total, *blocks, legendre)
+
+
+def combine_kernel(count, parity, lat_count, *refs):
+    out = refs[-1]
+    slot = 0
+    for own, partner in zip(refs[:count], refs[count:-1]):
+        wide, other = own[...].astype(jnp.float32), partner[...].astype(jnp.float32)
+        grid = other + jnp.where(parity[0] == 0, 1.0, -1.0) * wide
+        lat = lax.broadcasted_iota(jnp.int32, grid.shape, 2)
+        out[:, slot : slot + own.shape[1], :] = jnp.where(lat < lat_count[0], grid, 0.0).astype(out.dtype)
+        slot += own.shape[1]
+
+
+def combine(halves, parity, lat_count):
+    owns, partners = zip(*halves)
+    fields, _, lats = owns[0].shape
+    vmem = pl.BlockSpec(memory_space=pltpu.VMEM)
+    scalar = pl.BlockSpec(memory_space=pltpu.SMEM)
+    return pl.pallas_call(
+        functools.partial(combine_kernel, len(owns)),
+        in_specs=[scalar] * 2 + [vmem] * (2 * len(owns)),
+        out_specs=vmem,
+        out_shape=jax.ShapeDtypeStruct((fields, sum(own.shape[1] for own in owns), lats), jnp.bfloat16),
+        compiler_params=pltpu.CompilerParams(vmem_limit_bytes=VMEM),
+        name="combine",
+    )(parity.reshape(1), lat_count, *owns, *partners)
+
+
+def place_kernel(first_slot, slots, count, *refs):
+    pieces, out, done = refs[:count], refs[-2], refs[-1]
+    copies = []
+    for piece in pieces:
+        sets, _, width, _ = piece.shape
+        for group in range(sets):
+            target = out.at[:, pl.ds(group * slots + first_slot, width), :]
+            copies.append(pltpu.make_async_copy(piece.at[group], target, done.at[len(copies)]))
+        first_slot += width
+    for copy in copies:
+        copy.start()
+    for copy in copies:
+        copy.wait()
+
+
+def place(pieces, first_slot, slots, out):
+    sets, fields, _, lats = pieces[0].shape
+    vmem = pl.BlockSpec(memory_space=pltpu.VMEM)
+    hbm = pl.BlockSpec(memory_space=pltpu.HBM)
+    held = [] if out is None else [out]
+    return pl.pallas_call(
+        functools.partial(place_kernel, first_slot, slots, len(pieces)),
+        in_specs=[vmem] * len(pieces) + [hbm] * len(held),
+        out_specs=hbm,
+        scratch_shapes=[pltpu.SemaphoreType.DMA((len(pieces) * sets,))],
+        out_shape=jax.ShapeDtypeStruct((fields, sets * slots, lats), jnp.bfloat16),
+        input_output_aliases={len(pieces): 0} if held else {},
+        compiler_params=pltpu.CompilerParams(vmem_limit_bytes=VMEM),
+        name="place",
+    )(*pieces, *held)
 
 
 def shards(coeffs, legendre, wavenumber, band_rows):
@@ -76,7 +135,6 @@
     fields = coeffs.shape[2] // pair_count
     first, total = owner_limits(wavenumber, parity)
     order = (me if rows % 16 == 0 else 0) ^ jnp.arange(bands, dtype=jnp.int32)
-    valid_lat = jnp.arange(lats, dtype=jnp.int32) < band_rows[0]
     assert sum(CHUNKS) == pair_count
     plan = [(sum(CHUNKS[:chunk]), pairs) for chunk, pairs in enumerate(CHUNKS)]
     def swap(value, step):
@@ -87,14 +145,8 @@
         place, shape = (0, start * fields), (1, rows, pairs * fields)
         return [lax.dynamic_slice(coeffs, (which, *place), shape)[0] for which in (parity, 1 - parity)]
 
-    def combine(own, partner):
-        own, partner = own.astype(jnp.float32), partner.astype(jnp.float32)
-        grid = jnp.where(parity == 0, own + partner, partner - own)
-        return jnp.where(valid_lat, grid, 0.0).astype(jnp.bfloat16)
-
     def redistribute(grid):
-        piece = lax.all_to_all(grid, "mset", split_axis=0, concat_axis=1, tiled=True)
-        return piece.reshape(fields // sets, sets, -1, lats)
+        return lax.all_to_all(grid.reshape(sets, fields // sets, -1, lats), "mset", 0, 0)
 
     def spread(mine, near):
         held = [mine, near]
@@ -120,11 +172,12 @@
         own_rows[chunk] = payload[0]
         near[chunk] = swap(payload[1], 1)
 
-    def send_far(chunk):
+    def send_far(chunk, after=None):
         parts = [own_rows[chunk], near[chunk]]
-        if chunk >= 2:
-            parts, far[chunk - 2] = lax.optimization_barrier((parts, far[chunk - 2]))
+        if after is not None:
+            parts, after = lax.optimization_barrier((parts, after))
         far[chunk] = spread(*parts)
+        return after
 
     first_rows = payloads_of(0)
     coeffs, first_rows = lax.optimization_barrier((coeffs, first_rows))
@@ -134,10 +187,10 @@
     send_far(1)
     pieces, ready = [], []
     for chunk, (start, pairs) in enumerate(plan):
-        if chunk + 2 < len(plan):
-            send_far(chunk + 2)
         if 3 <= chunk + 3 < len(plan):
             send_near(chunk + 3)
+        if chunk < 1:
+            far[chunk], near[chunk + 2] = lax.optimization_barrier((far[chunk], near[chunk + 2]))
         blocks = far[chunk]
         if rows % 16:
             stacked = jnp.concatenate(blocks).reshape(bands, rows, -1)
@@ -145,12 +198,15 @@
         own = parity_sums(
             blocks, rows if rows % 16 == 0 else depth, order, first, total, legendre, start, pairs, fields
         )
+        if chunk + 2 < len(plan):
+            own = send_far(chunk + 2, own)
         ready.append((own, swap(own, 1)))
         if chunk == GROUPS[len(pieces)][-1]:
             ready, pieces[-1:] = lax.optimization_barrier((ready, pieces[-1:]))
-            pieces.append(redistribute(jnp.concatenate([combine(*part) for part in ready], axis=1)))
+            pieces.append(redistribute(combine(ready, parity, band_rows)))
             ready = []
-    return jnp.concatenate(pieces, axis=2).reshape(fields // sets, sets * 2 * pair_count, lats)
+    ahead = place(pieces[:-1], 0, 2 * pair_count, None)
+    return place(pieces[-1:], sum(piece.shape[2] for piece in pieces[:-1]), 2 * pair_count, ahead)
 
 
 def solution(mesh):

time: 166 us -> 161 us (0.970)
  blocking collectives: 16.1 us -> 0 us
  waiting for transfers between devices: 63.2 us -> 76.2 us
  other arithmetic: 17.1 us -> 6.76 us
  Pallas kernels: 17.5 us -> 27.1 us
  local copies, waits for them, and re-layouts: 15.1 us -> 10.6 us
  starting transfers between devices: 34.9 us -> 38.4 us
    all_to_all x1 -> x0, blocking collectives: 16.1 us -> none  [redistribute(): lax.all_to_all(grid, 'mset', split_axis=0, concat_axis=1, tiled=True)]
    pallas_call x0 -> x5, Pallas kernels: none -> 10.3 us  [the longest x3 7.05 us: combine(): pl.pallas_call(functools.partial(combine_kernel, len(owns)), in_specs=[sc...]
    all_to_all x2 -> x3, waiting for transfers between devices: 0.01 us -> 10.2 us  [redistribute(): lax.all_to_all(grid.reshape(sets, fields // sets, -1, lats), 'mset', 0, 0)]
    convert_element_type x4 -> x0, other arithmetic: 6.32 us -> none  [combine(): return jnp.where(valid_lat, grid, 0.0).astype(jnp.bfloat16)]
    all_to_all x2 -> x3, starting transfers between devices: 8.31 us -> 12.2 us  [redistribute(): lax.all_to_all(grid.reshape(sets, fields // sets, -1, lats), 'mset', 0, 0)]
    slice x2, local copies, waits for them, and re-layouts: 7.36 us -> 4.52 us  [parity_sums(): legendre = legendre[start:start + pairs]]
    ppermute x19, waiting for transfers between devices: 63.2 us -> 66 us  [swap(): lax.ppermute(value, 'band', [(band, band ^ step) for band in range(bands)])]
    concatenate x3 -> x0, other arithmetic: 2.46 us -> none  [the longest x1 1.4 us: shards(): jnp.concatenate(pieces, axis=2)]
  transfers between devices with their start and end apart: 21 -> 22, of which waited for: 9 -> 10; matrix products, arithmetic and copies ran while one was open for 15% -> 10% of each run, Pallas kernels for 11% -> 15%
where the time goes in v2:
time: 161 us; the launch traced here: 160 us
  waiting for transfers between devices  76.2 us (47%)
  starting transfers between devices  38.4 us (24%)
  Pallas kernels  27.1 us (17%)
  local copies, waits for them, and re-layouts  10.6 us (7%)
  other arithmetic  6.76 us (4%)
    ppermute x19, waiting for transfers between devices, swap(): lax.ppermute(value, 'band', [(band, band ^ step) for band in range(bands)])  66 us
    ppermute x19, starting transfers between devices, swap(): lax.ppermute(value, 'band', [(band, band ^ step) for band in range(bands)])  26.2 us
    pallas_call x6, Pallas kernels, parity_sums(): pl.pallas_call(functools.partial(sums_kernel, rows, fields, start), in_sp...  16.8 us
    all_to_all x3, starting transfers between devices, redistribute(): lax.all_to_all(grid.reshape(sets, fields // sets, -1, lats), 'mset', 0, 0)  12.2 us
    all_to_all x3, waiting for transfers between devices, redistribute(): lax.all_to_all(grid.reshape(sets, fields // sets, -1, lats), 'mset', 0, 0)  10.2 us
    pallas_call x3, Pallas kernels, combine(): pl.pallas_call(functools.partial(combine_kernel, len(owns)), in_specs=[sc...  7.05 us
    concatenate x5, other arithmetic, spread(): held.append(swap(jnp.concatenate(held), bit))  6.75 us
    squeeze x3, local copies, waits for them, and re-layouts, payloads_of(): lax.dynamic_slice(coeffs, (which, *place), shape)[0]  5.3 us
  transfers between devices with their start and end apart: 22, of which 10 were waited for; matrix products, arithmetic and copies ran while one was open for 10% of the time, Pallas kernels for 15%

profile of v2, /device:TPU:0, one launch (start us, length us, event | category | flops | bytes accessed | tf_op | source)
XLA Modules:
  0.0 159.9 jit_solution(16645833884774994289)
XLA Ops:
  1.1 3.1 %collective-permute-start.1 = (bf16[176,768]{1,0:T(8,128)(2,1)S(1)}, bf16[176,768]{1,0:T(8,128)(2,1)S(1)}, u32[]{:S(2)}, u32[]{:S(2)}) collective-permute-start(bf16[176,768]{1,0:T(8,128)(2,1)S(1)} %get-tuple-element.61), channel_id=1, source_target_pairs={{0,1},{1,0},{2,3},{3,2},{4,5},{5,4},{6,7},{7,6},{8,9},{9,8},{10,11... | collective-permute-start | bytes 811016 | tf_op jit(solution)/shard_map/ppermute | solution.py:141
  4.2 2.5 %collective-permute-start.3 = (bf16[176,768]{1,0:T(8,128)(2,1)S(1)}, bf16[176,768]{1,0:T(8,128)(2,1)S(1)}, u32[]{:S(2)}, u32[]{:S(2)}) collective-permute-start(bf16[176,768]{1,0:T(8,128)(2,1)S(1)} %get-tuple-element.61), channel_id=1, source_target_pairs={{0,3},{1,2},{2,1},{3,0},{4,7},{5,6},{6,5},{7,4},{8,11},{9,10},{10,... | collective-permute-start | bytes 811016 | tf_op jit(solution)/shard_map/ppermute | solution.py:141
  6.7 2.3 %dynamic-slice_bitcast_fusion = (bf16[176,768]{1,0:T(8,128)(2,1)S(1)}, bf16[176,768]{1,0:T(8,128)(2,1)}, bf16[176,768]{1,0:T(8,128)(2,1)}, bf16[176,768]{1,0:T(8...) fusion(bf16[2,176,3840]{2,1,0:T(8,128)(2,1)} %param.4, s32[]{:T(128)S(6)} %select_n.32, s32[]{:T(128)S(6)} %select_n.33), kind=kLoop, calls=%fused_computation.5 | loop fusion | bytes 3244040 | tf_op jit(solution)/shard_map/squeeze | solution.py:146
  10.9 3.1 %fusion.1 = (bf16[8,704,128]{2,1,0:T(8,128)(2,1)S(1)}, bf16[8,704,128]{2,1,0:T(8,128)(2,1)S(1)}, bf16[8,704,128]{2,1,0:T(8,128)(2,1)S(1)}, bf16[8,704,128]{2,1,0:T(8,128)(2,1)S(1)}) fusion(bf16[40,704,128]{2,1,0:T(8,128)(2,1)} %param.5), kind=kLoop, calls=%fused_computation.29 | loop fusion | bytes 11534336 | tf_op jit(solution)/shard_map/slice | solution.py:51
  15.4 12.8 %collective-permute-done.refs_1_ = bf16[176,768]{1,0:T(8,128)(2,1)S(1)} collective-permute-done((bf16[176,768]{1,0:T(8,128)(2,1)S(1)}, bf16[176,768]{1,0:T(8,128)(2,1)S(1)}, u32[]{:S(2)}, u32[]{:S(2)}) %collective-permute-start) | collective-permute-done | bytes 270368 | tf_op jit(solution)/shard_map/ppermute | solution.py:141
  31.6 2.9 %collective-permute-start.8 = (bf16[352,768]{1,0:T(8,128)(2,1)}, bf16[352,768]{1,0:T(8,128)(2,1)}, u32[]{:S(2)}, u32[]{:S(2)}) collective-permute-start(bf16[352,768]{1,0:T(8,128)(2,1)} %pad_maximum_fusion.1), channel_id=1, source_target_pairs={{0,2},{1,3},{2,0},{3,1},{4,6},{5,7},{6,4},{7,5},{8,10},{9,11},{10,... | collective-permute-start | bytes 1622024 | tf_op jit(solution)/shard_map/ppermute | solution.py:141
  34.6 3.5 %collective-permute-done.4.refs_1_ = bf16[176,768]{1,0:T(8,128)(2,1)S(1)} collective-permute-done((bf16[176,768]{1,0:T(8,128)(2,1)S(1)}, bf16[176,768]{1,0:T(8,128)(2,1)S(1)}, u32[]{:S(2)}, u32[]{:S(2)}) %collective-permute-start.4) | collective-permute-done | bytes 270368 | tf_op jit(solution)/shard_map/ppermute | solution.py:141
  38.8 2.7 %parity_sums.6.refs_0_ = bf16[96,16,128]{2,1,0:T(8,128)(2,1)} custom-call(s32[4]{0:T(128)S(1)} %iota_xor_fusion.order, s32[40]{0:T(128)S(1)} %get-tuple-element.112.first, s32[40]{0:T(128)S(1)} %get-tuple-element.111.total, bf16[176,768]{1,0:T(8,128)(2,1)S(1)} %get-tuple-element.68.refs_0_, bf16[176,768]{1,0:T(8,128)(2,1)S(1)} %collective-permute-done.1.refs_1_, ...), custom_call_target="tpu_custom_call" | custom-call | flops 799999983616 | bytes 838860800 | tf_op jit(solution)/shard_map/parity_sums/pallas_call | solution.py:54
  42.4 3.7 %collective-permute-start.5 = (bf16[352,768]{1,0:T(8,128)(2,1)}, bf16[352,768]{1,0:T(8,128)(2,1)}, u32[]{:S(2)}, u32[]{:S(2)}) collective-permute-start(bf16[352,768]{1,0:T(8,128)(2,1)} %pad_maximum_fusion), channel_id=1, source_target_pairs={{0,2},{1,3},{2,0},{3,1},{4,6},{5,7},{6,4},{7,5},{8,10},{9,11},{10,... | collective-permute-start | bytes 1622024 | tf_op jit(solution)/shard_map/ppermute | solution.py:141
  46.0 13.2 %collective-permute-done.8.refs_2_ = bf16[352,768]{1,0:T(8,128)(2,1)} collective-permute-done((bf16[352,768]{1,0:T(8,128)(2,1)}, bf16[352,768]{1,0:T(8,128)(2,1)}, u32[]{:S(2)}, u32[]{:S(2)}) %collective-permute-start.8) | collective-permute-done | bytes 540704 | tf_op jit(solution)/shard_map/ppermute | solution.py:141
  59.3 3.3 %parity_sums.7.refs_1_ = bf16[96,16,128]{2,1,0:T(8,128)(2,1)} custom-call(s32[4]{0:T(128)S(1)} %iota_xor_fusion.order, s32[40]{0:T(128)S(1)} %get-tuple-element.112.first, s32[40]{0:T(128)S(1)} %get-tuple-element.111.total, bf16[176,768]{1,0:T(8,128)(2,1)S(1)} %get-tuple-element.79.refs_0_, bf16[176,768]{1,0:T(8,128)(2,1)S(1)} %collective-permute-done.refs_1_, ...), custom_call_target="tpu_custom_call" | custom-call | flops 799999983616 | bytes 838860800 | tf_op jit(solution)/shard_map/parity_sums/pallas_call | solution.py:54
  62.6 2.0 %collective-permute-start.11 = (bf16[176,384]{1,0:T(8,128)(2,1)}, bf16[176,384]{1,0:T(8,128)(2,1)}, u32[]{:S(2)}, u32[]{:S(2)}) collective-permute-start(bf16[176,384]{1,0:T(8,128)(2,1)} %get-tuple-element.86), channel_id=1, source_target_pairs={{0,1},{1,0},{2,3},{3,2},{4,5},{5,4},{6,7},{7,6},{8,9},{9,8},{10,11... | collective-permute-start | bytes 405512 | tf_op jit(solution)/shard_map/ppermute | solution.py:141
  67.1 15.4 %collective-permute-done.5.refs_2_ = bf16[352,768]{1,0:T(8,128)(2,1)} collective-permute-done((bf16[352,768]{1,0:T(8,128)(2,1)}, bf16[352,768]{1,0:T(8,128)(2,1)}, u32[]{:S(2)}, u32[]{:S(2)}) %collective-permute-start.5) | collective-permute-done | bytes 540704 | tf_op jit(solution)/shard_map/ppermute | solution.py:141
  82.5 3.2 %parity_sums.9.refs_0_ = bf16[96,16,128]{2,1,0:T(8,128)(2,1)} custom-call(s32[4]{0:T(128)S(1)} %iota_xor_fusion.order, s32[40]{0:T(128)S(1)} %get-tuple-element.112.first, s32[40]{0:T(128)S(1)} %get-tuple-element.111.total, bf16[176,768]{1,0:T(8,128)(2,1)S(1)} %copy-done.3, bf16[176,768]{1,0:T(8,128)(2,1)S(1)} %copy-done.10, ...), custom_call_target="tpu_custom_call" | custom-call | flops 799999983616 | bytes 838860800 | tf_op jit(solution)/shard_map/parity_sums/pallas_call | solution.py:54
  85.7 2.8 %collective-permute-done.11.refs_1_ = bf16[176,384]{1,0:T(8,128)(2,1)} collective-permute-done((bf16[176,384]{1,0:T(8,128)(2,1)}, bf16[176,384]{1,0:T(8,128)(2,1)}, u32[]{:S(2)}, u32[]{:S(2)}) %collective-permute-start.11) | collective-permute-done | bytes 135200 | tf_op jit(solution)/shard_map/ppermute | solution.py:141
  88.5 2.0 %collective-permute-start.6 = (bf16[176,384]{1,0:T(8,128)(2,1)}, bf16[176,384]{1,0:T(8,128)(2,1)}, u32[]{:S(2)}, u32[]{:S(2)}) collective-permute-start(bf16[176,384]{1,0:T(8,128)(2,1)} %get-tuple-element.75), channel_id=1, source_target_pairs={{0,1},{1,0},{2,3},{3,2},{4,5},{5,4},{6,7},{7,6},{8,9},{9,8},{10,11... | collective-permute-start | bytes 405512 | tf_op jit(solution)/shard_map/ppermute | solution.py:141
  93.4 2.6 %combine.3 = bf16[96,32,128]{2,1,0:T(8,128)(2,1)} custom-call(s32[1]{0:T(128)} %bitcast.parity, s32[1]{0:T(128)S(6)} %copy.7.lat_count, bf16[96,16,128]{2,1,0:T(8,128)(2,1)} %parity_sums.6.refs_0_, bf16[96,16,128]{2,1,0:T(8,128)(2,1)} %parity_sums.7.refs_1_, bf16[96,16,128]{2,1,0:T(8,128)(2,1)} %collective-permute-done.17.refs_2_, ...), custom_call_target="tpu_custom_call" | custom-call | tf_op jit(solution)/shard_map/combine/pallas_call | solution.py:86
  96.0 4.2 %all-to-all-start = ((bf16[8,12,32,128]{3,2,1,0:T(8,128)(2,1)}), bf16[8,12,32,128]{3,2,1,0:T(8,128)(2,1)}, u32[]{:S(2)}, u32[]{:S(2)}) async-start(bf16[8,12,32,128]{3,2,1,0:T(8,128)(2,1)} %bitcast.13), calls=%async_computation | async-start | bytes 1572864 | tf_op jit(solution)/shard_map/all_to_all | solution.py:149
  100.2 5.5 %collective-permute-done.9.refs_2_ = bf16[352,768]{1,0:T(8,128)(2,1)} collective-permute-done((bf16[352,768]{1,0:T(8,128)(2,1)}, bf16[352,768]{1,0:T(8,128)(2,1)}, u32[]{:S(2)}, u32[]{:S(2)}) %collective-permute-start.9) | collective-permute-done | bytes 540704 | tf_op jit(solution)/shard_map/ppermute | solution.py:141
  105.7 3.3 %parity_sums.8.refs_0_ = bf16[96,16,128]{2,1,0:T(8,128)(2,1)} custom-call(s32[4]{0:T(128)S(1)} %iota_xor_fusion.order, s32[40]{0:T(128)S(1)} %get-tuple-element.112.first, s32[40]{0:T(128)S(1)} %get-tuple-element.111.total, bf16[176,768]{1,0:T(8,128)(2,1)S(1)} %copy-done.1, bf16[176,768]{1,0:T(8,128)(2,1)} %collective-permute-done.7.refs_1_, ...), custom_call_target="tpu_custom_call" | custom-call | flops 799999983616 | bytes 838860800 | tf_op jit(solution)/shard_map/parity_sums/pallas_call | solution.py:54
  109.0 2.2 %collective-permute-done.6.refs_1_ = bf16[176,384]{1,0:T(8,128)(2,1)} collective-permute-done((bf16[176,384]{1,0:T(8,128)(2,1)}, bf16[176,384]{1,0:T(8,128)(2,1)}, u32[]{:S(2)}, u32[]{:S(2)}) %collective-permute-start.6) | collective-permute-done | bytes 135200 | tf_op jit(solution)/shard_map/ppermute | solution.py:141
  114.4 2.5 %collective-permute-start.10 = (bf16[96,16,128]{2,1,0:T(8,128)(2,1)}, bf16[96,16,128]{2,1,0:T(8,128)(2,1)}, u32[]{:S(2)}, u32[]{:S(2)}) collective-permute-start(bf16[96,16,128]{2,1,0:T(8,128)(2,1)} %parity_sums.8.refs_0_), channel_id=1, source_target_pairs={{0,1},{1,0},{2,3},{3,2},{4,5},{5,4},{6,7},{7,6},{8,9},{9,8},{10,11... | collective-permute-start | bytes 1179656 | tf_op jit(solution)/shard_map/ppermute | solution.py:141
  116.9 5.2 %collective-permute-done.12.refs_2_ = bf16[352,384]{1,0:T(8,128)(2,1)} collective-permute-done((bf16[352,384]{1,0:T(8,128)(2,1)}, bf16[352,384]{1,0:T(8,128)(2,1)}, u32[]{:S(2)}, u32[]{:S(2)}) %collective-permute-start.12) | collective-permute-done | bytes 270368 | tf_op jit(solution)/shard_map/ppermute | solution.py:141
  122.1 2.5 %parity_sums.10.refs_1_ = bf16[96,8,128]{2,1,0:T(8,128)(2,1)} custom-call(s32[4]{0:T(128)S(1)} %iota_xor_fusion.order, s32[40]{0:T(128)S(1)} %get-tuple-element.112.first, s32[40]{0:T(128)S(1)} %get-tuple-element.111.total, bf16[176,384]{1,0:T(8,128)(2,1)S(1)} %copy-done.7, bf16[176,384]{1,0:T(8,128)(2,1)} %collective-permute-done.11.refs_1_, ...), custom_call_target="tpu_custom_call" | custom-call | flops 399999991808 | bytes 419430400 | tf_op jit(solution)/shard_map/parity_sums/pallas_call | solution.py:54
  124.6 2.0 %combine.4 = bf16[96,16,128]{2,1,0:T(8,128)(2,1)} custom-call(s32[1]{0:T(128)} %bitcast.parity, s32[1]{0:T(128)S(6)} %copy.7.lat_count, bf16[96,16,128]{2,1,0:T(8,128)(2,1)} %parity_sums.9.refs_0_, bf16[96,16,128]{2,1,0:T(8,128)(2,1)} %collective-permute-done.16.refs_1_), custom_call_target="tpu_custom_call" | custom-call | tf_op jit(solution)/shard_map/combine/pallas_call | solution.py:86
  126.6 4.1 %all-to-all-start.1 = ((bf16[8,12,16,128]{3,2,1,0:T(8,128)(2,1)}), bf16[8,12,16,128]{3,2,1,0:T(8,128)(2,1)}, u32[]{:S(2)}, u32[]{:S(2)}) async-start(bf16[8,12,16,128]{3,2,1,0:T(8,128)(2,1)} %bitcast.14), calls=%async_computation.1 | async-start | bytes 786432 | tf_op jit(solution)/shard_map/all_to_all | solution.py:149
  132.5 2.1 %collective-permute-start.15 = (bf16[96,8,128]{2,1,0:T(8,128)(2,1)S(1)}, bf16[96,8,128]{2,1,0:T(8,128)(2,1)S(1)}, u32[]{:S(2)}, u32[]{:S(2)}) collective-permute-start(bf16[96,8,128]{2,1,0:T(8,128)(2,1)S(1)} %parity_sums.11.refs_2_), channel_id=1, source_target_pairs={{0,1},{1,0},{2,3},{3,2},{4,5},{5,4},{6,7},{7,6},{8,9},{9,8},{10,11... | collective-permute-start | bytes 589832 | tf_op jit(solution)/shard_map/ppermute | solution.py:141
  134.6 5.4 %collective-permute-done.15.refs_5_ = bf16[96,8,128]{2,1,0:T(8,128)(2,1)S(1)} collective-permute-done((bf16[96,8,128]{2,1,0:T(8,128)(2,1)S(1)}, bf16[96,8,128]{2,1,0:T(8,128)(2,1)S(1)}, u32[]{:S(2)}, u32[]{:S(2)}) %collective-permute-start.15) | collective-permute-done | bytes 196640 | tf_op jit(solution)/shard_map/ppermute | solution.py:141
  140.0 2.5 %combine.5 = bf16[96,32,128]{2,1,0:T(8,128)(2,1)} custom-call(s32[1]{0:T(128)} %bitcast.parity, s32[1]{0:T(128)S(6)} %copy.7.lat_count, bf16[96,16,128]{2,1,0:T(8,128)(2,1)} %parity_sums.8.refs_0_, bf16[96,8,128]{2,1,0:T(8,128)(2,1)} %parity_sums.10.refs_1_, bf16[96,8,128]{2,1,0:T(8,128)(2,1)S(1)} %parity_sums.11.refs_2_, ...), custom_call_target="tpu_custom_call" | custom-call | tf_op jit(solution)/shard_map/combine/pallas_call | solution.py:86
  142.5 3.9 %all-to-all-start.2 = ((bf16[8,12,32,128]{3,2,1,0:T(8,128)(2,1)}), bf16[8,12,32,128]{3,2,1,0:T(8,128)(2,1)S(1)}, u32[]{:S(2)}, u32[]{:S(2)}) async-start(bf16[8,12,32,128]{3,2,1,0:T(8,128)(2,1)} %bitcast.15), calls=%async_computation.2 | async-start | bytes 1572864 | tf_op jit(solution)/shard_map/all_to_all | solution.py:149
  146.3 2.4 %place.2.refs_1_ = bf16[12,640,128]{2,1,0:T(8,128)(2,1)} custom-call(bf16[8,12,32,128]{3,2,1,0:T(8,128)(2,1)} %all-to-all-done.refs_0_, bf16[8,12,16,128]{3,2,1,0:T(8,128)(2,1)} %all-to-all-done.1.refs_1_), custom_call_target="tpu_custom_call" | custom-call | tf_op jit(solution)/shard_map/place/pallas_call | solution.py:116
  148.7 10.2 %all-to-all-done.2.refs_0_ = bf16[8,12,32,128]{3,2,1,0:T(8,128)(2,1)S(1)} async-done(((bf16[8,12,32,128]{3,2,1,0:T(8,128)(2,1)}), bf16[8,12,32,128]{3,2,1,0:T(8,128)(2,1)S(1)}, u32[]{:S(2)}, u32[]{:S(2)}) %all-to-all-start.2) | async-done | bytes 786464 | tf_op jit(solution)/shard_map/all_to_all | solution.py:149
  (59 shorter events, 20.2 us)
Async XLA Ops:
  1.1 9.8 %copy-start.11 = (s32[40]{0:T(128)S(1)}, s32[40]{0:T(128)}, u32[]{:S(2)}) copy-start(s32[40]{0:T(128)} %param.6) | copy-start | bytes 484
  1.1 33.4 %collective-permute-start.1 = (bf16[176,768]{1,0:T(8,128)(2,1)S(1)}, bf16[176,768]{1,0:T(8,128)(2,1)S(1)}, u32[]{:S(2)}, u32[]{:S(2)}) collective-permute-start(bf16[176,768]{1,0:T(8,128)(2,1)S(1)} %get-tuple-element.61), channel_id=1, source_target_pairs={{0,1},{1,0},{2,3},{3,2},{4,5},{5,4},{6,7},{7,6},{8,9},{9,8},{10,11... | collective-permute-start | bytes 811016 | tf_op jit(solution)/shard_map/ppermute | solution.py:141
  4.2 30.4 %collective-permute-start.3 = (bf16[176,768]{1,0:T(8,128)(2,1)S(1)}, bf16[176,768]{1,0:T(8,128)(2,1)S(1)}, u32[]{:S(2)}, u32[]{:S(2)}) collective-permute-start(bf16[176,768]{1,0:T(8,128)(2,1)S(1)} %get-tuple-element.61), channel_id=1, source_target_pairs={{0,3},{1,2},{2,1},{3,0},{4,7},{5,6},{6,5},{7,4},{8,11},{9,10},{10,... | collective-permute-start | bytes 811016 | tf_op jit(solution)/shard_map/ppermute | solution.py:141
  8.9 19.2 %collective-permute-start = (bf16[176,768]{1,0:T(8,128)(2,1)S(1)}, bf16[176,768]{1,0:T(8,128)(2,1)S(1)}, u32[]{:S(2)}, u32[]{:S(2)}) collective-permute-start(bf16[176,768]{1,0:T(8,128)(2,1)S(1)} %get-tuple-element.122), channel_id=1, source_target_pairs={{0,1},{1,0},{2,3},{3,2},{4,5},{5,4},{6,7},{7,6},{8,9},{9,8},{10,11... | collective-permute-start | bytes 811016 | tf_op jit(solution)/shard_map/ppermute | solution.py:141
  9.6 24.9 %collective-permute-start.2 = (bf16[176,768]{1,0:T(8,128)(2,1)S(1)}, bf16[176,768]{1,0:T(8,128)(2,1)S(1)}, u32[]{:S(2)}, u32[]{:S(2)}) collective-permute-start(bf16[176,768]{1,0:T(8,128)(2,1)S(1)} %get-tuple-element.68.refs_0_), channel_id=1, source_target_pairs={{0,2},{1,3},{2,0},{3,1},{4,6},{5,7},{6,4},{7,5},{8,10},{9,11},{10,... | collective-permute-start | bytes 811016 | tf_op jit(solution)/shard_map/ppermute | solution.py:141
  28.2 9.9 %collective-permute-start.4 = (bf16[176,768]{1,0:T(8,128)(2,1)S(1)}, bf16[176,768]{1,0:T(8,128)(2,1)S(1)}, u32[]{:S(2)}, u32[]{:S(2)}) collective-permute-start(bf16[176,768]{1,0:T(8,128)(2,1)S(1)} %get-tuple-element.66), channel_id=1, source_target_pairs={{0,1},{1,0},{2,3},{3,2},{4,5},{5,4},{6,7},{7,6},{8,9},{9,8},{10,11... | collective-permute-start | bytes 811016 | tf_op jit(solution)/shard_map/ppermute | solution.py:141
  31.6 27.6 %collective-permute-start.8 = (bf16[352,768]{1,0:T(8,128)(2,1)}, bf16[352,768]{1,0:T(8,128)(2,1)}, u32[]{:S(2)}, u32[]{:S(2)}) collective-permute-start(bf16[352,768]{1,0:T(8,128)(2,1)} %pad_maximum_fusion.1), channel_id=1, source_target_pairs={{0,2},{1,3},{2,0},{3,1},{4,6},{5,7},{6,4},{7,5},{8,10},{9,11},{10,... | collective-permute-start | bytes 1622024 | tf_op jit(solution)/shard_map/ppermute | solution.py:141
  34.5 28.0 %collective-permute-start.7 = (bf16[176,768]{1,0:T(8,128)(2,1)}, bf16[176,768]{1,0:T(8,128)(2,1)}, u32[]{:S(2)}, u32[]{:S(2)}) collective-permute-start(bf16[176,768]{1,0:T(8,128)(2,1)} %get-tuple-element.77), channel_id=1, source_target_pairs={{0,1},{1,0},{2,3},{3,2},{4,5},{5,4},{6,7},{7,6},{8,9},{9,8},{10,11... | collective-permute-start | bytes 811016 | tf_op jit(solution)/shard_map/ppermute | solution.py:141
  38.8 2.7 %copy-start.9 = (bf16[176,768]{1,0:T(8,128)(2,1)S(1)}, bf16[176,768]{1,0:T(8,128)(2,1)}, u32[]{:S(2)}) copy-start(bf16[176,768]{1,0:T(8,128)(2,1)} %copy-done.8) | copy-start | bytes 811012
  41.5 50.7 %collective-permute-start.17 = (bf16[96,16,128]{2,1,0:T(8,128)(2,1)}, bf16[96,16,128]{2,1,0:T(8,128)(2,1)}, u32[]{:S(2)}, u32[]{:S(2)}) collective-permute-start(bf16[96,16,128]{2,1,0:T(8,128)(2,1)} %parity_sums.6.refs_0_), channel_id=1, source_target_pairs={{0,1},{1,0},{2,3},{3,2},{4,5},{5,4},{6,7},{7,6},{8,9},{9,8},{10,11... | collective-permute-start | bytes 1179656 | tf_op jit(solution)/shard_map/ppermute | solution.py:141
  42.4 40.1 %collective-permute-start.5 = (bf16[352,768]{1,0:T(8,128)(2,1)}, bf16[352,768]{1,0:T(8,128)(2,1)}, u32[]{:S(2)}, u32[]{:S(2)}) collective-permute-start(bf16[352,768]{1,0:T(8,128)(2,1)} %pad_maximum_fusion), channel_id=1, source_target_pairs={{0,2},{1,3},{2,0},{3,1},{4,6},{5,7},{6,4},{7,5},{8,10},{9,11},{10,... | collective-permute-start | bytes 1622024 | tf_op jit(solution)/shard_map/ppermute | solution.py:141
  59.3 5.3 %copy-start = (bf16[176,768]{1,0:T(8,128)(2,1)S(1)}, bf16[176,768]{1,0:T(8,128)(2,1)}, u32[]{:S(2)}) copy-start(bf16[176,768]{1,0:T(8,128)(2,1)} %get-tuple-element.82.refs_0_) | copy-start | bytes 811012
  59.3 23.2 %copy-start.3 = (bf16[176,768]{1,0:T(8,128)(2,1)S(1)}, bf16[176,768]{1,0:T(8,128)(2,1)}, u32[]{:S(2)}) copy-start(bf16[176,768]{1,0:T(8,128)(2,1)} %get-tuple-element.87.refs_0_) | copy-start | bytes 811012
  59.3 23.2 %copy-start.10 = (bf16[176,768]{1,0:T(8,128)(2,1)S(1)}, bf16[176,768]{1,0:T(8,128)(2,1)}, u32[]{:S(2)}) copy-start(bf16[176,768]{1,0:T(8,128)(2,1)} %copy-done.8) | copy-start | bytes 811012
  62.6 30.9 %collective-permute-start.18 = (bf16[96,16,128]{2,1,0:T(8,128)(2,1)}, bf16[96,16,128]{2,1,0:T(8,128)(2,1)}, u32[]{:S(2)}, u32[]{:S(2)}) collective-permute-start(bf16[96,16,128]{2,1,0:T(8,128)(2,1)} %parity_sums.7.refs_1_), channel_id=1, source_target_pairs={{0,1},{1,0},{2,3},{3,2},{4,5},{5,4},{6,7},{7,6},{8,9},{9,8},{10,11... | collective-permute-start | bytes 1179656 | tf_op jit(solution)/shard_map/ppermute | solution.py:141
  62.6 25.9 %collective-permute-start.11 = (bf16[176,384]{1,0:T(8,128)(2,1)}, bf16[176,384]{1,0:T(8,128)(2,1)}, u32[]{:S(2)}, u32[]{:S(2)}) collective-permute-start(bf16[176,384]{1,0:T(8,128)(2,1)} %get-tuple-element.86), channel_id=1, source_target_pairs={{0,1},{1,0},{2,3},{3,2},{4,5},{5,4},{6,7},{7,6},{8,9},{9,8},{10,11... | collective-permute-start | bytes 405512 | tf_op jit(solution)/shard_map/ppermute | solution.py:141
  66.4 39.3 %collective-permute-start.9 = (bf16[352,768]{1,0:T(8,128)(2,1)}, bf16[352,768]{1,0:T(8,128)(2,1)}, u32[]{:S(2)}, u32[]{:S(2)}) collective-permute-start(bf16[352,768]{1,0:T(8,128)(2,1)} %pad_maximum_fusion.2), channel_id=1, source_target_pairs={{0,2},{1,3},{2,0},{3,1},{4,6},{5,7},{6,4},{7,5},{8,10},{9,11},{10,... | collective-permute-start | bytes 1622024 | tf_op jit(solution)/shard_map/ppermute | solution.py:141
  82.5 8.0 %copy-start.6 = (bf16[176,384]{1,0:T(8,128)(2,1)S(1)}, bf16[176,384]{1,0:T(8,128)(2,1)}, u32[]{:S(2)}) copy-start(bf16[176,384]{1,0:T(8,128)(2,1)} %get-tuple-element.90.refs_0_) | copy-start | bytes 405508
  88.5 36.1 %collective-permute-start.16 = (bf16[96,16,128]{2,1,0:T(8,128)(2,1)}, bf16[96,16,128]{2,1,0:T(8,128)(2,1)}, u32[]{:S(2)}, u32[]{:S(2)}) collective-permute-start(bf16[96,16,128]{2,1,0:T(8,128)(2,1)} %parity_sums.9.refs_0_), channel_id=1, source_target_pairs={{0,1},{1,0},{2,3},{3,2},{4,5},{5,4},{6,7},{7,6},{8,9},{9,8},{10,11... | collective-permute-start | bytes 1179656 | tf_op jit(solution)/shard_map/ppermute | solution.py:141
  88.5 22.7 %collective-permute-start.6 = (bf16[176,384]{1,0:T(8,128)(2,1)}, bf16[176,384]{1,0:T(8,128)(2,1)}, u32[]{:S(2)}, u32[]{:S(2)}) collective-permute-start(bf16[176,384]{1,0:T(8,128)(2,1)} %get-tuple-element.75), channel_id=1, source_target_pairs={{0,1},{1,0},{2,3},{3,2},{4,5},{5,4},{6,7},{7,6},{8,9},{9,8},{10,11... | collective-permute-start | bytes 405512 | tf_op jit(solution)/shard_map/ppermute | solution.py:141
  92.1 29.9 %collective-permute-start.12 = (bf16[352,384]{1,0:T(8,128)(2,1)}, bf16[352,384]{1,0:T(8,128)(2,1)}, u32[]{:S(2)}, u32[]{:S(2)}) collective-permute-start(bf16[352,384]{1,0:T(8,128)(2,1)} %pad_maximum_fusion.3), channel_id=1, source_target_pairs={{0,2},{1,3},{2,0},{3,1},{4,6},{5,7},{6,4},{7,5},{8,10},{9,11},{10,... | collective-permute-start | bytes 811016 | tf_op jit(solution)/shard_map/ppermute | solution.py:141
  93.4 12.3 %copy-start.1 = (bf16[176,768]{1,0:T(8,128)(2,1)S(1)}, bf16[176,768]{1,0:T(8,128)(2,1)}, u32[]{:S(2)}) copy-start(bf16[176,768]{1,0:T(8,128)(2,1)} %get-tuple-element.82.refs_0_) | copy-start | bytes 811012
  96.0 28.6 %all-to-all-start = ((bf16[8,12,32,128]{3,2,1,0:T(8,128)(2,1)}), bf16[8,12,32,128]{3,2,1,0:T(8,128)(2,1)}, u32[]{:S(2)}, u32[]{:S(2)}) async-start(bf16[8,12,32,128]{3,2,1,0:T(8,128)(2,1)} %bitcast.13), calls=%async_computation | async-start | bytes 1572864 | tf_op jit(solution)/shard_map/all_to_all | solution.py:149
  105.7 5.5 %copy-start.4 = (bf16[176,384]{1,0:T(8,128)(2,1)S(1)}, bf16[176,384]{1,0:T(8,128)(2,1)}, u32[]{:S(2)}) copy-start(bf16[176,384]{1,0:T(8,128)(2,1)} %get-tuple-element.92.refs_0_) | copy-start | bytes 405508
  105.7 16.4 %copy-start.7 = (bf16[176,384]{1,0:T(8,128)(2,1)S(1)}, bf16[176,384]{1,0:T(8,128)(2,1)}, u32[]{:S(2)}) copy-start(bf16[176,384]{1,0:T(8,128)(2,1)} %get-tuple-element.90.refs_0_) | copy-start | bytes 405508
  112.9 17.8 %collective-permute-start.14 = (bf16[352,384]{1,0:T(8,128)(2,1)}, bf16[352,384]{1,0:T(8,128)(2,1)}, u32[]{:S(2)}, u32[]{:S(2)}) collective-permute-start(bf16[352,384]{1,0:T(8,128)(2,1)} %pad_maximum_fusion.4), channel_id=1, source_target_pairs={{0,2},{1,3},{2,0},{3,1},{4,6},{5,7},{6,4},{7,5},{8,10},{9,11},{10,... | collective-permute-start | bytes 811016 | tf_op jit(solution)/shard_map/ppermute | solution.py:141
  114.4 20.2 %collective-permute-start.10 = (bf16[96,16,128]{2,1,0:T(8,128)(2,1)}, bf16[96,16,128]{2,1,0:T(8,128)(2,1)}, u32[]{:S(2)}, u32[]{:S(2)}) collective-permute-start(bf16[96,16,128]{2,1,0:T(8,128)(2,1)} %parity_sums.8.refs_0_), channel_id=1, source_target_pairs={{0,1},{1,0},{2,3},{3,2},{4,5},{5,4},{6,7},{7,6},{8,9},{9,8},{10,11... | collective-permute-start | bytes 1179656 | tf_op jit(solution)/shard_map/ppermute | solution.py:141
  124.6 6.2 %copy-start.5 = (bf16[176,384]{1,0:T(8,128)(2,1)S(1)}, bf16[176,384]{1,0:T(8,128)(2,1)}, u32[]{:S(2)}) copy-start(bf16[176,384]{1,0:T(8,128)(2,1)} %get-tuple-element.92.refs_0_) | copy-start | bytes 405508
  124.6 10.0 %collective-permute-start.13 = (bf16[96,8,128]{2,1,0:T(8,128)(2,1)}, bf16[96,8,128]{2,1,0:T(8,128)(2,1)}, u32[]{:S(2)}, u32[]{:S(2)}) collective-permute-start(bf16[96,8,128]{2,1,0:T(8,128)(2,1)} %parity_sums.10.refs_1_), channel_id=1, source_target_pairs={{0,1},{1,0},{2,3},{3,2},{4,5},{5,4},{6,7},{7,6},{8,9},{9,8},{10,11... | collective-permute-start | bytes 589832 | tf_op jit(solution)/shard_map/ppermute | solution.py:141
  126.6 13.4 %all-to-all-start.1 = ((bf16[8,12,16,128]{3,2,1,0:T(8,128)(2,1)}), bf16[8,12,16,128]{3,2,1,0:T(8,128)(2,1)}, u32[]{:S(2)}, u32[]{:S(2)}) async-start(bf16[8,12,16,128]{3,2,1,0:T(8,128)(2,1)} %bitcast.14), calls=%async_computation.1 | async-start | bytes 786432 | tf_op jit(solution)/shard_map/all_to_all | solution.py:149
  132.5 7.5 %collective-permute-start.15 = (bf16[96,8,128]{2,1,0:T(8,128)(2,1)S(1)}, bf16[96,8,128]{2,1,0:T(8,128)(2,1)S(1)}, u32[]{:S(2)}, u32[]{:S(2)}) collective-permute-start(bf16[96,8,128]{2,1,0:T(8,128)(2,1)S(1)} %parity_sums.11.refs_2_), channel_id=1, source_target_pairs={{0,1},{1,0},{2,3},{3,2},{4,5},{5,4},{6,7},{7,6},{8,9},{9,8},{10,11... | collective-permute-start | bytes 589832 | tf_op jit(solution)/shard_map/ppermute | solution.py:141
  142.5 16.5 %all-to-all-start.2 = ((bf16[8,12,32,128]{3,2,1,0:T(8,128)(2,1)}), bf16[8,12,32,128]{3,2,1,0:T(8,128)(2,1)S(1)}, u32[]{:S(2)}, u32[]{:S(2)}) async-start(bf16[8,12,32,128]{3,2,1,0:T(8,128)(2,1)} %bitcast.15), calls=%async_computation.2 | async-start | bytes 1572864 | tf_op jit(solution)/shard_map/all_to_all | solution.py:149
  (2 other events, 3.4 us)

commit v3 on v1

--- a/solution.py
+++ b/solution.py
@@ -8,8 +8,9 @@
 from jax.sharding import PartitionSpec as P
 
 TRUNC = 1279
+VMEM = 24 * 2**20
 CHUNKS = (8, 8, 8, 8, 4, 4)
-GROUPS = ((0, 1), (2,), (3, 4, 5))
+GROUPS = ((0, 1), (2, 3), (4, 5))
 
 
 def owner_limits(wavenumber, parity):
@@ -60,10 +61,53 @@
             pltpu.VMEM((fields, 2 * pairs, lats), jnp.float32),
         ],
         out_shape=jax.ShapeDtypeStruct((fields, 2 * pairs, lats), jnp.bfloat16),
-        compiler_params=pltpu.CompilerParams(vmem_limit_bytes=24 * 2**20),
+        compiler_params=pltpu.CompilerParams(vmem_limit_bytes=VMEM),
         cost_estimate=pl.CostEstimate(flops=pairs * 10**11, bytes_accessed=pairs * 100 * 2**20, transcendentals=0),
         name="parity_sums",
     )(order, first, total, *blocks, legendre)
+
+
+def finish_kernel(first_slot, slots, count, parity, lat_count, *refs):
+    owns, partners, (out, result, done) = refs[:count], refs[count : 2 * count], refs[-3:]
+    sets, _, width, _ = result.shape
+    sign = jnp.where(parity[0] == 0, 1.0, -1.0)
+    copies = []
+    for group in range(sets):
+        slot = 0
+        for own, partner in zip(owns, partners):
+            grid = partner[group].astype(jnp.float32) + sign * own[group].astype(jnp.float32)
+            lat = lax.broadcasted_iota(jnp.int32, grid.shape, 2)
+            grid = jnp.where(lat < lat_count[0], grid, 0.0)
+            result[group, :, slot : slot + own.shape[2], :] = grid.astype(result.dtype)
+            slot += own.shape[2]
+        target = out.at[:, pl.ds(group * slots + first_slot, width), :]
+        copies.append(pltpu.make_async_copy(result.at[group], target, done.at[group]))
+        copies[-1].start()
+    for copy in copies:
+        copy.wait()
+
+
+def finish(halves, parity, lat_count, first_slot, slots, out):
+    owns, partners = zip(*halves)
+    sets, fields, _, lats = owns[0].shape
+    width = sum(own.shape[2] for own in owns)
+    vmem = pl.BlockSpec(memory_space=pltpu.VMEM)
+    hbm = pl.BlockSpec(memory_space=pltpu.HBM)
+    scalar = pl.BlockSpec(memory_space=pltpu.SMEM)
+    held = [] if out is None else [out]
+    return pl.pallas_call(
+        functools.partial(finish_kernel, first_slot, slots, len(owns)),
+        in_specs=[scalar] * 2 + [vmem] * (2 * len(owns)) + [hbm] * len(held),
+        out_specs=hbm,
+        scratch_shapes=[
+            pltpu.VMEM((sets, fields, width, lats), jnp.bfloat16),
+            pltpu.SemaphoreType.DMA((sets,)),
+        ],
+        out_shape=jax.ShapeDtypeStruct((fields, sets * slots, lats), jnp.bfloat16),
+        input_output_aliases={2 + 2 * len(owns): 0} if held else {},
+        compiler_params=pltpu.CompilerParams(vmem_limit_bytes=VMEM),
+        name="finish",
+    )(parity.reshape(1), lat_count, *owns, *partners, *held)
 
 
 def shards(coeffs, legendre, wavenumber, band_rows):
@@ -76,7 +120,6 @@
     fields = coeffs.shape[2] // pair_count
     first, total = owner_limits(wavenumber, parity)
     order = (me if rows % 16 == 0 else 0) ^ jnp.arange(bands, dtype=jnp.int32)
-    valid_lat = jnp.arange(lats, dtype=jnp.int32) < band_rows[0]
     assert sum(CHUNKS) == pair_count
     plan = [(sum(CHUNKS[:chunk]), pairs) for chunk, pairs in enumerate(CHUNKS)]
     def swap(value, step):
@@ -87,14 +130,8 @@
         place, shape = (0, start * fields), (1, rows, pairs * fields)
         return [lax.dynamic_slice(coeffs, (which, *place), shape)[0] for which in (parity, 1 - parity)]
 
-    def combine(own, partner):
-        own, partner = own.astype(jnp.float32), partner.astype(jnp.float32)
-        grid = jnp.where(parity == 0, own + partner, partner - own)
-        return jnp.where(valid_lat, grid, 0.0).astype(jnp.bfloat16)
-
     def redistribute(grid):
-        piece = lax.all_to_all(grid, "mset", split_axis=0, concat_axis=1, tiled=True)
-        return piece.reshape(fields // sets, sets, -1, lats)
+        return lax.all_to_all(grid.reshape(sets, fields // sets, -1, lats), "mset", 0, 0)
 
     def spread(mine, near):
         held = [mine, near]
@@ -120,11 +157,12 @@
         own_rows[chunk] = payload[0]
         near[chunk] = swap(payload[1], 1)
 
-    def send_far(chunk):
+    def send_far(chunk, after=None):
         parts = [own_rows[chunk], near[chunk]]
-        if chunk >= 2:
-            parts, far[chunk - 2] = lax.optimization_barrier((parts, far[chunk - 2]))
+        if after is not None:
+            parts, after = lax.optimization_barrier((parts, after))
         far[chunk] = spread(*parts)
+        return after
 
     first_rows = payloads_of(0)
     coeffs, first_rows = lax.optimization_barrier((coeffs, first_rows))
@@ -132,12 +170,12 @@
     send_near(1)
     send_near(2)
     send_far(1)
-    pieces, ready = [], []
+    out, written, ready = None, 0, []
     for chunk, (start, pairs) in enumerate(plan):
-        if chunk + 2 < len(plan):
-            send_far(chunk + 2)
         if 3 <= chunk + 3 < len(plan):
             send_near(chunk + 3)
+        if chunk < 1:
+            far[chunk], near[chunk + 2] = lax.optimization_barrier((far[chunk], near[chunk + 2]))
         blocks = far[chunk]
         if rows % 16:
             stacked = jnp.concatenate(blocks).reshape(bands, rows, -1)
@@ -145,12 +183,15 @@
         own = parity_sums(
             blocks, rows if rows % 16 == 0 else depth, order, first, total, legendre, start, pairs, fields
         )
-        ready.append((own, swap(own, 1)))
-        if chunk == GROUPS[len(pieces)][-1]:
-            ready, pieces[-1:] = lax.optimization_barrier((ready, pieces[-1:]))
-            pieces.append(redistribute(jnp.concatenate([combine(*part) for part in ready], axis=1)))
-            ready = []
-    return jnp.concatenate(pieces, axis=2).reshape(fields // sets, sets * 2 * pair_count, lats)
+        if chunk + 2 < len(plan):
+            own = send_far(chunk + 2, own)
+        piece = redistribute(own)
+        ready.append((piece, swap(piece, 1)))
+        if chunk == GROUPS[written][-1]:
+            first_slot = 2 * plan[GROUPS[written][0]][0]
+            out = finish(ready, parity, band_rows, first_slot, 2 * pair_count, out)
+            written, ready = written + 1, []
+    return out
 
 
 def solution(mesh):

time: 166 us -> 163 us (0.982)
  starting transfers between devices: 34.9 us -> 51.2 us
  blocking collectives: 16.1 us -> 0 us
  other arithmetic: 17.1 us -> 7.85 us
  Pallas kernels: 17.5 us -> 21.7 us
  local copies, waits for them, and re-layouts: 15.1 us -> 17 us
    all_to_all x1 -> x0, blocking collectives: 16.1 us -> none  [redistribute(): lax.all_to_all(grid, 'mset', split_axis=0, concat_axis=1, tiled=True)]
    all_to_all x2 -> x6, starting transfers between devices: 8.31 us -> 23.9 us  [redistribute(): lax.all_to_all(grid.reshape(sets, fields // sets, -1, lats), 'mset', 0, 0)]
    all_to_all x2 -> x6, waiting for transfers between devices: 0.01 us -> 8.11 us  [redistribute(): lax.all_to_all(grid.reshape(sets, fields // sets, -1, lats), 'mset', 0, 0)]
    ppermute x19, waiting for transfers between devices: 63.2 us -> 55.3 us  [swap(): lax.ppermute(value, 'band', [(band, band ^ step) for band in range(bands)])]
    pallas_call x0 -> x3, Pallas kernels: none -> 6.47 us  [finish(): pl.pallas_call(functools.partial(finish_kernel, first_slot, slots, len(ow...]
    convert_element_type x4 -> x0, other arithmetic: 6.32 us -> none  [combine(): return jnp.where(valid_lat, grid, 0.0).astype(jnp.bfloat16)]
    unnamed x30 -> x42, local copies, waits for them, and re-layouts: 0.06 us -> 4.79 us
    concatenate x3 -> x0, other arithmetic: 2.46 us -> none  [the longest x1 1.4 us: shards(): jnp.concatenate(pieces, axis=2)]
  transfers between devices with their start and end apart: 21 -> 25, of which waited for: 9 -> 9; matrix products, arithmetic and copies ran while one was open for 15% -> 12% of each run, Pallas kernels for 11% -> 12%
where the time goes in v3:
time: 163 us; the launch traced here: 162 us
  waiting for transfers between devices  63.4 us (39%)
  starting transfers between devices  51.2 us (31%)
  Pallas kernels  21.7 us (13%)
  local copies, waits for them, and re-layouts  17 us (10%)
  other arithmetic  7.85 us (5%)
    ppermute x19, waiting for transfers between devices, swap(): lax.ppermute(value, 'band', [(band, band ^ step) for band in range(bands)])  55.3 us
    ppermute x19, starting transfers between devices, swap(): lax.ppermute(value, 'band', [(band, band ^ step) for band in range(bands)])  27.2 us
    all_to_all x6, starting transfers between devices, redistribute(): lax.all_to_all(grid.reshape(sets, fields // sets, -1, lats), 'mset', 0, 0)  23.9 us
    pallas_call x6, Pallas kernels, parity_sums(): pl.pallas_call(functools.partial(sums_kernel, rows, fields, start), in_sp...  15.2 us
    all_to_all x6, waiting for transfers between devices, redistribute(): lax.all_to_all(grid.reshape(sets, fields // sets, -1, lats), 'mset', 0, 0)  8.11 us
    concatenate x5, other arithmetic, spread(): held.append(swap(jnp.concatenate(held), bit))  7.83 us
    slice x2, local copies, waits for them, and re-layouts, parity_sums(): legendre = legendre[start:start + pairs]  6.84 us
    pallas_call x3, Pallas kernels, finish(): pl.pallas_call(functools.partial(finish_kernel, first_slot, slots, len(ow...  6.47 us
  transfers between devices with their start and end apart: 25, of which 9 were waited for; matrix products, arithmetic and copies ran while one was open for 12% of the time, Pallas kernels for 12%

profile of v3, /device:TPU:0, one launch (start us, length us, event | category | flops | bytes accessed | tf_op | source)
XLA Modules:
  0.0 162.1 jit_solution(4995263560301696793)
XLA Ops:
  1.1 3.1 %collective-permute-start.3 = (bf16[176,768]{1,0:T(8,128)(2,1)S(1)}, bf16[176,768]{1,0:T(8,128)(2,1)S(1)}, u32[]{:S(2)}, u32[]{:S(2)}) collective-permute-start(bf16[176,768]{1,0:T(8,128)(2,1)S(1)} %get-tuple-element.50), channel_id=1, source_target_pairs={{0,1},{1,0},{2,3},{3,2},{4,5},{5,4},{6,7},{7,6},{8,9},{9,8},{10,11... | collective-permute-start | bytes 811016 | tf_op jit(solution)/shard_map/ppermute | solution.py:126
  4.2 2.5 %collective-permute-start.5 = (bf16[176,768]{1,0:T(8,128)(2,1)S(1)}, bf16[176,768]{1,0:T(8,128)(2,1)S(1)}, u32[]{:S(2)}, u32[]{:S(2)}) collective-permute-start(bf16[176,768]{1,0:T(8,128)(2,1)S(1)} %get-tuple-element.50), channel_id=1, source_target_pairs={{0,3},{1,2},{2,1},{3,0},{4,7},{5,6},{6,5},{7,4},{8,11},{9,10},{10,... | collective-permute-start | bytes 811016 | tf_op jit(solution)/shard_map/ppermute | solution.py:126
  10.9 4.3 %fusion.1 = (bf16[8,704,128]{2,1,0:T(8,128)(2,1)S(1)}, bf16[8,704,128]{2,1,0:T(8,128)(2,1)}, bf16[8,704,128]{2,1,0:T(8,128)(2,1)S(1)}, bf16[8,704,128]{2,1,0:T(8,128)(2,1)S(1)}) fusion(bf16[40,704,128]{2,1,0:T(8,128)(2,1)} %param.5), kind=kLoop, calls=%fused_computation.29 | loop fusion | bytes 11534336 | tf_op jit(solution)/shard_map/slice | solution.py:51
  15.2 2.6 %fusion = (bf16[4,704,128]{2,1,0:T(8,128)(2,1)}, bf16[4,704,128]{2,1,0:T(8,128)(2,1)}) fusion(bf16[40,704,128]{2,1,0:T(8,128)(2,1)} %param.5), kind=kLoop, calls=%fused_computation.28 | loop fusion | bytes 2883584 | tf_op jit(solution)/shard_map/slice | solution.py:51
  17.7 10.5 %collective-permute-done.refs_1_ = bf16[176,768]{1,0:T(8,128)(2,1)S(1)} collective-permute-done((bf16[176,768]{1,0:T(8,128)(2,1)S(1)}, bf16[176,768]{1,0:T(8,128)(2,1)S(1)}, u32[]{:S(2)}, u32[]{:S(2)}) %collective-permute-start) | collective-permute-done | bytes 270368 | tf_op jit(solution)/shard_map/ppermute | solution.py:126
  31.1 2.8 %collective-permute-start.1 = (bf16[352,768]{1,0:T(8,128)(2,1)}, bf16[352,768]{1,0:T(8,128)(2,1)}, u32[]{:S(2)}, u32[]{:S(2)}) collective-permute-start(bf16[352,768]{1,0:T(8,128)(2,1)} %pad_maximum_fusion), channel_id=1, source_target_pairs={{0,2},{1,3},{2,0},{3,1},{4,6},{5,7},{6,4},{7,5},{8,10},{9,11},{10,... | collective-permute-start | bytes 1622024 | tf_op jit(solution)/shard_map/ppermute | solution.py:126
  34.1 5.4 %collective-permute-done.6.refs_1_ = bf16[176,768]{1,0:T(8,128)(2,1)S(1)} collective-permute-done((bf16[176,768]{1,0:T(8,128)(2,1)S(1)}, bf16[176,768]{1,0:T(8,128)(2,1)S(1)}, u32[]{:S(2)}, u32[]{:S(2)}) %collective-permute-start.6) | collective-permute-done | bytes 270368 | tf_op jit(solution)/shard_map/ppermute | solution.py:126
  42.8 4.2 %all-to-all-start.4 = ((bf16[8,12,16,128]{3,2,1,0:T(8,128)(2,1)}), bf16[8,12,16,128]{3,2,1,0:T(8,128)(2,1)}, u32[]{:S(2)}, u32[]{:S(2)}) async-start(bf16[8,12,16,128]{3,2,1,0:T(8,128)(2,1)} %bitcast.32), calls=%async_computation.4 | async-start | bytes 786432 | tf_op jit(solution)/shard_map/all_to_all | solution.py:134
  48.9 21.2 %collective-permute-done.1.refs_2_ = bf16[352,768]{1,0:T(8,128)(2,1)} collective-permute-done((bf16[352,768]{1,0:T(8,128)(2,1)}, bf16[352,768]{1,0:T(8,128)(2,1)}, u32[]{:S(2)}, u32[]{:S(2)}) %collective-permute-start.1) | collective-permute-done | bytes 540704 | tf_op jit(solution)/shard_map/ppermute | solution.py:126
  72.5 3.2 %parity_sums.9 = bf16[96,16,128]{2,1,0:T(8,128)(2,1)} custom-call(s32[4]{0:T(128)S(1)} %iota_xor_fusion.order, s32[40]{0:T(128)S(1)} %get-tuple-element.84.first, s32[40]{0:T(128)S(1)} %get-tuple-element.83.total, bf16[176,768]{1,0:T(8,128)(2,1)S(1)} %copy-done.6, bf16[176,768]{1,0:T(8,128)(2,1)S(1)} %copy-done.19, ...), custom_call_target="tpu_custom_call" | custom-call | flops 799999983616 | bytes 838860800 | tf_op jit(solution)/shard_map/parity_sums/pallas_call | solution.py:54
  77.6 2.9 %collective-permute-start.2 = (bf16[176,384]{1,0:T(8,128)(2,1)}, bf16[176,384]{1,0:T(8,128)(2,1)}, u32[]{:S(2)}, u32[]{:S(2)}) collective-permute-start(bf16[176,384]{1,0:T(8,128)(2,1)} %get-tuple-element.47), channel_id=1, source_target_pairs={{0,1},{1,0},{2,3},{3,2},{4,5},{5,4},{6,7},{7,6},{8,9},{9,8},{10,11... | collective-permute-start | bytes 405512 | tf_op jit(solution)/shard_map/ppermute | solution.py:126
  80.5 4.1 %all-to-all-start.5 = ((bf16[8,12,16,128]{3,2,1,0:T(8,128)(2,1)}), bf16[8,12,16,128]{3,2,1,0:T(8,128)(2,1)}, u32[]{:S(2)}, u32[]{:S(2)}) async-start(bf16[8,12,16,128]{3,2,1,0:T(8,128)(2,1)} %bitcast.18), calls=%async_computation.5 | async-start | bytes 786432 | tf_op jit(solution)/shard_map/all_to_all | solution.py:134
  84.7 8.6 %collective-permute-done.7.refs_2_ = bf16[352,768]{1,0:T(8,128)(2,1)} collective-permute-done((bf16[352,768]{1,0:T(8,128)(2,1)}, bf16[352,768]{1,0:T(8,128)(2,1)}, u32[]{:S(2)}, u32[]{:S(2)}) %collective-permute-start.7) | collective-permute-done | bytes 540704 | tf_op jit(solution)/shard_map/ppermute | solution.py:126
  94.2 2.5 %parity_sums.7 = bf16[96,16,128]{2,1,0:T(8,128)(2,1)S(1)} custom-call(s32[4]{0:T(128)S(1)} %iota_xor_fusion.order, s32[40]{0:T(128)S(1)} %get-tuple-element.84.first, s32[40]{0:T(128)S(1)} %get-tuple-element.83.total, bf16[176,768]{1,0:T(8,128)(2,1)S(1)} %copy-done.4, bf16[176,768]{1,0:T(8,128)(2,1)S(1)} %copy-done.17, ...), custom_call_target="tpu_custom_call" | custom-call | flops 799999983616 | bytes 838860800 | tf_op jit(solution)/shard_map/parity_sums/pallas_call | solution.py:54
  98.5 3.1 %collective-permute-start.8 = (bf16[352,384]{1,0:T(8,128)(2,1)}, bf16[352,384]{1,0:T(8,128)(2,1)}, u32[]{:S(2)}, u32[]{:S(2)}) collective-permute-start(bf16[352,384]{1,0:T(8,128)(2,1)} %pad_maximum_fusion.3), channel_id=1, source_target_pairs={{0,2},{1,3},{2,0},{3,1},{4,6},{5,7},{6,4},{7,5},{8,10},{9,11},{10,... | collective-permute-start | bytes 811016 | tf_op jit(solution)/shard_map/ppermute | solution.py:126
  101.6 4.1 %all-to-all-start.2 = ((bf16[8,12,16,128]{3,2,1,0:T(8,128)(2,1)}), bf16[8,12,16,128]{3,2,1,0:T(8,128)(2,1)}, u32[]{:S(2)}, u32[]{:S(2)}) async-start(bf16[8,12,16,128]{3,2,1,0:T(8,128)(2,1)} %bitcast.31), calls=%async_computation.2 | async-start | bytes 786432 | tf_op jit(solution)/shard_map/all_to_all | solution.py:134
  105.8 4.7 %collective-permute-done.11.refs_2_ = bf16[352,768]{1,0:T(8,128)(2,1)} collective-permute-done((bf16[352,768]{1,0:T(8,128)(2,1)}, bf16[352,768]{1,0:T(8,128)(2,1)}, u32[]{:S(2)}, u32[]{:S(2)}) %collective-permute-start.11) | collective-permute-done | bytes 540704 | tf_op jit(solution)/shard_map/ppermute | solution.py:126
  110.4 2.6 %parity_sums.10 = bf16[96,16,128]{2,1,0:T(8,128)(2,1)S(1)} custom-call(s32[4]{0:T(128)S(1)} %iota_xor_fusion.order, s32[40]{0:T(128)S(1)} %get-tuple-element.84.first, s32[40]{0:T(128)S(1)} %get-tuple-element.83.total, bf16[176,768]{1,0:T(8,128)(2,1)S(1)} %copy-done.2, bf16[176,768]{1,0:T(8,128)(2,1)} %collective-permute-done.10.refs_1_, ...), custom_call_target="tpu_custom_call" | custom-call | flops 799999983616 | bytes 838860800 | tf_op jit(solution)/shard_map/parity_sums/pallas_call | solution.py:54
  113.1 4.9 %collective-permute-done.9.refs_1_ = bf16[176,384]{1,0:T(8,128)(2,1)} collective-permute-done((bf16[176,384]{1,0:T(8,128)(2,1)}, bf16[176,384]{1,0:T(8,128)(2,1)}, u32[]{:S(2)}, u32[]{:S(2)}) %collective-permute-start.9) | collective-permute-done | bytes 135200 | tf_op jit(solution)/shard_map/ppermute | solution.py:126
  120.1 4.1 %all-to-all-start.3 = ((bf16[8,12,16,128]{3,2,1,0:T(8,128)(2,1)}), bf16[8,12,16,128]{3,2,1,0:T(8,128)(2,1)}, u32[]{:S(2)}, u32[]{:S(2)}) async-start(bf16[8,12,16,128]{3,2,1,0:T(8,128)(2,1)} %bitcast.33), calls=%async_computation.3 | async-start | bytes 786432 | tf_op jit(solution)/shard_map/all_to_all | solution.py:134
  124.3 2.5 %parity_sums.8 = bf16[96,8,128]{2,1,0:T(8,128)(2,1)} custom-call(s32[4]{0:T(128)S(1)} %iota_xor_fusion.order, s32[40]{0:T(128)S(1)} %get-tuple-element.84.first, s32[40]{0:T(128)S(1)} %get-tuple-element.83.total, bf16[176,384]{1,0:T(8,128)(2,1)S(1)} %copy-done.12, bf16[176,384]{1,0:T(8,128)(2,1)} %collective-permute-done.2.refs_1_, ...), custom_call_target="tpu_custom_call" | custom-call | flops 399999991808 | bytes 419430400 | tf_op jit(solution)/shard_map/parity_sums/pallas_call | solution.py:54
  126.8 2.5 %collective-permute-start.15 = (bf16[8,12,16,128]{3,2,1,0:T(8,128)(2,1)}, bf16[8,12,16,128]{3,2,1,0:T(8,128)(2,1)}, u32[]{:S(2)}, u32[]{:S(2)}) collective-permute-start(bf16[8,12,16,128]{3,2,1,0:T(8,128)(2,1)} %all-to-all-done.2.refs_0_), channel_id=1, source_target_pairs={{0,1},{1,0},{2,3},{3,2},{4,5},{5,4},{6,7},{7,6},{8,9},{9,8},{10,11... | collective-permute-start | bytes 1179656 | tf_op jit(solution)/shard_map/ppermute | solution.py:126
  129.3 3.3 %all-to-all-done.3.refs_1_ = bf16[8,12,16,128]{3,2,1,0:T(8,128)(2,1)} async-done(((bf16[8,12,16,128]{3,2,1,0:T(8,128)(2,1)}), bf16[8,12,16,128]{3,2,1,0:T(8,128)(2,1)}, u32[]{:S(2)}, u32[]{:S(2)}) %all-to-all-start.3) | async-done | bytes 393248 | tf_op jit(solution)/shard_map/all_to_all | solution.py:134
  132.6 4.0 %all-to-all-start = ((bf16[8,12,8,128]{3,2,1,0:T(8,128)(2,1)}), bf16[8,12,8,128]{3,2,1,0:T(8,128)(2,1)}, u32[]{:S(2)}, u32[]{:S(2)}) async-start(bf16[8,12,8,128]{3,2,1,0:T(8,128)(2,1)} %bitcast.13), calls=%async_computation | async-start | bytes 393216 | tf_op jit(solution)/shard_map/all_to_all | solution.py:134
  136.6 2.5 %collective-permute-start.16 = (bf16[8,12,16,128]{3,2,1,0:T(8,128)(2,1)}, bf16[8,12,16,128]{3,2,1,0:T(8,128)(2,1)}, u32[]{:S(2)}, u32[]{:S(2)}) collective-permute-start(bf16[8,12,16,128]{3,2,1,0:T(8,128)(2,1)} %all-to-all-done.3.refs_1_), channel_id=1, source_target_pairs={{0,1},{1,0},{2,3},{3,2},{4,5},{5,4},{6,7},{7,6},{8,9},{9,8},{10,11... | collective-permute-start | bytes 1179656 | tf_op jit(solution)/shard_map/ppermute | solution.py:126
  139.2 2.5 %parity_sums.11 = bf16[96,8,128]{2,1,0:T(8,128)(2,1)} custom-call(s32[4]{0:T(128)S(1)} %iota_xor_fusion.order, s32[40]{0:T(128)S(1)} %get-tuple-element.84.first, s32[40]{0:T(128)S(1)} %get-tuple-element.83.total, bf16[176,384]{1,0:T(8,128)(2,1)S(1)} %copy-done.10, bf16[176,384]{1,0:T(8,128)(2,1)} %collective-permute-done.9.refs_1_, ...), custom_call_target="tpu_custom_call" | custom-call | flops 399999991808 | bytes 419430400 | tf_op jit(solution)/shard_map/parity_sums/pallas_call | solution.py:54
  142.9 3.4 %all-to-all-start.1 = ((bf16[8,12,8,128]{3,2,1,0:T(8,128)(2,1)}), bf16[8,12,8,128]{3,2,1,0:T(8,128)(2,1)S(1)}, u32[]{:S(2)}, u32[]{:S(2)}) async-start(bf16[8,12,8,128]{3,2,1,0:T(8,128)(2,1)} %bitcast.14), calls=%async_computation.1 | async-start | bytes 393216 | tf_op jit(solution)/shard_map/all_to_all | solution.py:134
  146.3 2.5 %collective-permute-start.13 = (bf16[8,12,8,128]{3,2,1,0:T(8,128)(2,1)}, bf16[8,12,8,128]{3,2,1,0:T(8,128)(2,1)S(1)}, u32[]{:S(2)}, u32[]{:S(2)}) collective-permute-start(bf16[8,12,8,128]{3,2,1,0:T(8,128)(2,1)} %all-to-all-done.refs_0_), channel_id=1, source_target_pairs={{0,1},{1,0},{2,3},{3,2},{4,5},{5,4},{6,7},{7,6},{8,9},{9,8},{10,11... | collective-permute-start | bytes 589832 | tf_op jit(solution)/shard_map/ppermute | solution.py:126
  148.8 3.6 %all-to-all-done.1.refs_1_ = bf16[8,12,8,128]{3,2,1,0:T(8,128)(2,1)S(1)} async-done(((bf16[8,12,8,128]{3,2,1,0:T(8,128)(2,1)}), bf16[8,12,8,128]{3,2,1,0:T(8,128)(2,1)S(1)}, u32[]{:S(2)}, u32[]{:S(2)}) %all-to-all-start.1) | async-done | bytes 196640 | tf_op jit(solution)/shard_map/all_to_all | solution.py:134
  152.4 2.5 %collective-permute-start.14 = (bf16[8,12,8,128]{3,2,1,0:T(8,128)(2,1)S(1)}, bf16[8,12,8,128]{3,2,1,0:T(8,128)(2,1)S(1)}, u32[]{:S(2)}, u32[]{:S(2)}) collective-permute-start(bf16[8,12,8,128]{3,2,1,0:T(8,128)(2,1)S(1)} %all-to-all-done.1.refs_1_), channel_id=1, source_target_pairs={{0,1},{1,0},{2,3},{3,2},{4,5},{5,4},{6,7},{7,6},{8,9},{9,8},{10,11... | collective-permute-start | bytes 589832 | tf_op jit(solution)/shard_map/ppermute | solution.py:126
  155.6 2.3 %finish.3.refs_4_ = bf16[12,640,128]{2,1,0:T(8,128)(2,1)} custom-call(s32[1]{0:T(128)} %bitcast.parity, s32[1]{0:T(128)S(6)} %copy.9.lat_count, bf16[8,12,16,128]{3,2,1,0:T(8,128)(2,1)} %all-to-all-done.4.refs_0_, bf16[8,12,16,128]{3,2,1,0:T(8,128)(2,1)} %all-to-all-done.5.refs_1_, bf16[8,12,16,128]{3,2,1,0:T(8,128)(2,1)} %collective-permute-done.17.refs_2_, ...), custom_call_target="tpu_custom_call" | custom-call | tf_op jit(solution)/shard_map/finish/pallas_call | solution.py:98
  157.9 2.3 %finish.4.refs_4_ = bf16[12,640,128]{2,1,0:T(8,128)(2,1)} custom-call(s32[1]{0:T(128)} %bitcast.parity, s32[1]{0:T(128)S(6)} %copy.9.lat_count, bf16[8,12,16,128]{3,2,1,0:T(8,128)(2,1)} %all-to-all-done.2.refs_0_, bf16[8,12,16,128]{3,2,1,0:T(8,128)(2,1)} %all-to-all-done.3.refs_1_, ...), custom_call_target="tpu_custom_call", output_to_operand_aliasing={{}: (6, {})} | custom-call | tf_op jit(solution)/shard_map/finish/pallas_call | solution.py:98
  (81 shorter events, 25.9 us)
Async XLA Ops:
  1.1 32.8 %collective-permute-start.3 = (bf16[176,768]{1,0:T(8,128)(2,1)S(1)}, bf16[176,768]{1,0:T(8,128)(2,1)S(1)}, u32[]{:S(2)}, u32[]{:S(2)}) collective-permute-start(bf16[176,768]{1,0:T(8,128)(2,1)S(1)} %get-tuple-element.50), channel_id=1, source_target_pairs={{0,1},{1,0},{2,3},{3,2},{4,5},{5,4},{6,7},{7,6},{8,9},{9,8},{10,11... | collective-permute-start | bytes 811016 | tf_op jit(solution)/shard_map/ppermute | solution.py:126
  4.2 29.7 %collective-permute-start.5 = (bf16[176,768]{1,0:T(8,128)(2,1)S(1)}, bf16[176,768]{1,0:T(8,128)(2,1)S(1)}, u32[]{:S(2)}, u32[]{:S(2)}) collective-permute-start(bf16[176,768]{1,0:T(8,128)(2,1)S(1)} %get-tuple-element.50), channel_id=1, source_target_pairs={{0,3},{1,2},{2,1},{3,0},{4,7},{5,6},{6,5},{7,4},{8,11},{9,10},{10,... | collective-permute-start | bytes 811016 | tf_op jit(solution)/shard_map/ppermute | solution.py:126
  9.0 21.3 %copy-start.5 = (bf16[176,768]{1,0:T(8,128)(2,1)}, bf16[176,768]{1,0:T(8,128)(2,1)S(1)}, u32[]{:S(2)}) copy-start(bf16[176,768]{1,0:T(8,128)(2,1)S(1)} %get-tuple-element.72.refs_0_) | copy-start | bytes 811012
  9.0 19.2 %collective-permute-start = (bf16[176,768]{1,0:T(8,128)(2,1)S(1)}, bf16[176,768]{1,0:T(8,128)(2,1)S(1)}, u32[]{:S(2)}, u32[]{:S(2)}) collective-permute-start(bf16[176,768]{1,0:T(8,128)(2,1)S(1)} %get-tuple-element.93), channel_id=1, source_target_pairs={{0,1},{1,0},{2,3},{3,2},{4,5},{5,4},{6,7},{7,6},{8,9},{9,8},{10,11... | collective-permute-start | bytes 811016 | tf_op jit(solution)/shard_map/ppermute | solution.py:126
  9.6 24.2 %collective-permute-start.4 = (bf16[176,768]{1,0:T(8,128)(2,1)S(1)}, bf16[176,768]{1,0:T(8,128)(2,1)S(1)}, u32[]{:S(2)}, u32[]{:S(2)}) collective-permute-start(bf16[176,768]{1,0:T(8,128)(2,1)S(1)} %get-tuple-element.57.refs_0_), channel_id=1, source_target_pairs={{0,2},{1,3},{2,0},{3,1},{4,6},{5,7},{6,4},{7,5},{8,10},{9,11},{10,... | collective-permute-start | bytes 811016 | tf_op jit(solution)/shard_map/ppermute | solution.py:126
  28.2 13.9 %copy-start.18 = (bf16[176,768]{1,0:T(8,128)(2,1)}, bf16[176,768]{1,0:T(8,128)(2,1)S(1)}, u32[]{:S(2)}) copy-start(bf16[176,768]{1,0:T(8,128)(2,1)S(1)} %collective-permute-done.refs_1_) | copy-start | bytes 811012
  28.2 11.2 %collective-permute-start.6 = (bf16[176,768]{1,0:T(8,128)(2,1)S(1)}, bf16[176,768]{1,0:T(8,128)(2,1)S(1)}, u32[]{:S(2)}, u32[]{:S(2)}) collective-permute-start(bf16[176,768]{1,0:T(8,128)(2,1)S(1)} %get-tuple-element.55), channel_id=1, source_target_pairs={{0,1},{1,0},{2,3},{3,2},{4,5},{5,4},{6,7},{7,6},{8,9},{9,8},{10,11... | collective-permute-start | bytes 811016 | tf_op jit(solution)/shard_map/ppermute | solution.py:126
  31.1 39.1 %collective-permute-start.1 = (bf16[352,768]{1,0:T(8,128)(2,1)}, bf16[352,768]{1,0:T(8,128)(2,1)}, u32[]{:S(2)}, u32[]{:S(2)}) collective-permute-start(bf16[352,768]{1,0:T(8,128)(2,1)} %pad_maximum_fusion), channel_id=1, source_target_pairs={{0,2},{1,3},{2,0},{3,1},{4,6},{5,7},{6,4},{7,5},{8,10},{9,11},{10,... | collective-permute-start | bytes 1622024 | tf_op jit(solution)/shard_map/ppermute | solution.py:126
  33.9 41.9 %collective-permute-start.10 = (bf16[176,768]{1,0:T(8,128)(2,1)}, bf16[176,768]{1,0:T(8,128)(2,1)}, u32[]{:S(2)}, u32[]{:S(2)}) collective-permute-start(bf16[176,768]{1,0:T(8,128)(2,1)} %get-tuple-element.71), channel_id=1, source_target_pairs={{0,1},{1,0},{2,3},{3,2},{4,5},{5,4},{6,7},{7,6},{8,9},{9,8},{10,11... | collective-permute-start | bytes 811016 | tf_op jit(solution)/shard_map/ppermute | solution.py:126
  42.8 27.3 %copy-start.6 = (bf16[176,768]{1,0:T(8,128)(2,1)S(1)}, bf16[176,768]{1,0:T(8,128)(2,1)}, u32[]{:S(2)}) copy-start(bf16[176,768]{1,0:T(8,128)(2,1)} %copy-done.5) | copy-start | bytes 811012
  42.8 37.6 %all-to-all-start.4 = ((bf16[8,12,16,128]{3,2,1,0:T(8,128)(2,1)}), bf16[8,12,16,128]{3,2,1,0:T(8,128)(2,1)}, u32[]{:S(2)}, u32[]{:S(2)}) async-start(bf16[8,12,16,128]{3,2,1,0:T(8,128)(2,1)} %bitcast.32), calls=%async_computation.4 | async-start | bytes 786432 | tf_op jit(solution)/shard_map/all_to_all | solution.py:134
  48.9 44.4 %collective-permute-start.7 = (bf16[352,768]{1,0:T(8,128)(2,1)}, bf16[352,768]{1,0:T(8,128)(2,1)}, u32[]{:S(2)}, u32[]{:S(2)}) collective-permute-start(bf16[352,768]{1,0:T(8,128)(2,1)} %pad_maximum_fusion.1), channel_id=1, source_target_pairs={{0,2},{1,3},{2,0},{3,1},{4,6},{5,7},{6,4},{7,5},{8,10},{9,11},{10,... | collective-permute-start | bytes 1622024 | tf_op jit(solution)/shard_map/ppermute | solution.py:126
  75.7 17.5 %copy-start.4 = (bf16[176,768]{1,0:T(8,128)(2,1)S(1)}, bf16[176,768]{1,0:T(8,128)(2,1)}, u32[]{:S(2)}) copy-start(bf16[176,768]{1,0:T(8,128)(2,1)} %get-tuple-element.63.refs_0_) | copy-start | bytes 811012
  77.6 32.9 %collective-permute-start.11 = (bf16[352,768]{1,0:T(8,128)(2,1)}, bf16[352,768]{1,0:T(8,128)(2,1)}, u32[]{:S(2)}, u32[]{:S(2)}) collective-permute-start(bf16[352,768]{1,0:T(8,128)(2,1)} %pad_maximum_fusion.2), channel_id=1, source_target_pairs={{0,2},{1,3},{2,0},{3,1},{4,6},{5,7},{6,4},{7,5},{8,10},{9,11},{10,... | collective-permute-start | bytes 1622024 | tf_op jit(solution)/shard_map/ppermute | solution.py:126
  77.6 19.1 %collective-permute-start.2 = (bf16[176,384]{1,0:T(8,128)(2,1)}, bf16[176,384]{1,0:T(8,128)(2,1)}, u32[]{:S(2)}, u32[]{:S(2)}) collective-permute-start(bf16[176,384]{1,0:T(8,128)(2,1)} %get-tuple-element.47), channel_id=1, source_target_pairs={{0,1},{1,0},{2,3},{3,2},{4,5},{5,4},{6,7},{7,6},{8,9},{9,8},{10,11... | collective-permute-start | bytes 405512 | tf_op jit(solution)/shard_map/ppermute | solution.py:126
  80.5 21.1 %all-to-all-start.5 = ((bf16[8,12,16,128]{3,2,1,0:T(8,128)(2,1)}), bf16[8,12,16,128]{3,2,1,0:T(8,128)(2,1)}, u32[]{:S(2)}, u32[]{:S(2)}) async-start(bf16[8,12,16,128]{3,2,1,0:T(8,128)(2,1)} %bitcast.18), calls=%async_computation.5 | async-start | bytes 786432 | tf_op jit(solution)/shard_map/all_to_all | solution.py:134
  84.6 64.2 %collective-permute-start.17 = (bf16[8,12,16,128]{3,2,1,0:T(8,128)(2,1)}, bf16[8,12,16,128]{3,2,1,0:T(8,128)(2,1)}, u32[]{:S(2)}, u32[]{:S(2)}) collective-permute-start(bf16[8,12,16,128]{3,2,1,0:T(8,128)(2,1)} %all-to-all-done.4.refs_0_), channel_id=1, source_target_pairs={{0,1},{1,0},{2,3},{3,2},{4,5},{5,4},{6,7},{7,6},{8,9},{9,8},{10,11... | collective-permute-start | bytes 1179656 | tf_op jit(solution)/shard_map/ppermute | solution.py:126
  93.3 24.7 %collective-permute-start.9 = (bf16[176,384]{1,0:T(8,128)(2,1)}, bf16[176,384]{1,0:T(8,128)(2,1)}, u32[]{:S(2)}, u32[]{:S(2)}) collective-permute-start(bf16[176,384]{1,0:T(8,128)(2,1)} %get-tuple-element.69), channel_id=1, source_target_pairs={{0,1},{1,0},{2,3},{3,2},{4,5},{5,4},{6,7},{7,6},{8,9},{9,8},{10,11... | collective-permute-start | bytes 405512 | tf_op jit(solution)/shard_map/ppermute | solution.py:126
  94.2 16.2 %copy-start.2 = (bf16[176,768]{1,0:T(8,128)(2,1)S(1)}, bf16[176,768]{1,0:T(8,128)(2,1)}, u32[]{:S(2)}) copy-start(bf16[176,768]{1,0:T(8,128)(2,1)} %get-tuple-element.75.refs_0_) | copy-start | bytes 811012
  98.5 25.7 %collective-permute-start.8 = (bf16[352,384]{1,0:T(8,128)(2,1)}, bf16[352,384]{1,0:T(8,128)(2,1)}, u32[]{:S(2)}, u32[]{:S(2)}) collective-permute-start(bf16[352,384]{1,0:T(8,128)(2,1)} %pad_maximum_fusion.3), channel_id=1, source_target_pairs={{0,2},{1,3},{2,0},{3,1},{4,6},{5,7},{6,4},{7,5},{8,10},{9,11},{10,... | collective-permute-start | bytes 811016 | tf_op jit(solution)/shard_map/ppermute | solution.py:126
  101.6 18.6 %all-to-all-start.2 = ((bf16[8,12,16,128]{3,2,1,0:T(8,128)(2,1)}), bf16[8,12,16,128]{3,2,1,0:T(8,128)(2,1)}, u32[]{:S(2)}, u32[]{:S(2)}) async-start(bf16[8,12,16,128]{3,2,1,0:T(8,128)(2,1)} %bitcast.31), calls=%async_computation.2 | async-start | bytes 786432 | tf_op jit(solution)/shard_map/all_to_all | solution.py:134
  105.7 49.9 %collective-permute-start.18 = (bf16[8,12,16,128]{3,2,1,0:T(8,128)(2,1)}, bf16[8,12,16,128]{3,2,1,0:T(8,128)(2,1)}, u32[]{:S(2)}, u32[]{:S(2)}) collective-permute-start(bf16[8,12,16,128]{3,2,1,0:T(8,128)(2,1)} %all-to-all-done.5.refs_1_), channel_id=1, source_target_pairs={{0,1},{1,0},{2,3},{3,2},{4,5},{5,4},{6,7},{7,6},{8,9},{9,8},{10,11... | collective-permute-start | bytes 1179656 | tf_op jit(solution)/shard_map/ppermute | solution.py:126
  119.6 19.6 %collective-permute-start.12 = (bf16[352,384]{1,0:T(8,128)(2,1)}, bf16[352,384]{1,0:T(8,128)(2,1)}, u32[]{:S(2)}, u32[]{:S(2)}) collective-permute-start(bf16[352,384]{1,0:T(8,128)(2,1)} %pad_maximum_fusion.4), channel_id=1, source_target_pairs={{0,2},{1,3},{2,0},{3,1},{4,6},{5,7},{6,4},{7,5},{8,10},{9,11},{10,... | collective-permute-start | bytes 811016 | tf_op jit(solution)/shard_map/ppermute | solution.py:126
  120.1 12.4 %all-to-all-start.3 = ((bf16[8,12,16,128]{3,2,1,0:T(8,128)(2,1)}), bf16[8,12,16,128]{3,2,1,0:T(8,128)(2,1)}, u32[]{:S(2)}, u32[]{:S(2)}) async-start(bf16[8,12,16,128]{3,2,1,0:T(8,128)(2,1)} %bitcast.33), calls=%async_computation.3 | async-start | bytes 786432 | tf_op jit(solution)/shard_map/all_to_all | solution.py:134
  124.3 14.9 %copy-start.7 = (bf16[4,704,128]{2,1,0:T(8,128)(2,1)S(1)}, bf16[4,704,128]{2,1,0:T(8,128)(2,1)}, u32[]{:S(2)}) copy-start(bf16[4,704,128]{2,1,0:T(8,128)(2,1)} %get-tuple-element.85.refs_3_) | copy-start | bytes 2162692
  124.3 14.9 %copy-start.10 = (bf16[176,384]{1,0:T(8,128)(2,1)S(1)}, bf16[176,384]{1,0:T(8,128)(2,1)}, u32[]{:S(2)}) copy-start(bf16[176,384]{1,0:T(8,128)(2,1)} %get-tuple-element.77.refs_0_) | copy-start | bytes 405508
  126.8 31.1 %collective-permute-start.15 = (bf16[8,12,16,128]{3,2,1,0:T(8,128)(2,1)}, bf16[8,12,16,128]{3,2,1,0:T(8,128)(2,1)}, u32[]{:S(2)}, u32[]{:S(2)}) collective-permute-start(bf16[8,12,16,128]{3,2,1,0:T(8,128)(2,1)} %all-to-all-done.2.refs_0_), channel_id=1, source_target_pairs={{0,1},{1,0},{2,3},{3,2},{4,5},{5,4},{6,7},{7,6},{8,9},{9,8},{10,11... | collective-permute-start | bytes 1179656 | tf_op jit(solution)/shard_map/ppermute | solution.py:126
  132.6 10.3 %all-to-all-start = ((bf16[8,12,8,128]{3,2,1,0:T(8,128)(2,1)}), bf16[8,12,8,128]{3,2,1,0:T(8,128)(2,1)}, u32[]{:S(2)}, u32[]{:S(2)}) async-start(bf16[8,12,8,128]{3,2,1,0:T(8,128)(2,1)} %bitcast.13), calls=%async_computation | async-start | bytes 393216 | tf_op jit(solution)/shard_map/all_to_all | solution.py:134
  136.6 21.3 %collective-permute-start.16 = (bf16[8,12,16,128]{3,2,1,0:T(8,128)(2,1)}, bf16[8,12,16,128]{3,2,1,0:T(8,128)(2,1)}, u32[]{:S(2)}, u32[]{:S(2)}) collective-permute-start(bf16[8,12,16,128]{3,2,1,0:T(8,128)(2,1)} %all-to-all-done.3.refs_1_), channel_id=1, source_target_pairs={{0,1},{1,0},{2,3},{3,2},{4,5},{5,4},{6,7},{7,6},{8,9},{9,8},{10,11... | collective-permute-start | bytes 1179656 | tf_op jit(solution)/shard_map/ppermute | solution.py:126
  142.9 9.6 %all-to-all-start.1 = ((bf16[8,12,8,128]{3,2,1,0:T(8,128)(2,1)}), bf16[8,12,8,128]{3,2,1,0:T(8,128)(2,1)S(1)}, u32[]{:S(2)}, u32[]{:S(2)}) async-start(bf16[8,12,8,128]{3,2,1,0:T(8,128)(2,1)} %bitcast.14), calls=%async_computation.1 | async-start | bytes 393216 | tf_op jit(solution)/shard_map/all_to_all | solution.py:134
  146.3 14.0 %collective-permute-start.13 = (bf16[8,12,8,128]{3,2,1,0:T(8,128)(2,1)}, bf16[8,12,8,128]{3,2,1,0:T(8,128)(2,1)S(1)}, u32[]{:S(2)}, u32[]{:S(2)}) collective-permute-start(bf16[8,12,8,128]{3,2,1,0:T(8,128)(2,1)} %all-to-all-done.refs_0_), channel_id=1, source_target_pairs={{0,1},{1,0},{2,3},{3,2},{4,5},{5,4},{6,7},{7,6},{8,9},{9,8},{10,11... | collective-permute-start | bytes 589832 | tf_op jit(solution)/shard_map/ppermute | solution.py:126
  152.4 7.9 %collective-permute-start.14 = (bf16[8,12,8,128]{3,2,1,0:T(8,128)(2,1)S(1)}, bf16[8,12,8,128]{3,2,1,0:T(8,128)(2,1)S(1)}, u32[]{:S(2)}, u32[]{:S(2)}) collective-permute-start(bf16[8,12,8,128]{3,2,1,0:T(8,128)(2,1)S(1)} %all-to-all-done.1.refs_1_), channel_id=1, source_target_pairs={{0,1},{1,0},{2,3},{3,2},{4,5},{5,4},{6,7},{7,6},{8,9},{9,8},{10,11... | collective-permute-start | bytes 589832 | tf_op jit(solution)/shard_map/ppermute | solution.py:126
  (14 other events, 70.7 us)

commit v4 on v3

--- a/solution.py
+++ b/solution.py
@@ -170,12 +170,27 @@
     send_near(1)
     send_near(2)
     send_far(1)
-    out, written, ready = None, 0, []
+    out, written, sums = None, 0, []
+
+    def write():
+        nonlocal out, written
+        first_slot = 2 * plan[GROUPS[written][0]][0]
+        parts = [sums[chunk] for chunk in GROUPS[written]]
+        out = finish(parts, parity, band_rows, first_slot, 2 * pair_count, out)
+        written += 1
+
     for chunk, (start, pairs) in enumerate(plan):
         if 3 <= chunk + 3 < len(plan):
             send_near(chunk + 3)
         if chunk < 1:
             far[chunk], near[chunk + 2] = lax.optimization_barrier((far[chunk], near[chunk + 2]))
+        if 0 < chunk < len(plan) - 0:
+            far[chunk], piece = lax.optimization_barrier((far[chunk], piece))
+            sums.append((piece, swap(piece, 1)))
+        elif chunk > 0:
+            sums.append((piece, swap(piece, 1)))
+        if 2 <= chunk < len(plan) - 1:
+            far[chunk], sums[chunk - 2] = lax.optimization_barrier((far[chunk], sums[chunk - 2]))
         blocks = far[chunk]
         if rows % 16:
             stacked = jnp.concatenate(blocks).reshape(bands, rows, -1)
@@ -186,11 +201,9 @@
         if chunk + 2 < len(plan):
             own = send_far(chunk + 2, own)
         piece = redistribute(own)
-        ready.append((piece, swap(piece, 1)))
-        if chunk == GROUPS[written][-1]:
-            first_slot = 2 * plan[GROUPS[written][0]][0]
-            out = finish(ready, parity, band_rows, first_slot, 2 * pair_count, out)
-            written, ready = written + 1, []
+    sums.append((piece, swap(piece, 1)))
+    while written < len(GROUPS):
+        write()
     return out
 
 

time: 163 us -> 163 us (level)
  starting transfers between devices: 51.2 us -> 42.7 us
  waiting for transfers between devices: 63.4 us -> 71.8 us
    all_to_all x6, waiting for transfers between devices: 8.11 us -> 16 us  [redistribute(): lax.all_to_all(grid.reshape(sets, fields // sets, -1, lats), 'mset', 0, 0)]
    ppermute x19, starting transfers between devices: 27.2 us -> 19.7 us  [swap(): lax.ppermute(value, 'band', [(band, band ^ step) for band in range(bands)])]
    unnamed x42 -> x48, local copies, waits for them, and re-layouts: 4.79 us -> 7.19 us
  transfers between devices with their start and end apart: 25 -> 25, of which waited for: 9 -> 14; matrix products, arithmetic and copies ran while one was open for 12% -> 11% of each run, Pallas kernels for 12% -> 12%
where the time goes in v4:
time: 163 us; the launch traced here: 162 us
  waiting for transfers between devices  71.8 us (44%)
  starting transfers between devices  42.7 us (26%)
  Pallas kernels  20.4 us (13%)
  local copies, waits for them, and re-layouts  18.2 us (11%)
  other arithmetic  7.74 us (5%)
    ppermute x19, waiting for transfers between devices, swap(): lax.ppermute(value, 'band', [(band, band ^ step) for band in range(bands)])  55.8 us
    all_to_all x6, starting transfers between devices, redistribute(): lax.all_to_all(grid.reshape(sets, fields // sets, -1, lats), 'mset', 0, 0)  23 us
    ppermute x19, starting transfers between devices, swap(): lax.ppermute(value, 'band', [(band, band ^ step) for band in range(bands)])  19.7 us
    all_to_all x6, waiting for transfers between devices, redistribute(): lax.all_to_all(grid.reshape(sets, fields // sets, -1, lats), 'mset', 0, 0)  16 us
    pallas_call x6, Pallas kernels, parity_sums(): pl.pallas_call(functools.partial(sums_kernel, rows, fields, start), in_sp...  15.1 us
    concatenate x5, other arithmetic, spread(): held.append(swap(jnp.concatenate(held), bit))  7.72 us
    unnamed x48, local copies, waits for them, and re-layouts  7.19 us
    slice x2, local copies, waits for them, and re-layouts, parity_sums(): legendre = legendre[start:start + pairs]  5.73 us
  transfers between devices with their start and end apart: 25, of which 14 were waited for; matrix products, arithmetic and copies ran while one was open for 11% of the time, Pallas kernels for 12%

profile of v4, /device:TPU:0, one launch (start us, length us, event | category | flops | bytes accessed | tf_op | source)
XLA Modules:
  0.0 161.9 jit_solution(17837078969332767144)
XLA Ops:
  1.1 3.1 %collective-permute-start.1 = (bf16[176,768]{1,0:T(8,128)(2,1)S(1)}, bf16[176,768]{1,0:T(8,128)(2,1)S(1)}, u32[]{:S(2)}, u32[]{:S(2)}) collective-permute-start(bf16[176,768]{1,0:T(8,128)(2,1)S(1)} %get-tuple-element.82), channel_id=1, source_target_pairs={{0,1},{1,0},{2,3},{3,2},{4,5},{5,4},{6,7},{7,6},{8,9},{9,8},{10,11... | collective-permute-start | bytes 811016 | tf_op jit(solution)/shard_map/ppermute | solution.py:126
  4.2 2.5 %collective-permute-start.3 = (bf16[176,768]{1,0:T(8,128)(2,1)S(1)}, bf16[176,768]{1,0:T(8,128)(2,1)S(1)}, u32[]{:S(2)}, u32[]{:S(2)}) collective-permute-start(bf16[176,768]{1,0:T(8,128)(2,1)S(1)} %get-tuple-element.82), channel_id=1, source_target_pairs={{0,3},{1,2},{2,1},{3,0},{4,7},{5,6},{6,5},{7,4},{8,11},{9,10},{10,... | collective-permute-start | bytes 811016 | tf_op jit(solution)/shard_map/ppermute | solution.py:126
  6.6 2.3 %dynamic-slice_bitcast_fusion = (bf16[176,768]{1,0:T(8,128)(2,1)S(1)}, bf16[176,768]{1,0:T(8,128)(2,1)}, bf16[176,768]{1,0:T(8,128)(2,1)}, bf16[176,768]{1,0:T(8...) fusion(bf16[2,176,3840]{2,1,0:T(8,128)(2,1)} %param.4, s32[]{:T(128)S(6)} %select_n.32, s32[]{:T(128)S(6)} %select_n.33), kind=kLoop, calls=%fused_computation.5 | loop fusion | bytes 3244040 | tf_op jit(solution)/shard_map/squeeze | solution.py:131
  10.9 4.3 %fusion.1 = (bf16[8,704,128]{2,1,0:T(8,128)(2,1)S(1)}, bf16[8,704,128]{2,1,0:T(8,128)(2,1)S(1)}, bf16[8,704,128]{2,1,0:T(8,128)(2,1)}, bf16[8,704,128]{2,1,0:T(8,128)(2,1)S(1)}) fusion(bf16[40,704,128]{2,1,0:T(8,128)(2,1)} %param.5), kind=kLoop, calls=%fused_computation.29 | loop fusion | bytes 11534336 | tf_op jit(solution)/shard_map/slice | solution.py:51
  15.2 13.0 %collective-permute-done.refs_1_ = bf16[176,768]{1,0:T(8,128)(2,1)S(1)} collective-permute-done((bf16[176,768]{1,0:T(8,128)(2,1)S(1)}, bf16[176,768]{1,0:T(8,128)(2,1)S(1)}, u32[]{:S(2)}, u32[]{:S(2)}) %collective-permute-start) | collective-permute-done | bytes 270368 | tf_op jit(solution)/shard_map/ppermute | solution.py:126
  29.1 2.9 %collective-permute-start.8 = (bf16[352,768]{1,0:T(8,128)(2,1)}, bf16[352,768]{1,0:T(8,128)(2,1)}, u32[]{:S(2)}, u32[]{:S(2)}) collective-permute-start(bf16[352,768]{1,0:T(8,128)(2,1)} %pad_maximum_fusion.1), channel_id=1, source_target_pairs={{0,2},{1,3},{2,0},{3,1},{4,6},{5,7},{6,4},{7,5},{8,10},{9,11},{10,... | collective-permute-start | bytes 1622024 | tf_op jit(solution)/shard_map/ppermute | solution.py:126
  32.0 7.8 %collective-permute-done.4.refs_1_ = bf16[176,768]{1,0:T(8,128)(2,1)S(1)} collective-permute-done((bf16[176,768]{1,0:T(8,128)(2,1)S(1)}, bf16[176,768]{1,0:T(8,128)(2,1)S(1)}, u32[]{:S(2)}, u32[]{:S(2)}) %collective-permute-start.4) | collective-permute-done | bytes 270368 | tf_op jit(solution)/shard_map/ppermute | solution.py:126
  43.2 4.2 %all-to-all-start = ((bf16[8,12,16,128]{3,2,1,0:T(8,128)(2,1)}), bf16[8,12,16,128]{3,2,1,0:T(8,128)(2,1)}, u32[]{:S(2)}, u32[]{:S(2)}) async-start(bf16[8,12,16,128]{3,2,1,0:T(8,128)(2,1)} %bitcast.31), calls=%async_computation | async-start | bytes 786432 | tf_op jit(solution)/shard_map/all_to_all | solution.py:134
  51.2 2.9 %collective-permute-start.5 = (bf16[352,768]{1,0:T(8,128)(2,1)}, bf16[352,768]{1,0:T(8,128)(2,1)}, u32[]{:S(2)}, u32[]{:S(2)}) collective-permute-start(bf16[352,768]{1,0:T(8,128)(2,1)} %pad_maximum_fusion), channel_id=1, source_target_pairs={{0,2},{1,3},{2,0},{3,1},{4,6},{5,7},{6,4},{7,5},{8,10},{9,11},{10,... | collective-permute-start | bytes 1622024 | tf_op jit(solution)/shard_map/ppermute | solution.py:126
  58.1 2.5 %parity_sums.7 = bf16[96,16,128]{2,1,0:T(8,128)(2,1)S(1)} custom-call(s32[4]{0:T(128)S(1)} %iota_xor_fusion.order, s32[40]{0:T(128)S(1)} %get-tuple-element.154.first, s32[40]{0:T(128)S(1)} %get-tuple-element.153.total, bf16[176,768]{1,0:T(8,128)(2,1)S(1)} %copy-done.10, bf16[176,768]{1,0:T(8,128)(2,1)S(1)} %copy-done.22, ...), custom_call_target="tpu_custom_call" | custom-call | flops 799999983616 | bytes 838860800 | tf_op jit(solution)/shard_map/parity_sums/pallas_call | solution.py:54
  61.3 3.4 %collective-permute-done.7.refs_1_ = bf16[176,768]{1,0:T(8,128)(2,1)} collective-permute-done((bf16[176,768]{1,0:T(8,128)(2,1)}, bf16[176,768]{1,0:T(8,128)(2,1)}, u32[]{:S(2)}, u32[]{:S(2)}) %collective-permute-start.7) | collective-permute-done | bytes 270368 | tf_op jit(solution)/shard_map/ppermute | solution.py:126
  64.7 4.1 %all-to-all-start.1 = ((bf16[8,12,16,128]{3,2,1,0:T(8,128)(2,1)}), bf16[8,12,16,128]{3,2,1,0:T(8,128)(2,1)}, u32[]{:S(2)}, u32[]{:S(2)}) async-start(bf16[8,12,16,128]{3,2,1,0:T(8,128)(2,1)} %bitcast.32), calls=%async_computation.1 | async-start | bytes 786432 | tf_op jit(solution)/shard_map/all_to_all | solution.py:134
  70.7 2.0 %collective-permute-start.9 = (bf16[352,768]{1,0:T(8,128)(2,1)}, bf16[352,768]{1,0:T(8,128)(2,1)}, u32[]{:S(2)}, u32[]{:S(2)}) collective-permute-start(bf16[352,768]{1,0:T(8,128)(2,1)} %pad_maximum_fusion.2), channel_id=1, source_target_pairs={{0,2},{1,3},{2,0},{3,1},{4,6},{5,7},{6,4},{7,5},{8,10},{9,11},{10,... | collective-permute-start | bytes 1622024 | tf_op jit(solution)/shard_map/ppermute | solution.py:126
  72.7 6.5 %collective-permute-done.5.refs_2_ = bf16[352,768]{1,0:T(8,128)(2,1)} collective-permute-done((bf16[352,768]{1,0:T(8,128)(2,1)}, bf16[352,768]{1,0:T(8,128)(2,1)}, u32[]{:S(2)}, u32[]{:S(2)}) %collective-permute-start.5) | collective-permute-done | bytes 540704 | tf_op jit(solution)/shard_map/ppermute | solution.py:126
  79.2 5.2 %collective-permute-done.11.refs_2_ = bf16[8,12,16,128]{3,2,1,0:T(8,128)(2,1)} collective-permute-done((bf16[8,12,16,128]{3,2,1,0:T(8,128)(2,1)}, bf16[8,12,16,128]{3,2,1,0:T(8,128)(2,1)}, u32[]{:S(2)}, u32[]{:S(2)}) %collective-permute-start.11) | collective-permute-done | bytes 393248 | tf_op jit(solution)/shard_map/ppermute | solution.py:126
  86.4 2.5 %parity_sums.8 = bf16[96,16,128]{2,1,0:T(8,128)(2,1)S(1)} custom-call(s32[4]{0:T(128)S(1)} %iota_xor_fusion.order, s32[40]{0:T(128)S(1)} %get-tuple-element.154.first, s32[40]{0:T(128)S(1)} %get-tuple-element.153.total, bf16[176,768]{1,0:T(8,128)(2,1)S(1)} %copy-done.8, bf16[176,768]{1,0:T(8,128)(2,1)S(1)} %copy-done.20, ...), custom_call_target="tpu_custom_call" | custom-call | flops 799999983616 | bytes 838860800 | tf_op jit(solution)/shard_map/parity_sums/pallas_call | solution.py:54
  89.6 3.7 %all-to-all-start.2 = ((bf16[8,12,16,128]{3,2,1,0:T(8,128)(2,1)}), bf16[8,12,16,128]{3,2,1,0:T(8,128)(2,1)S(1)}, u32[]{:S(2)}, u32[]{:S(2)}) async-start(bf16[8,12,16,128]{3,2,1,0:T(8,128)(2,1)} %bitcast.33), calls=%async_computation.2 | async-start | bytes 786432 | tf_op jit(solution)/shard_map/all_to_all | solution.py:134
  95.0 2.0 %collective-permute-start.14 = (bf16[352,384]{1,0:T(8,128)(2,1)}, bf16[352,384]{1,0:T(8,128)(2,1)}, u32[]{:S(2)}, u32[]{:S(2)}) collective-permute-start(bf16[352,384]{1,0:T(8,128)(2,1)} %pad_maximum_fusion.4), channel_id=1, source_target_pairs={{0,2},{1,3},{2,0},{3,1},{4,6},{5,7},{6,4},{7,5},{8,10},{9,11},{10,... | collective-permute-start | bytes 811016 | tf_op jit(solution)/shard_map/ppermute | solution.py:126
  97.1 5.4 %collective-permute-done.9.refs_2_ = bf16[352,768]{1,0:T(8,128)(2,1)} collective-permute-done((bf16[352,768]{1,0:T(8,128)(2,1)}, bf16[352,768]{1,0:T(8,128)(2,1)}, u32[]{:S(2)}, u32[]{:S(2)}) %collective-permute-start.9) | collective-permute-done | bytes 540704 | tf_op jit(solution)/shard_map/ppermute | solution.py:126
  102.4 4.7 %collective-permute-done.12.refs_3_ = bf16[8,12,16,128]{3,2,1,0:T(8,128)(2,1)} collective-permute-done((bf16[8,12,16,128]{3,2,1,0:T(8,128)(2,1)}, bf16[8,12,16,128]{3,2,1,0:T(8,128)(2,1)}, u32[]{:S(2)}, u32[]{:S(2)}) %collective-permute-start.12) | collective-permute-done | bytes 393248 | tf_op jit(solution)/shard_map/ppermute | solution.py:126
  107.1 3.3 %parity_sums.9 = bf16[96,16,128]{2,1,0:T(8,128)(2,1)} custom-call(s32[4]{0:T(128)S(1)} %iota_xor_fusion.order, s32[40]{0:T(128)S(1)} %get-tuple-element.154.first, s32[40]{0:T(128)S(1)} %get-tuple-element.153.total, bf16[176,768]{1,0:T(8,128)(2,1)S(1)} %copy-done.6, bf16[176,768]{1,0:T(8,128)(2,1)} %collective-permute-done.7.refs_1_, ...), custom_call_target="tpu_custom_call" | custom-call | flops 799999983616 | bytes 838860800 | tf_op jit(solution)/shard_map/parity_sums/pallas_call | solution.py:54
  110.4 3.7 %all-to-all-start.3 = ((bf16[8,12,16,128]{3,2,1,0:T(8,128)(2,1)}), bf16[8,12,16,128]{3,2,1,0:T(8,128)(2,1)S(1)}, u32[]{:S(2)}, u32[]{:S(2)}) async-start(bf16[8,12,16,128]{3,2,1,0:T(8,128)(2,1)} %bitcast.16), calls=%async_computation.3 | async-start | bytes 786432 | tf_op jit(solution)/shard_map/all_to_all | solution.py:134
  117.3 2.0 %collective-permute-start.13 = (bf16[352,384]{1,0:T(8,128)(2,1)}, bf16[352,384]{1,0:T(8,128)(2,1)}, u32[]{:S(2)}, u32[]{:S(2)}) collective-permute-start(bf16[352,384]{1,0:T(8,128)(2,1)} %pad_maximum_fusion.3), channel_id=1, source_target_pairs={{0,2},{1,3},{2,0},{3,1},{4,6},{5,7},{6,4},{7,5},{8,10},{9,11},{10,... | collective-permute-start | bytes 811016 | tf_op jit(solution)/shard_map/ppermute | solution.py:126
  119.4 3.1 %all-to-all-done.3.refs_1_ = bf16[8,12,16,128]{3,2,1,0:T(8,128)(2,1)S(1)} async-done(((bf16[8,12,16,128]{3,2,1,0:T(8,128)(2,1)}), bf16[8,12,16,128]{3,2,1,0:T(8,128)(2,1)S(1)}, u32[]{:S(2)}, u32[]{:S(2)}) %all-to-all-start.3) | async-done | bytes 393248 | tf_op jit(solution)/shard_map/all_to_all | solution.py:134
  122.5 7.6 %collective-permute-done.15.refs_2_ = bf16[8,12,16,128]{3,2,1,0:T(8,128)(2,1)S(1)} collective-permute-done((bf16[8,12,16,128]{3,2,1,0:T(8,128)(2,1)}, bf16[8,12,16,128]{3,2,1,0:T(8,128)(2,1)S(1)}, u32[]{:S(2)}, u32[]{:S(2)}) %collective-permute-start.15) | collective-permute-done | bytes 393248 | tf_op jit(solution)/shard_map/ppermute | solution.py:126
  130.1 2.5 %parity_sums.10 = bf16[96,8,128]{2,1,0:T(8,128)(2,1)} custom-call(s32[4]{0:T(128)S(1)} %iota_xor_fusion.order, s32[40]{0:T(128)S(1)} %get-tuple-element.154.first, s32[40]{0:T(128)S(1)} %get-tuple-element.153.total, bf16[176,384]{1,0:T(8,128)(2,1)S(1)} %copy-done.15, bf16[176,384]{1,0:T(8,128)(2,1)} %collective-permute-done.10.refs_1_, ...), custom_call_target="tpu_custom_call" | custom-call | flops 399999991808 | bytes 419430400 | tf_op jit(solution)/shard_map/parity_sums/pallas_call | solution.py:54
  132.6 3.8 %all-to-all-start.4 = ((bf16[8,12,8,128]{3,2,1,0:T(8,128)(2,1)}), bf16[8,12,8,128]{3,2,1,0:T(8,128)(2,1)S(1)}, u32[]{:S(2)}, u32[]{:S(2)}) async-start(bf16[8,12,8,128]{3,2,1,0:T(8,128)(2,1)} %bitcast.17), calls=%async_computation.4 | async-start | bytes 393216 | tf_op jit(solution)/shard_map/all_to_all | solution.py:134
  136.4 6.2 %all-to-all-done.4.refs_0_ = bf16[8,12,8,128]{3,2,1,0:T(8,128)(2,1)S(1)} async-done(((bf16[8,12,8,128]{3,2,1,0:T(8,128)(2,1)}), bf16[8,12,8,128]{3,2,1,0:T(8,128)(2,1)S(1)}, u32[]{:S(2)}, u32[]{:S(2)}) %all-to-all-start.4) | async-done | bytes 196640 | tf_op jit(solution)/shard_map/all_to_all | solution.py:134
  142.6 2.5 %parity_sums.11 = bf16[96,8,128]{2,1,0:T(8,128)(2,1)} custom-call(s32[4]{0:T(128)S(1)} %iota_xor_fusion.order, s32[40]{0:T(128)S(1)} %get-tuple-element.154.first, s32[40]{0:T(128)S(1)} %get-tuple-element.153.total, bf16[176,384]{1,0:T(8,128)(2,1)S(1)} %copy-done.14, bf16[176,384]{1,0:T(8,128)(2,1)} %collective-permute-done.6.refs_1_, ...), custom_call_target="tpu_custom_call" | custom-call | flops 399999991808 | bytes 419430400 | tf_op jit(solution)/shard_map/parity_sums/pallas_call | solution.py:54
  145.2 3.4 %all-to-all-start.5 = ((bf16[8,12,8,128]{3,2,1,0:T(8,128)(2,1)}), bf16[8,12,8,128]{3,2,1,0:T(8,128)(2,1)S(1)}, u32[]{:S(2)}, u32[]{:S(2)}) async-start(bf16[8,12,8,128]{3,2,1,0:T(8,128)(2,1)} %bitcast.18), calls=%async_computation.5 | async-start | bytes 393216 | tf_op jit(solution)/shard_map/all_to_all | solution.py:134
  148.7 6.1 %all-to-all-done.5.refs_1_ = bf16[8,12,8,128]{3,2,1,0:T(8,128)(2,1)S(1)} async-done(((bf16[8,12,8,128]{3,2,1,0:T(8,128)(2,1)}), bf16[8,12,8,128]{3,2,1,0:T(8,128)(2,1)S(1)}, u32[]{:S(2)}, u32[]{:S(2)}) %all-to-all-start.5) | async-done | bytes 196640 | tf_op jit(solution)/shard_map/all_to_all | solution.py:134
  155.4 2.4 %finish.3.refs_4_ = bf16[12,640,128]{2,1,0:T(8,128)(2,1)} custom-call(s32[1]{0:T(128)} %bitcast.parity, s32[1]{0:T(128)S(6)} %copy.9.lat_count, bf16[8,12,16,128]{3,2,1,0:T(8,128)(2,1)} %all-to-all-done.refs_0_, bf16[8,12,16,128]{3,2,1,0:T(8,128)(2,1)} %all-to-all-done.1.refs_1_, bf16[8,12,16,128]{3,2,1,0:T(8,128)(2,1)} %collective-permute-done.11.refs_2_, ...), custom_call_target="tpu_custom_call" | custom-call | tf_op jit(solution)/shard_map/finish/pallas_call | solution.py:98
  (87 shorter events, 29.2 us)
Async XLA Ops:
  1.1 27.2 %collective-permute-start.1 = (bf16[176,768]{1,0:T(8,128)(2,1)S(1)}, bf16[176,768]{1,0:T(8,128)(2,1)S(1)}, u32[]{:S(2)}, u32[]{:S(2)}) collective-permute-start(bf16[176,768]{1,0:T(8,128)(2,1)S(1)} %get-tuple-element.82), channel_id=1, source_target_pairs={{0,1},{1,0},{2,3},{3,2},{4,5},{5,4},{6,7},{7,6},{8,9},{9,8},{10,11... | collective-permute-start | bytes 811016 | tf_op jit(solution)/shard_map/ppermute | solution.py:126
  4.2 24.1 %collective-permute-start.3 = (bf16[176,768]{1,0:T(8,128)(2,1)S(1)}, bf16[176,768]{1,0:T(8,128)(2,1)S(1)}, u32[]{:S(2)}, u32[]{:S(2)}) collective-permute-start(bf16[176,768]{1,0:T(8,128)(2,1)S(1)} %get-tuple-element.82), channel_id=1, source_target_pairs={{0,3},{1,2},{2,1},{3,0},{4,7},{5,6},{6,5},{7,4},{8,11},{9,10},{10,... | collective-permute-start | bytes 811016 | tf_op jit(solution)/shard_map/ppermute | solution.py:126
  8.9 19.3 %copy-start.9 = (bf16[176,768]{1,0:T(8,128)(2,1)}, bf16[176,768]{1,0:T(8,128)(2,1)S(1)}, u32[]{:S(2)}) copy-start(bf16[176,768]{1,0:T(8,128)(2,1)S(1)} %get-tuple-element.104.refs_0_) | copy-start | bytes 811012
  8.9 19.3 %copy-start.23 = (s32[40]{0:T(128)S(1)}, s32[40]{0:T(128)}, u32[]{:S(2)}) copy-start(s32[40]{0:T(128)} %param.6) | copy-start | bytes 484
  8.9 19.3 %collective-permute-start = (bf16[176,768]{1,0:T(8,128)(2,1)S(1)}, bf16[176,768]{1,0:T(8,128)(2,1)S(1)}, u32[]{:S(2)}, u32[]{:S(2)}) collective-permute-start(bf16[176,768]{1,0:T(8,128)(2,1)S(1)} %get-tuple-element.164), channel_id=1, source_target_pairs={{0,1},{1,0},{2,3},{3,2},{4,5},{5,4},{6,7},{7,6},{8,9},{9,8},{10,11... | collective-permute-start | bytes 811016 | tf_op jit(solution)/shard_map/ppermute | solution.py:126
  9.6 18.6 %collective-permute-start.2 = (bf16[176,768]{1,0:T(8,128)(2,1)S(1)}, bf16[176,768]{1,0:T(8,128)(2,1)S(1)}, u32[]{:S(2)}, u32[]{:S(2)}) collective-permute-start(bf16[176,768]{1,0:T(8,128)(2,1)S(1)} %get-tuple-element.89.refs_0_), channel_id=1, source_target_pairs={{0,2},{1,3},{2,0},{3,1},{4,6},{5,7},{6,4},{7,5},{8,10},{9,11},{10,... | collective-permute-start | bytes 811016 | tf_op jit(solution)/shard_map/ppermute | solution.py:126
  28.2 14.3 %copy-start.21 = (bf16[176,768]{1,0:T(8,128)(2,1)}, bf16[176,768]{1,0:T(8,128)(2,1)S(1)}, u32[]{:S(2)}) copy-start(bf16[176,768]{1,0:T(8,128)(2,1)S(1)} %collective-permute-done.refs_1_) | copy-start | bytes 811012
  28.2 11.6 %collective-permute-start.4 = (bf16[176,768]{1,0:T(8,128)(2,1)S(1)}, bf16[176,768]{1,0:T(8,128)(2,1)S(1)}, u32[]{:S(2)}, u32[]{:S(2)}) collective-permute-start(bf16[176,768]{1,0:T(8,128)(2,1)S(1)} %get-tuple-element.87), channel_id=1, source_target_pairs={{0,1},{1,0},{2,3},{3,2},{4,5},{5,4},{6,7},{7,6},{8,9},{9,8},{10,11... | collective-permute-start | bytes 811016 | tf_op jit(solution)/shard_map/ppermute | solution.py:126
  29.1 26.1 %collective-permute-start.8 = (bf16[352,768]{1,0:T(8,128)(2,1)}, bf16[352,768]{1,0:T(8,128)(2,1)}, u32[]{:S(2)}, u32[]{:S(2)}) collective-permute-start(bf16[352,768]{1,0:T(8,128)(2,1)} %pad_maximum_fusion.1), channel_id=1, source_target_pairs={{0,2},{1,3},{2,0},{3,1},{4,6},{5,7},{6,4},{7,5},{8,10},{9,11},{10,... | collective-permute-start | bytes 1622024 | tf_op jit(solution)/shard_map/ppermute | solution.py:126
  43.2 12.6 %copy-start.10 = (bf16[176,768]{1,0:T(8,128)(2,1)S(1)}, bf16[176,768]{1,0:T(8,128)(2,1)}, u32[]{:S(2)}) copy-start(bf16[176,768]{1,0:T(8,128)(2,1)} %copy-done.9) | copy-start | bytes 811012
  43.2 12.6 %all-to-all-start = ((bf16[8,12,16,128]{3,2,1,0:T(8,128)(2,1)}), bf16[8,12,16,128]{3,2,1,0:T(8,128)(2,1)}, u32[]{:S(2)}, u32[]{:S(2)}) async-start(bf16[8,12,16,128]{3,2,1,0:T(8,128)(2,1)} %bitcast.31), calls=%async_computation | async-start | bytes 786432 | tf_op jit(solution)/shard_map/all_to_all | solution.py:134
  49.4 15.3 %collective-permute-start.7 = (bf16[176,768]{1,0:T(8,128)(2,1)}, bf16[176,768]{1,0:T(8,128)(2,1)}, u32[]{:S(2)}, u32[]{:S(2)}) collective-permute-start(bf16[176,768]{1,0:T(8,128)(2,1)} %get-tuple-element.98), channel_id=1, source_target_pairs={{0,1},{1,0},{2,3},{3,2},{4,5},{5,4},{6,7},{7,6},{8,9},{9,8},{10,11... | collective-permute-start | bytes 811016 | tf_op jit(solution)/shard_map/ppermute | solution.py:126
  51.2 28.0 %collective-permute-start.5 = (bf16[352,768]{1,0:T(8,128)(2,1)}, bf16[352,768]{1,0:T(8,128)(2,1)}, u32[]{:S(2)}, u32[]{:S(2)}) collective-permute-start(bf16[352,768]{1,0:T(8,128)(2,1)} %pad_maximum_fusion), channel_id=1, source_target_pairs={{0,2},{1,3},{2,0},{3,1},{4,6},{5,7},{6,4},{7,5},{8,10},{9,11},{10,... | collective-permute-start | bytes 1622024 | tf_op jit(solution)/shard_map/ppermute | solution.py:126
  55.8 28.7 %collective-permute-start.11 = (bf16[8,12,16,128]{3,2,1,0:T(8,128)(2,1)}, bf16[8,12,16,128]{3,2,1,0:T(8,128)(2,1)}, u32[]{:S(2)}, u32[]{:S(2)}) collective-permute-start(bf16[8,12,16,128]{3,2,1,0:T(8,128)(2,1)} %all-to-all-done.refs_0_), channel_id=1, source_target_pairs={{0,1},{1,0},{2,3},{3,2},{4,5},{5,4},{6,7},{7,6},{8,9},{9,8},{10,11... | collective-permute-start | bytes 1179656 | tf_op jit(solution)/shard_map/ppermute | solution.py:126
  58.1 10.8 %copy-start.5 = (bf16[176,768]{1,0:T(8,128)(2,1)S(1)}, bf16[176,768]{1,0:T(8,128)(2,1)}, u32[]{:S(2)}) copy-start(bf16[176,768]{1,0:T(8,128)(2,1)} %get-tuple-element.127.refs_0_) | copy-start | bytes 811012
  64.7 14.5 %all-to-all-start.1 = ((bf16[8,12,16,128]{3,2,1,0:T(8,128)(2,1)}), bf16[8,12,16,128]{3,2,1,0:T(8,128)(2,1)}, u32[]{:S(2)}, u32[]{:S(2)}) async-start(bf16[8,12,16,128]{3,2,1,0:T(8,128)(2,1)} %bitcast.32), calls=%async_computation.1 | async-start | bytes 786432 | tf_op jit(solution)/shard_map/all_to_all | solution.py:134
  68.8 20.8 %collective-permute-start.10 = (bf16[176,384]{1,0:T(8,128)(2,1)}, bf16[176,384]{1,0:T(8,128)(2,1)}, u32[]{:S(2)}, u32[]{:S(2)}) collective-permute-start(bf16[176,384]{1,0:T(8,128)(2,1)} %get-tuple-element.110), channel_id=1, source_target_pairs={{0,1},{1,0},{2,3},{3,2},{4,5},{5,4},{6,7},{7,6},{8,9},{9,8},{10,11... | collective-permute-start | bytes 405512 | tf_op jit(solution)/shard_map/ppermute | solution.py:126
  70.7 31.7 %collective-permute-start.9 = (bf16[352,768]{1,0:T(8,128)(2,1)}, bf16[352,768]{1,0:T(8,128)(2,1)}, u32[]{:S(2)}, u32[]{:S(2)}) collective-permute-start(bf16[352,768]{1,0:T(8,128)(2,1)} %pad_maximum_fusion.2), channel_id=1, source_target_pairs={{0,2},{1,3},{2,0},{3,1},{4,6},{5,7},{6,4},{7,5},{8,10},{9,11},{10,... | collective-permute-start | bytes 1622024 | tf_op jit(solution)/shard_map/ppermute | solution.py:126
  79.2 27.9 %collective-permute-start.12 = (bf16[8,12,16,128]{3,2,1,0:T(8,128)(2,1)}, bf16[8,12,16,128]{3,2,1,0:T(8,128)(2,1)}, u32[]{:S(2)}, u32[]{:S(2)}) collective-permute-start(bf16[8,12,16,128]{3,2,1,0:T(8,128)(2,1)} %all-to-all-done.1.refs_1_), channel_id=1, source_target_pairs={{0,1},{1,0},{2,3},{3,2},{4,5},{5,4},{6,7},{7,6},{8,9},{9,8},{10,11... | collective-permute-start | bytes 1179656 | tf_op jit(solution)/shard_map/ppermute | solution.py:126
  86.4 20.7 %copy-start.6 = (bf16[176,768]{1,0:T(8,128)(2,1)S(1)}, bf16[176,768]{1,0:T(8,128)(2,1)}, u32[]{:S(2)}) copy-start(bf16[176,768]{1,0:T(8,128)(2,1)} %get-tuple-element.127.refs_0_) | copy-start | bytes 811012
  89.6 12.8 %all-to-all-start.2 = ((bf16[8,12,16,128]{3,2,1,0:T(8,128)(2,1)}), bf16[8,12,16,128]{3,2,1,0:T(8,128)(2,1)S(1)}, u32[]{:S(2)}, u32[]{:S(2)}) async-start(bf16[8,12,16,128]{3,2,1,0:T(8,128)(2,1)} %bitcast.33), calls=%async_computation.2 | async-start | bytes 786432 | tf_op jit(solution)/shard_map/all_to_all | solution.py:134
  93.3 17.0 %collective-permute-start.6 = (bf16[176,384]{1,0:T(8,128)(2,1)}, bf16[176,384]{1,0:T(8,128)(2,1)}, u32[]{:S(2)}, u32[]{:S(2)}) collective-permute-start(bf16[176,384]{1,0:T(8,128)(2,1)} %get-tuple-element.96), channel_id=1, source_target_pairs={{0,1},{1,0},{2,3},{3,2},{4,5},{5,4},{6,7},{7,6},{8,9},{9,8},{10,11... | collective-permute-start | bytes 405512 | tf_op jit(solution)/shard_map/ppermute | solution.py:126
  95.0 24.3 %collective-permute-start.14 = (bf16[352,384]{1,0:T(8,128)(2,1)}, bf16[352,384]{1,0:T(8,128)(2,1)}, u32[]{:S(2)}, u32[]{:S(2)}) collective-permute-start(bf16[352,384]{1,0:T(8,128)(2,1)} %pad_maximum_fusion.4), channel_id=1, source_target_pairs={{0,2},{1,3},{2,0},{3,1},{4,6},{5,7},{6,4},{7,5},{8,10},{9,11},{10,... | collective-permute-start | bytes 811016 | tf_op jit(solution)/shard_map/ppermute | solution.py:126
  110.4 12.1 %all-to-all-start.3 = ((bf16[8,12,16,128]{3,2,1,0:T(8,128)(2,1)}), bf16[8,12,16,128]{3,2,1,0:T(8,128)(2,1)S(1)}, u32[]{:S(2)}, u32[]{:S(2)}) async-start(bf16[8,12,16,128]{3,2,1,0:T(8,128)(2,1)} %bitcast.16), calls=%async_computation.3 | async-start | bytes 786432 | tf_op jit(solution)/shard_map/all_to_all | solution.py:134
  114.1 15.9 %collective-permute-start.15 = (bf16[8,12,16,128]{3,2,1,0:T(8,128)(2,1)}, bf16[8,12,16,128]{3,2,1,0:T(8,128)(2,1)S(1)}, u32[]{:S(2)}, u32[]{:S(2)}) collective-permute-start(bf16[8,12,16,128]{3,2,1,0:T(8,128)(2,1)} %copy-done), channel_id=1, source_target_pairs={{0,1},{1,0},{2,3},{3,2},{4,5},{5,4},{6,7},{7,6},{8,9},{9,8},{10,11... | collective-permute-start | bytes 1179656 | tf_op jit(solution)/shard_map/ppermute | solution.py:126
  117.3 19.1 %collective-permute-start.13 = (bf16[352,384]{1,0:T(8,128)(2,1)}, bf16[352,384]{1,0:T(8,128)(2,1)}, u32[]{:S(2)}, u32[]{:S(2)}) collective-permute-start(bf16[352,384]{1,0:T(8,128)(2,1)} %pad_maximum_fusion.3), channel_id=1, source_target_pairs={{0,2},{1,3},{2,0},{3,1},{4,6},{5,7},{6,4},{7,5},{8,10},{9,11},{10,... | collective-permute-start | bytes 811016 | tf_op jit(solution)/shard_map/ppermute | solution.py:126
  130.1 12.6 %copy-start.14 = (bf16[176,384]{1,0:T(8,128)(2,1)S(1)}, bf16[176,384]{1,0:T(8,128)(2,1)}, u32[]{:S(2)}) copy-start(bf16[176,384]{1,0:T(8,128)(2,1)} %get-tuple-element.143.refs_0_) | copy-start | bytes 405508
  132.6 10.1 %all-to-all-start.4 = ((bf16[8,12,8,128]{3,2,1,0:T(8,128)(2,1)}), bf16[8,12,8,128]{3,2,1,0:T(8,128)(2,1)S(1)}, u32[]{:S(2)}, u32[]{:S(2)}) async-start(bf16[8,12,8,128]{3,2,1,0:T(8,128)(2,1)} %bitcast.17), calls=%async_computation.4 | async-start | bytes 393216 | tf_op jit(solution)/shard_map/all_to_all | solution.py:134
  136.4 21.4 %collective-permute-start.18 = (bf16[8,12,16,128]{3,2,1,0:T(8,128)(2,1)}, bf16[8,12,16,128]{3,2,1,0:T(8,128)(2,1)}, u32[]{:S(2)}, u32[]{:S(2)}) collective-permute-start(bf16[8,12,16,128]{3,2,1,0:T(8,128)(2,1)} %copy-done.2), channel_id=1, source_target_pairs={{0,1},{1,0},{2,3},{3,2},{4,5},{5,4},{6,7},{7,6},{8,9},{9,8},{10,11... | collective-permute-start | bytes 1179656 | tf_op jit(solution)/shard_map/ppermute | solution.py:126
  145.2 9.6 %all-to-all-start.5 = ((bf16[8,12,8,128]{3,2,1,0:T(8,128)(2,1)}), bf16[8,12,8,128]{3,2,1,0:T(8,128)(2,1)S(1)}, u32[]{:S(2)}, u32[]{:S(2)}) async-start(bf16[8,12,8,128]{3,2,1,0:T(8,128)(2,1)} %bitcast.18), calls=%async_computation.5 | async-start | bytes 393216 | tf_op jit(solution)/shard_map/all_to_all | solution.py:134
  148.6 11.4 %collective-permute-start.16 = (bf16[8,12,8,128]{3,2,1,0:T(8,128)(2,1)}, bf16[8,12,8,128]{3,2,1,0:T(8,128)(2,1)S(1)}, u32[]{:S(2)}, u32[]{:S(2)}) collective-permute-start(bf16[8,12,8,128]{3,2,1,0:T(8,128)(2,1)} %copy-done.11), channel_id=1, source_target_pairs={{0,1},{1,0},{2,3},{3,2},{4,5},{5,4},{6,7},{7,6},{8,9},{9,8},{10,11... | collective-permute-start | bytes 589832 | tf_op jit(solution)/shard_map/ppermute | solution.py:126
  154.7 6.3 %collective-permute-start.17 = (bf16[8,12,8,128]{3,2,1,0:T(8,128)(2,1)S(1)}, bf16[8,12,8,128]{3,2,1,0:T(8,128)(2,1)S(1)}, u32[]{:S(2)}, u32[]{:S(2)}) collective-permute-start(bf16[8,12,8,128]{3,2,1,0:T(8,128)(2,1)S(1)} %all-to-all-done.5.refs_1_), channel_id=1, source_target_pairs={{0,1},{1,0},{2,3},{3,2},{4,5},{5,4},{6,7},{7,6},{8,9},{9,8},{10,11... | collective-permute-start | bytes 589832 | tf_op jit(solution)/shard_map/ppermute | solution.py:126
  (17 other events, 50.6 us)

commit v5 on v4

--- a/solution.py
+++ b/solution.py
@@ -10,6 +10,7 @@
 TRUNC = 1279
 VMEM = 24 * 2**20
 CHUNKS = (8, 8, 8, 8, 4, 4)
+MIRRORED = {2: 0, 3: 1, 5: 2}
 GROUPS = ((0, 1), (2, 3), (4, 5))
 
 
@@ -189,8 +190,12 @@
             sums.append((piece, swap(piece, 1)))
         elif chunk > 0:
             sums.append((piece, swap(piece, 1)))
-        if 2 <= chunk < len(plan) - 1:
-            far[chunk], sums[chunk - 2] = lax.optimization_barrier((far[chunk], sums[chunk - 2]))
+        if chunk in MIRRORED:
+            back = MIRRORED[chunk]
+            far[chunk], sums[back] = lax.optimization_barrier((far[chunk], sums[back]))
+        if chunk == GROUPS[0][-1] + 3:
+            write()
+            far[chunk], out = lax.optimization_barrier((far[chunk], out))
         blocks = far[chunk]
         if rows % 16:
             stacked = jnp.concatenate(blocks).reshape(bands, rows, -1)

time: 163 us -> 157 us (0.963)
  waiting for transfers between devices: 71.8 us -> 65.2 us
    all_to_all x6, waiting for transfers between devices: 16 us -> 10.1 us  [redistribute(): lax.all_to_all(grid.reshape(sets, fields // sets, -1, lats), 'mset', 0, 0)]
    unnamed x48 -> x42, local copies, waits for them, and re-layouts: 7.19 us -> 6.45 us
  transfers between devices with their start and end apart: 25 -> 25, of which waited for: 14 -> 15; matrix products, arithmetic and copies ran while one was open for 11% -> 11% of each run, Pallas kernels for 12% -> 13%
where the time goes in v5:
time: 157 us; the launch traced here: 156 us
  waiting for transfers between devices  65.2 us (42%)
  starting transfers between devices  43.4 us (28%)
  Pallas kernels  20.7 us (13%)
  local copies, waits for them, and re-layouts  17.5 us (11%)
  other arithmetic  7.78 us (5%)
    ppermute x19, waiting for transfers between devices, swap(): lax.ppermute(value, 'band', [(band, band ^ step) for band in range(bands)])  55.1 us
    all_to_all x6, starting transfers between devices, redistribute(): lax.all_to_all(grid.reshape(sets, fields // sets, -1, lats), 'mset', 0, 0)  23.7 us
    ppermute x19, starting transfers between devices, swap(): lax.ppermute(value, 'band', [(band, band ^ step) for band in range(bands)])  19.7 us
    pallas_call x6, Pallas kernels, parity_sums(): pl.pallas_call(functools.partial(sums_kernel, rows, fields, start), in_sp...  15.2 us
    all_to_all x6, waiting for transfers between devices, redistribute(): lax.all_to_all(grid.reshape(sets, fields // sets, -1, lats), 'mset', 0, 0)  10.1 us
    concatenate x5, other arithmetic, spread(): held.append(swap(jnp.concatenate(held), bit))  7.77 us
    unnamed x42, local copies, waits for them, and re-layouts  6.45 us
    slice x2, local copies, waits for them, and re-layouts, parity_sums(): legendre = legendre[start:start + pairs]  5.77 us
  transfers between devices with their start and end apart: 25, of which 15 were waited for; matrix products, arithmetic and copies ran while one was open for 11% of the time, Pallas kernels for 13%

profile of v5, /device:TPU:0, one launch (start us, length us, event | category | flops | bytes accessed | tf_op | source)
XLA Modules:
  0.0 155.6 jit_solution(11900042217097725103)
XLA Ops:
  1.1 3.1 %collective-permute-start.1 = (bf16[176,768]{1,0:T(8,128)(2,1)S(1)}, bf16[176,768]{1,0:T(8,128)(2,1)S(1)}, u32[]{:S(2)}, u32[]{:S(2)}) collective-permute-start(bf16[176,768]{1,0:T(8,128)(2,1)S(1)} %get-tuple-element.86), channel_id=1, source_target_pairs={{0,1},{1,0},{2,3},{3,2},{4,5},{5,4},{6,7},{7,6},{8,9},{9,8},{10,11... | collective-permute-start | bytes 811016 | tf_op jit(solution)/shard_map/ppermute | solution.py:127
  4.2 2.5 %collective-permute-start.3 = (bf16[176,768]{1,0:T(8,128)(2,1)S(1)}, bf16[176,768]{1,0:T(8,128)(2,1)S(1)}, u32[]{:S(2)}, u32[]{:S(2)}) collective-permute-start(bf16[176,768]{1,0:T(8,128)(2,1)S(1)} %get-tuple-element.86), channel_id=1, source_target_pairs={{0,3},{1,2},{2,1},{3,0},{4,7},{5,6},{6,5},{7,4},{8,11},{9,10},{10,... | collective-permute-start | bytes 811016 | tf_op jit(solution)/shard_map/ppermute | solution.py:127
  6.6 2.3 %dynamic-slice_bitcast_fusion = (bf16[176,768]{1,0:T(8,128)(2,1)S(1)}, bf16[176,768]{1,0:T(8,128)(2,1)}, bf16[176,768]{1,0:T(8,128)(2,1)}, bf16[176,768]{1,0:T(8...) fusion(bf16[2,176,3840]{2,1,0:T(8,128)(2,1)} %param.4, s32[]{:T(128)S(6)} %select_n.32, s32[]{:T(128)S(6)} %select_n.33), kind=kLoop, calls=%fused_computation.5 | loop fusion | bytes 3244040 | tf_op jit(solution)/shard_map/squeeze | solution.py:132
  10.9 4.3 %fusion.1 = (bf16[8,704,128]{2,1,0:T(8,128)(2,1)S(1)}, bf16[8,704,128]{2,1,0:T(8,128)(2,1)S(1)}, bf16[8,704,128]{2,1,0:T(8,128)(2,1)}, bf16[8,704,128]{2,1,0:T(8,128)(2,1)S(1)}) fusion(bf16[40,704,128]{2,1,0:T(8,128)(2,1)} %param.5), kind=kLoop, calls=%fused_computation.29 | loop fusion | bytes 11534336 | tf_op jit(solution)/shard_map/slice | solution.py:52
  15.2 13.0 %collective-permute-done.refs_1_ = bf16[176,768]{1,0:T(8,128)(2,1)S(1)} collective-permute-done((bf16[176,768]{1,0:T(8,128)(2,1)S(1)}, bf16[176,768]{1,0:T(8,128)(2,1)S(1)}, u32[]{:S(2)}, u32[]{:S(2)}) %collective-permute-start) | collective-permute-done | bytes 270368 | tf_op jit(solution)/shard_map/ppermute | solution.py:127
  29.2 2.9 %collective-permute-start.8 = (bf16[352,768]{1,0:T(8,128)(2,1)}, bf16[352,768]{1,0:T(8,128)(2,1)}, u32[]{:S(2)}, u32[]{:S(2)}) collective-permute-start(bf16[352,768]{1,0:T(8,128)(2,1)} %pad_maximum_fusion.1), channel_id=1, source_target_pairs={{0,2},{1,3},{2,0},{3,1},{4,6},{5,7},{6,4},{7,5},{8,10},{9,11},{10,... | collective-permute-start | bytes 1622024 | tf_op jit(solution)/shard_map/ppermute | solution.py:127
  32.0 7.8 %collective-permute-done.4.refs_1_ = bf16[176,768]{1,0:T(8,128)(2,1)S(1)} collective-permute-done((bf16[176,768]{1,0:T(8,128)(2,1)S(1)}, bf16[176,768]{1,0:T(8,128)(2,1)S(1)}, u32[]{:S(2)}, u32[]{:S(2)}) %collective-permute-start.4) | collective-permute-done | bytes 270368 | tf_op jit(solution)/shard_map/ppermute | solution.py:127
  43.3 4.2 %all-to-all-start = ((bf16[8,12,16,128]{3,2,1,0:T(8,128)(2,1)}), bf16[8,12,16,128]{3,2,1,0:T(8,128)(2,1)}, u32[]{:S(2)}, u32[]{:S(2)}) async-start(bf16[8,12,16,128]{3,2,1,0:T(8,128)(2,1)} %bitcast.31), calls=%async_computation | async-start | bytes 786432 | tf_op jit(solution)/shard_map/all_to_all | solution.py:135
  51.2 2.9 %collective-permute-start.5 = (bf16[352,768]{1,0:T(8,128)(2,1)}, bf16[352,768]{1,0:T(8,128)(2,1)}, u32[]{:S(2)}, u32[]{:S(2)}) collective-permute-start(bf16[352,768]{1,0:T(8,128)(2,1)} %pad_maximum_fusion), channel_id=1, source_target_pairs={{0,2},{1,3},{2,0},{3,1},{4,6},{5,7},{6,4},{7,5},{8,10},{9,11},{10,... | collective-permute-start | bytes 1622024 | tf_op jit(solution)/shard_map/ppermute | solution.py:127
  58.2 2.5 %parity_sums.7 = bf16[96,16,128]{2,1,0:T(8,128)(2,1)S(1)} custom-call(s32[4]{0:T(128)S(1)} %iota_xor_fusion.order, s32[40]{0:T(128)S(1)} %get-tuple-element.162.first, s32[40]{0:T(128)S(1)} %get-tuple-element.161.total, bf16[176,768]{1,0:T(8,128)(2,1)S(1)} %copy-done.7, bf16[176,768]{1,0:T(8,128)(2,1)S(1)} %copy-done.19, ...), custom_call_target="tpu_custom_call" | custom-call | flops 799999983616 | bytes 838860800 | tf_op jit(solution)/shard_map/parity_sums/pallas_call | solution.py:55
  61.4 3.3 %collective-permute-done.7.refs_1_ = bf16[176,768]{1,0:T(8,128)(2,1)} collective-permute-done((bf16[176,768]{1,0:T(8,128)(2,1)}, bf16[176,768]{1,0:T(8,128)(2,1)}, u32[]{:S(2)}, u32[]{:S(2)}) %collective-permute-start.7) | collective-permute-done | bytes 270368 | tf_op jit(solution)/shard_map/ppermute | solution.py:127
  64.7 4.1 %all-to-all-start.1 = ((bf16[8,12,16,128]{3,2,1,0:T(8,128)(2,1)}), bf16[8,12,16,128]{3,2,1,0:T(8,128)(2,1)}, u32[]{:S(2)}, u32[]{:S(2)}) async-start(bf16[8,12,16,128]{3,2,1,0:T(8,128)(2,1)} %bitcast.32), calls=%async_computation.1 | async-start | bytes 786432 | tf_op jit(solution)/shard_map/all_to_all | solution.py:135
  72.8 6.5 %collective-permute-done.5.refs_2_ = bf16[352,768]{1,0:T(8,128)(2,1)} collective-permute-done((bf16[352,768]{1,0:T(8,128)(2,1)}, bf16[352,768]{1,0:T(8,128)(2,1)}, u32[]{:S(2)}, u32[]{:S(2)}) %collective-permute-start.5) | collective-permute-done | bytes 540704 | tf_op jit(solution)/shard_map/ppermute | solution.py:127
  79.2 5.3 %collective-permute-done.11.refs_2_ = bf16[8,12,16,128]{3,2,1,0:T(8,128)(2,1)} collective-permute-done((bf16[8,12,16,128]{3,2,1,0:T(8,128)(2,1)}, bf16[8,12,16,128]{3,2,1,0:T(8,128)(2,1)}, u32[]{:S(2)}, u32[]{:S(2)}) %collective-permute-start.11) | collective-permute-done | bytes 393248 | tf_op jit(solution)/shard_map/ppermute | solution.py:127
  85.4 2.4 %parity_sums.8 = bf16[96,16,128]{2,1,0:T(8,128)(2,1)S(1)} custom-call(s32[4]{0:T(128)S(1)} %iota_xor_fusion.order, s32[40]{0:T(128)S(1)} %get-tuple-element.162.first, s32[40]{0:T(128)S(1)} %get-tuple-element.161.total, bf16[176,768]{1,0:T(8,128)(2,1)S(1)} %copy-done.5, bf16[176,768]{1,0:T(8,128)(2,1)S(1)} %copy-done.17, ...), custom_call_target="tpu_custom_call" | custom-call | flops 799999983616 | bytes 838860800 | tf_op jit(solution)/shard_map/parity_sums/pallas_call | solution.py:55
  88.6 4.1 %all-to-all-start.2 = ((bf16[8,12,16,128]{3,2,1,0:T(8,128)(2,1)}), bf16[8,12,16,128]{3,2,1,0:T(8,128)(2,1)}, u32[]{:S(2)}, u32[]{:S(2)}) async-start(bf16[8,12,16,128]{3,2,1,0:T(8,128)(2,1)} %bitcast.33), calls=%async_computation.2 | async-start | bytes 786432 | tf_op jit(solution)/shard_map/all_to_all | solution.py:135
  95.2 2.1 %collective-permute-start.14 = (bf16[352,384]{1,0:T(8,128)(2,1)}, bf16[352,384]{1,0:T(8,128)(2,1)}, u32[]{:S(2)}, u32[]{:S(2)}) collective-permute-start(bf16[352,384]{1,0:T(8,128)(2,1)} %pad_maximum_fusion.4), channel_id=1, source_target_pairs={{0,2},{1,3},{2,0},{3,1},{4,6},{5,7},{6,4},{7,5},{8,10},{9,11},{10,... | collective-permute-start | bytes 811016 | tf_op jit(solution)/shard_map/ppermute | solution.py:127
  97.2 5.2 %collective-permute-done.9.refs_2_ = bf16[352,768]{1,0:T(8,128)(2,1)} collective-permute-done((bf16[352,768]{1,0:T(8,128)(2,1)}, bf16[352,768]{1,0:T(8,128)(2,1)}, u32[]{:S(2)}, u32[]{:S(2)}) %collective-permute-start.9) | collective-permute-done | bytes 540704 | tf_op jit(solution)/shard_map/ppermute | solution.py:127
  102.4 4.7 %collective-permute-done.12.refs_3_ = bf16[8,12,16,128]{3,2,1,0:T(8,128)(2,1)} collective-permute-done((bf16[8,12,16,128]{3,2,1,0:T(8,128)(2,1)}, bf16[8,12,16,128]{3,2,1,0:T(8,128)(2,1)}, u32[]{:S(2)}, u32[]{:S(2)}) %collective-permute-start.12) | collective-permute-done | bytes 393248 | tf_op jit(solution)/shard_map/ppermute | solution.py:127
  107.1 3.3 %parity_sums.9 = bf16[96,16,128]{2,1,0:T(8,128)(2,1)} custom-call(s32[4]{0:T(128)S(1)} %iota_xor_fusion.order, s32[40]{0:T(128)S(1)} %get-tuple-element.162.first, s32[40]{0:T(128)S(1)} %get-tuple-element.161.total, bf16[176,768]{1,0:T(8,128)(2,1)S(1)} %copy-done.3, bf16[176,768]{1,0:T(8,128)(2,1)} %collective-permute-done.7.refs_1_, ...), custom_call_target="tpu_custom_call" | custom-call | flops 799999983616 | bytes 838860800 | tf_op jit(solution)/shard_map/parity_sums/pallas_call | solution.py:55
  110.4 3.7 %all-to-all-start.3 = ((bf16[8,12,16,128]{3,2,1,0:T(8,128)(2,1)}), bf16[8,12,16,128]{3,2,1,0:T(8,128)(2,1)S(1)}, u32[]{:S(2)}, u32[]{:S(2)}) async-start(bf16[8,12,16,128]{3,2,1,0:T(8,128)(2,1)} %bitcast.16), calls=%async_computation.3 | async-start | bytes 786432 | tf_op jit(solution)/shard_map/all_to_all | solution.py:135
  117.3 2.1 %collective-permute-start.15 = (bf16[8,12,16,128]{3,2,1,0:T(8,128)(2,1)}, bf16[8,12,16,128]{3,2,1,0:T(8,128)(2,1)}, u32[]{:S(2)}, u32[]{:S(2)}) collective-permute-start(bf16[8,12,16,128]{3,2,1,0:T(8,128)(2,1)} %all-to-all-done.2.refs_0_), channel_id=1, source_target_pairs={{0,1},{1,0},{2,3},{3,2},{4,5},{5,4},{6,7},{7,6},{8,9},{9,8},{10,11... | collective-permute-start | bytes 1179656 | tf_op jit(solution)/shard_map/ppermute | solution.py:127
  119.4 2.4 %finish.3.refs_4_ = bf16[12,640,128]{2,1,0:T(8,128)(2,1)} custom-call(s32[1]{0:T(128)} %bitcast.parity, s32[1]{0:T(128)S(6)} %copy.9.lat_count, bf16[8,12,16,128]{3,2,1,0:T(8,128)(2,1)} %all-to-all-done.refs_0_, bf16[8,12,16,128]{3,2,1,0:T(8,128)(2,1)} %all-to-all-done.1.refs_1_, bf16[8,12,16,128]{3,2,1,0:T(8,128)(2,1)} %collective-permute-done.11.refs_2_, ...), custom_call_target="tpu_custom_call" | custom-call | tf_op jit(solution)/shard_map/finish/pallas_call | solution.py:99
  122.5 2.6 %parity_sums.10 = bf16[96,8,128]{2,1,0:T(8,128)(2,1)} custom-call(s32[4]{0:T(128)S(1)} %iota_xor_fusion.order, s32[40]{0:T(128)S(1)} %get-tuple-element.162.first, s32[40]{0:T(128)S(1)} %get-tuple-element.161.total, bf16[176,384]{1,0:T(8,128)(2,1)S(1)} %copy-done.12, bf16[176,384]{1,0:T(8,128)(2,1)} %collective-permute-done.10.refs_1_, ...), custom_call_target="tpu_custom_call" | custom-call | flops 399999991808 | bytes 419430400 | tf_op jit(solution)/shard_map/parity_sums/pallas_call | solution.py:55
  125.1 3.5 %all-to-all-start.4 = ((bf16[8,12,8,128]{3,2,1,0:T(8,128)(2,1)}), bf16[8,12,8,128]{3,2,1,0:T(8,128)(2,1)S(1)}, u32[]{:S(2)}, u32[]{:S(2)}) async-start(bf16[8,12,8,128]{3,2,1,0:T(8,128)(2,1)} %bitcast.17), calls=%async_computation.4 | async-start | bytes 393216 | tf_op jit(solution)/shard_map/all_to_all | solution.py:135
  128.6 3.6 %collective-permute-done.13.refs_2_ = bf16[352,384]{1,0:T(8,128)(2,1)} collective-permute-done((bf16[352,384]{1,0:T(8,128)(2,1)}, bf16[352,384]{1,0:T(8,128)(2,1)}, u32[]{:S(2)}, u32[]{:S(2)}) %collective-permute-start.13) | collective-permute-done | bytes 270368 | tf_op jit(solution)/shard_map/ppermute | solution.py:127
  132.3 2.6 %all-to-all-done.4.refs_0_ = bf16[8,12,8,128]{3,2,1,0:T(8,128)(2,1)S(1)} async-done(((bf16[8,12,8,128]{3,2,1,0:T(8,128)(2,1)}), bf16[8,12,8,128]{3,2,1,0:T(8,128)(2,1)S(1)}, u32[]{:S(2)}, u32[]{:S(2)}) %all-to-all-start.4) | async-done | bytes 196640 | tf_op jit(solution)/shard_map/all_to_all | solution.py:135
  135.5 2.5 %parity_sums.11 = bf16[96,8,128]{2,1,0:T(8,128)(2,1)} custom-call(s32[4]{0:T(128)S(1)} %iota_xor_fusion.order, s32[40]{0:T(128)S(1)} %get-tuple-element.162.first, s32[40]{0:T(128)S(1)} %get-tuple-element.161.total, bf16[176,384]{1,0:T(8,128)(2,1)S(1)} %copy-done.11, bf16[176,384]{1,0:T(8,128)(2,1)} %collective-permute-done.6.refs_1_, ...), custom_call_target="tpu_custom_call" | custom-call | flops 399999991808 | bytes 419430400 | tf_op jit(solution)/shard_map/parity_sums/pallas_call | solution.py:55
  138.1 4.1 %all-to-all-start.5 = ((bf16[8,12,8,128]{3,2,1,0:T(8,128)(2,1)}), bf16[8,12,8,128]{3,2,1,0:T(8,128)(2,1)S(1)}, u32[]{:S(2)}, u32[]{:S(2)}) async-start(bf16[8,12,8,128]{3,2,1,0:T(8,128)(2,1)} %bitcast.18), calls=%async_computation.5 | async-start | bytes 393216 | tf_op jit(solution)/shard_map/all_to_all | solution.py:135
  142.2 6.1 %all-to-all-done.5.refs_1_ = bf16[8,12,8,128]{3,2,1,0:T(8,128)(2,1)S(1)} async-done(((bf16[8,12,8,128]{3,2,1,0:T(8,128)(2,1)}), bf16[8,12,8,128]{3,2,1,0:T(8,128)(2,1)S(1)}, u32[]{:S(2)}, u32[]{:S(2)}) %all-to-all-start.5) | async-done | bytes 196640 | tf_op jit(solution)/shard_map/all_to_all | solution.py:135
  148.4 2.2 %finish.4.refs_4_ = bf16[12,640,128]{2,1,0:T(8,128)(2,1)} custom-call(s32[1]{0:T(128)} %bitcast.parity, s32[1]{0:T(128)S(6)} %copy.9.lat_count, bf16[8,12,16,128]{3,2,1,0:T(8,128)(2,1)} %all-to-all-done.2.refs_0_, bf16[8,12,16,128]{3,2,1,0:T(8,128)(2,1)S(1)} %copy-done.1, ...), custom_call_target="tpu_custom_call", output_to_operand_aliasing={{}: (6, {})} | custom-call | tf_op jit(solution)/shard_map/finish/pallas_call | solution.py:99
  150.6 4.1 %collective-permute-done.17.refs_3_ = bf16[8,12,8,128]{3,2,1,0:T(8,128)(2,1)S(1)} collective-permute-done((bf16[8,12,8,128]{3,2,1,0:T(8,128)(2,1)S(1)}, bf16[8,12,8,128]{3,2,1,0:T(8,128)(2,1)S(1)}, u32[]{:S(2)}, u32[]{:S(2)}) %collective-permute-start.17) | collective-permute-done | bytes 196640 | tf_op jit(solution)/shard_map/ppermute | solution.py:127
  (81 shorter events, 28.6 us)
Async XLA Ops:
  1.1 27.2 %collective-permute-start.1 = (bf16[176,768]{1,0:T(8,128)(2,1)S(1)}, bf16[176,768]{1,0:T(8,128)(2,1)S(1)}, u32[]{:S(2)}, u32[]{:S(2)}) collective-permute-start(bf16[176,768]{1,0:T(8,128)(2,1)S(1)} %get-tuple-element.86), channel_id=1, source_target_pairs={{0,1},{1,0},{2,3},{3,2},{4,5},{5,4},{6,7},{7,6},{8,9},{9,8},{10,11... | collective-permute-start | bytes 811016 | tf_op jit(solution)/shard_map/ppermute | solution.py:127
  4.2 24.1 %collective-permute-start.3 = (bf16[176,768]{1,0:T(8,128)(2,1)S(1)}, bf16[176,768]{1,0:T(8,128)(2,1)S(1)}, u32[]{:S(2)}, u32[]{:S(2)}) collective-permute-start(bf16[176,768]{1,0:T(8,128)(2,1)S(1)} %get-tuple-element.86), channel_id=1, source_target_pairs={{0,3},{1,2},{2,1},{3,0},{4,7},{5,6},{6,5},{7,4},{8,11},{9,10},{10,... | collective-permute-start | bytes 811016 | tf_op jit(solution)/shard_map/ppermute | solution.py:127
  9.0 19.3 %copy-start.6 = (bf16[176,768]{1,0:T(8,128)(2,1)}, bf16[176,768]{1,0:T(8,128)(2,1)S(1)}, u32[]{:S(2)}) copy-start(bf16[176,768]{1,0:T(8,128)(2,1)S(1)} %get-tuple-element.108.refs_0_) | copy-start | bytes 811012
  9.0 19.3 %copy-start.20 = (s32[40]{0:T(128)S(1)}, s32[40]{0:T(128)}, u32[]{:S(2)}) copy-start(s32[40]{0:T(128)} %param.6) | copy-start | bytes 484
  9.0 19.3 %collective-permute-start = (bf16[176,768]{1,0:T(8,128)(2,1)S(1)}, bf16[176,768]{1,0:T(8,128)(2,1)S(1)}, u32[]{:S(2)}, u32[]{:S(2)}) collective-permute-start(bf16[176,768]{1,0:T(8,128)(2,1)S(1)} %get-tuple-element.172), channel_id=1, source_target_pairs={{0,1},{1,0},{2,3},{3,2},{4,5},{5,4},{6,7},{7,6},{8,9},{9,8},{10,11... | collective-permute-start | bytes 811016 | tf_op jit(solution)/shard_map/ppermute | solution.py:127
  9.7 18.6 %collective-permute-start.2 = (bf16[176,768]{1,0:T(8,128)(2,1)S(1)}, bf16[176,768]{1,0:T(8,128)(2,1)S(1)}, u32[]{:S(2)}, u32[]{:S(2)}) collective-permute-start(bf16[176,768]{1,0:T(8,128)(2,1)S(1)} %get-tuple-element.93.refs_0_), channel_id=1, source_target_pairs={{0,2},{1,3},{2,0},{3,1},{4,6},{5,7},{6,4},{7,5},{8,10},{9,11},{10,... | collective-permute-start | bytes 811016 | tf_op jit(solution)/shard_map/ppermute | solution.py:127
  28.2 14.3 %copy-start.18 = (bf16[176,768]{1,0:T(8,128)(2,1)}, bf16[176,768]{1,0:T(8,128)(2,1)S(1)}, u32[]{:S(2)}) copy-start(bf16[176,768]{1,0:T(8,128)(2,1)S(1)} %collective-permute-done.refs_1_) | copy-start | bytes 811012
  28.2 11.6 %collective-permute-start.4 = (bf16[176,768]{1,0:T(8,128)(2,1)S(1)}, bf16[176,768]{1,0:T(8,128)(2,1)S(1)}, u32[]{:S(2)}, u32[]{:S(2)}) collective-permute-start(bf16[176,768]{1,0:T(8,128)(2,1)S(1)} %get-tuple-element.91), channel_id=1, source_target_pairs={{0,1},{1,0},{2,3},{3,2},{4,5},{5,4},{6,7},{7,6},{8,9},{9,8},{10,11... | collective-permute-start | bytes 811016 | tf_op jit(solution)/shard_map/ppermute | solution.py:127
  29.2 26.0 %collective-permute-start.8 = (bf16[352,768]{1,0:T(8,128)(2,1)}, bf16[352,768]{1,0:T(8,128)(2,1)}, u32[]{:S(2)}, u32[]{:S(2)}) collective-permute-start(bf16[352,768]{1,0:T(8,128)(2,1)} %pad_maximum_fusion.1), channel_id=1, source_target_pairs={{0,2},{1,3},{2,0},{3,1},{4,6},{5,7},{6,4},{7,5},{8,10},{9,11},{10,... | collective-permute-start | bytes 1622024 | tf_op jit(solution)/shard_map/ppermute | solution.py:127
  43.3 12.6 %copy-start.7 = (bf16[176,768]{1,0:T(8,128)(2,1)S(1)}, bf16[176,768]{1,0:T(8,128)(2,1)}, u32[]{:S(2)}) copy-start(bf16[176,768]{1,0:T(8,128)(2,1)} %copy-done.6) | copy-start | bytes 811012
  43.3 12.6 %all-to-all-start = ((bf16[8,12,16,128]{3,2,1,0:T(8,128)(2,1)}), bf16[8,12,16,128]{3,2,1,0:T(8,128)(2,1)}, u32[]{:S(2)}, u32[]{:S(2)}) async-start(bf16[8,12,16,128]{3,2,1,0:T(8,128)(2,1)} %bitcast.31), calls=%async_computation | async-start | bytes 786432 | tf_op jit(solution)/shard_map/all_to_all | solution.py:135
  49.4 15.3 %collective-permute-start.7 = (bf16[176,768]{1,0:T(8,128)(2,1)}, bf16[176,768]{1,0:T(8,128)(2,1)}, u32[]{:S(2)}, u32[]{:S(2)}) collective-permute-start(bf16[176,768]{1,0:T(8,128)(2,1)} %get-tuple-element.102), channel_id=1, source_target_pairs={{0,1},{1,0},{2,3},{3,2},{4,5},{5,4},{6,7},{7,6},{8,9},{9,8},{10,11... | collective-permute-start | bytes 811016 | tf_op jit(solution)/shard_map/ppermute | solution.py:127
  51.2 28.0 %collective-permute-start.5 = (bf16[352,768]{1,0:T(8,128)(2,1)}, bf16[352,768]{1,0:T(8,128)(2,1)}, u32[]{:S(2)}, u32[]{:S(2)}) collective-permute-start(bf16[352,768]{1,0:T(8,128)(2,1)} %pad_maximum_fusion), channel_id=1, source_target_pairs={{0,2},{1,3},{2,0},{3,1},{4,6},{5,7},{6,4},{7,5},{8,10},{9,11},{10,... | collective-permute-start | bytes 1622024 | tf_op jit(solution)/shard_map/ppermute | solution.py:127
  55.8 28.6 %collective-permute-start.11 = (bf16[8,12,16,128]{3,2,1,0:T(8,128)(2,1)}, bf16[8,12,16,128]{3,2,1,0:T(8,128)(2,1)}, u32[]{:S(2)}, u32[]{:S(2)}) collective-permute-start(bf16[8,12,16,128]{3,2,1,0:T(8,128)(2,1)} %all-to-all-done.refs_0_), channel_id=1, source_target_pairs={{0,1},{1,0},{2,3},{3,2},{4,5},{5,4},{6,7},{7,6},{8,9},{9,8},{10,11... | collective-permute-start | bytes 1179656 | tf_op jit(solution)/shard_map/ppermute | solution.py:127
  61.4 23.1 %copy-start.5 = (bf16[176,768]{1,0:T(8,128)(2,1)S(1)}, bf16[176,768]{1,0:T(8,128)(2,1)}, u32[]{:S(2)}) copy-start(bf16[176,768]{1,0:T(8,128)(2,1)} %get-tuple-element.123.refs_0_) | copy-start | bytes 811012
  64.7 14.5 %all-to-all-start.1 = ((bf16[8,12,16,128]{3,2,1,0:T(8,128)(2,1)}), bf16[8,12,16,128]{3,2,1,0:T(8,128)(2,1)}, u32[]{:S(2)}, u32[]{:S(2)}) async-start(bf16[8,12,16,128]{3,2,1,0:T(8,128)(2,1)} %bitcast.32), calls=%async_computation.1 | async-start | bytes 786432 | tf_op jit(solution)/shard_map/all_to_all | solution.py:135
  68.8 19.8 %collective-permute-start.10 = (bf16[176,384]{1,0:T(8,128)(2,1)}, bf16[176,384]{1,0:T(8,128)(2,1)}, u32[]{:S(2)}, u32[]{:S(2)}) collective-permute-start(bf16[176,384]{1,0:T(8,128)(2,1)} %get-tuple-element.114), channel_id=1, source_target_pairs={{0,1},{1,0},{2,3},{3,2},{4,5},{5,4},{6,7},{7,6},{8,9},{9,8},{10,11... | collective-permute-start | bytes 405512 | tf_op jit(solution)/shard_map/ppermute | solution.py:127
  70.7 31.7 %collective-permute-start.9 = (bf16[352,768]{1,0:T(8,128)(2,1)}, bf16[352,768]{1,0:T(8,128)(2,1)}, u32[]{:S(2)}, u32[]{:S(2)}) collective-permute-start(bf16[352,768]{1,0:T(8,128)(2,1)} %pad_maximum_fusion.2), channel_id=1, source_target_pairs={{0,2},{1,3},{2,0},{3,1},{4,6},{5,7},{6,4},{7,5},{8,10},{9,11},{10,... | collective-permute-start | bytes 1622024 | tf_op jit(solution)/shard_map/ppermute | solution.py:127
  79.2 27.9 %collective-permute-start.12 = (bf16[8,12,16,128]{3,2,1,0:T(8,128)(2,1)}, bf16[8,12,16,128]{3,2,1,0:T(8,128)(2,1)}, u32[]{:S(2)}, u32[]{:S(2)}) collective-permute-start(bf16[8,12,16,128]{3,2,1,0:T(8,128)(2,1)} %all-to-all-done.1.refs_1_), channel_id=1, source_target_pairs={{0,1},{1,0},{2,3},{3,2},{4,5},{5,4},{6,7},{7,6},{8,9},{9,8},{10,11... | collective-permute-start | bytes 1179656 | tf_op jit(solution)/shard_map/ppermute | solution.py:127
  88.6 13.8 %all-to-all-start.2 = ((bf16[8,12,16,128]{3,2,1,0:T(8,128)(2,1)}), bf16[8,12,16,128]{3,2,1,0:T(8,128)(2,1)}, u32[]{:S(2)}, u32[]{:S(2)}) async-start(bf16[8,12,16,128]{3,2,1,0:T(8,128)(2,1)} %bitcast.33), calls=%async_computation.2 | async-start | bytes 786432 | tf_op jit(solution)/shard_map/all_to_all | solution.py:135
  93.4 17.0 %collective-permute-start.6 = (bf16[176,384]{1,0:T(8,128)(2,1)}, bf16[176,384]{1,0:T(8,128)(2,1)}, u32[]{:S(2)}, u32[]{:S(2)}) collective-permute-start(bf16[176,384]{1,0:T(8,128)(2,1)} %get-tuple-element.100), channel_id=1, source_target_pairs={{0,1},{1,0},{2,3},{3,2},{4,5},{5,4},{6,7},{7,6},{8,9},{9,8},{10,11... | collective-permute-start | bytes 405512 | tf_op jit(solution)/shard_map/ppermute | solution.py:127
  95.2 26.6 %collective-permute-start.14 = (bf16[352,384]{1,0:T(8,128)(2,1)}, bf16[352,384]{1,0:T(8,128)(2,1)}, u32[]{:S(2)}, u32[]{:S(2)}) collective-permute-start(bf16[352,384]{1,0:T(8,128)(2,1)} %pad_maximum_fusion.4), channel_id=1, source_target_pairs={{0,2},{1,3},{2,0},{3,1},{4,6},{5,7},{6,4},{7,5},{8,10},{9,11},{10,... | collective-permute-start | bytes 811016 | tf_op jit(solution)/shard_map/ppermute | solution.py:127
  110.4 12.1 %all-to-all-start.3 = ((bf16[8,12,16,128]{3,2,1,0:T(8,128)(2,1)}), bf16[8,12,16,128]{3,2,1,0:T(8,128)(2,1)S(1)}, u32[]{:S(2)}, u32[]{:S(2)}) async-start(bf16[8,12,16,128]{3,2,1,0:T(8,128)(2,1)} %bitcast.16), calls=%async_computation.3 | async-start | bytes 786432 | tf_op jit(solution)/shard_map/all_to_all | solution.py:135
  117.3 15.0 %collective-permute-start.13 = (bf16[352,384]{1,0:T(8,128)(2,1)}, bf16[352,384]{1,0:T(8,128)(2,1)}, u32[]{:S(2)}, u32[]{:S(2)}) collective-permute-start(bf16[352,384]{1,0:T(8,128)(2,1)} %pad_maximum_fusion.3), channel_id=1, source_target_pairs={{0,2},{1,3},{2,0},{3,1},{4,6},{5,7},{6,4},{7,5},{8,10},{9,11},{10,... | collective-permute-start | bytes 811016 | tf_op jit(solution)/shard_map/ppermute | solution.py:127
  117.3 18.1 %collective-permute-start.15 = (bf16[8,12,16,128]{3,2,1,0:T(8,128)(2,1)}, bf16[8,12,16,128]{3,2,1,0:T(8,128)(2,1)}, u32[]{:S(2)}, u32[]{:S(2)}) collective-permute-start(bf16[8,12,16,128]{3,2,1,0:T(8,128)(2,1)} %all-to-all-done.2.refs_0_), channel_id=1, source_target_pairs={{0,1},{1,0},{2,3},{3,2},{4,5},{5,4},{6,7},{7,6},{8,9},{9,8},{10,11... | collective-permute-start | bytes 1179656 | tf_op jit(solution)/shard_map/ppermute | solution.py:127
  122.5 13.0 %copy-start.11 = (bf16[176,384]{1,0:T(8,128)(2,1)S(1)}, bf16[176,384]{1,0:T(8,128)(2,1)}, u32[]{:S(2)}) copy-start(bf16[176,384]{1,0:T(8,128)(2,1)} %get-tuple-element.154.refs_0_) | copy-start | bytes 405508
  125.1 9.7 %all-to-all-start.4 = ((bf16[8,12,8,128]{3,2,1,0:T(8,128)(2,1)}), bf16[8,12,8,128]{3,2,1,0:T(8,128)(2,1)S(1)}, u32[]{:S(2)}, u32[]{:S(2)}) async-start(bf16[8,12,8,128]{3,2,1,0:T(8,128)(2,1)} %bitcast.17), calls=%async_computation.4 | async-start | bytes 393216 | tf_op jit(solution)/shard_map/all_to_all | solution.py:135
  128.6 19.7 %collective-permute-start.18 = (bf16[8,12,16,128]{3,2,1,0:T(8,128)(2,1)}, bf16[8,12,16,128]{3,2,1,0:T(8,128)(2,1)}, u32[]{:S(2)}, u32[]{:S(2)}) collective-permute-start(bf16[8,12,16,128]{3,2,1,0:T(8,128)(2,1)} %copy-done), channel_id=1, source_target_pairs={{0,1},{1,0},{2,3},{3,2},{4,5},{5,4},{6,7},{7,6},{8,9},{9,8},{10,11... | collective-permute-start | bytes 1179656 | tf_op jit(solution)/shard_map/ppermute | solution.py:127
  135.5 12.8 %copy-start.1 = (bf16[8,12,16,128]{3,2,1,0:T(8,128)(2,1)S(1)}, bf16[8,12,16,128]{3,2,1,0:T(8,128)(2,1)}, u32[]{:S(2)}) copy-start(bf16[8,12,16,128]{3,2,1,0:T(8,128)(2,1)} %copy-done) | copy-start | bytes 1179652
  138.1 10.3 %all-to-all-start.5 = ((bf16[8,12,8,128]{3,2,1,0:T(8,128)(2,1)}), bf16[8,12,8,128]{3,2,1,0:T(8,128)(2,1)S(1)}, u32[]{:S(2)}, u32[]{:S(2)}) async-start(bf16[8,12,8,128]{3,2,1,0:T(8,128)(2,1)} %bitcast.18), calls=%async_computation.5 | async-start | bytes 393216 | tf_op jit(solution)/shard_map/all_to_all | solution.py:135
  142.1 8.5 %collective-permute-start.16 = (bf16[8,12,8,128]{3,2,1,0:T(8,128)(2,1)S(1)}, bf16[8,12,8,128]{3,2,1,0:T(8,128)(2,1)S(1)}, u32[]{:S(2)}, u32[]{:S(2)}) collective-permute-start(bf16[8,12,8,128]{3,2,1,0:T(8,128)(2,1)S(1)} %copy-done.9), channel_id=1, source_target_pairs={{0,1},{1,0},{2,3},{3,2},{4,5},{5,4},{6,7},{7,6},{8,9},{9,8},{10,11... | collective-permute-start | bytes 589832 | tf_op jit(solution)/shard_map/ppermute | solution.py:127
  148.4 6.3 %collective-permute-start.17 = (bf16[8,12,8,128]{3,2,1,0:T(8,128)(2,1)S(1)}, bf16[8,12,8,128]{3,2,1,0:T(8,128)(2,1)S(1)}, u32[]{:S(2)}, u32[]{:S(2)}) collective-permute-start(bf16[8,12,8,128]{3,2,1,0:T(8,128)(2,1)S(1)} %all-to-all-done.5.refs_1_), channel_id=1, source_target_pairs={{0,1},{1,0},{2,3},{3,2},{4,5},{5,4},{6,7},{7,6},{8,9},{9,8},{10,11... | collective-permute-start | bytes 589832 | tf_op jit(solution)/shard_map/ppermute | solution.py:127
  (14 other events, 37.7 us)

commit v6 on v5

--- a/solution.py
+++ b/solution.py
@@ -10,7 +10,7 @@
 TRUNC = 1279
 VMEM = 24 * 2**20
 CHUNKS = (8, 8, 8, 8, 4, 4)
-MIRRORED = {2: 0, 3: 1, 5: 2}
+MIRRORED = {3: 0, 4: 1, 5: 2}
 GROUPS = ((0, 1), (2, 3), (4, 5))
 
 

time: 157 us -> 159 us (1.013)
    all_to_all x6, waiting for transfers between devices: 10.1 us -> 15.1 us  [redistribute(): lax.all_to_all(grid.reshape(sets, fields // sets, -1, lats), 'mset', 0, 0)]
    ppermute x19, waiting for transfers between devices: 55.1 us -> 50.6 us  [swap(): lax.ppermute(value, 'band', [(band, band ^ step) for band in range(bands)])]
    ppermute x19, starting transfers between devices: 19.7 us -> 21.5 us  [swap(): lax.ppermute(value, 'band', [(band, band ^ step) for band in range(bands)])]
    unnamed x42 -> x46, local copies, waits for them, and re-layouts: 6.45 us -> 6.84 us
  transfers between devices with their start and end apart: 25 -> 25, of which waited for: 15 -> 11; matrix products, arithmetic and copies ran while one was open for 11% -> 11% of each run, Pallas kernels for 13% -> 13%
where the time goes in v6:
time: 159 us; the launch traced here: 158 us
  waiting for transfers between devices  65.7 us (41%)
  starting transfers between devices  43.9 us (28%)
  Pallas kernels  21.4 us (13%)
  local copies, waits for them, and re-layouts  17.9 us (11%)
  other arithmetic  7.8 us (5%)
    ppermute x19, waiting for transfers between devices, swap(): lax.ppermute(value, 'band', [(band, band ^ step) for band in range(bands)])  50.6 us
    all_to_all x6, starting transfers between devices, redistribute(): lax.all_to_all(grid.reshape(sets, fields // sets, -1, lats), 'mset', 0, 0)  22.4 us
    ppermute x19, starting transfers between devices, swap(): lax.ppermute(value, 'band', [(band, band ^ step) for band in range(bands)])  21.5 us
    pallas_call x6, Pallas kernels, parity_sums(): pl.pallas_call(functools.partial(sums_kernel, rows, fields, start), in_sp...  16 us
    all_to_all x6, waiting for transfers between devices, redistribute(): lax.all_to_all(grid.reshape(sets, fields // sets, -1, lats), 'mset', 0, 0)  15.1 us
    concatenate x5, other arithmetic, spread(): held.append(swap(jnp.concatenate(held), bit))  7.78 us
    unnamed x46, local copies, waits for them, and re-layouts  6.84 us
    slice x2, local copies, waits for them, and re-layouts, parity_sums(): legendre = legendre[start:start + pairs]  5.79 us
  transfers between devices with their start and end apart: 25, of which 11 were waited for; matrix products, arithmetic and copies ran while one was open for 11% of the time, Pallas kernels for 13%

profile of v6, /device:TPU:0, one launch (start us, length us, event | category | flops | bytes accessed | tf_op | source)
XLA Modules:
  0.0 157.8 jit_solution(10509755457834357209)
XLA Ops:
  1.1 3.1 %collective-permute-start.1 = (bf16[176,768]{1,0:T(8,128)(2,1)S(1)}, bf16[176,768]{1,0:T(8,128)(2,1)S(1)}, u32[]{:S(2)}, u32[]{:S(2)}) collective-permute-start(bf16[176,768]{1,0:T(8,128)(2,1)S(1)} %get-tuple-element.86), channel_id=1, source_target_pairs={{0,1},{1,0},{2,3},{3,2},{4,5},{5,4},{6,7},{7,6},{8,9},{9,8},{10,11... | collective-permute-start | bytes 811016 | tf_op jit(solution)/shard_map/ppermute | solution.py:127
  4.2 2.5 %collective-permute-start.3 = (bf16[176,768]{1,0:T(8,128)(2,1)S(1)}, bf16[176,768]{1,0:T(8,128)(2,1)S(1)}, u32[]{:S(2)}, u32[]{:S(2)}) collective-permute-start(bf16[176,768]{1,0:T(8,128)(2,1)S(1)} %get-tuple-element.86), channel_id=1, source_target_pairs={{0,3},{1,2},{2,1},{3,0},{4,7},{5,6},{6,5},{7,4},{8,11},{9,10},{10,... | collective-permute-start | bytes 811016 | tf_op jit(solution)/shard_map/ppermute | solution.py:127
  6.6 2.3 %dynamic-slice_bitcast_fusion = (bf16[176,768]{1,0:T(8,128)(2,1)S(1)}, bf16[176,768]{1,0:T(8,128)(2,1)}, bf16[176,768]{1,0:T(8,128)(2,1)}, bf16[176,768]{1,0:T(8...) fusion(bf16[2,176,3840]{2,1,0:T(8,128)(2,1)} %param.4, s32[]{:T(128)S(6)} %select_n.32, s32[]{:T(128)S(6)} %select_n.33), kind=kLoop, calls=%fused_computation.5 | loop fusion | bytes 3244040 | tf_op jit(solution)/shard_map/squeeze | solution.py:132
  10.9 4.3 %fusion.1 = (bf16[8,704,128]{2,1,0:T(8,128)(2,1)S(1)}, bf16[8,704,128]{2,1,0:T(8,128)(2,1)S(1)}, bf16[8,704,128]{2,1,0:T(8,128)(2,1)}, bf16[8,704,128]{2,1,0:T(8,128)(2,1)S(1)}) fusion(bf16[40,704,128]{2,1,0:T(8,128)(2,1)} %param.5), kind=kLoop, calls=%fused_computation.29 | loop fusion | bytes 11534336 | tf_op jit(solution)/shard_map/slice | solution.py:52
  15.2 13.0 %collective-permute-done.refs_1_ = bf16[176,768]{1,0:T(8,128)(2,1)S(1)} collective-permute-done((bf16[176,768]{1,0:T(8,128)(2,1)S(1)}, bf16[176,768]{1,0:T(8,128)(2,1)S(1)}, u32[]{:S(2)}, u32[]{:S(2)}) %collective-permute-start) | collective-permute-done | bytes 270368 | tf_op jit(solution)/shard_map/ppermute | solution.py:127
  29.1 2.9 %collective-permute-start.8 = (bf16[352,768]{1,0:T(8,128)(2,1)}, bf16[352,768]{1,0:T(8,128)(2,1)}, u32[]{:S(2)}, u32[]{:S(2)}) collective-permute-start(bf16[352,768]{1,0:T(8,128)(2,1)} %pad_maximum_fusion.1), channel_id=1, source_target_pairs={{0,2},{1,3},{2,0},{3,1},{4,6},{5,7},{6,4},{7,5},{8,10},{9,11},{10,... | collective-permute-start | bytes 1622024 | tf_op jit(solution)/shard_map/ppermute | solution.py:127
  32.0 7.9 %collective-permute-done.4.refs_1_ = bf16[176,768]{1,0:T(8,128)(2,1)} collective-permute-done((bf16[176,768]{1,0:T(8,128)(2,1)S(1)}, bf16[176,768]{1,0:T(8,128)(2,1)}, u32[]{:S(2)}, u32[]{:S(2)}) %collective-permute-start.4) | collective-permute-done | bytes 270368 | tf_op jit(solution)/shard_map/ppermute | solution.py:127
  39.9 2.7 %parity_sums.6 = bf16[96,16,128]{2,1,0:T(8,128)(2,1)} custom-call(s32[4]{0:T(128)S(1)} %iota_xor_fusion.order, s32[40]{0:T(128)S(1)} %get-tuple-element.162.first, s32[40]{0:T(128)S(1)} %get-tuple-element.161.total, bf16[176,768]{1,0:T(8,128)(2,1)S(1)} %get-tuple-element.93.refs_0_, bf16[176,768]{1,0:T(8,128)(2,1)S(1)} %collective-permute-done.1.refs_1_, ...), custom_call_target="tpu_custom_call" | custom-call | flops 799999983616 | bytes 838860800 | tf_op jit(solution)/shard_map/parity_sums/pallas_call | solution.py:55
  42.6 4.2 %all-to-all-start = ((bf16[8,12,16,128]{3,2,1,0:T(8,128)(2,1)}), bf16[8,12,16,128]{3,2,1,0:T(8,128)(2,1)}, u32[]{:S(2)}, u32[]{:S(2)}) async-start(bf16[8,12,16,128]{3,2,1,0:T(8,128)(2,1)} %bitcast.13), calls=%async_computation | async-start | bytes 786432 | tf_op jit(solution)/shard_map/all_to_all | solution.py:135
  50.6 2.9 %collective-permute-start.5 = (bf16[352,768]{1,0:T(8,128)(2,1)}, bf16[352,768]{1,0:T(8,128)(2,1)}, u32[]{:S(2)}, u32[]{:S(2)}) collective-permute-start(bf16[352,768]{1,0:T(8,128)(2,1)} %pad_maximum_fusion), channel_id=1, source_target_pairs={{0,2},{1,3},{2,0},{3,1},{4,6},{5,7},{6,4},{7,5},{8,10},{9,11},{10,... | collective-permute-start | bytes 1622024 | tf_op jit(solution)/shard_map/ppermute | solution.py:127
  57.9 2.5 %parity_sums.7 = bf16[96,16,128]{2,1,0:T(8,128)(2,1)S(1)} custom-call(s32[4]{0:T(128)S(1)} %iota_xor_fusion.order, s32[40]{0:T(128)S(1)} %get-tuple-element.162.first, s32[40]{0:T(128)S(1)} %get-tuple-element.161.total, bf16[176,768]{1,0:T(8,128)(2,1)S(1)} %copy-done.9, bf16[176,768]{1,0:T(8,128)(2,1)S(1)} %copy-done.18, ...), custom_call_target="tpu_custom_call" | custom-call | flops 799999983616 | bytes 838860800 | tf_op jit(solution)/shard_map/parity_sums/pallas_call | solution.py:55
  61.1 3.2 %collective-permute-done.7.refs_1_ = bf16[176,768]{1,0:T(8,128)(2,1)} collective-permute-done((bf16[176,768]{1,0:T(8,128)(2,1)}, bf16[176,768]{1,0:T(8,128)(2,1)}, u32[]{:S(2)}, u32[]{:S(2)}) %collective-permute-start.7) | collective-permute-done | bytes 270368 | tf_op jit(solution)/shard_map/ppermute | solution.py:127
  64.3 3.9 %all-to-all-start.1 = ((bf16[8,12,16,128]{3,2,1,0:T(8,128)(2,1)}), bf16[8,12,16,128]{3,2,1,0:T(8,128)(2,1)S(1)}, u32[]{:S(2)}, u32[]{:S(2)}) async-start(bf16[8,12,16,128]{3,2,1,0:T(8,128)(2,1)} %bitcast.31), calls=%async_computation.1 | async-start | bytes 786432 | tf_op jit(solution)/shard_map/all_to_all | solution.py:135
  72.0 18.3 %collective-permute-done.5.refs_2_ = bf16[352,768]{1,0:T(8,128)(2,1)} collective-permute-done((bf16[352,768]{1,0:T(8,128)(2,1)}, bf16[352,768]{1,0:T(8,128)(2,1)}, u32[]{:S(2)}, u32[]{:S(2)}) %collective-permute-start.5) | collective-permute-done | bytes 540704 | tf_op jit(solution)/shard_map/ppermute | solution.py:127
  92.0 2.5 %parity_sums.8 = bf16[96,16,128]{2,1,0:T(8,128)(2,1)S(1)} custom-call(s32[4]{0:T(128)S(1)} %copy-done.20, s32[40]{0:T(128)S(1)} %get-tuple-element.162.first, s32[40]{0:T(128)S(1)} %get-tuple-element.161.total, bf16[176,768]{1,0:T(8,128)(2,1)S(1)} %copy-done.7, bf16[176,768]{1,0:T(8,128)(2,1)} %collective-permute-done.4.refs_1_, ...), custom_call_target="tpu_custom_call" | custom-call | flops 799999983616 | bytes 838860800 | tf_op jit(solution)/shard_map/parity_sums/pallas_call | solution.py:55
  95.3 4.1 %all-to-all-start.2 = ((bf16[8,12,16,128]{3,2,1,0:T(8,128)(2,1)}), bf16[8,12,16,128]{3,2,1,0:T(8,128)(2,1)}, u32[]{:S(2)}, u32[]{:S(2)}) async-start(bf16[8,12,16,128]{3,2,1,0:T(8,128)(2,1)} %bitcast.32), calls=%async_computation.2 | async-start | bytes 786432 | tf_op jit(solution)/shard_map/all_to_all | solution.py:135
  101.8 3.0 %collective-permute-start.13 = (bf16[352,384]{1,0:T(8,128)(2,1)}, bf16[352,384]{1,0:T(8,128)(2,1)}, u32[]{:S(2)}, u32[]{:S(2)}) collective-permute-start(bf16[352,384]{1,0:T(8,128)(2,1)} %pad_maximum_fusion.4), channel_id=1, source_target_pairs={{0,2},{1,3},{2,0},{3,1},{4,6},{5,7},{6,4},{7,5},{8,10},{9,11},{10,... | collective-permute-start | bytes 811016 | tf_op jit(solution)/shard_map/ppermute | solution.py:127
  104.8 2.9 %all-to-all-done.2.refs_0_ = bf16[8,12,16,128]{3,2,1,0:T(8,128)(2,1)} async-done(((bf16[8,12,16,128]{3,2,1,0:T(8,128)(2,1)}), bf16[8,12,16,128]{3,2,1,0:T(8,128)(2,1)}, u32[]{:S(2)}, u32[]{:S(2)}) %all-to-all-start.2) | async-done | bytes 393248 | tf_op jit(solution)/shard_map/all_to_all | solution.py:135
  108.3 3.3 %parity_sums.9 = bf16[96,16,128]{2,1,0:T(8,128)(2,1)} custom-call(s32[4]{0:T(128)S(1)} %copy-done.21, s32[40]{0:T(128)S(1)} %get-tuple-element.162.first, s32[40]{0:T(128)S(1)} %get-tuple-element.161.total, bf16[176,768]{1,0:T(8,128)(2,1)S(1)} %copy-done.5, bf16[176,768]{1,0:T(8,128)(2,1)} %collective-permute-done.7.refs_1_, ...), custom_call_target="tpu_custom_call" | custom-call | flops 799999983616 | bytes 838860800 | tf_op jit(solution)/shard_map/parity_sums/pallas_call | solution.py:55
  111.6 3.5 %all-to-all-start.3 = ((bf16[8,12,16,128]{3,2,1,0:T(8,128)(2,1)}), bf16[8,12,16,128]{3,2,1,0:T(8,128)(2,1)S(1)}, u32[]{:S(2)}, u32[]{:S(2)}) async-start(bf16[8,12,16,128]{3,2,1,0:T(8,128)(2,1)} %bitcast.16), calls=%async_computation.3 | async-start | bytes 786432 | tf_op jit(solution)/shard_map/all_to_all | solution.py:135
  118.3 3.0 %collective-permute-start.15 = (bf16[8,12,16,128]{3,2,1,0:T(8,128)(2,1)}, bf16[8,12,16,128]{3,2,1,0:T(8,128)(2,1)}, u32[]{:S(2)}, u32[]{:S(2)}) collective-permute-start(bf16[8,12,16,128]{3,2,1,0:T(8,128)(2,1)} %all-to-all-done.2.refs_0_), channel_id=1, source_target_pairs={{0,1},{1,0},{2,3},{3,2},{4,5},{5,4},{6,7},{7,6},{8,9},{9,8},{10,11... | collective-permute-start | bytes 1179656 | tf_op jit(solution)/shard_map/ppermute | solution.py:127
  121.3 2.1 %all-to-all-done.3.refs_1_ = bf16[8,12,16,128]{3,2,1,0:T(8,128)(2,1)S(1)} async-done(((bf16[8,12,16,128]{3,2,1,0:T(8,128)(2,1)}), bf16[8,12,16,128]{3,2,1,0:T(8,128)(2,1)S(1)}, u32[]{:S(2)}, u32[]{:S(2)}) %all-to-all-start.3) | async-done | bytes 393248 | tf_op jit(solution)/shard_map/all_to_all | solution.py:135
  123.4 2.4 %finish.3.refs_4_ = bf16[12,640,128]{2,1,0:T(8,128)(2,1)} custom-call(s32[1]{0:T(128)} %bitcast.parity, s32[1]{0:T(128)S(6)} %copy.9.lat_count, bf16[8,12,16,128]{3,2,1,0:T(8,128)(2,1)} %all-to-all-done.refs_0_, bf16[8,12,16,128]{3,2,1,0:T(8,128)(2,1)S(1)} %copy-done.3, bf16[8,12,16,128]{3,2,1,0:T(8,128)(2,1)} %collective-permute-done.11.refs_2_, ...), custom_call_target="tpu_custom_call" | custom-call | tf_op jit(solution)/shard_map/finish/pallas_call | solution.py:99
  125.8 2.5 %parity_sums.10 = bf16[96,8,128]{2,1,0:T(8,128)(2,1)} custom-call(s32[4]{0:T(128)S(1)} %copy-done.21, s32[40]{0:T(128)S(1)} %get-tuple-element.162.first, s32[40]{0:T(128)S(1)} %get-tuple-element.161.total, bf16[176,384]{1,0:T(8,128)(2,1)S(1)} %copy-done.14, bf16[176,384]{1,0:T(8,128)(2,1)} %collective-permute-done.10.refs_1_, ...), custom_call_target="tpu_custom_call" | custom-call | flops 399999991808 | bytes 419430400 | tf_op jit(solution)/shard_map/parity_sums/pallas_call | solution.py:55
  128.3 3.4 %all-to-all-start.4 = ((bf16[8,12,8,128]{3,2,1,0:T(8,128)(2,1)}), bf16[8,12,8,128]{3,2,1,0:T(8,128)(2,1)S(1)}, u32[]{:S(2)}, u32[]{:S(2)}) async-start(bf16[8,12,8,128]{3,2,1,0:T(8,128)(2,1)} %bitcast.17), calls=%async_computation.4 | async-start | bytes 393216 | tf_op jit(solution)/shard_map/all_to_all | solution.py:135
  131.8 2.1 %collective-permute-done.12.refs_2_ = bf16[352,384]{1,0:T(8,128)(2,1)} collective-permute-done((bf16[352,384]{1,0:T(8,128)(2,1)}, bf16[352,384]{1,0:T(8,128)(2,1)}, u32[]{:S(2)}, u32[]{:S(2)}) %collective-permute-start.12) | collective-permute-done | bytes 270368 | tf_op jit(solution)/shard_map/ppermute | solution.py:127
  133.9 4.0 %all-to-all-done.4.refs_0_ = bf16[8,12,8,128]{3,2,1,0:T(8,128)(2,1)S(1)} async-done(((bf16[8,12,8,128]{3,2,1,0:T(8,128)(2,1)}), bf16[8,12,8,128]{3,2,1,0:T(8,128)(2,1)S(1)}, u32[]{:S(2)}, u32[]{:S(2)}) %all-to-all-start.4) | async-done | bytes 196640 | tf_op jit(solution)/shard_map/all_to_all | solution.py:135
  138.5 2.5 %parity_sums.11 = bf16[96,8,128]{2,1,0:T(8,128)(2,1)} custom-call(s32[4]{0:T(128)S(1)} %copy-done.21, s32[40]{0:T(128)S(1)} %get-tuple-element.162.first, s32[40]{0:T(128)S(1)} %get-tuple-element.161.total, bf16[176,384]{1,0:T(8,128)(2,1)S(1)} %copy-done.13, bf16[176,384]{1,0:T(8,128)(2,1)} %collective-permute-done.6.refs_1_, ...), custom_call_target="tpu_custom_call" | custom-call | flops 399999991808 | bytes 419430400 | tf_op jit(solution)/shard_map/parity_sums/pallas_call | solution.py:55
  141.1 3.4 %all-to-all-start.5 = ((bf16[8,12,8,128]{3,2,1,0:T(8,128)(2,1)}), bf16[8,12,8,128]{3,2,1,0:T(8,128)(2,1)S(1)}, u32[]{:S(2)}, u32[]{:S(2)}) async-start(bf16[8,12,8,128]{3,2,1,0:T(8,128)(2,1)} %bitcast.18), calls=%async_computation.5 | async-start | bytes 393216 | tf_op jit(solution)/shard_map/all_to_all | solution.py:135
  144.5 6.1 %all-to-all-done.5.refs_1_ = bf16[8,12,8,128]{3,2,1,0:T(8,128)(2,1)S(1)} async-done(((bf16[8,12,8,128]{3,2,1,0:T(8,128)(2,1)}), bf16[8,12,8,128]{3,2,1,0:T(8,128)(2,1)S(1)}, u32[]{:S(2)}, u32[]{:S(2)}) %all-to-all-start.5) | async-done | bytes 196640 | tf_op jit(solution)/shard_map/all_to_all | solution.py:135
  150.6 2.2 %finish.4.refs_4_ = bf16[12,640,128]{2,1,0:T(8,128)(2,1)} custom-call(s32[1]{0:T(128)} %bitcast.parity, s32[1]{0:T(128)S(6)} %copy.9.lat_count, bf16[8,12,16,128]{3,2,1,0:T(8,128)(2,1)} %all-to-all-done.2.refs_0_, bf16[8,12,16,128]{3,2,1,0:T(8,128)(2,1)S(1)} %copy-done.1, ...), custom_call_target="tpu_custom_call", output_to_operand_aliasing={{}: (6, {})} | custom-call | tf_op jit(solution)/shard_map/finish/pallas_call | solution.py:99
  152.9 4.1 %collective-permute-done.17.refs_3_ = bf16[8,12,8,128]{3,2,1,0:T(8,128)(2,1)S(1)} collective-permute-done((bf16[8,12,8,128]{3,2,1,0:T(8,128)(2,1)S(1)}, bf16[8,12,8,128]{3,2,1,0:T(8,128)(2,1)S(1)}, u32[]{:S(2)}, u32[]{:S(2)}) %collective-permute-start.17) | collective-permute-done | bytes 196640 | tf_op jit(solution)/shard_map/ppermute | solution.py:127
  (85 shorter events, 26.3 us)
Async XLA Ops:
  1.1 27.2 %collective-permute-start.1 = (bf16[176,768]{1,0:T(8,128)(2,1)S(1)}, bf16[176,768]{1,0:T(8,128)(2,1)S(1)}, u32[]{:S(2)}, u32[]{:S(2)}) collective-permute-start(bf16[176,768]{1,0:T(8,128)(2,1)S(1)} %get-tuple-element.86), channel_id=1, source_target_pairs={{0,1},{1,0},{2,3},{3,2},{4,5},{5,4},{6,7},{7,6},{8,9},{9,8},{10,11... | collective-permute-start | bytes 811016 | tf_op jit(solution)/shard_map/ppermute | solution.py:127
  4.2 24.1 %collective-permute-start.3 = (bf16[176,768]{1,0:T(8,128)(2,1)S(1)}, bf16[176,768]{1,0:T(8,128)(2,1)S(1)}, u32[]{:S(2)}, u32[]{:S(2)}) collective-permute-start(bf16[176,768]{1,0:T(8,128)(2,1)S(1)} %get-tuple-element.86), channel_id=1, source_target_pairs={{0,3},{1,2},{2,1},{3,0},{4,7},{5,6},{6,5},{7,4},{8,11},{9,10},{10,... | collective-permute-start | bytes 811016 | tf_op jit(solution)/shard_map/ppermute | solution.py:127
  8.9 19.3 %copy-start.8 = (bf16[176,768]{1,0:T(8,128)(2,1)}, bf16[176,768]{1,0:T(8,128)(2,1)S(1)}, u32[]{:S(2)}) copy-start(bf16[176,768]{1,0:T(8,128)(2,1)S(1)} %get-tuple-element.108.refs_0_) | copy-start | bytes 811012
  8.9 19.3 %copy-start.22 = (s32[40]{0:T(128)S(1)}, s32[40]{0:T(128)}, u32[]{:S(2)}) copy-start(s32[40]{0:T(128)} %param.6) | copy-start | bytes 484
  8.9 19.2 %collective-permute-start = (bf16[176,768]{1,0:T(8,128)(2,1)S(1)}, bf16[176,768]{1,0:T(8,128)(2,1)S(1)}, u32[]{:S(2)}, u32[]{:S(2)}) collective-permute-start(bf16[176,768]{1,0:T(8,128)(2,1)S(1)} %get-tuple-element.172), channel_id=1, source_target_pairs={{0,1},{1,0},{2,3},{3,2},{4,5},{5,4},{6,7},{7,6},{8,9},{9,8},{10,11... | collective-permute-start | bytes 811016 | tf_op jit(solution)/shard_map/ppermute | solution.py:127
  9.6 18.6 %collective-permute-start.2 = (bf16[176,768]{1,0:T(8,128)(2,1)S(1)}, bf16[176,768]{1,0:T(8,128)(2,1)S(1)}, u32[]{:S(2)}, u32[]{:S(2)}) collective-permute-start(bf16[176,768]{1,0:T(8,128)(2,1)S(1)} %get-tuple-element.93.refs_0_), channel_id=1, source_target_pairs={{0,2},{1,3},{2,0},{3,1},{4,6},{5,7},{6,4},{7,5},{8,10},{9,11},{10,... | collective-permute-start | bytes 811016 | tf_op jit(solution)/shard_map/ppermute | solution.py:127
  28.2 14.4 %copy-start.17 = (bf16[176,768]{1,0:T(8,128)(2,1)}, bf16[176,768]{1,0:T(8,128)(2,1)S(1)}, u32[]{:S(2)}) copy-start(bf16[176,768]{1,0:T(8,128)(2,1)S(1)} %collective-permute-done.refs_1_) | copy-start | bytes 811012
  28.2 11.7 %collective-permute-start.4 = (bf16[176,768]{1,0:T(8,128)(2,1)S(1)}, bf16[176,768]{1,0:T(8,128)(2,1)}, u32[]{:S(2)}, u32[]{:S(2)}) collective-permute-start(bf16[176,768]{1,0:T(8,128)(2,1)S(1)} %get-tuple-element.91), channel_id=1, source_target_pairs={{0,1},{1,0},{2,3},{3,2},{4,5},{5,4},{6,7},{7,6},{8,9},{9,8},{10,11... | collective-permute-start | bytes 811016 | tf_op jit(solution)/shard_map/ppermute | solution.py:127
  28.2 27.3 %copy-start.19 = (s32[4]{0:T(128)}, s32[4]{0:T(128)S(1)}, u32[]{:S(2)}) copy-start(s32[4]{0:T(128)S(1)} %iota_xor_fusion.order) | copy-start | bytes 52
  29.1 26.4 %collective-permute-start.8 = (bf16[352,768]{1,0:T(8,128)(2,1)}, bf16[352,768]{1,0:T(8,128)(2,1)}, u32[]{:S(2)}, u32[]{:S(2)}) collective-permute-start(bf16[352,768]{1,0:T(8,128)(2,1)} %pad_maximum_fusion.1), channel_id=1, source_target_pairs={{0,2},{1,3},{2,0},{3,1},{4,6},{5,7},{6,4},{7,5},{8,10},{9,11},{10,... | collective-permute-start | bytes 1622024 | tf_op jit(solution)/shard_map/ppermute | solution.py:127
  42.6 12.9 %copy-start.18 = (bf16[176,768]{1,0:T(8,128)(2,1)S(1)}, bf16[176,768]{1,0:T(8,128)(2,1)}, u32[]{:S(2)}) copy-start(bf16[176,768]{1,0:T(8,128)(2,1)} %copy-done.17) | copy-start | bytes 811012
  42.6 12.9 %all-to-all-start = ((bf16[8,12,16,128]{3,2,1,0:T(8,128)(2,1)}), bf16[8,12,16,128]{3,2,1,0:T(8,128)(2,1)}, u32[]{:S(2)}, u32[]{:S(2)}) async-start(bf16[8,12,16,128]{3,2,1,0:T(8,128)(2,1)} %bitcast.13), calls=%async_computation | async-start | bytes 786432 | tf_op jit(solution)/shard_map/all_to_all | solution.py:135
  48.8 15.5 %collective-permute-start.7 = (bf16[176,768]{1,0:T(8,128)(2,1)}, bf16[176,768]{1,0:T(8,128)(2,1)}, u32[]{:S(2)}, u32[]{:S(2)}) collective-permute-start(bf16[176,768]{1,0:T(8,128)(2,1)} %get-tuple-element.102), channel_id=1, source_target_pairs={{0,1},{1,0},{2,3},{3,2},{4,5},{5,4},{6,7},{7,6},{8,9},{9,8},{10,11... | collective-permute-start | bytes 811016 | tf_op jit(solution)/shard_map/ppermute | solution.py:127
  50.6 39.7 %collective-permute-start.5 = (bf16[352,768]{1,0:T(8,128)(2,1)}, bf16[352,768]{1,0:T(8,128)(2,1)}, u32[]{:S(2)}, u32[]{:S(2)}) collective-permute-start(bf16[352,768]{1,0:T(8,128)(2,1)} %pad_maximum_fusion), channel_id=1, source_target_pairs={{0,2},{1,3},{2,0},{3,1},{4,6},{5,7},{6,4},{7,5},{8,10},{9,11},{10,... | collective-permute-start | bytes 1622024 | tf_op jit(solution)/shard_map/ppermute | solution.py:127
  64.3 26.0 %all-to-all-start.1 = ((bf16[8,12,16,128]{3,2,1,0:T(8,128)(2,1)}), bf16[8,12,16,128]{3,2,1,0:T(8,128)(2,1)S(1)}, u32[]{:S(2)}, u32[]{:S(2)}) async-start(bf16[8,12,16,128]{3,2,1,0:T(8,128)(2,1)} %bitcast.31), calls=%async_computation.1 | async-start | bytes 786432 | tf_op jit(solution)/shard_map/all_to_all | solution.py:135
  68.2 27.1 %collective-permute-start.10 = (bf16[176,384]{1,0:T(8,128)(2,1)}, bf16[176,384]{1,0:T(8,128)(2,1)}, u32[]{:S(2)}, u32[]{:S(2)}) collective-permute-start(bf16[176,384]{1,0:T(8,128)(2,1)} %get-tuple-element.114), channel_id=1, source_target_pairs={{0,1},{1,0},{2,3},{3,2},{4,5},{5,4},{6,7},{7,6},{8,9},{9,8},{10,11... | collective-permute-start | bytes 405512 | tf_op jit(solution)/shard_map/ppermute | solution.py:127
  70.0 34.8 %collective-permute-start.9 = (bf16[352,768]{1,0:T(8,128)(2,1)}, bf16[352,768]{1,0:T(8,128)(2,1)}, u32[]{:S(2)}, u32[]{:S(2)}) collective-permute-start(bf16[352,768]{1,0:T(8,128)(2,1)} %pad_maximum_fusion.2), channel_id=1, source_target_pairs={{0,2},{1,3},{2,0},{3,1},{4,6},{5,7},{6,4},{7,5},{8,10},{9,11},{10,... | collective-permute-start | bytes 1622024 | tf_op jit(solution)/shard_map/ppermute | solution.py:127
  72.0 35.7 %collective-permute-start.11 = (bf16[8,12,16,128]{3,2,1,0:T(8,128)(2,1)}, bf16[8,12,16,128]{3,2,1,0:T(8,128)(2,1)}, u32[]{:S(2)}, u32[]{:S(2)}) collective-permute-start(bf16[8,12,16,128]{3,2,1,0:T(8,128)(2,1)} %all-to-all-done.refs_0_), channel_id=1, source_target_pairs={{0,1},{1,0},{2,3},{3,2},{4,5},{5,4},{6,7},{7,6},{8,9},{9,8},{10,11... | collective-permute-start | bytes 1179656 | tf_op jit(solution)/shard_map/ppermute | solution.py:127
  95.3 12.5 %all-to-all-start.2 = ((bf16[8,12,16,128]{3,2,1,0:T(8,128)(2,1)}), bf16[8,12,16,128]{3,2,1,0:T(8,128)(2,1)}, u32[]{:S(2)}, u32[]{:S(2)}) async-start(bf16[8,12,16,128]{3,2,1,0:T(8,128)(2,1)} %bitcast.32), calls=%async_computation.2 | async-start | bytes 786432 | tf_op jit(solution)/shard_map/all_to_all | solution.py:135
  100.0 11.6 %collective-permute-start.6 = (bf16[176,384]{1,0:T(8,128)(2,1)}, bf16[176,384]{1,0:T(8,128)(2,1)}, u32[]{:S(2)}, u32[]{:S(2)}) collective-permute-start(bf16[176,384]{1,0:T(8,128)(2,1)} %get-tuple-element.100), channel_id=1, source_target_pairs={{0,1},{1,0},{2,3},{3,2},{4,5},{5,4},{6,7},{7,6},{8,9},{9,8},{10,11... | collective-permute-start | bytes 405512 | tf_op jit(solution)/shard_map/ppermute | solution.py:127
  101.8 19.5 %collective-permute-start.13 = (bf16[352,384]{1,0:T(8,128)(2,1)}, bf16[352,384]{1,0:T(8,128)(2,1)}, u32[]{:S(2)}, u32[]{:S(2)}) collective-permute-start(bf16[352,384]{1,0:T(8,128)(2,1)} %pad_maximum_fusion.4), channel_id=1, source_target_pairs={{0,2},{1,3},{2,0},{3,1},{4,6},{5,7},{6,4},{7,5},{8,10},{9,11},{10,... | collective-permute-start | bytes 811016 | tf_op jit(solution)/shard_map/ppermute | solution.py:127
  104.8 18.6 %collective-permute-start.14 = (bf16[8,12,16,128]{3,2,1,0:T(8,128)(2,1)}, bf16[8,12,16,128]{3,2,1,0:T(8,128)(2,1)}, u32[]{:S(2)}, u32[]{:S(2)}) collective-permute-start(bf16[8,12,16,128]{3,2,1,0:T(8,128)(2,1)} %copy-done.2), channel_id=1, source_target_pairs={{0,1},{1,0},{2,3},{3,2},{4,5},{5,4},{6,7},{7,6},{8,9},{9,8},{10,11... | collective-permute-start | bytes 1179656 | tf_op jit(solution)/shard_map/ppermute | solution.py:127
  111.6 11.7 %all-to-all-start.3 = ((bf16[8,12,16,128]{3,2,1,0:T(8,128)(2,1)}), bf16[8,12,16,128]{3,2,1,0:T(8,128)(2,1)S(1)}, u32[]{:S(2)}, u32[]{:S(2)}) async-start(bf16[8,12,16,128]{3,2,1,0:T(8,128)(2,1)} %bitcast.16), calls=%async_computation.3 | async-start | bytes 786432 | tf_op jit(solution)/shard_map/all_to_all | solution.py:135
  118.3 15.6 %collective-permute-start.12 = (bf16[352,384]{1,0:T(8,128)(2,1)}, bf16[352,384]{1,0:T(8,128)(2,1)}, u32[]{:S(2)}, u32[]{:S(2)}) collective-permute-start(bf16[352,384]{1,0:T(8,128)(2,1)} %pad_maximum_fusion.3), channel_id=1, source_target_pairs={{0,2},{1,3},{2,0},{3,1},{4,6},{5,7},{6,4},{7,5},{8,10},{9,11},{10,... | collective-permute-start | bytes 811016 | tf_op jit(solution)/shard_map/ppermute | solution.py:127
  118.3 19.6 %collective-permute-start.15 = (bf16[8,12,16,128]{3,2,1,0:T(8,128)(2,1)}, bf16[8,12,16,128]{3,2,1,0:T(8,128)(2,1)}, u32[]{:S(2)}, u32[]{:S(2)}) collective-permute-start(bf16[8,12,16,128]{3,2,1,0:T(8,128)(2,1)} %all-to-all-done.2.refs_0_), channel_id=1, source_target_pairs={{0,1},{1,0},{2,3},{3,2},{4,5},{5,4},{6,7},{7,6},{8,9},{9,8},{10,11... | collective-permute-start | bytes 1179656 | tf_op jit(solution)/shard_map/ppermute | solution.py:127
  125.8 12.7 %copy-start.13 = (bf16[176,384]{1,0:T(8,128)(2,1)S(1)}, bf16[176,384]{1,0:T(8,128)(2,1)}, u32[]{:S(2)}) copy-start(bf16[176,384]{1,0:T(8,128)(2,1)} %get-tuple-element.154.refs_0_) | copy-start | bytes 405508
  128.3 9.6 %all-to-all-start.4 = ((bf16[8,12,8,128]{3,2,1,0:T(8,128)(2,1)}), bf16[8,12,8,128]{3,2,1,0:T(8,128)(2,1)S(1)}, u32[]{:S(2)}, u32[]{:S(2)}) async-start(bf16[8,12,8,128]{3,2,1,0:T(8,128)(2,1)} %bitcast.17), calls=%async_computation.4 | async-start | bytes 393216 | tf_op jit(solution)/shard_map/all_to_all | solution.py:135
  131.7 18.9 %collective-permute-start.18 = (bf16[8,12,16,128]{3,2,1,0:T(8,128)(2,1)}, bf16[8,12,16,128]{3,2,1,0:T(8,128)(2,1)}, u32[]{:S(2)}, u32[]{:S(2)}) collective-permute-start(bf16[8,12,16,128]{3,2,1,0:T(8,128)(2,1)} %copy-done), channel_id=1, source_target_pairs={{0,1},{1,0},{2,3},{3,2},{4,5},{5,4},{6,7},{7,6},{8,9},{9,8},{10,11... | collective-permute-start | bytes 1179656 | tf_op jit(solution)/shard_map/ppermute | solution.py:127
  138.5 12.1 %copy-start.1 = (bf16[8,12,16,128]{3,2,1,0:T(8,128)(2,1)S(1)}, bf16[8,12,16,128]{3,2,1,0:T(8,128)(2,1)}, u32[]{:S(2)}) copy-start(bf16[8,12,16,128]{3,2,1,0:T(8,128)(2,1)} %copy-done) | copy-start | bytes 1179652
  141.1 9.6 %all-to-all-start.5 = ((bf16[8,12,8,128]{3,2,1,0:T(8,128)(2,1)}), bf16[8,12,8,128]{3,2,1,0:T(8,128)(2,1)S(1)}, u32[]{:S(2)}, u32[]{:S(2)}) async-start(bf16[8,12,8,128]{3,2,1,0:T(8,128)(2,1)} %bitcast.18), calls=%async_computation.5 | async-start | bytes 393216 | tf_op jit(solution)/shard_map/all_to_all | solution.py:135
  144.5 8.4 %collective-permute-start.16 = (bf16[8,12,8,128]{3,2,1,0:T(8,128)(2,1)S(1)}, bf16[8,12,8,128]{3,2,1,0:T(8,128)(2,1)S(1)}, u32[]{:S(2)}, u32[]{:S(2)}) collective-permute-start(bf16[8,12,8,128]{3,2,1,0:T(8,128)(2,1)S(1)} %copy-done.11), channel_id=1, source_target_pairs={{0,1},{1,0},{2,3},{3,2},{4,5},{5,4},{6,7},{7,6},{8,9},{9,8},{10,11... | collective-permute-start | bytes 589832 | tf_op jit(solution)/shard_map/ppermute | solution.py:127
  150.6 6.3 %collective-permute-start.17 = (bf16[8,12,8,128]{3,2,1,0:T(8,128)(2,1)S(1)}, bf16[8,12,8,128]{3,2,1,0:T(8,128)(2,1)S(1)}, u32[]{:S(2)}, u32[]{:S(2)}) collective-permute-start(bf16[8,12,8,128]{3,2,1,0:T(8,128)(2,1)S(1)} %all-to-all-done.5.refs_1_), channel_id=1, source_target_pairs={{0,1},{1,0},{2,3},{3,2},{4,5},{5,4},{6,7},{7,6},{8,9},{9,8},{10,11... | collective-permute-start | bytes 589832 | tf_op jit(solution)/shard_map/ppermute | solution.py:127
  (16 other events, 50.6 us)

commit v7 on v6

--- a/solution.py
+++ b/solution.py
@@ -10,7 +10,7 @@
 TRUNC = 1279
 VMEM = 24 * 2**20
 CHUNKS = (8, 8, 8, 8, 4, 4)
-MIRRORED = {3: 0, 4: 1, 5: 2}
+MIRRORED = {2: 0, 4: 1, 5: 2}
 GROUPS = ((0, 1), (2, 3), (4, 5))
 
 

time: 159 us -> 158 us (level)
    all_to_all x6, waiting for transfers between devices: 15.1 us -> 12.3 us  [redistribute(): lax.all_to_all(grid.reshape(sets, fields // sets, -1, lats), 'mset', 0, 0)]
    ppermute x19, waiting for transfers between devices: 50.6 us -> 53.2 us  [swap(): lax.ppermute(value, 'band', [(band, band ^ step) for band in range(bands)])]
  transfers between devices with their start and end apart: 25 -> 25, of which waited for: 11 -> 13; matrix products, arithmetic and copies ran while one was open for 11% -> 11% of each run, Pallas kernels for 13% -> 13%
where the time goes in v7:
time: 158 us; the launch traced here: 157 us
  waiting for transfers between devices  65.5 us (41%)
  starting transfers between devices  43.3 us (27%)
  Pallas kernels  21.4 us (14%)
  local copies, waits for them, and re-layouts  17.8 us (11%)
  other arithmetic  7.8 us (5%)
    ppermute x19, waiting for transfers between devices, swap(): lax.ppermute(value, 'band', [(band, band ^ step) for band in range(bands)])  53.2 us
    all_to_all x6, starting transfers between devices, redistribute(): lax.all_to_all(grid.reshape(sets, fields // sets, -1, lats), 'mset', 0, 0)  22.7 us
    ppermute x19, starting transfers between devices, swap(): lax.ppermute(value, 'band', [(band, band ^ step) for band in range(bands)])  20.6 us
    pallas_call x6, Pallas kernels, parity_sums(): pl.pallas_call(functools.partial(sums_kernel, rows, fields, start), in_sp...  16 us
    all_to_all x6, waiting for transfers between devices, redistribute(): lax.all_to_all(grid.reshape(sets, fields // sets, -1, lats), 'mset', 0, 0)  12.3 us
    concatenate x5, other arithmetic, spread(): held.append(swap(jnp.concatenate(held), bit))  7.78 us
    unnamed x46, local copies, waits for them, and re-layouts  6.69 us
    slice x2, local copies, waits for them, and re-layouts, parity_sums(): legendre = legendre[start:start + pairs]  5.79 us
  transfers between devices with their start and end apart: 25, of which 13 were waited for; matrix products, arithmetic and copies ran while one was open for 11% of the time, Pallas kernels for 13%

profile of v7, /device:TPU:0, one launch (start us, length us, event | category | flops | bytes accessed | tf_op | source)
XLA Modules:
  0.0 156.8 jit_solution(17548216899428629448)
XLA Ops:
  1.1 3.1 %collective-permute-start.1 = (bf16[176,768]{1,0:T(8,128)(2,1)S(1)}, bf16[176,768]{1,0:T(8,128)(2,1)S(1)}, u32[]{:S(2)}, u32[]{:S(2)}) collective-permute-start(bf16[176,768]{1,0:T(8,128)(2,1)S(1)} %get-tuple-element.86), channel_id=1, source_target_pairs={{0,1},{1,0},{2,3},{3,2},{4,5},{5,4},{6,7},{7,6},{8,9},{9,8},{10,11... | collective-permute-start | bytes 811016 | tf_op jit(solution)/shard_map/ppermute | solution.py:127
  4.2 2.5 %collective-permute-start.3 = (bf16[176,768]{1,0:T(8,128)(2,1)S(1)}, bf16[176,768]{1,0:T(8,128)(2,1)S(1)}, u32[]{:S(2)}, u32[]{:S(2)}) collective-permute-start(bf16[176,768]{1,0:T(8,128)(2,1)S(1)} %get-tuple-element.86), channel_id=1, source_target_pairs={{0,3},{1,2},{2,1},{3,0},{4,7},{5,6},{6,5},{7,4},{8,11},{9,10},{10,... | collective-permute-start | bytes 811016 | tf_op jit(solution)/shard_map/ppermute | solution.py:127
  6.6 2.3 %dynamic-slice_bitcast_fusion = (bf16[176,768]{1,0:T(8,128)(2,1)S(1)}, bf16[176,768]{1,0:T(8,128)(2,1)}, bf16[176,768]{1,0:T(8,128)(2,1)}, bf16[176,768]{1,0:T(8...) fusion(bf16[2,176,3840]{2,1,0:T(8,128)(2,1)} %param.4, s32[]{:T(128)S(6)} %select_n.32, s32[]{:T(128)S(6)} %select_n.33), kind=kLoop, calls=%fused_computation.5 | loop fusion | bytes 3244040 | tf_op jit(solution)/shard_map/squeeze | solution.py:132
  10.9 4.3 %fusion.1 = (bf16[8,704,128]{2,1,0:T(8,128)(2,1)S(1)}, bf16[8,704,128]{2,1,0:T(8,128)(2,1)S(1)}, bf16[8,704,128]{2,1,0:T(8,128)(2,1)}, bf16[8,704,128]{2,1,0:T(8,128)(2,1)S(1)}) fusion(bf16[40,704,128]{2,1,0:T(8,128)(2,1)} %param.5), kind=kLoop, calls=%fused_computation.29 | loop fusion | bytes 11534336 | tf_op jit(solution)/shard_map/slice | solution.py:52
  15.2 13.0 %collective-permute-done.refs_1_ = bf16[176,768]{1,0:T(8,128)(2,1)S(1)} collective-permute-done((bf16[176,768]{1,0:T(8,128)(2,1)S(1)}, bf16[176,768]{1,0:T(8,128)(2,1)S(1)}, u32[]{:S(2)}, u32[]{:S(2)}) %collective-permute-start) | collective-permute-done | bytes 270368 | tf_op jit(solution)/shard_map/ppermute | solution.py:127
  29.1 2.9 %collective-permute-start.8 = (bf16[352,768]{1,0:T(8,128)(2,1)}, bf16[352,768]{1,0:T(8,128)(2,1)}, u32[]{:S(2)}, u32[]{:S(2)}) collective-permute-start(bf16[352,768]{1,0:T(8,128)(2,1)} %pad_maximum_fusion.1), channel_id=1, source_target_pairs={{0,2},{1,3},{2,0},{3,1},{4,6},{5,7},{6,4},{7,5},{8,10},{9,11},{10,... | collective-permute-start | bytes 1622024 | tf_op jit(solution)/shard_map/ppermute | solution.py:127
  32.0 7.9 %collective-permute-done.4.refs_1_ = bf16[176,768]{1,0:T(8,128)(2,1)} collective-permute-done((bf16[176,768]{1,0:T(8,128)(2,1)S(1)}, bf16[176,768]{1,0:T(8,128)(2,1)}, u32[]{:S(2)}, u32[]{:S(2)}) %collective-permute-start.4) | collective-permute-done | bytes 270368 | tf_op jit(solution)/shard_map/ppermute | solution.py:127
  39.9 2.7 %parity_sums.6 = bf16[96,16,128]{2,1,0:T(8,128)(2,1)} custom-call(s32[4]{0:T(128)S(1)} %iota_xor_fusion.order, s32[40]{0:T(128)S(1)} %get-tuple-element.162.first, s32[40]{0:T(128)S(1)} %get-tuple-element.161.total, bf16[176,768]{1,0:T(8,128)(2,1)S(1)} %get-tuple-element.93.refs_0_, bf16[176,768]{1,0:T(8,128)(2,1)S(1)} %collective-permute-done.1.refs_1_, ...), custom_call_target="tpu_custom_call" | custom-call | flops 799999983616 | bytes 838860800 | tf_op jit(solution)/shard_map/parity_sums/pallas_call | solution.py:55
  42.6 4.2 %all-to-all-start = ((bf16[8,12,16,128]{3,2,1,0:T(8,128)(2,1)}), bf16[8,12,16,128]{3,2,1,0:T(8,128)(2,1)}, u32[]{:S(2)}, u32[]{:S(2)}) async-start(bf16[8,12,16,128]{3,2,1,0:T(8,128)(2,1)} %bitcast.13), calls=%async_computation | async-start | bytes 786432 | tf_op jit(solution)/shard_map/all_to_all | solution.py:135
  50.6 2.9 %collective-permute-start.5 = (bf16[352,768]{1,0:T(8,128)(2,1)}, bf16[352,768]{1,0:T(8,128)(2,1)}, u32[]{:S(2)}, u32[]{:S(2)}) collective-permute-start(bf16[352,768]{1,0:T(8,128)(2,1)} %pad_maximum_fusion), channel_id=1, source_target_pairs={{0,2},{1,3},{2,0},{3,1},{4,6},{5,7},{6,4},{7,5},{8,10},{9,11},{10,... | collective-permute-start | bytes 1622024 | tf_op jit(solution)/shard_map/ppermute | solution.py:127
  57.9 2.5 %parity_sums.7 = bf16[96,16,128]{2,1,0:T(8,128)(2,1)S(1)} custom-call(s32[4]{0:T(128)S(1)} %iota_xor_fusion.order, s32[40]{0:T(128)S(1)} %get-tuple-element.162.first, s32[40]{0:T(128)S(1)} %get-tuple-element.161.total, bf16[176,768]{1,0:T(8,128)(2,1)S(1)} %copy-done.9, bf16[176,768]{1,0:T(8,128)(2,1)S(1)} %copy-done.18, ...), custom_call_target="tpu_custom_call" | custom-call | flops 799999983616 | bytes 838860800 | tf_op jit(solution)/shard_map/parity_sums/pallas_call | solution.py:55
  61.1 3.3 %collective-permute-done.7.refs_1_ = bf16[176,768]{1,0:T(8,128)(2,1)} collective-permute-done((bf16[176,768]{1,0:T(8,128)(2,1)}, bf16[176,768]{1,0:T(8,128)(2,1)}, u32[]{:S(2)}, u32[]{:S(2)}) %collective-permute-start.7) | collective-permute-done | bytes 270368 | tf_op jit(solution)/shard_map/ppermute | solution.py:127
  64.3 3.9 %all-to-all-start.1 = ((bf16[8,12,16,128]{3,2,1,0:T(8,128)(2,1)}), bf16[8,12,16,128]{3,2,1,0:T(8,128)(2,1)S(1)}, u32[]{:S(2)}, u32[]{:S(2)}) async-start(bf16[8,12,16,128]{3,2,1,0:T(8,128)(2,1)} %bitcast.32), calls=%async_computation.1 | async-start | bytes 786432 | tf_op jit(solution)/shard_map/all_to_all | solution.py:135
  72.1 6.7 %collective-permute-done.5.refs_2_ = bf16[352,768]{1,0:T(8,128)(2,1)} collective-permute-done((bf16[352,768]{1,0:T(8,128)(2,1)}, bf16[352,768]{1,0:T(8,128)(2,1)}, u32[]{:S(2)}, u32[]{:S(2)}) %collective-permute-start.5) | collective-permute-done | bytes 540704 | tf_op jit(solution)/shard_map/ppermute | solution.py:127
  78.7 5.4 %collective-permute-done.11.refs_2_ = bf16[8,12,16,128]{3,2,1,0:T(8,128)(2,1)} collective-permute-done((bf16[8,12,16,128]{3,2,1,0:T(8,128)(2,1)}, bf16[8,12,16,128]{3,2,1,0:T(8,128)(2,1)}, u32[]{:S(2)}, u32[]{:S(2)}) %collective-permute-start.11) | collective-permute-done | bytes 393248 | tf_op jit(solution)/shard_map/ppermute | solution.py:127
  85.7 2.5 %parity_sums.8 = bf16[96,16,128]{2,1,0:T(8,128)(2,1)S(1)} custom-call(s32[4]{0:T(128)S(1)} %copy-done.20, s32[40]{0:T(128)S(1)} %get-tuple-element.162.first, s32[40]{0:T(128)S(1)} %get-tuple-element.161.total, bf16[176,768]{1,0:T(8,128)(2,1)S(1)} %copy-done.7, bf16[176,768]{1,0:T(8,128)(2,1)} %collective-permute-done.4.refs_1_, ...), custom_call_target="tpu_custom_call" | custom-call | flops 799999983616 | bytes 838860800 | tf_op jit(solution)/shard_map/parity_sums/pallas_call | solution.py:55
  89.0 4.1 %all-to-all-start.2 = ((bf16[8,12,16,128]{3,2,1,0:T(8,128)(2,1)}), bf16[8,12,16,128]{3,2,1,0:T(8,128)(2,1)}, u32[]{:S(2)}, u32[]{:S(2)}) async-start(bf16[8,12,16,128]{3,2,1,0:T(8,128)(2,1)} %bitcast.31), calls=%async_computation.2 | async-start | bytes 786432 | tf_op jit(solution)/shard_map/all_to_all | solution.py:135
  97.6 4.3 %collective-permute-done.9.refs_2_ = bf16[352,768]{1,0:T(8,128)(2,1)} collective-permute-done((bf16[352,768]{1,0:T(8,128)(2,1)}, bf16[352,768]{1,0:T(8,128)(2,1)}, u32[]{:S(2)}, u32[]{:S(2)}) %collective-permute-start.9) | collective-permute-done | bytes 540704 | tf_op jit(solution)/shard_map/ppermute | solution.py:127
  102.6 3.3 %parity_sums.9 = bf16[96,16,128]{2,1,0:T(8,128)(2,1)} custom-call(s32[4]{0:T(128)S(1)} %copy-done.21, s32[40]{0:T(128)S(1)} %get-tuple-element.162.first, s32[40]{0:T(128)S(1)} %get-tuple-element.161.total, bf16[176,768]{1,0:T(8,128)(2,1)S(1)} %copy-done.5, bf16[176,768]{1,0:T(8,128)(2,1)} %collective-permute-done.7.refs_1_, ...), custom_call_target="tpu_custom_call" | custom-call | flops 799999983616 | bytes 838860800 | tf_op jit(solution)/shard_map/parity_sums/pallas_call | solution.py:55
  105.9 4.4 %collective-permute-done.6.refs_1_ = bf16[176,384]{1,0:T(8,128)(2,1)} collective-permute-done((bf16[176,384]{1,0:T(8,128)(2,1)}, bf16[176,384]{1,0:T(8,128)(2,1)}, u32[]{:S(2)}, u32[]{:S(2)}) %collective-permute-start.6) | collective-permute-done | bytes 135200 | tf_op jit(solution)/shard_map/ppermute | solution.py:127
  110.3 3.7 %all-to-all-start.3 = ((bf16[8,12,16,128]{3,2,1,0:T(8,128)(2,1)}), bf16[8,12,16,128]{3,2,1,0:T(8,128)(2,1)S(1)}, u32[]{:S(2)}, u32[]{:S(2)}) async-start(bf16[8,12,16,128]{3,2,1,0:T(8,128)(2,1)} %bitcast.16), calls=%async_computation.3 | async-start | bytes 786432 | tf_op jit(solution)/shard_map/all_to_all | solution.py:135
  117.6 2.5 %collective-permute-start.15 = (bf16[8,12,16,128]{3,2,1,0:T(8,128)(2,1)}, bf16[8,12,16,128]{3,2,1,0:T(8,128)(2,1)}, u32[]{:S(2)}, u32[]{:S(2)}) collective-permute-start(bf16[8,12,16,128]{3,2,1,0:T(8,128)(2,1)} %all-to-all-done.2.refs_0_), channel_id=1, source_target_pairs={{0,1},{1,0},{2,3},{3,2},{4,5},{5,4},{6,7},{7,6},{8,9},{9,8},{10,11... | collective-permute-start | bytes 1179656 | tf_op jit(solution)/shard_map/ppermute | solution.py:127
  120.1 2.2 %all-to-all-done.3.refs_1_ = bf16[8,12,16,128]{3,2,1,0:T(8,128)(2,1)S(1)} async-done(((bf16[8,12,16,128]{3,2,1,0:T(8,128)(2,1)}), bf16[8,12,16,128]{3,2,1,0:T(8,128)(2,1)S(1)}, u32[]{:S(2)}, u32[]{:S(2)}) %all-to-all-start.3) | async-done | bytes 393248 | tf_op jit(solution)/shard_map/all_to_all | solution.py:135
  122.4 2.4 %finish.3.refs_4_ = bf16[12,640,128]{2,1,0:T(8,128)(2,1)} custom-call(s32[1]{0:T(128)} %bitcast.parity, s32[1]{0:T(128)S(6)} %copy.9.lat_count, bf16[8,12,16,128]{3,2,1,0:T(8,128)(2,1)} %all-to-all-done.refs_0_, bf16[8,12,16,128]{3,2,1,0:T(8,128)(2,1)S(1)} %copy-done.3, bf16[8,12,16,128]{3,2,1,0:T(8,128)(2,1)} %collective-permute-done.11.refs_2_, ...), custom_call_target="tpu_custom_call" | custom-call | tf_op jit(solution)/shard_map/finish/pallas_call | solution.py:99
  124.8 2.5 %parity_sums.10 = bf16[96,8,128]{2,1,0:T(8,128)(2,1)} custom-call(s32[4]{0:T(128)S(1)} %copy-done.21, s32[40]{0:T(128)S(1)} %get-tuple-element.162.first, s32[40]{0:T(128)S(1)} %get-tuple-element.161.total, bf16[176,384]{1,0:T(8,128)(2,1)S(1)} %copy-done.14, bf16[176,384]{1,0:T(8,128)(2,1)} %collective-permute-done.10.refs_1_, ...), custom_call_target="tpu_custom_call" | custom-call | flops 399999991808 | bytes 419430400 | tf_op jit(solution)/shard_map/parity_sums/pallas_call | solution.py:55
  127.3 3.4 %all-to-all-start.4 = ((bf16[8,12,8,128]{3,2,1,0:T(8,128)(2,1)}), bf16[8,12,8,128]{3,2,1,0:T(8,128)(2,1)S(1)}, u32[]{:S(2)}, u32[]{:S(2)}) async-start(bf16[8,12,8,128]{3,2,1,0:T(8,128)(2,1)} %bitcast.17), calls=%async_computation.4 | async-start | bytes 393216 | tf_op jit(solution)/shard_map/all_to_all | solution.py:135
  132.9 3.9 %all-to-all-done.4.refs_0_ = bf16[8,12,8,128]{3,2,1,0:T(8,128)(2,1)S(1)} async-done(((bf16[8,12,8,128]{3,2,1,0:T(8,128)(2,1)}), bf16[8,12,8,128]{3,2,1,0:T(8,128)(2,1)S(1)}, u32[]{:S(2)}, u32[]{:S(2)}) %all-to-all-start.4) | async-done | bytes 196640 | tf_op jit(solution)/shard_map/all_to_all | solution.py:135
  137.5 2.5 %parity_sums.11 = bf16[96,8,128]{2,1,0:T(8,128)(2,1)} custom-call(s32[4]{0:T(128)S(1)} %copy-done.21, s32[40]{0:T(128)S(1)} %get-tuple-element.162.first, s32[40]{0:T(128)S(1)} %get-tuple-element.161.total, bf16[176,384]{1,0:T(8,128)(2,1)S(1)} %copy-done.13, bf16[176,384]{1,0:T(8,128)(2,1)} %collective-permute-done.6.refs_1_, ...), custom_call_target="tpu_custom_call" | custom-call | flops 399999991808 | bytes 419430400 | tf_op jit(solution)/shard_map/parity_sums/pallas_call | solution.py:55
  140.0 3.4 %all-to-all-start.5 = ((bf16[8,12,8,128]{3,2,1,0:T(8,128)(2,1)}), bf16[8,12,8,128]{3,2,1,0:T(8,128)(2,1)S(1)}, u32[]{:S(2)}, u32[]{:S(2)}) async-start(bf16[8,12,8,128]{3,2,1,0:T(8,128)(2,1)} %bitcast.18), calls=%async_computation.5 | async-start | bytes 393216 | tf_op jit(solution)/shard_map/all_to_all | solution.py:135
  143.5 6.1 %all-to-all-done.5.refs_1_ = bf16[8,12,8,128]{3,2,1,0:T(8,128)(2,1)S(1)} async-done(((bf16[8,12,8,128]{3,2,1,0:T(8,128)(2,1)}), bf16[8,12,8,128]{3,2,1,0:T(8,128)(2,1)S(1)}, u32[]{:S(2)}, u32[]{:S(2)}) %all-to-all-start.5) | async-done | bytes 196640 | tf_op jit(solution)/shard_map/all_to_all | solution.py:135
  149.6 2.2 %finish.4.refs_4_ = bf16[12,640,128]{2,1,0:T(8,128)(2,1)} custom-call(s32[1]{0:T(128)} %bitcast.parity, s32[1]{0:T(128)S(6)} %copy.9.lat_count, bf16[8,12,16,128]{3,2,1,0:T(8,128)(2,1)} %all-to-all-done.2.refs_0_, bf16[8,12,16,128]{3,2,1,0:T(8,128)(2,1)S(1)} %copy-done.1, ...), custom_call_target="tpu_custom_call", output_to_operand_aliasing={{}: (6, {})} | custom-call | tf_op jit(solution)/shard_map/finish/pallas_call | solution.py:99
  151.9 4.1 %collective-permute-done.17.refs_3_ = bf16[8,12,8,128]{3,2,1,0:T(8,128)(2,1)S(1)} collective-permute-done((bf16[8,12,8,128]{3,2,1,0:T(8,128)(2,1)S(1)}, bf16[8,12,8,128]{3,2,1,0:T(8,128)(2,1)S(1)}, u32[]{:S(2)}, u32[]{:S(2)}) %collective-permute-start.17) | collective-permute-done | bytes 196640 | tf_op jit(solution)/shard_map/ppermute | solution.py:127
  (85 shorter events, 30.8 us)
Async XLA Ops:
  1.1 27.2 %collective-permute-start.1 = (bf16[176,768]{1,0:T(8,128)(2,1)S(1)}, bf16[176,768]{1,0:T(8,128)(2,1)S(1)}, u32[]{:S(2)}, u32[]{:S(2)}) collective-permute-start(bf16[176,768]{1,0:T(8,128)(2,1)S(1)} %get-tuple-element.86), channel_id=1, source_target_pairs={{0,1},{1,0},{2,3},{3,2},{4,5},{5,4},{6,7},{7,6},{8,9},{9,8},{10,11... | collective-permute-start | bytes 811016 | tf_op jit(solution)/shard_map/ppermute | solution.py:127
  4.2 24.1 %collective-permute-start.3 = (bf16[176,768]{1,0:T(8,128)(2,1)S(1)}, bf16[176,768]{1,0:T(8,128)(2,1)S(1)}, u32[]{:S(2)}, u32[]{:S(2)}) collective-permute-start(bf16[176,768]{1,0:T(8,128)(2,1)S(1)} %get-tuple-element.86), channel_id=1, source_target_pairs={{0,3},{1,2},{2,1},{3,0},{4,7},{5,6},{6,5},{7,4},{8,11},{9,10},{10,... | collective-permute-start | bytes 811016 | tf_op jit(solution)/shard_map/ppermute | solution.py:127
  8.9 19.3 %copy-start.8 = (bf16[176,768]{1,0:T(8,128)(2,1)}, bf16[176,768]{1,0:T(8,128)(2,1)S(1)}, u32[]{:S(2)}) copy-start(bf16[176,768]{1,0:T(8,128)(2,1)S(1)} %get-tuple-element.108.refs_0_) | copy-start | bytes 811012
  8.9 19.3 %copy-start.22 = (s32[40]{0:T(128)S(1)}, s32[40]{0:T(128)}, u32[]{:S(2)}) copy-start(s32[40]{0:T(128)} %param.6) | copy-start | bytes 484
  8.9 19.2 %collective-permute-start = (bf16[176,768]{1,0:T(8,128)(2,1)S(1)}, bf16[176,768]{1,0:T(8,128)(2,1)S(1)}, u32[]{:S(2)}, u32[]{:S(2)}) collective-permute-start(bf16[176,768]{1,0:T(8,128)(2,1)S(1)} %get-tuple-element.172), channel_id=1, source_target_pairs={{0,1},{1,0},{2,3},{3,2},{4,5},{5,4},{6,7},{7,6},{8,9},{9,8},{10,11... | collective-permute-start | bytes 811016 | tf_op jit(solution)/shard_map/ppermute | solution.py:127
  9.6 18.6 %collective-permute-start.2 = (bf16[176,768]{1,0:T(8,128)(2,1)S(1)}, bf16[176,768]{1,0:T(8,128)(2,1)S(1)}, u32[]{:S(2)}, u32[]{:S(2)}) collective-permute-start(bf16[176,768]{1,0:T(8,128)(2,1)S(1)} %get-tuple-element.93.refs_0_), channel_id=1, source_target_pairs={{0,2},{1,3},{2,0},{3,1},{4,6},{5,7},{6,4},{7,5},{8,10},{9,11},{10,... | collective-permute-start | bytes 811016 | tf_op jit(solution)/shard_map/ppermute | solution.py:127
  28.2 14.4 %copy-start.17 = (bf16[176,768]{1,0:T(8,128)(2,1)}, bf16[176,768]{1,0:T(8,128)(2,1)S(1)}, u32[]{:S(2)}) copy-start(bf16[176,768]{1,0:T(8,128)(2,1)S(1)} %collective-permute-done.refs_1_) | copy-start | bytes 811012
  28.2 11.7 %collective-permute-start.4 = (bf16[176,768]{1,0:T(8,128)(2,1)S(1)}, bf16[176,768]{1,0:T(8,128)(2,1)}, u32[]{:S(2)}, u32[]{:S(2)}) collective-permute-start(bf16[176,768]{1,0:T(8,128)(2,1)S(1)} %get-tuple-element.91), channel_id=1, source_target_pairs={{0,1},{1,0},{2,3},{3,2},{4,5},{5,4},{6,7},{7,6},{8,9},{9,8},{10,11... | collective-permute-start | bytes 811016 | tf_op jit(solution)/shard_map/ppermute | solution.py:127
  28.2 27.3 %copy-start.19 = (s32[4]{0:T(128)}, s32[4]{0:T(128)S(1)}, u32[]{:S(2)}) copy-start(s32[4]{0:T(128)S(1)} %iota_xor_fusion.order) | copy-start | bytes 52
  29.1 26.4 %collective-permute-start.8 = (bf16[352,768]{1,0:T(8,128)(2,1)}, bf16[352,768]{1,0:T(8,128)(2,1)}, u32[]{:S(2)}, u32[]{:S(2)}) collective-permute-start(bf16[352,768]{1,0:T(8,128)(2,1)} %pad_maximum_fusion.1), channel_id=1, source_target_pairs={{0,2},{1,3},{2,0},{3,1},{4,6},{5,7},{6,4},{7,5},{8,10},{9,11},{10,... | collective-permute-start | bytes 1622024 | tf_op jit(solution)/shard_map/ppermute | solution.py:127
  42.6 12.9 %copy-start.18 = (bf16[176,768]{1,0:T(8,128)(2,1)S(1)}, bf16[176,768]{1,0:T(8,128)(2,1)}, u32[]{:S(2)}) copy-start(bf16[176,768]{1,0:T(8,128)(2,1)} %copy-done.17) | copy-start | bytes 811012
  42.6 12.9 %all-to-all-start = ((bf16[8,12,16,128]{3,2,1,0:T(8,128)(2,1)}), bf16[8,12,16,128]{3,2,1,0:T(8,128)(2,1)}, u32[]{:S(2)}, u32[]{:S(2)}) async-start(bf16[8,12,16,128]{3,2,1,0:T(8,128)(2,1)} %bitcast.13), calls=%async_computation | async-start | bytes 786432 | tf_op jit(solution)/shard_map/all_to_all | solution.py:135
  48.8 15.6 %collective-permute-start.7 = (bf16[176,768]{1,0:T(8,128)(2,1)}, bf16[176,768]{1,0:T(8,128)(2,1)}, u32[]{:S(2)}, u32[]{:S(2)}) collective-permute-start(bf16[176,768]{1,0:T(8,128)(2,1)} %get-tuple-element.102), channel_id=1, source_target_pairs={{0,1},{1,0},{2,3},{3,2},{4,5},{5,4},{6,7},{7,6},{8,9},{9,8},{10,11... | collective-permute-start | bytes 811016 | tf_op jit(solution)/shard_map/ppermute | solution.py:127
  50.6 28.2 %collective-permute-start.5 = (bf16[352,768]{1,0:T(8,128)(2,1)}, bf16[352,768]{1,0:T(8,128)(2,1)}, u32[]{:S(2)}, u32[]{:S(2)}) collective-permute-start(bf16[352,768]{1,0:T(8,128)(2,1)} %pad_maximum_fusion), channel_id=1, source_target_pairs={{0,2},{1,3},{2,0},{3,1},{4,6},{5,7},{6,4},{7,5},{8,10},{9,11},{10,... | collective-permute-start | bytes 1622024 | tf_op jit(solution)/shard_map/ppermute | solution.py:127
  55.5 28.6 %collective-permute-start.11 = (bf16[8,12,16,128]{3,2,1,0:T(8,128)(2,1)}, bf16[8,12,16,128]{3,2,1,0:T(8,128)(2,1)}, u32[]{:S(2)}, u32[]{:S(2)}) collective-permute-start(bf16[8,12,16,128]{3,2,1,0:T(8,128)(2,1)} %all-to-all-done.refs_0_), channel_id=1, source_target_pairs={{0,1},{1,0},{2,3},{3,2},{4,5},{5,4},{6,7},{7,6},{8,9},{9,8},{10,11... | collective-permute-start | bytes 1179656 | tf_op jit(solution)/shard_map/ppermute | solution.py:127
  64.3 14.4 %all-to-all-start.1 = ((bf16[8,12,16,128]{3,2,1,0:T(8,128)(2,1)}), bf16[8,12,16,128]{3,2,1,0:T(8,128)(2,1)S(1)}, u32[]{:S(2)}, u32[]{:S(2)}) async-start(bf16[8,12,16,128]{3,2,1,0:T(8,128)(2,1)} %bitcast.32), calls=%async_computation.1 | async-start | bytes 786432 | tf_op jit(solution)/shard_map/all_to_all | solution.py:135
  68.2 20.7 %collective-permute-start.10 = (bf16[176,384]{1,0:T(8,128)(2,1)}, bf16[176,384]{1,0:T(8,128)(2,1)}, u32[]{:S(2)}, u32[]{:S(2)}) collective-permute-start(bf16[176,384]{1,0:T(8,128)(2,1)} %get-tuple-element.114), channel_id=1, source_target_pairs={{0,1},{1,0},{2,3},{3,2},{4,5},{5,4},{6,7},{7,6},{8,9},{9,8},{10,11... | collective-permute-start | bytes 405512 | tf_op jit(solution)/shard_map/ppermute | solution.py:127
  70.0 31.9 %collective-permute-start.9 = (bf16[352,768]{1,0:T(8,128)(2,1)}, bf16[352,768]{1,0:T(8,128)(2,1)}, u32[]{:S(2)}, u32[]{:S(2)}) collective-permute-start(bf16[352,768]{1,0:T(8,128)(2,1)} %pad_maximum_fusion.2), channel_id=1, source_target_pairs={{0,2},{1,3},{2,0},{3,1},{4,6},{5,7},{6,4},{7,5},{8,10},{9,11},{10,... | collective-permute-start | bytes 1622024 | tf_op jit(solution)/shard_map/ppermute | solution.py:127
  89.0 13.0 %all-to-all-start.2 = ((bf16[8,12,16,128]{3,2,1,0:T(8,128)(2,1)}), bf16[8,12,16,128]{3,2,1,0:T(8,128)(2,1)}, u32[]{:S(2)}, u32[]{:S(2)}) async-start(bf16[8,12,16,128]{3,2,1,0:T(8,128)(2,1)} %bitcast.31), calls=%async_computation.2 | async-start | bytes 786432 | tf_op jit(solution)/shard_map/all_to_all | solution.py:135
  93.7 16.6 %collective-permute-start.6 = (bf16[176,384]{1,0:T(8,128)(2,1)}, bf16[176,384]{1,0:T(8,128)(2,1)}, u32[]{:S(2)}, u32[]{:S(2)}) collective-permute-start(bf16[176,384]{1,0:T(8,128)(2,1)} %get-tuple-element.100), channel_id=1, source_target_pairs={{0,1},{1,0},{2,3},{3,2},{4,5},{5,4},{6,7},{7,6},{8,9},{9,8},{10,11... | collective-permute-start | bytes 405512 | tf_op jit(solution)/shard_map/ppermute | solution.py:127
  93.8 28.6 %collective-permute-start.14 = (bf16[8,12,16,128]{3,2,1,0:T(8,128)(2,1)}, bf16[8,12,16,128]{3,2,1,0:T(8,128)(2,1)}, u32[]{:S(2)}, u32[]{:S(2)}) collective-permute-start(bf16[8,12,16,128]{3,2,1,0:T(8,128)(2,1)} %copy-done.2), channel_id=1, source_target_pairs={{0,1},{1,0},{2,3},{3,2},{4,5},{5,4},{6,7},{7,6},{8,9},{9,8},{10,11... | collective-permute-start | bytes 1179656 | tf_op jit(solution)/shard_map/ppermute | solution.py:127
  97.5 22.6 %collective-permute-start.13 = (bf16[352,384]{1,0:T(8,128)(2,1)}, bf16[352,384]{1,0:T(8,128)(2,1)}, u32[]{:S(2)}, u32[]{:S(2)}) collective-permute-start(bf16[352,384]{1,0:T(8,128)(2,1)} %pad_maximum_fusion.4), channel_id=1, source_target_pairs={{0,2},{1,3},{2,0},{3,1},{4,6},{5,7},{6,4},{7,5},{8,10},{9,11},{10,... | collective-permute-start | bytes 811016 | tf_op jit(solution)/shard_map/ppermute | solution.py:127
  110.3 12.1 %all-to-all-start.3 = ((bf16[8,12,16,128]{3,2,1,0:T(8,128)(2,1)}), bf16[8,12,16,128]{3,2,1,0:T(8,128)(2,1)S(1)}, u32[]{:S(2)}, u32[]{:S(2)}) async-start(bf16[8,12,16,128]{3,2,1,0:T(8,128)(2,1)} %bitcast.16), calls=%async_computation.3 | async-start | bytes 786432 | tf_op jit(solution)/shard_map/all_to_all | solution.py:135
  117.2 15.7 %collective-permute-start.12 = (bf16[352,384]{1,0:T(8,128)(2,1)}, bf16[352,384]{1,0:T(8,128)(2,1)}, u32[]{:S(2)}, u32[]{:S(2)}) collective-permute-start(bf16[352,384]{1,0:T(8,128)(2,1)} %pad_maximum_fusion.3), channel_id=1, source_target_pairs={{0,2},{1,3},{2,0},{3,1},{4,6},{5,7},{6,4},{7,5},{8,10},{9,11},{10,... | collective-permute-start | bytes 811016 | tf_op jit(solution)/shard_map/ppermute | solution.py:127
  117.6 19.2 %collective-permute-start.15 = (bf16[8,12,16,128]{3,2,1,0:T(8,128)(2,1)}, bf16[8,12,16,128]{3,2,1,0:T(8,128)(2,1)}, u32[]{:S(2)}, u32[]{:S(2)}) collective-permute-start(bf16[8,12,16,128]{3,2,1,0:T(8,128)(2,1)} %all-to-all-done.2.refs_0_), channel_id=1, source_target_pairs={{0,1},{1,0},{2,3},{3,2},{4,5},{5,4},{6,7},{7,6},{8,9},{9,8},{10,11... | collective-permute-start | bytes 1179656 | tf_op jit(solution)/shard_map/ppermute | solution.py:127
  124.8 12.7 %copy-start.13 = (bf16[176,384]{1,0:T(8,128)(2,1)S(1)}, bf16[176,384]{1,0:T(8,128)(2,1)}, u32[]{:S(2)}) copy-start(bf16[176,384]{1,0:T(8,128)(2,1)} %get-tuple-element.154.refs_0_) | copy-start | bytes 405508
  127.3 9.6 %all-to-all-start.4 = ((bf16[8,12,8,128]{3,2,1,0:T(8,128)(2,1)}), bf16[8,12,8,128]{3,2,1,0:T(8,128)(2,1)S(1)}, u32[]{:S(2)}, u32[]{:S(2)}) async-start(bf16[8,12,8,128]{3,2,1,0:T(8,128)(2,1)} %bitcast.17), calls=%async_computation.4 | async-start | bytes 393216 | tf_op jit(solution)/shard_map/all_to_all | solution.py:135
  130.7 18.9 %collective-permute-start.18 = (bf16[8,12,16,128]{3,2,1,0:T(8,128)(2,1)}, bf16[8,12,16,128]{3,2,1,0:T(8,128)(2,1)}, u32[]{:S(2)}, u32[]{:S(2)}) collective-permute-start(bf16[8,12,16,128]{3,2,1,0:T(8,128)(2,1)} %copy-done), channel_id=1, source_target_pairs={{0,1},{1,0},{2,3},{3,2},{4,5},{5,4},{6,7},{7,6},{8,9},{9,8},{10,11... | collective-permute-start | bytes 1179656 | tf_op jit(solution)/shard_map/ppermute | solution.py:127
  137.5 12.1 %copy-start.1 = (bf16[8,12,16,128]{3,2,1,0:T(8,128)(2,1)S(1)}, bf16[8,12,16,128]{3,2,1,0:T(8,128)(2,1)}, u32[]{:S(2)}) copy-start(bf16[8,12,16,128]{3,2,1,0:T(8,128)(2,1)} %copy-done) | copy-start | bytes 1179652
  140.0 9.6 %all-to-all-start.5 = ((bf16[8,12,8,128]{3,2,1,0:T(8,128)(2,1)}), bf16[8,12,8,128]{3,2,1,0:T(8,128)(2,1)S(1)}, u32[]{:S(2)}, u32[]{:S(2)}) async-start(bf16[8,12,8,128]{3,2,1,0:T(8,128)(2,1)} %bitcast.18), calls=%async_computation.5 | async-start | bytes 393216 | tf_op jit(solution)/shard_map/all_to_all | solution.py:135
  143.4 8.4 %collective-permute-start.16 = (bf16[8,12,8,128]{3,2,1,0:T(8,128)(2,1)S(1)}, bf16[8,12,8,128]{3,2,1,0:T(8,128)(2,1)S(1)}, u32[]{:S(2)}, u32[]{:S(2)}) collective-permute-start(bf16[8,12,8,128]{3,2,1,0:T(8,128)(2,1)S(1)} %copy-done.11), channel_id=1, source_target_pairs={{0,1},{1,0},{2,3},{3,2},{4,5},{5,4},{6,7},{7,6},{8,9},{9,8},{10,11... | collective-permute-start | bytes 589832 | tf_op jit(solution)/shard_map/ppermute | solution.py:127
  149.6 6.3 %collective-permute-start.17 = (bf16[8,12,8,128]{3,2,1,0:T(8,128)(2,1)S(1)}, bf16[8,12,8,128]{3,2,1,0:T(8,128)(2,1)S(1)}, u32[]{:S(2)}, u32[]{:S(2)}) collective-permute-start(bf16[8,12,8,128]{3,2,1,0:T(8,128)(2,1)S(1)} %all-to-all-done.5.refs_1_), channel_id=1, source_target_pairs={{0,1},{1,0},{2,3},{3,2},{4,5},{5,4},{6,7},{7,6},{8,9},{9,8},{10,11... | collective-permute-start | bytes 589832 | tf_op jit(solution)/shard_map/ppermute | solution.py:127
  (16 other events, 55.8 us)

commit v8 on v6

--- a/solution.py
+++ b/solution.py
@@ -126,8 +126,8 @@
     def swap(value, step):
         return lax.ppermute(value, "band", [(band, band ^ step) for band in range(bands)])
 
-    def payloads_of(chunk):
-        start, pairs = plan[chunk]
+    def payloads_of(chunk, pairs):
+        start = plan[chunk][0]
         place, shape = (0, start * fields), (1, rows, pairs * fields)
         return [lax.dynamic_slice(coeffs, (which, *place), shape)[0] for which in (parity, 1 - parity)]
 
@@ -146,17 +146,21 @@
         far[0] = [payload[0]] + [swap(payload[step % 2], step) for step in range(1, bands)]
         near[0] = far[0][1]
 
-    def send_near(chunk):
-        payload = payloads_of(chunk)
-        if chunk >= 2:
-            earlier = far[chunk - 3] if chunk >= 3 else near[chunk - 1]
-            payload, earlier = lax.optimization_barrier((payload, earlier))
-            if chunk >= 3:
-                far[chunk - 3] = earlier
-            else:
-                near[chunk - 1] = earlier
-        own_rows[chunk] = payload[0]
-        near[chunk] = swap(payload[1], 1)
+    def send_near(chunk, after=None):
+        both = range(chunk, min(chunk + 2, len(plan)) if chunk == len(plan) - 2 else chunk + 1)
+        if chunk in near:
+            return after
+        payload = payloads_of(chunk, sum(plan[part][1] for part in both))
+        if chunk == 2:
+            payload, near[1] = lax.optimization_barrier((payload, near[1]))
+        elif chunk > 2:
+            payload, after = lax.optimization_barrier((payload, after))
+        arrived = swap(payload[1], 1)
+        for part in both:
+            offset, pairs = plan[part][0] - plan[chunk][0], plan[part][1]
+            columns = slice(offset * fields, (offset + pairs) * fields)
+            own_rows[part], near[part] = payload[0][:, columns], arrived[:, columns]
+        return after
 
     def send_far(chunk, after=None):
         parts = [own_rows[chunk], near[chunk]]
@@ -165,7 +169,7 @@
         far[chunk] = spread(*parts)
         return after
 
-    first_rows = payloads_of(0)
+    first_rows = payloads_of(0, plan[0][1])
     coeffs, first_rows = lax.optimization_barrier((coeffs, first_rows))
     send_direct(first_rows)
     send_near(1)
@@ -181,8 +185,6 @@
         written += 1
 
     for chunk, (start, pairs) in enumerate(plan):
-        if 3 <= chunk + 3 < len(plan):
-            send_near(chunk + 3)
         if chunk < 1:
             far[chunk], near[chunk + 2] = lax.optimization_barrier((far[chunk], near[chunk + 2]))
         if 0 < chunk < len(plan) - 0:
@@ -193,7 +195,7 @@
         if chunk in MIRRORED:
             back = MIRRORED[chunk]
             far[chunk], sums[back] = lax.optimization_barrier((far[chunk], sums[back]))
-        if chunk == GROUPS[0][-1] + 3:
+        if chunk == GROUPS[0][-1] + 4:
             write()
             far[chunk], out = lax.optimization_barrier((far[chunk], out))
         blocks = far[chunk]
@@ -203,6 +205,8 @@
         own = parity_sums(
             blocks, rows if rows % 16 == 0 else depth, order, first, total, legendre, start, pairs, fields
         )
+        if chunk + 3 < len(plan):
+            own = send_near(chunk + 3, own)
         if chunk + 2 < len(plan):
             own = send_far(chunk + 2, own)
         piece = redistribute(own)

time: 159 us -> 166 us (1.044)
  waiting for transfers between devices: 65.7 us -> 70.7 us
  local copies, waits for them, and re-layouts: 17.9 us -> 21.2 us
    ppermute x19 -> x18, waiting for transfers between devices: 50.6 us -> 57.8 us  [swap(): lax.ppermute(value, 'band', [(band, band ^ step) for band in range(bands)])]
    slice x0 -> x2, local copies, waits for them, and re-layouts: none -> 2.48 us  [send_near(): own_rows[part], near[part] = (payload[0][:, columns], arrived[:, columns])]
    unnamed x46 -> x58, local copies, waits for them, and re-layouts: 6.84 us -> 9.2 us
    all_to_all x6, waiting for transfers between devices: 15.1 us -> 12.9 us  [redistribute(): lax.all_to_all(grid.reshape(sets, fields // sets, -1, lats), 'mset', 0, 0)]
    squeeze x3 -> x2, local copies, waits for them, and re-layouts: 5.31 us -> 3.74 us  [payloads_of(): lax.dynamic_slice(coeffs, (which, *place), shape)[0]]
    ppermute x19 -> x18, starting transfers between devices: 21.5 us -> 20.9 us  [swap(): lax.ppermute(value, 'band', [(band, band ^ step) for band in range(bands)])]
  transfers between devices with their start and end apart: 25 -> 24, of which waited for: 11 -> 11; matrix products, arithmetic and copies ran while one was open for 11% -> 11% of each run, Pallas kernels for 13% -> 12%
where the time goes in v8:
time: 166 us; the launch traced here: 165 us
  waiting for transfers between devices  70.7 us (43%)
  starting transfers between devices  44.4 us (27%)
  local copies, waits for them, and re-layouts  21.2 us (13%)
  Pallas kernels  20.4 us (12%)
  other arithmetic  6.91 us (4%)
    ppermute x18, waiting for transfers between devices, swap(): lax.ppermute(value, 'band', [(band, band ^ step) for band in range(bands)])  57.8 us
    all_to_all x6, starting transfers between devices, redistribute(): lax.all_to_all(grid.reshape(sets, fields // sets, -1, lats), 'mset', 0, 0)  23.5 us
    ppermute x18, starting transfers between devices, swap(): lax.ppermute(value, 'band', [(band, band ^ step) for band in range(bands)])  20.9 us
    pallas_call x6, Pallas kernels, parity_sums(): pl.pallas_call(functools.partial(sums_kernel, rows, fields, start), in_sp...  15 us
    all_to_all x6, waiting for transfers between devices, redistribute(): lax.all_to_all(grid.reshape(sets, fields // sets, -1, lats), 'mset', 0, 0)  12.9 us
    unnamed x58, local copies, waits for them, and re-layouts  9.2 us
    concatenate x5, other arithmetic, spread(): held.append(swap(jnp.concatenate(held), bit))  6.89 us
    slice x2, local copies, waits for them, and re-layouts, parity_sums(): legendre = legendre[start:start + pairs]  5.79 us
  transfers between devices with their start and end apart: 24, of which 11 were waited for; matrix products, arithmetic and copies ran while one was open for 11% of the time, Pallas kernels for 12%

profile of v8, /device:TPU:0, one launch (start us, length us, event | category | flops | bytes accessed | tf_op | source)
XLA Modules:
  0.0 164.6 jit_solution(7823136663653898228)
XLA Ops:
  1.1 3.1 %collective-permute-start.2 = (bf16[176,768]{1,0:T(8,128)(2,1)S(1)}, bf16[176,768]{1,0:T(8,128)(2,1)S(1)}, u32[]{:S(2)}, u32[]{:S(2)}) collective-permute-start(bf16[176,768]{1,0:T(8,128)(2,1)S(1)} %get-tuple-element.77), channel_id=1, source_target_pairs={{0,1},{1,0},{2,3},{3,2},{4,5},{5,4},{6,7},{7,6},{8,9},{9,8},{10,11... | collective-permute-start | bytes 811016 | tf_op jit(solution)/shard_map/ppermute | solution.py:127
  4.2 2.5 %collective-permute-start.4 = (bf16[176,768]{1,0:T(8,128)(2,1)S(1)}, bf16[176,768]{1,0:T(8,128)(2,1)S(1)}, u32[]{:S(2)}, u32[]{:S(2)}) collective-permute-start(bf16[176,768]{1,0:T(8,128)(2,1)S(1)} %get-tuple-element.77), channel_id=1, source_target_pairs={{0,3},{1,2},{2,1},{3,0},{4,7},{5,6},{6,5},{7,4},{8,11},{9,10},{10,... | collective-permute-start | bytes 811016 | tf_op jit(solution)/shard_map/ppermute | solution.py:127
  6.6 2.7 %dynamic-slice_bitcast_fusion = (bf16[176,768]{1,0:T(8,128)(2,1)}, bf16[176,768]{1,0:T(8,128)(2,1)}, bf16[176,768]{1,0:T(8,128)(2,1)S(1)}, bf16[176,768]{1,0:T(8...) fusion(bf16[2,176,3840]{2,1,0:T(8,128)(2,1)} %param.4, ...), kind=kLoop, calls=%fused_computation.5 | loop fusion | bytes 4325384 | tf_op jit(solution)/shard_map/squeeze | solution.py:132
  11.3 4.3 %fusion.1 = (bf16[8,704,128]{2,1,0:T(8,128)(2,1)S(1)}, bf16[8,704,128]{2,1,0:T(8,128)(2,1)S(1)}, bf16[8,704,128]{2,1,0:T(8,128)(2,1)}, bf16[8,704,128]{2,1,0:T(8,128)(2,1)S(1)}) fusion(bf16[40,704,128]{2,1,0:T(8,128)(2,1)} %param.5), kind=kLoop, calls=%fused_computation.27 | loop fusion | bytes 11534336 | tf_op jit(solution)/shard_map/slice | solution.py:52
  15.6 13.0 %collective-permute-done.refs_1_ = bf16[176,768]{1,0:T(8,128)(2,1)S(1)} collective-permute-done((bf16[176,768]{1,0:T(8,128)(2,1)S(1)}, bf16[176,768]{1,0:T(8,128)(2,1)S(1)}, u32[]{:S(2)}, u32[]{:S(2)}) %collective-permute-start) | collective-permute-done | bytes 270368 | tf_op jit(solution)/shard_map/ppermute | solution.py:127
  29.5 2.5 %collective-permute-start.1 = (bf16[352,768]{1,0:T(8,128)(2,1)}, bf16[352,768]{1,0:T(8,128)(2,1)}, u32[]{:S(2)}, u32[]{:S(2)}) collective-permute-start(bf16[352,768]{1,0:T(8,128)(2,1)} %pad_maximum_fusion), channel_id=1, source_target_pairs={{0,2},{1,3},{2,0},{3,1},{4,6},{5,7},{6,4},{7,5},{8,10},{9,11},{10,... | collective-permute-start | bytes 1622024 | tf_op jit(solution)/shard_map/ppermute | solution.py:127
  32.0 8.0 %collective-permute-done.5.refs_1_ = bf16[176,768]{1,0:T(8,128)(2,1)S(1)} collective-permute-done((bf16[176,768]{1,0:T(8,128)(2,1)S(1)}, bf16[176,768]{1,0:T(8,128)(2,1)S(1)}, u32[]{:S(2)}, u32[]{:S(2)}) %collective-permute-start.5) | collective-permute-done | bytes 270368 | tf_op jit(solution)/shard_map/ppermute | solution.py:127
  40.7 1.9 %parity_sums.6 = bf16[96,16,128]{2,1,0:T(8,128)(2,1)S(1)} custom-call(s32[4]{0:T(128)S(1)} %iota_xor_fusion.order, s32[40]{0:T(128)S(1)} %get-tuple-element.142.first, s32[40]{0:T(128)S(1)} %get-tuple-element.141.total, bf16[176,768]{1,0:T(8,128)(2,1)S(1)} %get-tuple-element.80.refs_0_, bf16[176,768]{1,0:T(8,128)(2,1)S(1)} %collective-permute-done.2.refs_1_, ...), custom_call_target="tpu_custom_call" | custom-call | flops 799999983616 | bytes 838860800 | tf_op jit(solution)/shard_map/parity_sums/pallas_call | solution.py:55
  43.4 4.2 %all-to-all-start = ((bf16[8,12,16,128]{3,2,1,0:T(8,128)(2,1)}), bf16[8,12,16,128]{3,2,1,0:T(8,128)(2,1)}, u32[]{:S(2)}, u32[]{:S(2)}) async-start(bf16[8,12,16,128]{3,2,1,0:T(8,128)(2,1)} %bitcast.28), calls=%async_computation | async-start | bytes 786432 | tf_op jit(solution)/shard_map/all_to_all | solution.py:135
  50.3 2.5 %collective-permute-start.7 = (bf16[176,768]{1,0:T(8,128)(2,1)}, bf16[176,768]{1,0:T(8,128)(2,1)}, u32[]{:S(2)}, u32[]{:S(2)}) collective-permute-start(bf16[176,768]{1,0:T(8,128)(2,1)} %get-tuple-element.92), channel_id=1, source_target_pairs={{0,1},{1,0},{2,3},{3,2},{4,5},{5,4},{6,7},{7,6},{8,9},{9,8},{10,11... | collective-permute-start | bytes 811016 | tf_op jit(solution)/shard_map/ppermute | solution.py:127
  52.8 16.2 %collective-permute-done.1.refs_2_ = bf16[352,768]{1,0:T(8,128)(2,1)} collective-permute-done((bf16[352,768]{1,0:T(8,128)(2,1)}, bf16[352,768]{1,0:T(8,128)(2,1)}, u32[]{:S(2)}, u32[]{:S(2)}) %collective-permute-start.1) | collective-permute-done | bytes 540704 | tf_op jit(solution)/shard_map/ppermute | solution.py:127
  71.4 2.4 %parity_sums.7 = bf16[96,16,128]{2,1,0:T(8,128)(2,1)S(1)} custom-call(s32[4]{0:T(128)S(1)} %iota_xor_fusion.order, s32[40]{0:T(128)S(1)} %get-tuple-element.142.first, s32[40]{0:T(128)S(1)} %get-tuple-element.141.total, bf16[176,768]{1,0:T(8,128)(2,1)S(1)} %copy-done.9, bf16[176,768]{1,0:T(8,128)(2,1)S(1)} %copy-done.24, ...), custom_call_target="tpu_custom_call" | custom-call | flops 799999983616 | bytes 838860800 | tf_op jit(solution)/shard_map/parity_sums/pallas_call | solution.py:55
  74.6 3.7 %all-to-all-start.1 = ((bf16[8,12,16,128]{3,2,1,0:T(8,128)(2,1)}), bf16[8,12,16,128]{3,2,1,0:T(8,128)(2,1)S(1)}, u32[]{:S(2)}, u32[]{:S(2)}) async-start(bf16[8,12,16,128]{3,2,1,0:T(8,128)(2,1)} %bitcast.27), calls=%async_computation.1 | async-start | bytes 786432 | tf_op jit(solution)/shard_map/all_to_all | solution.py:135
  81.8 2.3 %collective-permute-start.8 = (bf16[352,768]{1,0:T(8,128)(2,1)}, bf16[352,768]{1,0:T(8,128)(2,1)}, u32[]{:S(2)}, u32[]{:S(2)}) collective-permute-start(bf16[352,768]{1,0:T(8,128)(2,1)} %pad_maximum_fusion.1), channel_id=1, source_target_pairs={{0,2},{1,3},{2,0},{3,1},{4,6},{5,7},{6,4},{7,5},{8,10},{9,11},{10,... | collective-permute-start | bytes 1622024 | tf_op jit(solution)/shard_map/ppermute | solution.py:127
  84.2 5.1 %collective-permute-done.6 = bf16[176,768]{1,0:T(8,128)(2,1)S(1)} collective-permute-done((bf16[176,768]{1,0:T(8,128)(2,1)}, bf16[176,768]{1,0:T(8,128)(2,1)S(1)}, u32[]{:S(2)}, u32[]{:S(2)}) %collective-permute-start.6) | collective-permute-done | bytes 270368 | tf_op jit(solution)/shard_map/ppermute | solution.py:127
  92.8 2.4 %parity_sums.8 = bf16[96,16,128]{2,1,0:T(8,128)(2,1)S(1)} custom-call(s32[4]{0:T(128)S(1)} %copy-done.26, s32[40]{0:T(128)S(1)} %get-tuple-element.142.first, s32[40]{0:T(128)S(1)} %get-tuple-element.141.total, bf16[176,768]{1,0:T(8,128)(2,1)S(1)} %copy-done.7, bf16[176,768]{1,0:T(8,128)(2,1)S(1)} %copy-done.22, ...), custom_call_target="tpu_custom_call" | custom-call | flops 799999983616 | bytes 838860800 | tf_op jit(solution)/shard_map/parity_sums/pallas_call | solution.py:55
  96.0 4.2 %all-to-all-start.2 = ((bf16[8,12,16,128]{3,2,1,0:T(8,128)(2,1)}), bf16[8,12,16,128]{3,2,1,0:T(8,128)(2,1)}, u32[]{:S(2)}, u32[]{:S(2)}) async-start(bf16[8,12,16,128]{3,2,1,0:T(8,128)(2,1)} %bitcast.29), calls=%async_computation.2 | async-start | bytes 786432 | tf_op jit(solution)/shard_map/all_to_all | solution.py:135
  102.1 2.4 %collective-permute-start.13 = (bf16[8,12,16,128]{3,2,1,0:T(8,128)(2,1)}, bf16[8,12,16,128]{3,2,1,0:T(8,128)(2,1)}, u32[]{:S(2)}, u32[]{:S(2)}) collective-permute-start(bf16[8,12,16,128]{3,2,1,0:T(8,128)(2,1)} %copy-done.2), channel_id=1, source_target_pairs={{0,1},{1,0},{2,3},{3,2},{4,5},{5,4},{6,7},{7,6},{8,9},{9,8},{10,11... | collective-permute-start | bytes 1179656 | tf_op jit(solution)/shard_map/ppermute | solution.py:127
  104.5 11.1 %collective-permute-done.8.refs_2_ = bf16[352,768]{1,0:T(8,128)(2,1)} collective-permute-done((bf16[352,768]{1,0:T(8,128)(2,1)}, bf16[352,768]{1,0:T(8,128)(2,1)}, u32[]{:S(2)}, u32[]{:S(2)}) %collective-permute-start.8) | collective-permute-done | bytes 540704 | tf_op jit(solution)/shard_map/ppermute | solution.py:127
  116.3 3.3 %parity_sums.9 = bf16[96,16,128]{2,1,0:T(8,128)(2,1)} custom-call(s32[4]{0:T(128)S(1)} %copy-done.27, s32[40]{0:T(128)S(1)} %get-tuple-element.142.first, s32[40]{0:T(128)S(1)} %get-tuple-element.141.total, bf16[176,768]{1,0:T(8,128)(2,1)S(1)} %copy-done.5, bf16[176,768]{1,0:T(8,128)(2,1)} %collective-permute-done.7.refs_1_, ...), custom_call_target="tpu_custom_call" | custom-call | flops 799999983616 | bytes 838860800 | tf_op jit(solution)/shard_map/parity_sums/pallas_call | solution.py:55
  119.6 4.2 %all-to-all-start.3 = ((bf16[8,12,16,128]{3,2,1,0:T(8,128)(2,1)}), bf16[8,12,16,128]{3,2,1,0:T(8,128)(2,1)S(1)}, u32[]{:S(2)}, u32[]{:S(2)}) async-start(bf16[8,12,16,128]{3,2,1,0:T(8,128)(2,1)} %bitcast.14), calls=%async_computation.3 | async-start | bytes 786432 | tf_op jit(solution)/shard_map/all_to_all | solution.py:135
  126.1 2.4 %collective-permute-start.14 = (bf16[8,12,16,128]{3,2,1,0:T(8,128)(2,1)}, bf16[8,12,16,128]{3,2,1,0:T(8,128)(2,1)}, u32[]{:S(2)}, u32[]{:S(2)}) collective-permute-start(bf16[8,12,16,128]{3,2,1,0:T(8,128)(2,1)} %all-to-all-done.2.refs_0_), channel_id=1, source_target_pairs={{0,1},{1,0},{2,3},{3,2},{4,5},{5,4},{6,7},{7,6},{8,9},{9,8},{10,11... | collective-permute-start | bytes 1179656 | tf_op jit(solution)/shard_map/ppermute | solution.py:127
  128.5 3.7 %all-to-all-done.3.refs_1_ = bf16[8,12,16,128]{3,2,1,0:T(8,128)(2,1)S(1)} async-done(((bf16[8,12,16,128]{3,2,1,0:T(8,128)(2,1)}), bf16[8,12,16,128]{3,2,1,0:T(8,128)(2,1)S(1)}, u32[]{:S(2)}, u32[]{:S(2)}) %all-to-all-start.3) | async-done | bytes 393248 | tf_op jit(solution)/shard_map/all_to_all | solution.py:135
  132.2 2.5 %parity_sums.10 = bf16[96,8,128]{2,1,0:T(8,128)(2,1)} custom-call(s32[4]{0:T(128)S(1)} %copy-done.27, s32[40]{0:T(128)S(1)} %get-tuple-element.142.first, s32[40]{0:T(128)S(1)} %get-tuple-element.141.total, bf16[176,384]{1,0:T(8,128)(2,1)S(1)} %copy-done.16, bf16[176,384]{1,0:T(8,128)(2,1)S(1)} %copy-done.17, ...), custom_call_target="tpu_custom_call" | custom-call | flops 399999991808 | bytes 419430400 | tf_op jit(solution)/shard_map/parity_sums/pallas_call | solution.py:55
  134.7 3.4 %all-to-all-start.4 = ((bf16[8,12,8,128]{3,2,1,0:T(8,128)(2,1)}), bf16[8,12,8,128]{3,2,1,0:T(8,128)(2,1)S(1)}, u32[]{:S(2)}, u32[]{:S(2)}) async-start(bf16[8,12,8,128]{3,2,1,0:T(8,128)(2,1)} %bitcast.15), calls=%async_computation.4 | async-start | bytes 393216 | tf_op jit(solution)/shard_map/all_to_all | solution.py:135
  138.9 2.3 %finish.3.refs_4_ = bf16[12,640,128]{2,1,0:T(8,128)(2,1)} custom-call(s32[1]{0:T(128)} %bitcast.parity, s32[1]{0:T(128)S(6)} %copy.9.lat_count, bf16[8,12,16,128]{3,2,1,0:T(8,128)(2,1)} %all-to-all-done.refs_0_, bf16[8,12,16,128]{3,2,1,0:T(8,128)(2,1)S(1)} %copy-done.3, bf16[8,12,16,128]{3,2,1,0:T(8,128)(2,1)} %collective-permute-done.10.refs_2_, ...), custom_call_target="tpu_custom_call" | custom-call | tf_op jit(solution)/shard_map/finish/pallas_call | solution.py:99
  141.3 3.0 %all-to-all-done.4.refs_0_ = bf16[8,12,8,128]{3,2,1,0:T(8,128)(2,1)S(1)} async-done(((bf16[8,12,8,128]{3,2,1,0:T(8,128)(2,1)}), bf16[8,12,8,128]{3,2,1,0:T(8,128)(2,1)S(1)}, u32[]{:S(2)}, u32[]{:S(2)}) %all-to-all-start.4) | async-done | bytes 196640 | tf_op jit(solution)/shard_map/all_to_all | solution.py:135
  145.0 2.5 %parity_sums.11 = bf16[96,8,128]{2,1,0:T(8,128)(2,1)} custom-call(s32[4]{0:T(128)S(1)} %copy-done.27, s32[40]{0:T(128)S(1)} %get-tuple-element.142.first, s32[40]{0:T(128)S(1)} %get-tuple-element.141.total, bf16[176,384]{1,0:T(8,128)(2,1)S(1)} %copy-done.13, bf16[176,384]{1,0:T(8,128)(2,1)S(1)} %copy-done.15, ...), custom_call_target="tpu_custom_call" | custom-call | flops 399999991808 | bytes 419430400 | tf_op jit(solution)/shard_map/parity_sums/pallas_call | solution.py:55
  147.4 3.7 %all-to-all-start.5 = ((bf16[8,12,8,128]{3,2,1,0:T(8,128)(2,1)}), bf16[8,12,8,128]{3,2,1,0:T(8,128)(2,1)S(1)}, u32[]{:S(2)}, u32[]{:S(2)}) async-start(bf16[8,12,8,128]{3,2,1,0:T(8,128)(2,1)} %bitcast.16), calls=%async_computation.5 | async-start | bytes 393216 | tf_op jit(solution)/shard_map/all_to_all | solution.py:135
  151.2 6.1 %all-to-all-done.5.refs_1_ = bf16[8,12,8,128]{3,2,1,0:T(8,128)(2,1)S(1)} async-done(((bf16[8,12,8,128]{3,2,1,0:T(8,128)(2,1)}), bf16[8,12,8,128]{3,2,1,0:T(8,128)(2,1)S(1)}, u32[]{:S(2)}, u32[]{:S(2)}) %all-to-all-start.5) | async-done | bytes 196640 | tf_op jit(solution)/shard_map/all_to_all | solution.py:135
  157.4 2.2 %finish.4.refs_4_ = bf16[12,640,128]{2,1,0:T(8,128)(2,1)} custom-call(s32[1]{0:T(128)} %bitcast.parity, s32[1]{0:T(128)S(6)} %copy.9.lat_count, bf16[8,12,16,128]{3,2,1,0:T(8,128)(2,1)} %all-to-all-done.2.refs_0_, bf16[8,12,16,128]{3,2,1,0:T(8,128)(2,1)S(1)} %copy-done.1, ...), custom_call_target="tpu_custom_call", output_to_operand_aliasing={{}: (6, {})} | custom-call | tf_op jit(solution)/shard_map/finish/pallas_call | solution.py:99
  159.7 4.1 %collective-permute-done.16.refs_3_ = bf16[8,12,8,128]{3,2,1,0:T(8,128)(2,1)S(1)} collective-permute-done((bf16[8,12,8,128]{3,2,1,0:T(8,128)(2,1)S(1)}, bf16[8,12,8,128]{3,2,1,0:T(8,128)(2,1)S(1)}, u32[]{:S(2)}, u32[]{:S(2)}) %collective-permute-start.16) | collective-permute-done | bytes 196640 | tf_op jit(solution)/shard_map/ppermute | solution.py:127
  (96 shorter events, 25.6 us)
Async XLA Ops:
  1.1 30.9 %collective-permute-start.2 = (bf16[176,768]{1,0:T(8,128)(2,1)S(1)}, bf16[176,768]{1,0:T(8,128)(2,1)S(1)}, u32[]{:S(2)}, u32[]{:S(2)}) collective-permute-start(bf16[176,768]{1,0:T(8,128)(2,1)S(1)} %get-tuple-element.77), channel_id=1, source_target_pairs={{0,1},{1,0},{2,3},{3,2},{4,5},{5,4},{6,7},{7,6},{8,9},{9,8},{10,11... | collective-permute-start | bytes 811016 | tf_op jit(solution)/shard_map/ppermute | solution.py:127
  4.2 27.8 %collective-permute-start.4 = (bf16[176,768]{1,0:T(8,128)(2,1)S(1)}, bf16[176,768]{1,0:T(8,128)(2,1)S(1)}, u32[]{:S(2)}, u32[]{:S(2)}) collective-permute-start(bf16[176,768]{1,0:T(8,128)(2,1)S(1)} %get-tuple-element.77), channel_id=1, source_target_pairs={{0,3},{1,2},{2,1},{3,0},{4,7},{5,6},{6,5},{7,4},{8,11},{9,10},{10,... | collective-permute-start | bytes 811016 | tf_op jit(solution)/shard_map/ppermute | solution.py:127
  9.3 19.4 %copy-start.8 = (bf16[176,768]{1,0:T(8,128)(2,1)}, bf16[176,768]{1,0:T(8,128)(2,1)S(1)}, u32[]{:S(2)}) copy-start(bf16[176,768]{1,0:T(8,128)(2,1)S(1)} %get-tuple-element.86.refs_0_) | copy-start | bytes 811012
  9.3 19.3 %copy-start.28 = (s32[40]{0:T(128)S(1)}, s32[40]{0:T(128)}, u32[]{:S(2)}) copy-start(s32[40]{0:T(128)} %param.6) | copy-start | bytes 484
  9.3 19.3 %collective-permute-start = (bf16[176,768]{1,0:T(8,128)(2,1)S(1)}, bf16[176,768]{1,0:T(8,128)(2,1)S(1)}, u32[]{:S(2)}, u32[]{:S(2)}) collective-permute-start(bf16[176,768]{1,0:T(8,128)(2,1)S(1)} %get-tuple-element.151), channel_id=1, source_target_pairs={{0,1},{1,0},{2,3},{3,2},{4,5},{5,4},{6,7},{7,6},{8,9},{9,8},{10,11... | collective-permute-start | bytes 811016 | tf_op jit(solution)/shard_map/ppermute | solution.py:127
  10.0 21.9 %collective-permute-start.3 = (bf16[176,768]{1,0:T(8,128)(2,1)S(1)}, bf16[176,768]{1,0:T(8,128)(2,1)S(1)}, u32[]{:S(2)}, u32[]{:S(2)}) collective-permute-start(bf16[176,768]{1,0:T(8,128)(2,1)S(1)} %get-tuple-element.80.refs_0_), channel_id=1, source_target_pairs={{0,2},{1,3},{2,0},{3,1},{4,6},{5,7},{6,4},{7,5},{8,10},{9,11},{10,... | collective-permute-start | bytes 811016 | tf_op jit(solution)/shard_map/ppermute | solution.py:127
  28.6 14.0 %copy-start.23 = (bf16[176,768]{1,0:T(8,128)(2,1)}, bf16[176,768]{1,0:T(8,128)(2,1)S(1)}, u32[]{:S(2)}) copy-start(bf16[176,768]{1,0:T(8,128)(2,1)S(1)} %collective-permute-done.refs_1_) | copy-start | bytes 811012
  28.6 11.3 %collective-permute-start.5 = (bf16[176,768]{1,0:T(8,128)(2,1)S(1)}, bf16[176,768]{1,0:T(8,128)(2,1)S(1)}, u32[]{:S(2)}, u32[]{:S(2)}) collective-permute-start(bf16[176,768]{1,0:T(8,128)(2,1)S(1)} %get-tuple-element.78), channel_id=1, source_target_pairs={{0,1},{1,0},{2,3},{3,2},{4,5},{5,4},{6,7},{7,6},{8,9},{9,8},{10,11... | collective-permute-start | bytes 811016 | tf_op jit(solution)/shard_map/ppermute | solution.py:127
  28.7 40.4 %copy-start.25 = (s32[4]{0:T(128)}, s32[4]{0:T(128)S(1)}, u32[]{:S(2)}) copy-start(s32[4]{0:T(128)S(1)} %iota_xor_fusion.order) | copy-start | bytes 52
  29.5 39.5 %collective-permute-start.1 = (bf16[352,768]{1,0:T(8,128)(2,1)}, bf16[352,768]{1,0:T(8,128)(2,1)}, u32[]{:S(2)}, u32[]{:S(2)}) collective-permute-start(bf16[352,768]{1,0:T(8,128)(2,1)} %pad_maximum_fusion), channel_id=1, source_target_pairs={{0,2},{1,3},{2,0},{3,1},{4,6},{5,7},{6,4},{7,5},{8,10},{9,11},{10,... | collective-permute-start | bytes 1622024 | tf_op jit(solution)/shard_map/ppermute | solution.py:127
  43.4 25.7 %copy-start.9 = (bf16[176,768]{1,0:T(8,128)(2,1)S(1)}, bf16[176,768]{1,0:T(8,128)(2,1)}, u32[]{:S(2)}) copy-start(bf16[176,768]{1,0:T(8,128)(2,1)} %copy-done.8) | copy-start | bytes 811012
  43.4 25.7 %all-to-all-start = ((bf16[8,12,16,128]{3,2,1,0:T(8,128)(2,1)}), bf16[8,12,16,128]{3,2,1,0:T(8,128)(2,1)}, u32[]{:S(2)}, u32[]{:S(2)}) async-start(bf16[8,12,16,128]{3,2,1,0:T(8,128)(2,1)} %bitcast.28), calls=%async_computation | async-start | bytes 786432 | tf_op jit(solution)/shard_map/all_to_all | solution.py:135
  49.4 40.6 %collective-permute-start.9 = (bf16[352,768]{1,0:T(8,128)(2,1)}, bf16[352,768]{1,0:T(8,128)(2,1)}, u32[]{:S(2)}, u32[]{:S(2)}) collective-permute-start(bf16[352,768]{1,0:T(8,128)(2,1)} %pad_maximum_fusion.2), channel_id=1, source_target_pairs={{0,2},{1,3},{2,0},{3,1},{4,6},{5,7},{6,4},{7,5},{8,10},{9,11},{10,... | collective-permute-start | bytes 1622024 | tf_op jit(solution)/shard_map/ppermute | solution.py:127
  50.3 24.2 %collective-permute-start.7 = (bf16[176,768]{1,0:T(8,128)(2,1)}, bf16[176,768]{1,0:T(8,128)(2,1)}, u32[]{:S(2)}, u32[]{:S(2)}) collective-permute-start(bf16[176,768]{1,0:T(8,128)(2,1)} %get-tuple-element.92), channel_id=1, source_target_pairs={{0,1},{1,0},{2,3},{3,2},{4,5},{5,4},{6,7},{7,6},{8,9},{9,8},{10,11... | collective-permute-start | bytes 811016 | tf_op jit(solution)/shard_map/ppermute | solution.py:127
  74.6 15.5 %all-to-all-start.1 = ((bf16[8,12,16,128]{3,2,1,0:T(8,128)(2,1)}), bf16[8,12,16,128]{3,2,1,0:T(8,128)(2,1)S(1)}, u32[]{:S(2)}, u32[]{:S(2)}) async-start(bf16[8,12,16,128]{3,2,1,0:T(8,128)(2,1)} %bitcast.27), calls=%async_computation.1 | async-start | bytes 786432 | tf_op jit(solution)/shard_map/all_to_all | solution.py:135
  78.3 11.0 %collective-permute-start.6 = (bf16[176,768]{1,0:T(8,128)(2,1)}, bf16[176,768]{1,0:T(8,128)(2,1)S(1)}, u32[]{:S(2)}, u32[]{:S(2)}) collective-permute-start(bf16[176,768]{1,0:T(8,128)(2,1)} %get-tuple-element.90), channel_id=1, source_target_pairs={{0,1},{1,0},{2,3},{3,2},{4,5},{5,4},{6,7},{7,6},{8,9},{9,8},{10,11... | collective-permute-start | bytes 811016 | tf_op jit(solution)/shard_map/ppermute | solution.py:127
  81.8 33.8 %collective-permute-start.8 = (bf16[352,768]{1,0:T(8,128)(2,1)}, bf16[352,768]{1,0:T(8,128)(2,1)}, u32[]{:S(2)}, u32[]{:S(2)}) collective-permute-start(bf16[352,768]{1,0:T(8,128)(2,1)} %pad_maximum_fusion.1), channel_id=1, source_target_pairs={{0,2},{1,3},{2,0},{3,1},{4,6},{5,7},{6,4},{7,5},{8,10},{9,11},{10,... | collective-permute-start | bytes 1622024 | tf_op jit(solution)/shard_map/ppermute | solution.py:127
  84.2 31.5 %collective-permute-start.10 = (bf16[8,12,16,128]{3,2,1,0:T(8,128)(2,1)}, bf16[8,12,16,128]{3,2,1,0:T(8,128)(2,1)}, u32[]{:S(2)}, u32[]{:S(2)}) collective-permute-start(bf16[8,12,16,128]{3,2,1,0:T(8,128)(2,1)} %all-to-all-done.refs_0_), channel_id=1, source_target_pairs={{0,1},{1,0},{2,3},{3,2},{4,5},{5,4},{6,7},{7,6},{8,9},{9,8},{10,11... | collective-permute-start | bytes 1179656 | tf_op jit(solution)/shard_map/ppermute | solution.py:127
  96.0 19.7 %all-to-all-start.2 = ((bf16[8,12,16,128]{3,2,1,0:T(8,128)(2,1)}), bf16[8,12,16,128]{3,2,1,0:T(8,128)(2,1)}, u32[]{:S(2)}, u32[]{:S(2)}) async-start(bf16[8,12,16,128]{3,2,1,0:T(8,128)(2,1)} %bitcast.29), calls=%async_computation.2 | async-start | bytes 786432 | tf_op jit(solution)/shard_map/all_to_all | solution.py:135
  101.9 26.5 %collective-permute-start.12 = (bf16[352,384]{1,0:T(8,128)(2,1)}, bf16[352,384]{1,0:T(8,128)(2,1)}, u32[]{:S(2)}, u32[]{:S(2)}) collective-permute-start(bf16[352,384]{1,0:T(8,128)(2,1)} %pad_maximum_fusion.4), channel_id=1, source_target_pairs={{0,2},{1,3},{2,0},{3,1},{4,6},{5,7},{6,4},{7,5},{8,10},{9,11},{10,... | collective-permute-start | bytes 811016 | tf_op jit(solution)/shard_map/ppermute | solution.py:127
  102.1 30.0 %collective-permute-start.13 = (bf16[8,12,16,128]{3,2,1,0:T(8,128)(2,1)}, bf16[8,12,16,128]{3,2,1,0:T(8,128)(2,1)}, u32[]{:S(2)}, u32[]{:S(2)}) collective-permute-start(bf16[8,12,16,128]{3,2,1,0:T(8,128)(2,1)} %copy-done.2), channel_id=1, source_target_pairs={{0,1},{1,0},{2,3},{3,2},{4,5},{5,4},{6,7},{7,6},{8,9},{9,8},{10,11... | collective-permute-start | bytes 1179656 | tf_op jit(solution)/shard_map/ppermute | solution.py:127
  119.6 12.6 %all-to-all-start.3 = ((bf16[8,12,16,128]{3,2,1,0:T(8,128)(2,1)}), bf16[8,12,16,128]{3,2,1,0:T(8,128)(2,1)S(1)}, u32[]{:S(2)}, u32[]{:S(2)}) async-start(bf16[8,12,16,128]{3,2,1,0:T(8,128)(2,1)} %bitcast.14), calls=%async_computation.3 | async-start | bytes 786432 | tf_op jit(solution)/shard_map/all_to_all | solution.py:135
  123.8 8.3 %copy-start.16 = (bf16[176,384]{1,0:T(8,128)(2,1)S(1)}, bf16[176,384]{1,0:T(8,128)(2,1)}, u32[]{:S(2)}) copy-start(bf16[176,384]{1,0:T(8,128)(2,1)} %get-tuple-element.119.refs_0_) | copy-start | bytes 405508
  123.8 8.3 %copy-start.17 = (bf16[176,384]{1,0:T(8,128)(2,1)S(1)}, bf16[176,384]{1,0:T(8,128)(2,1)}, u32[]{:S(2)}) copy-start(bf16[176,384]{1,0:T(8,128)(2,1)} %get-tuple-element.120.refs_1_) | copy-start | bytes 405508
  126.1 15.2 %collective-permute-start.11 = (bf16[352,384]{1,0:T(8,128)(2,1)}, bf16[352,384]{1,0:T(8,128)(2,1)}, u32[]{:S(2)}, u32[]{:S(2)}) collective-permute-start(bf16[352,384]{1,0:T(8,128)(2,1)} %pad_maximum_fusion.3), channel_id=1, source_target_pairs={{0,2},{1,3},{2,0},{3,1},{4,6},{5,7},{6,4},{7,5},{8,10},{9,11},{10,... | collective-permute-start | bytes 811016 | tf_op jit(solution)/shard_map/ppermute | solution.py:127
  126.1 18.4 %collective-permute-start.14 = (bf16[8,12,16,128]{3,2,1,0:T(8,128)(2,1)}, bf16[8,12,16,128]{3,2,1,0:T(8,128)(2,1)}, u32[]{:S(2)}, u32[]{:S(2)}) collective-permute-start(bf16[8,12,16,128]{3,2,1,0:T(8,128)(2,1)} %all-to-all-done.2.refs_0_), channel_id=1, source_target_pairs={{0,1},{1,0},{2,3},{3,2},{4,5},{5,4},{6,7},{7,6},{8,9},{9,8},{10,11... | collective-permute-start | bytes 1179656 | tf_op jit(solution)/shard_map/ppermute | solution.py:127
  134.7 9.6 %all-to-all-start.4 = ((bf16[8,12,8,128]{3,2,1,0:T(8,128)(2,1)}), bf16[8,12,8,128]{3,2,1,0:T(8,128)(2,1)S(1)}, u32[]{:S(2)}, u32[]{:S(2)}) async-start(bf16[8,12,8,128]{3,2,1,0:T(8,128)(2,1)} %bitcast.15), calls=%async_computation.4 | async-start | bytes 393216 | tf_op jit(solution)/shard_map/all_to_all | solution.py:135
  138.8 18.6 %collective-permute-start.17 = (bf16[8,12,16,128]{3,2,1,0:T(8,128)(2,1)}, bf16[8,12,16,128]{3,2,1,0:T(8,128)(2,1)}, u32[]{:S(2)}, u32[]{:S(2)}) collective-permute-start(bf16[8,12,16,128]{3,2,1,0:T(8,128)(2,1)} %copy-done), channel_id=1, source_target_pairs={{0,1},{1,0},{2,3},{3,2},{4,5},{5,4},{6,7},{7,6},{8,9},{9,8},{10,11... | collective-permute-start | bytes 1179656 | tf_op jit(solution)/shard_map/ppermute | solution.py:127
  145.0 12.4 %copy-start.1 = (bf16[8,12,16,128]{3,2,1,0:T(8,128)(2,1)S(1)}, bf16[8,12,16,128]{3,2,1,0:T(8,128)(2,1)}, u32[]{:S(2)}) copy-start(bf16[8,12,16,128]{3,2,1,0:T(8,128)(2,1)} %copy-done) | copy-start | bytes 1179652
  147.4 10.0 %all-to-all-start.5 = ((bf16[8,12,8,128]{3,2,1,0:T(8,128)(2,1)}), bf16[8,12,8,128]{3,2,1,0:T(8,128)(2,1)S(1)}, u32[]{:S(2)}, u32[]{:S(2)}) async-start(bf16[8,12,8,128]{3,2,1,0:T(8,128)(2,1)} %bitcast.16), calls=%async_computation.5 | async-start | bytes 393216 | tf_op jit(solution)/shard_map/all_to_all | solution.py:135
  151.2 8.5 %collective-permute-start.15 = (bf16[8,12,8,128]{3,2,1,0:T(8,128)(2,1)S(1)}, bf16[8,12,8,128]{3,2,1,0:T(8,128)(2,1)S(1)}, u32[]{:S(2)}, u32[]{:S(2)}) collective-permute-start(bf16[8,12,8,128]{3,2,1,0:T(8,128)(2,1)S(1)} %copy-done.11), channel_id=1, source_target_pairs={{0,1},{1,0},{2,3},{3,2},{4,5},{5,4},{6,7},{7,6},{8,9},{9,8},{10,11... | collective-permute-start | bytes 589832 | tf_op jit(solution)/shard_map/ppermute | solution.py:127
  157.4 6.3 %collective-permute-start.16 = (bf16[8,12,8,128]{3,2,1,0:T(8,128)(2,1)S(1)}, bf16[8,12,8,128]{3,2,1,0:T(8,128)(2,1)S(1)}, u32[]{:S(2)}, u32[]{:S(2)}) collective-permute-start(bf16[8,12,8,128]{3,2,1,0:T(8,128)(2,1)S(1)} %all-to-all-done.5.refs_1_), channel_id=1, source_target_pairs={{0,1},{1,0},{2,3},{3,2},{4,5},{5,4},{6,7},{7,6},{8,9},{9,8},{10,11... | collective-permute-start | bytes 589832 | tf_op jit(solution)/shard_map/ppermute | solution.py:127
  (21 other events, 57.6 us)

commit v9 on v7

--- a/solution.py
+++ b/solution.py
@@ -10,7 +10,7 @@
 TRUNC = 1279
 VMEM = 24 * 2**20
 CHUNKS = (8, 8, 8, 8, 4, 4)
-MIRRORED = {2: 0, 4: 1, 5: 2}
+MIRRORED = {2: 0, 3: 1}
 GROUPS = ((0, 1), (2, 3), (4, 5))
 
 

time: 158 us -> 159 us (level)
  waiting for transfers between devices: 65.5 us -> 67.8 us
    ppermute x19, waiting for transfers between devices: 53.2 us -> 56 us  [swap(): lax.ppermute(value, 'band', [(band, band ^ step) for band in range(bands)])]
    unnamed x46 -> x42, local copies, waits for them, and re-layouts: 6.69 us -> 6.93 us
  transfers between devices with their start and end apart: 25 -> 25, of which waited for: 13 -> 16; matrix products, arithmetic and copies ran while one was open for 11% -> 11% of each run, Pallas kernels for 13% -> 13%
where the time goes in v9:
time: 159 us; the launch traced here: 158 us
  waiting for transfers between devices  67.8 us (43%)
  starting transfers between devices  43 us (27%)
  Pallas kernels  20.7 us (13%)
  local copies, waits for them, and re-layouts  18 us (11%)
  other arithmetic  7.78 us (5%)
    ppermute x19, waiting for transfers between devices, swap(): lax.ppermute(value, 'band', [(band, band ^ step) for band in range(bands)])  56 us
    all_to_all x6, starting transfers between devices, redistribute(): lax.all_to_all(grid.reshape(sets, fields // sets, -1, lats), 'mset', 0, 0)  22.9 us
    ppermute x19, starting transfers between devices, swap(): lax.ppermute(value, 'band', [(band, band ^ step) for band in range(bands)])  20.1 us
    pallas_call x6, Pallas kernels, parity_sums(): pl.pallas_call(functools.partial(sums_kernel, rows, fields, start), in_sp...  15.2 us
    all_to_all x6, waiting for transfers between devices, redistribute(): lax.all_to_all(grid.reshape(sets, fields // sets, -1, lats), 'mset', 0, 0)  11.8 us
    concatenate x5, other arithmetic, spread(): held.append(swap(jnp.concatenate(held), bit))  7.77 us
    unnamed x42, local copies, waits for them, and re-layouts  6.93 us
    slice x2, local copies, waits for them, and re-layouts, parity_sums(): legendre = legendre[start:start + pairs]  5.77 us
  transfers between devices with their start and end apart: 25, of which 16 were waited for; matrix products, arithmetic and copies ran while one was open for 11% of the time, Pallas kernels for 13%

profile of v9, /device:TPU:0, one launch (start us, length us, event | category | flops | bytes accessed | tf_op | source)
XLA Modules:
  0.0 158.2 jit_solution(10360729274076345058)
XLA Ops:
  1.1 3.1 %collective-permute-start.1 = (bf16[176,768]{1,0:T(8,128)(2,1)S(1)}, bf16[176,768]{1,0:T(8,128)(2,1)S(1)}, u32[]{:S(2)}, u32[]{:S(2)}) collective-permute-start(bf16[176,768]{1,0:T(8,128)(2,1)S(1)} %get-tuple-element.81), channel_id=1, source_target_pairs={{0,1},{1,0},{2,3},{3,2},{4,5},{5,4},{6,7},{7,6},{8,9},{9,8},{10,11... | collective-permute-start | bytes 811016 | tf_op jit(solution)/shard_map/ppermute | solution.py:127
  4.2 2.5 %collective-permute-start.3 = (bf16[176,768]{1,0:T(8,128)(2,1)S(1)}, bf16[176,768]{1,0:T(8,128)(2,1)S(1)}, u32[]{:S(2)}, u32[]{:S(2)}) collective-permute-start(bf16[176,768]{1,0:T(8,128)(2,1)S(1)} %get-tuple-element.81), channel_id=1, source_target_pairs={{0,3},{1,2},{2,1},{3,0},{4,7},{5,6},{6,5},{7,4},{8,11},{9,10},{10,... | collective-permute-start | bytes 811016 | tf_op jit(solution)/shard_map/ppermute | solution.py:127
  6.6 2.3 %dynamic-slice_bitcast_fusion = (bf16[176,768]{1,0:T(8,128)(2,1)S(1)}, bf16[176,768]{1,0:T(8,128)(2,1)}, bf16[176,768]{1,0:T(8,128)(2,1)}, bf16[176,768]{1,0:T(8...) fusion(bf16[2,176,3840]{2,1,0:T(8,128)(2,1)} %param.4, s32[]{:T(128)S(6)} %select_n.32, s32[]{:T(128)S(6)} %select_n.33), kind=kLoop, calls=%fused_computation.5 | loop fusion | bytes 3244040 | tf_op jit(solution)/shard_map/squeeze | solution.py:132
  10.9 4.3 %fusion.1 = (bf16[8,704,128]{2,1,0:T(8,128)(2,1)S(1)}, bf16[8,704,128]{2,1,0:T(8,128)(2,1)S(1)}, bf16[8,704,128]{2,1,0:T(8,128)(2,1)}, bf16[8,704,128]{2,1,0:T(8,128)(2,1)S(1)}) fusion(bf16[40,704,128]{2,1,0:T(8,128)(2,1)} %param.5), kind=kLoop, calls=%fused_computation.29 | loop fusion | bytes 11534336 | tf_op jit(solution)/shard_map/slice | solution.py:52
  15.2 13.0 %collective-permute-done.refs_1_ = bf16[176,768]{1,0:T(8,128)(2,1)S(1)} collective-permute-done((bf16[176,768]{1,0:T(8,128)(2,1)S(1)}, bf16[176,768]{1,0:T(8,128)(2,1)S(1)}, u32[]{:S(2)}, u32[]{:S(2)}) %collective-permute-start) | collective-permute-done | bytes 270368 | tf_op jit(solution)/shard_map/ppermute | solution.py:127
  29.2 2.9 %collective-permute-start.8 = (bf16[352,768]{1,0:T(8,128)(2,1)}, bf16[352,768]{1,0:T(8,128)(2,1)}, u32[]{:S(2)}, u32[]{:S(2)}) collective-permute-start(bf16[352,768]{1,0:T(8,128)(2,1)} %pad_maximum_fusion.1), channel_id=1, source_target_pairs={{0,2},{1,3},{2,0},{3,1},{4,6},{5,7},{6,4},{7,5},{8,10},{9,11},{10,... | collective-permute-start | bytes 1622024 | tf_op jit(solution)/shard_map/ppermute | solution.py:127
  32.0 7.8 %collective-permute-done.4.refs_1_ = bf16[176,768]{1,0:T(8,128)(2,1)S(1)} collective-permute-done((bf16[176,768]{1,0:T(8,128)(2,1)S(1)}, bf16[176,768]{1,0:T(8,128)(2,1)S(1)}, u32[]{:S(2)}, u32[]{:S(2)}) %collective-permute-start.4) | collective-permute-done | bytes 270368 | tf_op jit(solution)/shard_map/ppermute | solution.py:127
  43.3 4.2 %all-to-all-start = ((bf16[8,12,16,128]{3,2,1,0:T(8,128)(2,1)}), bf16[8,12,16,128]{3,2,1,0:T(8,128)(2,1)}, u32[]{:S(2)}, u32[]{:S(2)}) async-start(bf16[8,12,16,128]{3,2,1,0:T(8,128)(2,1)} %bitcast.31), calls=%async_computation | async-start | bytes 786432 | tf_op jit(solution)/shard_map/all_to_all | solution.py:135
  51.2 2.9 %collective-permute-start.5 = (bf16[352,768]{1,0:T(8,128)(2,1)}, bf16[352,768]{1,0:T(8,128)(2,1)}, u32[]{:S(2)}, u32[]{:S(2)}) collective-permute-start(bf16[352,768]{1,0:T(8,128)(2,1)} %pad_maximum_fusion), channel_id=1, source_target_pairs={{0,2},{1,3},{2,0},{3,1},{4,6},{5,7},{6,4},{7,5},{8,10},{9,11},{10,... | collective-permute-start | bytes 1622024 | tf_op jit(solution)/shard_map/ppermute | solution.py:127
  58.2 2.5 %parity_sums.7 = bf16[96,16,128]{2,1,0:T(8,128)(2,1)S(1)} custom-call(s32[4]{0:T(128)S(1)} %iota_xor_fusion.order, s32[40]{0:T(128)S(1)} %get-tuple-element.152.first, s32[40]{0:T(128)S(1)} %get-tuple-element.151.total, bf16[176,768]{1,0:T(8,128)(2,1)S(1)} %copy-done.7, bf16[176,768]{1,0:T(8,128)(2,1)S(1)} %copy-done.19, ...), custom_call_target="tpu_custom_call" | custom-call | flops 799999983616 | bytes 838860800 | tf_op jit(solution)/shard_map/parity_sums/pallas_call | solution.py:55
  61.4 3.3 %collective-permute-done.7.refs_1_ = bf16[176,768]{1,0:T(8,128)(2,1)} collective-permute-done((bf16[176,768]{1,0:T(8,128)(2,1)}, bf16[176,768]{1,0:T(8,128)(2,1)}, u32[]{:S(2)}, u32[]{:S(2)}) %collective-permute-start.7) | collective-permute-done | bytes 270368 | tf_op jit(solution)/shard_map/ppermute | solution.py:127
  64.7 4.1 %all-to-all-start.1 = ((bf16[8,12,16,128]{3,2,1,0:T(8,128)(2,1)}), bf16[8,12,16,128]{3,2,1,0:T(8,128)(2,1)}, u32[]{:S(2)}, u32[]{:S(2)}) async-start(bf16[8,12,16,128]{3,2,1,0:T(8,128)(2,1)} %bitcast.32), calls=%async_computation.1 | async-start | bytes 786432 | tf_op jit(solution)/shard_map/all_to_all | solution.py:135
  70.7 2.0 %collective-permute-start.9 = (bf16[352,768]{1,0:T(8,128)(2,1)}, bf16[352,768]{1,0:T(8,128)(2,1)}, u32[]{:S(2)}, u32[]{:S(2)}) collective-permute-start(bf16[352,768]{1,0:T(8,128)(2,1)} %pad_maximum_fusion.2), channel_id=1, source_target_pairs={{0,2},{1,3},{2,0},{3,1},{4,6},{5,7},{6,4},{7,5},{8,10},{9,11},{10,... | collective-permute-start | bytes 1622024 | tf_op jit(solution)/shard_map/ppermute | solution.py:127
  72.8 6.5 %collective-permute-done.5.refs_2_ = bf16[352,768]{1,0:T(8,128)(2,1)} collective-permute-done((bf16[352,768]{1,0:T(8,128)(2,1)}, bf16[352,768]{1,0:T(8,128)(2,1)}, u32[]{:S(2)}, u32[]{:S(2)}) %collective-permute-start.5) | collective-permute-done | bytes 540704 | tf_op jit(solution)/shard_map/ppermute | solution.py:127
  79.2 5.3 %collective-permute-done.11.refs_2_ = bf16[8,12,16,128]{3,2,1,0:T(8,128)(2,1)} collective-permute-done((bf16[8,12,16,128]{3,2,1,0:T(8,128)(2,1)}, bf16[8,12,16,128]{3,2,1,0:T(8,128)(2,1)}, u32[]{:S(2)}, u32[]{:S(2)}) %collective-permute-start.11) | collective-permute-done | bytes 393248 | tf_op jit(solution)/shard_map/ppermute | solution.py:127
  85.4 2.4 %parity_sums.8 = bf16[96,16,128]{2,1,0:T(8,128)(2,1)S(1)} custom-call(s32[4]{0:T(128)S(1)} %iota_xor_fusion.order, s32[40]{0:T(128)S(1)} %get-tuple-element.152.first, s32[40]{0:T(128)S(1)} %get-tuple-element.151.total, bf16[176,768]{1,0:T(8,128)(2,1)S(1)} %copy-done.5, bf16[176,768]{1,0:T(8,128)(2,1)S(1)} %copy-done.17, ...), custom_call_target="tpu_custom_call" | custom-call | flops 799999983616 | bytes 838860800 | tf_op jit(solution)/shard_map/parity_sums/pallas_call | solution.py:55
  88.6 4.1 %all-to-all-start.2 = ((bf16[8,12,16,128]{3,2,1,0:T(8,128)(2,1)}), bf16[8,12,16,128]{3,2,1,0:T(8,128)(2,1)}, u32[]{:S(2)}, u32[]{:S(2)}) async-start(bf16[8,12,16,128]{3,2,1,0:T(8,128)(2,1)} %bitcast.33), calls=%async_computation.2 | async-start | bytes 786432 | tf_op jit(solution)/shard_map/all_to_all | solution.py:135
  95.2 2.1 %collective-permute-start.14 = (bf16[352,384]{1,0:T(8,128)(2,1)}, bf16[352,384]{1,0:T(8,128)(2,1)}, u32[]{:S(2)}, u32[]{:S(2)}) collective-permute-start(bf16[352,384]{1,0:T(8,128)(2,1)} %pad_maximum_fusion.4), channel_id=1, source_target_pairs={{0,2},{1,3},{2,0},{3,1},{4,6},{5,7},{6,4},{7,5},{8,10},{9,11},{10,... | collective-permute-start | bytes 811016 | tf_op jit(solution)/shard_map/ppermute | solution.py:127
  97.2 5.2 %collective-permute-done.9.refs_2_ = bf16[352,768]{1,0:T(8,128)(2,1)} collective-permute-done((bf16[352,768]{1,0:T(8,128)(2,1)}, bf16[352,768]{1,0:T(8,128)(2,1)}, u32[]{:S(2)}, u32[]{:S(2)}) %collective-permute-start.9) | collective-permute-done | bytes 540704 | tf_op jit(solution)/shard_map/ppermute | solution.py:127
  102.4 4.7 %collective-permute-done.12.refs_3_ = bf16[8,12,16,128]{3,2,1,0:T(8,128)(2,1)} collective-permute-done((bf16[8,12,16,128]{3,2,1,0:T(8,128)(2,1)}, bf16[8,12,16,128]{3,2,1,0:T(8,128)(2,1)}, u32[]{:S(2)}, u32[]{:S(2)}) %collective-permute-start.12) | collective-permute-done | bytes 393248 | tf_op jit(solution)/shard_map/ppermute | solution.py:127
  107.1 3.3 %parity_sums.9 = bf16[96,16,128]{2,1,0:T(8,128)(2,1)} custom-call(s32[4]{0:T(128)S(1)} %iota_xor_fusion.order, s32[40]{0:T(128)S(1)} %get-tuple-element.152.first, s32[40]{0:T(128)S(1)} %get-tuple-element.151.total, bf16[176,768]{1,0:T(8,128)(2,1)S(1)} %copy-done.3, bf16[176,768]{1,0:T(8,128)(2,1)} %collective-permute-done.7.refs_1_, ...), custom_call_target="tpu_custom_call" | custom-call | flops 799999983616 | bytes 838860800 | tf_op jit(solution)/shard_map/parity_sums/pallas_call | solution.py:55
  110.4 3.7 %all-to-all-start.3 = ((bf16[8,12,16,128]{3,2,1,0:T(8,128)(2,1)}), bf16[8,12,16,128]{3,2,1,0:T(8,128)(2,1)S(1)}, u32[]{:S(2)}, u32[]{:S(2)}) async-start(bf16[8,12,16,128]{3,2,1,0:T(8,128)(2,1)} %bitcast.16), calls=%async_computation.3 | async-start | bytes 786432 | tf_op jit(solution)/shard_map/all_to_all | solution.py:135
  117.3 2.4 %finish.3.refs_4_ = bf16[12,640,128]{2,1,0:T(8,128)(2,1)} custom-call(s32[1]{0:T(128)} %bitcast.parity, s32[1]{0:T(128)S(6)} %copy.9.lat_count, bf16[8,12,16,128]{3,2,1,0:T(8,128)(2,1)} %all-to-all-done.refs_0_, bf16[8,12,16,128]{3,2,1,0:T(8,128)(2,1)} %all-to-all-done.1.refs_1_, bf16[8,12,16,128]{3,2,1,0:T(8,128)(2,1)} %collective-permute-done.11.refs_2_, ...), custom_call_target="tpu_custom_call" | custom-call | tf_op jit(solution)/shard_map/finish/pallas_call | solution.py:99
  119.7 2.8 %all-to-all-done.3.refs_1_ = bf16[8,12,16,128]{3,2,1,0:T(8,128)(2,1)S(1)} async-done(((bf16[8,12,16,128]{3,2,1,0:T(8,128)(2,1)}), bf16[8,12,16,128]{3,2,1,0:T(8,128)(2,1)S(1)}, u32[]{:S(2)}, u32[]{:S(2)}) %all-to-all-start.3) | async-done | bytes 393248 | tf_op jit(solution)/shard_map/all_to_all | solution.py:135
  122.5 2.6 %parity_sums.10 = bf16[96,8,128]{2,1,0:T(8,128)(2,1)} custom-call(s32[4]{0:T(128)S(1)} %iota_xor_fusion.order, s32[40]{0:T(128)S(1)} %get-tuple-element.152.first, s32[40]{0:T(128)S(1)} %get-tuple-element.151.total, bf16[176,384]{1,0:T(8,128)(2,1)S(1)} %copy-done.12, bf16[176,384]{1,0:T(8,128)(2,1)} %collective-permute-done.10.refs_1_, ...), custom_call_target="tpu_custom_call" | custom-call | flops 399999991808 | bytes 419430400 | tf_op jit(solution)/shard_map/parity_sums/pallas_call | solution.py:55
  125.1 3.4 %all-to-all-start.4 = ((bf16[8,12,8,128]{3,2,1,0:T(8,128)(2,1)}), bf16[8,12,8,128]{3,2,1,0:T(8,128)(2,1)S(1)}, u32[]{:S(2)}, u32[]{:S(2)}) async-start(bf16[8,12,8,128]{3,2,1,0:T(8,128)(2,1)} %bitcast.17), calls=%async_computation.4 | async-start | bytes 393216 | tf_op jit(solution)/shard_map/all_to_all | solution.py:135
  132.2 2.5 %all-to-all-done.4.refs_0_ = bf16[8,12,8,128]{3,2,1,0:T(8,128)(2,1)S(1)} async-done(((bf16[8,12,8,128]{3,2,1,0:T(8,128)(2,1)}), bf16[8,12,8,128]{3,2,1,0:T(8,128)(2,1)S(1)}, u32[]{:S(2)}, u32[]{:S(2)}) %all-to-all-start.4) | async-done | bytes 196640 | tf_op jit(solution)/shard_map/all_to_all | solution.py:135
  135.4 2.5 %parity_sums.11 = bf16[96,8,128]{2,1,0:T(8,128)(2,1)} custom-call(s32[4]{0:T(128)S(1)} %iota_xor_fusion.order, s32[40]{0:T(128)S(1)} %get-tuple-element.152.first, s32[40]{0:T(128)S(1)} %get-tuple-element.151.total, bf16[176,384]{1,0:T(8,128)(2,1)S(1)} %copy-done.11, bf16[176,384]{1,0:T(8,128)(2,1)} %collective-permute-done.6.refs_1_, ...), custom_call_target="tpu_custom_call" | custom-call | flops 399999991808 | bytes 419430400 | tf_op jit(solution)/shard_map/parity_sums/pallas_call | solution.py:55
  137.9 3.4 %all-to-all-start.5 = ((bf16[8,12,8,128]{3,2,1,0:T(8,128)(2,1)}), bf16[8,12,8,128]{3,2,1,0:T(8,128)(2,1)S(1)}, u32[]{:S(2)}, u32[]{:S(2)}) async-start(bf16[8,12,8,128]{3,2,1,0:T(8,128)(2,1)} %bitcast.18), calls=%async_computation.5 | async-start | bytes 393216 | tf_op jit(solution)/shard_map/all_to_all | solution.py:135
  141.5 5.9 %all-to-all-done.5.refs_1_ = bf16[8,12,8,128]{3,2,1,0:T(8,128)(2,1)S(1)} async-done(((bf16[8,12,8,128]{3,2,1,0:T(8,128)(2,1)}), bf16[8,12,8,128]{3,2,1,0:T(8,128)(2,1)S(1)}, u32[]{:S(2)}, u32[]{:S(2)}) %all-to-all-start.5) | async-done | bytes 196640 | tf_op jit(solution)/shard_map/all_to_all | solution.py:135
  149.3 2.2 %finish.4.refs_4_ = bf16[12,640,128]{2,1,0:T(8,128)(2,1)} custom-call(s32[1]{0:T(128)} %bitcast.parity, s32[1]{0:T(128)S(6)} %copy.9.lat_count, bf16[8,12,16,128]{3,2,1,0:T(8,128)(2,1)} %all-to-all-done.2.refs_0_, bf16[8,12,16,128]{3,2,1,0:T(8,128)(2,1)S(1)} %copy-done.1, ...), custom_call_target="tpu_custom_call", output_to_operand_aliasing={{}: (6, {})} | custom-call | tf_op jit(solution)/shard_map/finish/pallas_call | solution.py:99
  153.4 3.9 %collective-permute-done.16.refs_3_ = bf16[8,12,8,128]{3,2,1,0:T(8,128)(2,1)S(1)} collective-permute-done((bf16[8,12,8,128]{3,2,1,0:T(8,128)(2,1)S(1)}, bf16[8,12,8,128]{3,2,1,0:T(8,128)(2,1)S(1)}, u32[]{:S(2)}, u32[]{:S(2)}) %collective-permute-start.16) | collective-permute-done | bytes 196640 | tf_op jit(solution)/shard_map/ppermute | solution.py:127
  (81 shorter events, 33.5 us)
Async XLA Ops:
  1.1 27.2 %collective-permute-start.1 = (bf16[176,768]{1,0:T(8,128)(2,1)S(1)}, bf16[176,768]{1,0:T(8,128)(2,1)S(1)}, u32[]{:S(2)}, u32[]{:S(2)}) collective-permute-start(bf16[176,768]{1,0:T(8,128)(2,1)S(1)} %get-tuple-element.81), channel_id=1, source_target_pairs={{0,1},{1,0},{2,3},{3,2},{4,5},{5,4},{6,7},{7,6},{8,9},{9,8},{10,11... | collective-permute-start | bytes 811016 | tf_op jit(solution)/shard_map/ppermute | solution.py:127
  4.2 24.1 %collective-permute-start.3 = (bf16[176,768]{1,0:T(8,128)(2,1)S(1)}, bf16[176,768]{1,0:T(8,128)(2,1)S(1)}, u32[]{:S(2)}, u32[]{:S(2)}) collective-permute-start(bf16[176,768]{1,0:T(8,128)(2,1)S(1)} %get-tuple-element.81), channel_id=1, source_target_pairs={{0,3},{1,2},{2,1},{3,0},{4,7},{5,6},{6,5},{7,4},{8,11},{9,10},{10,... | collective-permute-start | bytes 811016 | tf_op jit(solution)/shard_map/ppermute | solution.py:127
  9.0 19.3 %copy-start.6 = (bf16[176,768]{1,0:T(8,128)(2,1)}, bf16[176,768]{1,0:T(8,128)(2,1)S(1)}, u32[]{:S(2)}) copy-start(bf16[176,768]{1,0:T(8,128)(2,1)S(1)} %get-tuple-element.103.refs_0_) | copy-start | bytes 811012
  9.0 19.3 %copy-start.20 = (s32[40]{0:T(128)S(1)}, s32[40]{0:T(128)}, u32[]{:S(2)}) copy-start(s32[40]{0:T(128)} %param.6) | copy-start | bytes 484
  9.0 19.3 %collective-permute-start = (bf16[176,768]{1,0:T(8,128)(2,1)S(1)}, bf16[176,768]{1,0:T(8,128)(2,1)S(1)}, u32[]{:S(2)}, u32[]{:S(2)}) collective-permute-start(bf16[176,768]{1,0:T(8,128)(2,1)S(1)} %get-tuple-element.162), channel_id=1, source_target_pairs={{0,1},{1,0},{2,3},{3,2},{4,5},{5,4},{6,7},{7,6},{8,9},{9,8},{10,11... | collective-permute-start | bytes 811016 | tf_op jit(solution)/shard_map/ppermute | solution.py:127
  9.7 18.6 %collective-permute-start.2 = (bf16[176,768]{1,0:T(8,128)(2,1)S(1)}, bf16[176,768]{1,0:T(8,128)(2,1)S(1)}, u32[]{:S(2)}, u32[]{:S(2)}) collective-permute-start(bf16[176,768]{1,0:T(8,128)(2,1)S(1)} %get-tuple-element.88.refs_0_), channel_id=1, source_target_pairs={{0,2},{1,3},{2,0},{3,1},{4,6},{5,7},{6,4},{7,5},{8,10},{9,11},{10,... | collective-permute-start | bytes 811016 | tf_op jit(solution)/shard_map/ppermute | solution.py:127
  28.2 14.3 %copy-start.18 = (bf16[176,768]{1,0:T(8,128)(2,1)}, bf16[176,768]{1,0:T(8,128)(2,1)S(1)}, u32[]{:S(2)}) copy-start(bf16[176,768]{1,0:T(8,128)(2,1)S(1)} %collective-permute-done.refs_1_) | copy-start | bytes 811012
  28.2 11.6 %collective-permute-start.4 = (bf16[176,768]{1,0:T(8,128)(2,1)S(1)}, bf16[176,768]{1,0:T(8,128)(2,1)S(1)}, u32[]{:S(2)}, u32[]{:S(2)}) collective-permute-start(bf16[176,768]{1,0:T(8,128)(2,1)S(1)} %get-tuple-element.86), channel_id=1, source_target_pairs={{0,1},{1,0},{2,3},{3,2},{4,5},{5,4},{6,7},{7,6},{8,9},{9,8},{10,11... | collective-permute-start | bytes 811016 | tf_op jit(solution)/shard_map/ppermute | solution.py:127
  29.2 26.0 %collective-permute-start.8 = (bf16[352,768]{1,0:T(8,128)(2,1)}, bf16[352,768]{1,0:T(8,128)(2,1)}, u32[]{:S(2)}, u32[]{:S(2)}) collective-permute-start(bf16[352,768]{1,0:T(8,128)(2,1)} %pad_maximum_fusion.1), channel_id=1, source_target_pairs={{0,2},{1,3},{2,0},{3,1},{4,6},{5,7},{6,4},{7,5},{8,10},{9,11},{10,... | collective-permute-start | bytes 1622024 | tf_op jit(solution)/shard_map/ppermute | solution.py:127
  43.3 12.6 %copy-start.7 = (bf16[176,768]{1,0:T(8,128)(2,1)S(1)}, bf16[176,768]{1,0:T(8,128)(2,1)}, u32[]{:S(2)}) copy-start(bf16[176,768]{1,0:T(8,128)(2,1)} %copy-done.6) | copy-start | bytes 811012
  43.3 12.6 %all-to-all-start = ((bf16[8,12,16,128]{3,2,1,0:T(8,128)(2,1)}), bf16[8,12,16,128]{3,2,1,0:T(8,128)(2,1)}, u32[]{:S(2)}, u32[]{:S(2)}) async-start(bf16[8,12,16,128]{3,2,1,0:T(8,128)(2,1)} %bitcast.31), calls=%async_computation | async-start | bytes 786432 | tf_op jit(solution)/shard_map/all_to_all | solution.py:135
  49.4 15.3 %collective-permute-start.7 = (bf16[176,768]{1,0:T(8,128)(2,1)}, bf16[176,768]{1,0:T(8,128)(2,1)}, u32[]{:S(2)}, u32[]{:S(2)}) collective-permute-start(bf16[176,768]{1,0:T(8,128)(2,1)} %get-tuple-element.97), channel_id=1, source_target_pairs={{0,1},{1,0},{2,3},{3,2},{4,5},{5,4},{6,7},{7,6},{8,9},{9,8},{10,11... | collective-permute-start | bytes 811016 | tf_op jit(solution)/shard_map/ppermute | solution.py:127
  51.2 28.0 %collective-permute-start.5 = (bf16[352,768]{1,0:T(8,128)(2,1)}, bf16[352,768]{1,0:T(8,128)(2,1)}, u32[]{:S(2)}, u32[]{:S(2)}) collective-permute-start(bf16[352,768]{1,0:T(8,128)(2,1)} %pad_maximum_fusion), channel_id=1, source_target_pairs={{0,2},{1,3},{2,0},{3,1},{4,6},{5,7},{6,4},{7,5},{8,10},{9,11},{10,... | collective-permute-start | bytes 1622024 | tf_op jit(solution)/shard_map/ppermute | solution.py:127
  55.8 28.6 %collective-permute-start.11 = (bf16[8,12,16,128]{3,2,1,0:T(8,128)(2,1)}, bf16[8,12,16,128]{3,2,1,0:T(8,128)(2,1)}, u32[]{:S(2)}, u32[]{:S(2)}) collective-permute-start(bf16[8,12,16,128]{3,2,1,0:T(8,128)(2,1)} %all-to-all-done.refs_0_), channel_id=1, source_target_pairs={{0,1},{1,0},{2,3},{3,2},{4,5},{5,4},{6,7},{7,6},{8,9},{9,8},{10,11... | collective-permute-start | bytes 1179656 | tf_op jit(solution)/shard_map/ppermute | solution.py:127
  61.4 23.1 %copy-start.5 = (bf16[176,768]{1,0:T(8,128)(2,1)S(1)}, bf16[176,768]{1,0:T(8,128)(2,1)}, u32[]{:S(2)}) copy-start(bf16[176,768]{1,0:T(8,128)(2,1)} %get-tuple-element.118.refs_0_) | copy-start | bytes 811012
  64.7 14.5 %all-to-all-start.1 = ((bf16[8,12,16,128]{3,2,1,0:T(8,128)(2,1)}), bf16[8,12,16,128]{3,2,1,0:T(8,128)(2,1)}, u32[]{:S(2)}, u32[]{:S(2)}) async-start(bf16[8,12,16,128]{3,2,1,0:T(8,128)(2,1)} %bitcast.32), calls=%async_computation.1 | async-start | bytes 786432 | tf_op jit(solution)/shard_map/all_to_all | solution.py:135
  68.8 19.8 %collective-permute-start.10 = (bf16[176,384]{1,0:T(8,128)(2,1)}, bf16[176,384]{1,0:T(8,128)(2,1)}, u32[]{:S(2)}, u32[]{:S(2)}) collective-permute-start(bf16[176,384]{1,0:T(8,128)(2,1)} %get-tuple-element.109), channel_id=1, source_target_pairs={{0,1},{1,0},{2,3},{3,2},{4,5},{5,4},{6,7},{7,6},{8,9},{9,8},{10,11... | collective-permute-start | bytes 405512 | tf_op jit(solution)/shard_map/ppermute | solution.py:127
  70.7 31.7 %collective-permute-start.9 = (bf16[352,768]{1,0:T(8,128)(2,1)}, bf16[352,768]{1,0:T(8,128)(2,1)}, u32[]{:S(2)}, u32[]{:S(2)}) collective-permute-start(bf16[352,768]{1,0:T(8,128)(2,1)} %pad_maximum_fusion.2), channel_id=1, source_target_pairs={{0,2},{1,3},{2,0},{3,1},{4,6},{5,7},{6,4},{7,5},{8,10},{9,11},{10,... | collective-permute-start | bytes 1622024 | tf_op jit(solution)/shard_map/ppermute | solution.py:127
  79.2 27.9 %collective-permute-start.12 = (bf16[8,12,16,128]{3,2,1,0:T(8,128)(2,1)}, bf16[8,12,16,128]{3,2,1,0:T(8,128)(2,1)}, u32[]{:S(2)}, u32[]{:S(2)}) collective-permute-start(bf16[8,12,16,128]{3,2,1,0:T(8,128)(2,1)} %all-to-all-done.1.refs_1_), channel_id=1, source_target_pairs={{0,1},{1,0},{2,3},{3,2},{4,5},{5,4},{6,7},{7,6},{8,9},{9,8},{10,11... | collective-permute-start | bytes 1179656 | tf_op jit(solution)/shard_map/ppermute | solution.py:127
  88.6 13.8 %all-to-all-start.2 = ((bf16[8,12,16,128]{3,2,1,0:T(8,128)(2,1)}), bf16[8,12,16,128]{3,2,1,0:T(8,128)(2,1)}, u32[]{:S(2)}, u32[]{:S(2)}) async-start(bf16[8,12,16,128]{3,2,1,0:T(8,128)(2,1)} %bitcast.33), calls=%async_computation.2 | async-start | bytes 786432 | tf_op jit(solution)/shard_map/all_to_all | solution.py:135
  93.4 17.0 %collective-permute-start.6 = (bf16[176,384]{1,0:T(8,128)(2,1)}, bf16[176,384]{1,0:T(8,128)(2,1)}, u32[]{:S(2)}, u32[]{:S(2)}) collective-permute-start(bf16[176,384]{1,0:T(8,128)(2,1)} %get-tuple-element.95), channel_id=1, source_target_pairs={{0,1},{1,0},{2,3},{3,2},{4,5},{5,4},{6,7},{7,6},{8,9},{9,8},{10,11... | collective-permute-start | bytes 405512 | tf_op jit(solution)/shard_map/ppermute | solution.py:127
  95.2 24.5 %collective-permute-start.14 = (bf16[352,384]{1,0:T(8,128)(2,1)}, bf16[352,384]{1,0:T(8,128)(2,1)}, u32[]{:S(2)}, u32[]{:S(2)}) collective-permute-start(bf16[352,384]{1,0:T(8,128)(2,1)} %pad_maximum_fusion.4), channel_id=1, source_target_pairs={{0,2},{1,3},{2,0},{3,1},{4,6},{5,7},{6,4},{7,5},{8,10},{9,11},{10,... | collective-permute-start | bytes 811016 | tf_op jit(solution)/shard_map/ppermute | solution.py:127
  110.4 12.1 %all-to-all-start.3 = ((bf16[8,12,16,128]{3,2,1,0:T(8,128)(2,1)}), bf16[8,12,16,128]{3,2,1,0:T(8,128)(2,1)S(1)}, u32[]{:S(2)}, u32[]{:S(2)}) async-start(bf16[8,12,16,128]{3,2,1,0:T(8,128)(2,1)} %bitcast.16), calls=%async_computation.3 | async-start | bytes 786432 | tf_op jit(solution)/shard_map/all_to_all | solution.py:135
  117.3 14.9 %collective-permute-start.13 = (bf16[352,384]{1,0:T(8,128)(2,1)}, bf16[352,384]{1,0:T(8,128)(2,1)}, u32[]{:S(2)}, u32[]{:S(2)}) collective-permute-start(bf16[352,384]{1,0:T(8,128)(2,1)} %pad_maximum_fusion.3), channel_id=1, source_target_pairs={{0,2},{1,3},{2,0},{3,1},{4,6},{5,7},{6,4},{7,5},{8,10},{9,11},{10,... | collective-permute-start | bytes 811016 | tf_op jit(solution)/shard_map/ppermute | solution.py:127
  122.5 12.9 %copy-start.11 = (bf16[176,384]{1,0:T(8,128)(2,1)S(1)}, bf16[176,384]{1,0:T(8,128)(2,1)}, u32[]{:S(2)}) copy-start(bf16[176,384]{1,0:T(8,128)(2,1)} %get-tuple-element.145.refs_0_) | copy-start | bytes 405508
  125.1 9.6 %all-to-all-start.4 = ((bf16[8,12,8,128]{3,2,1,0:T(8,128)(2,1)}), bf16[8,12,8,128]{3,2,1,0:T(8,128)(2,1)S(1)}, u32[]{:S(2)}, u32[]{:S(2)}) async-start(bf16[8,12,8,128]{3,2,1,0:T(8,128)(2,1)} %bitcast.17), calls=%async_computation.4 | async-start | bytes 393216 | tf_op jit(solution)/shard_map/all_to_all | solution.py:135
  128.5 19.1 %collective-permute-start.17 = (bf16[8,12,16,128]{3,2,1,0:T(8,128)(2,1)}, bf16[8,12,16,128]{3,2,1,0:T(8,128)(2,1)}, u32[]{:S(2)}, u32[]{:S(2)}) collective-permute-start(bf16[8,12,16,128]{3,2,1,0:T(8,128)(2,1)} %all-to-all-done.2.refs_0_), channel_id=1, source_target_pairs={{0,1},{1,0},{2,3},{3,2},{4,5},{5,4},{6,7},{7,6},{8,9},{9,8},{10,11... | collective-permute-start | bytes 1179656 | tf_op jit(solution)/shard_map/ppermute | solution.py:127
  128.6 20.7 %collective-permute-start.18 = (bf16[8,12,16,128]{3,2,1,0:T(8,128)(2,1)}, bf16[8,12,16,128]{3,2,1,0:T(8,128)(2,1)}, u32[]{:S(2)}, u32[]{:S(2)}) collective-permute-start(bf16[8,12,16,128]{3,2,1,0:T(8,128)(2,1)} %copy-done), channel_id=1, source_target_pairs={{0,1},{1,0},{2,3},{3,2},{4,5},{5,4},{6,7},{7,6},{8,9},{9,8},{10,11... | collective-permute-start | bytes 1179656 | tf_op jit(solution)/shard_map/ppermute | solution.py:127
  135.4 14.0 %copy-start.1 = (bf16[8,12,16,128]{3,2,1,0:T(8,128)(2,1)S(1)}, bf16[8,12,16,128]{3,2,1,0:T(8,128)(2,1)}, u32[]{:S(2)}) copy-start(bf16[8,12,16,128]{3,2,1,0:T(8,128)(2,1)} %copy-done) | copy-start | bytes 1179652
  137.9 9.6 %all-to-all-start.5 = ((bf16[8,12,8,128]{3,2,1,0:T(8,128)(2,1)}), bf16[8,12,8,128]{3,2,1,0:T(8,128)(2,1)S(1)}, u32[]{:S(2)}, u32[]{:S(2)}) async-start(bf16[8,12,8,128]{3,2,1,0:T(8,128)(2,1)} %bitcast.18), calls=%async_computation.5 | async-start | bytes 393216 | tf_op jit(solution)/shard_map/all_to_all | solution.py:135
  141.3 12.1 %collective-permute-start.15 = (bf16[8,12,8,128]{3,2,1,0:T(8,128)(2,1)S(1)}, bf16[8,12,8,128]{3,2,1,0:T(8,128)(2,1)S(1)}, u32[]{:S(2)}, u32[]{:S(2)}) collective-permute-start(bf16[8,12,8,128]{3,2,1,0:T(8,128)(2,1)S(1)} %copy-done.9), channel_id=1, source_target_pairs={{0,1},{1,0},{2,3},{3,2},{4,5},{5,4},{6,7},{7,6},{8,9},{9,8},{10,11... | collective-permute-start | bytes 589832 | tf_op jit(solution)/shard_map/ppermute | solution.py:127
  147.4 9.9 %collective-permute-start.16 = (bf16[8,12,8,128]{3,2,1,0:T(8,128)(2,1)S(1)}, bf16[8,12,8,128]{3,2,1,0:T(8,128)(2,1)S(1)}, u32[]{:S(2)}, u32[]{:S(2)}) collective-permute-start(bf16[8,12,8,128]{3,2,1,0:T(8,128)(2,1)S(1)} %all-to-all-done.5.refs_1_), channel_id=1, source_target_pairs={{0,1},{1,0},{2,3},{3,2},{4,5},{5,4},{6,7},{7,6},{8,9},{9,8},{10,11... | collective-permute-start | bytes 589832 | tf_op jit(solution)/shard_map/ppermute | solution.py:127
  (14 other events, 39.1 us)

commit v10 on v5

--- a/solution.py
+++ b/solution.py
@@ -193,7 +193,7 @@
         if chunk in MIRRORED:
             back = MIRRORED[chunk]
             far[chunk], sums[back] = lax.optimization_barrier((far[chunk], sums[back]))
-        if chunk == GROUPS[0][-1] + 3:
+        if chunk == GROUPS[0][-1] + 4:
             write()
             far[chunk], out = lax.optimization_barrier((far[chunk], out))
         blocks = far[chunk]

time: 157 us -> 156 us (level)
    ppermute x19, waiting for transfers between devices: 55.1 us -> 52.1 us  [swap(): lax.ppermute(value, 'band', [(band, band ^ step) for band in range(bands)])]
    all_to_all x6, waiting for transfers between devices: 10.1 us -> 12 us  [redistribute(): lax.all_to_all(grid.reshape(sets, fields // sets, -1, lats), 'mset', 0, 0)]
    unnamed x42 -> x38, local copies, waits for them, and re-layouts: 6.45 us -> 6.27 us
  transfers between devices with their start and end apart: 25 -> 25, of which waited for: 15 -> 15; matrix products, arithmetic and copies ran while one was open for 11% -> 12% of each run, Pallas kernels for 13% -> 13%
where the time goes in v10:
time: 156 us; the launch traced here: 155 us
  waiting for transfers between devices  64.2 us (41%)
  starting transfers between devices  44.1 us (28%)
  Pallas kernels  20.6 us (13%)
  local copies, waits for them, and re-layouts  17.4 us (11%)
  other arithmetic  7.82 us (5%)
    ppermute x19, waiting for transfers between devices, swap(): lax.ppermute(value, 'band', [(band, band ^ step) for band in range(bands)])  52.1 us
    all_to_all x6, starting transfers between devices, redistribute(): lax.all_to_all(grid.reshape(sets, fields // sets, -1, lats), 'mset', 0, 0)  23.8 us
    ppermute x19, starting transfers between devices, swap(): lax.ppermute(value, 'band', [(band, band ^ step) for band in range(bands)])  20.3 us
    pallas_call x6, Pallas kernels, parity_sums(): pl.pallas_call(functools.partial(sums_kernel, rows, fields, start), in_sp...  15 us
    all_to_all x6, waiting for transfers between devices, redistribute(): lax.all_to_all(grid.reshape(sets, fields // sets, -1, lats), 'mset', 0, 0)  12 us
    concatenate x5, other arithmetic, spread(): held.append(swap(jnp.concatenate(held), bit))  7.8 us
    unnamed x38, local copies, waits for them, and re-layouts  6.27 us
    slice x2, local copies, waits for them, and re-layouts, parity_sums(): legendre = legendre[start:start + pairs]  5.78 us
  transfers between devices with their start and end apart: 25, of which 15 were waited for; matrix products, arithmetic and copies ran while one was open for 12% of the time, Pallas kernels for 13%

profile of v10, /device:TPU:0, one launch (start us, length us, event | category | flops | bytes accessed | tf_op | source)
XLA Modules:
  0.0 154.9 jit_solution(3319580427227007332)
XLA Ops:
  1.1 3.1 %collective-permute-start.1 = (bf16[176,768]{1,0:T(8,128)(2,1)S(1)}, bf16[176,768]{1,0:T(8,128)(2,1)S(1)}, u32[]{:S(2)}, u32[]{:S(2)}) collective-permute-start(bf16[176,768]{1,0:T(8,128)(2,1)S(1)} %get-tuple-element.86), channel_id=1, source_target_pairs={{0,1},{1,0},{2,3},{3,2},{4,5},{5,4},{6,7},{7,6},{8,9},{9,8},{10,11... | collective-permute-start | bytes 811016 | tf_op jit(solution)/shard_map/ppermute | solution.py:127
  4.2 2.5 %collective-permute-start.3 = (bf16[176,768]{1,0:T(8,128)(2,1)S(1)}, bf16[176,768]{1,0:T(8,128)(2,1)S(1)}, u32[]{:S(2)}, u32[]{:S(2)}) collective-permute-start(bf16[176,768]{1,0:T(8,128)(2,1)S(1)} %get-tuple-element.86), channel_id=1, source_target_pairs={{0,3},{1,2},{2,1},{3,0},{4,7},{5,6},{6,5},{7,4},{8,11},{9,10},{10,... | collective-permute-start | bytes 811016 | tf_op jit(solution)/shard_map/ppermute | solution.py:127
  6.6 2.3 %dynamic-slice_bitcast_fusion = (bf16[176,768]{1,0:T(8,128)(2,1)S(1)}, bf16[176,768]{1,0:T(8,128)(2,1)}, bf16[176,768]{1,0:T(8,128)(2,1)}, bf16[176,768]{1,0:T(8...) fusion(bf16[2,176,3840]{2,1,0:T(8,128)(2,1)} %param.4, s32[]{:T(128)S(6)} %select_n.32, s32[]{:T(128)S(6)} %select_n.33), kind=kLoop, calls=%fused_computation.5 | loop fusion | bytes 3244040 | tf_op jit(solution)/shard_map/squeeze | solution.py:132
  10.9 4.3 %fusion.1 = (bf16[8,704,128]{2,1,0:T(8,128)(2,1)S(1)}, bf16[8,704,128]{2,1,0:T(8,128)(2,1)S(1)}, bf16[8,704,128]{2,1,0:T(8,128)(2,1)}, bf16[8,704,128]{2,1,0:T(8,128)(2,1)S(1)}) fusion(bf16[40,704,128]{2,1,0:T(8,128)(2,1)} %param.5), kind=kLoop, calls=%fused_computation.29 | loop fusion | bytes 11534336 | tf_op jit(solution)/shard_map/slice | solution.py:52
  15.2 13.0 %collective-permute-done.refs_1_ = bf16[176,768]{1,0:T(8,128)(2,1)S(1)} collective-permute-done((bf16[176,768]{1,0:T(8,128)(2,1)S(1)}, bf16[176,768]{1,0:T(8,128)(2,1)S(1)}, u32[]{:S(2)}, u32[]{:S(2)}) %collective-permute-start) | collective-permute-done | bytes 270368 | tf_op jit(solution)/shard_map/ppermute | solution.py:127
  29.1 2.9 %collective-permute-start.8 = (bf16[352,768]{1,0:T(8,128)(2,1)}, bf16[352,768]{1,0:T(8,128)(2,1)}, u32[]{:S(2)}, u32[]{:S(2)}) collective-permute-start(bf16[352,768]{1,0:T(8,128)(2,1)} %pad_maximum_fusion.1), channel_id=1, source_target_pairs={{0,2},{1,3},{2,0},{3,1},{4,6},{5,7},{6,4},{7,5},{8,10},{9,11},{10,... | collective-permute-start | bytes 1622024 | tf_op jit(solution)/shard_map/ppermute | solution.py:127
  32.0 7.8 %collective-permute-done.4.refs_1_ = bf16[176,768]{1,0:T(8,128)(2,1)S(1)} collective-permute-done((bf16[176,768]{1,0:T(8,128)(2,1)S(1)}, bf16[176,768]{1,0:T(8,128)(2,1)S(1)}, u32[]{:S(2)}, u32[]{:S(2)}) %collective-permute-start.4) | collective-permute-done | bytes 270368 | tf_op jit(solution)/shard_map/ppermute | solution.py:127
  43.3 4.2 %all-to-all-start = ((bf16[8,12,16,128]{3,2,1,0:T(8,128)(2,1)}), bf16[8,12,16,128]{3,2,1,0:T(8,128)(2,1)}, u32[]{:S(2)}, u32[]{:S(2)}) async-start(bf16[8,12,16,128]{3,2,1,0:T(8,128)(2,1)} %bitcast.31), calls=%async_computation | async-start | bytes 786432 | tf_op jit(solution)/shard_map/all_to_all | solution.py:135
  51.3 2.9 %collective-permute-start.5 = (bf16[352,768]{1,0:T(8,128)(2,1)}, bf16[352,768]{1,0:T(8,128)(2,1)}, u32[]{:S(2)}, u32[]{:S(2)}) collective-permute-start(bf16[352,768]{1,0:T(8,128)(2,1)} %pad_maximum_fusion), channel_id=1, source_target_pairs={{0,2},{1,3},{2,0},{3,1},{4,6},{5,7},{6,4},{7,5},{8,10},{9,11},{10,... | collective-permute-start | bytes 1622024 | tf_op jit(solution)/shard_map/ppermute | solution.py:127
  58.2 2.5 %parity_sums.7 = bf16[96,16,128]{2,1,0:T(8,128)(2,1)S(1)} custom-call(s32[4]{0:T(128)S(1)} %iota_xor_fusion.order, s32[40]{0:T(128)S(1)} %get-tuple-element.162.first, s32[40]{0:T(128)S(1)} %get-tuple-element.161.total, bf16[176,768]{1,0:T(8,128)(2,1)S(1)} %copy-done.5, bf16[176,768]{1,0:T(8,128)(2,1)S(1)} %copy-done.17, ...), custom_call_target="tpu_custom_call" | custom-call | flops 799999983616 | bytes 838860800 | tf_op jit(solution)/shard_map/parity_sums/pallas_call | solution.py:55
  61.4 3.3 %collective-permute-done.7.refs_1_ = bf16[176,768]{1,0:T(8,128)(2,1)} collective-permute-done((bf16[176,768]{1,0:T(8,128)(2,1)}, bf16[176,768]{1,0:T(8,128)(2,1)}, u32[]{:S(2)}, u32[]{:S(2)}) %collective-permute-start.7) | collective-permute-done | bytes 270368 | tf_op jit(solution)/shard_map/ppermute | solution.py:127
  64.7 4.1 %all-to-all-start.1 = ((bf16[8,12,16,128]{3,2,1,0:T(8,128)(2,1)}), bf16[8,12,16,128]{3,2,1,0:T(8,128)(2,1)}, u32[]{:S(2)}, u32[]{:S(2)}) async-start(bf16[8,12,16,128]{3,2,1,0:T(8,128)(2,1)} %bitcast.32), calls=%async_computation.1 | async-start | bytes 786432 | tf_op jit(solution)/shard_map/all_to_all | solution.py:135
  72.7 6.5 %collective-permute-done.5.refs_2_ = bf16[352,768]{1,0:T(8,128)(2,1)} collective-permute-done((bf16[352,768]{1,0:T(8,128)(2,1)}, bf16[352,768]{1,0:T(8,128)(2,1)}, u32[]{:S(2)}, u32[]{:S(2)}) %collective-permute-start.5) | collective-permute-done | bytes 540704 | tf_op jit(solution)/shard_map/ppermute | solution.py:127
  79.3 5.2 %collective-permute-done.11.refs_2_ = bf16[8,12,16,128]{3,2,1,0:T(8,128)(2,1)} collective-permute-done((bf16[8,12,16,128]{3,2,1,0:T(8,128)(2,1)}, bf16[8,12,16,128]{3,2,1,0:T(8,128)(2,1)}, u32[]{:S(2)}, u32[]{:S(2)}) %collective-permute-start.11) | collective-permute-done | bytes 393248 | tf_op jit(solution)/shard_map/ppermute | solution.py:127
  85.4 2.4 %parity_sums.8 = bf16[96,16,128]{2,1,0:T(8,128)(2,1)S(1)} custom-call(s32[4]{0:T(128)S(1)} %iota_xor_fusion.order, s32[40]{0:T(128)S(1)} %get-tuple-element.162.first, s32[40]{0:T(128)S(1)} %get-tuple-element.161.total, bf16[176,768]{1,0:T(8,128)(2,1)S(1)} %copy-done.3, bf16[176,768]{1,0:T(8,128)(2,1)S(1)} %copy-done.15, ...), custom_call_target="tpu_custom_call" | custom-call | flops 799999983616 | bytes 838860800 | tf_op jit(solution)/shard_map/parity_sums/pallas_call | solution.py:55
  88.6 4.1 %all-to-all-start.2 = ((bf16[8,12,16,128]{3,2,1,0:T(8,128)(2,1)}), bf16[8,12,16,128]{3,2,1,0:T(8,128)(2,1)}, u32[]{:S(2)}, u32[]{:S(2)}) async-start(bf16[8,12,16,128]{3,2,1,0:T(8,128)(2,1)} %bitcast.33), calls=%async_computation.2 | async-start | bytes 786432 | tf_op jit(solution)/shard_map/all_to_all | solution.py:135
  94.5 2.1 %collective-permute-start.14 = (bf16[352,384]{1,0:T(8,128)(2,1)}, bf16[352,384]{1,0:T(8,128)(2,1)}, u32[]{:S(2)}, u32[]{:S(2)}) collective-permute-start(bf16[352,384]{1,0:T(8,128)(2,1)} %pad_maximum_fusion.4), channel_id=1, source_target_pairs={{0,2},{1,3},{2,0},{3,1},{4,6},{5,7},{6,4},{7,5},{8,10},{9,11},{10,... | collective-permute-start | bytes 811016 | tf_op jit(solution)/shard_map/ppermute | solution.py:127
  96.6 5.9 %collective-permute-done.9.refs_2_ = bf16[352,768]{1,0:T(8,128)(2,1)} collective-permute-done((bf16[352,768]{1,0:T(8,128)(2,1)}, bf16[352,768]{1,0:T(8,128)(2,1)}, u32[]{:S(2)}, u32[]{:S(2)}) %collective-permute-start.9) | collective-permute-done | bytes 540704 | tf_op jit(solution)/shard_map/ppermute | solution.py:127
  102.5 4.6 %collective-permute-done.12.refs_3_ = bf16[8,12,16,128]{3,2,1,0:T(8,128)(2,1)} collective-permute-done((bf16[8,12,16,128]{3,2,1,0:T(8,128)(2,1)}, bf16[8,12,16,128]{3,2,1,0:T(8,128)(2,1)}, u32[]{:S(2)}, u32[]{:S(2)}) %collective-permute-start.12) | collective-permute-done | bytes 393248 | tf_op jit(solution)/shard_map/ppermute | solution.py:127
  107.1 3.3 %parity_sums.9 = bf16[96,16,128]{2,1,0:T(8,128)(2,1)} custom-call(s32[4]{0:T(128)S(1)} %iota_xor_fusion.order, s32[40]{0:T(128)S(1)} %get-tuple-element.162.first, s32[40]{0:T(128)S(1)} %get-tuple-element.161.total, bf16[176,768]{1,0:T(8,128)(2,1)S(1)} %copy-done.1, bf16[176,768]{1,0:T(8,128)(2,1)} %collective-permute-done.7.refs_1_, ...), custom_call_target="tpu_custom_call" | custom-call | flops 799999983616 | bytes 838860800 | tf_op jit(solution)/shard_map/parity_sums/pallas_call | solution.py:55
  110.4 4.1 %all-to-all-start.3 = ((bf16[8,12,16,128]{3,2,1,0:T(8,128)(2,1)}), bf16[8,12,16,128]{3,2,1,0:T(8,128)(2,1)}, u32[]{:S(2)}, u32[]{:S(2)}) async-start(bf16[8,12,16,128]{3,2,1,0:T(8,128)(2,1)} %bitcast.16), calls=%async_computation.3 | async-start | bytes 786432 | tf_op jit(solution)/shard_map/all_to_all | solution.py:135
  117.6 2.1 %collective-permute-start.15 = (bf16[8,12,16,128]{3,2,1,0:T(8,128)(2,1)}, bf16[8,12,16,128]{3,2,1,0:T(8,128)(2,1)}, u32[]{:S(2)}, u32[]{:S(2)}) collective-permute-start(bf16[8,12,16,128]{3,2,1,0:T(8,128)(2,1)} %all-to-all-done.2.refs_0_), channel_id=1, source_target_pairs={{0,1},{1,0},{2,3},{3,2},{4,5},{5,4},{6,7},{7,6},{8,9},{9,8},{10,11... | collective-permute-start | bytes 1179656 | tf_op jit(solution)/shard_map/ppermute | solution.py:127
  119.7 3.1 %all-to-all-done.3.refs_1_ = bf16[8,12,16,128]{3,2,1,0:T(8,128)(2,1)} async-done(((bf16[8,12,16,128]{3,2,1,0:T(8,128)(2,1)}), bf16[8,12,16,128]{3,2,1,0:T(8,128)(2,1)}, u32[]{:S(2)}, u32[]{:S(2)}) %all-to-all-start.3) | async-done | bytes 393248 | tf_op jit(solution)/shard_map/all_to_all | solution.py:135
  122.8 2.5 %parity_sums.10 = bf16[96,8,128]{2,1,0:T(8,128)(2,1)} custom-call(s32[4]{0:T(128)S(1)} %iota_xor_fusion.order, s32[40]{0:T(128)S(1)} %get-tuple-element.162.first, s32[40]{0:T(128)S(1)} %get-tuple-element.161.total, bf16[176,384]{1,0:T(8,128)(2,1)S(1)} %copy-done.10, bf16[176,384]{1,0:T(8,128)(2,1)} %collective-permute-done.10.refs_1_, ...), custom_call_target="tpu_custom_call" | custom-call | flops 399999991808 | bytes 419430400 | tf_op jit(solution)/shard_map/parity_sums/pallas_call | solution.py:55
  125.3 3.4 %all-to-all-start.4 = ((bf16[8,12,8,128]{3,2,1,0:T(8,128)(2,1)}), bf16[8,12,8,128]{3,2,1,0:T(8,128)(2,1)S(1)}, u32[]{:S(2)}, u32[]{:S(2)}) async-start(bf16[8,12,8,128]{3,2,1,0:T(8,128)(2,1)} %bitcast.17), calls=%async_computation.4 | async-start | bytes 393216 | tf_op jit(solution)/shard_map/all_to_all | solution.py:135
  129.3 2.4 %finish.3.refs_4_ = bf16[12,640,128]{2,1,0:T(8,128)(2,1)} custom-call(s32[1]{0:T(128)} %bitcast.parity, s32[1]{0:T(128)S(6)} %copy.9.lat_count, bf16[8,12,16,128]{3,2,1,0:T(8,128)(2,1)} %all-to-all-done.refs_0_, bf16[8,12,16,128]{3,2,1,0:T(8,128)(2,1)} %all-to-all-done.1.refs_1_, bf16[8,12,16,128]{3,2,1,0:T(8,128)(2,1)} %collective-permute-done.11.refs_2_, ...), custom_call_target="tpu_custom_call" | custom-call | tf_op jit(solution)/shard_map/finish/pallas_call | solution.py:99
  132.5 2.4 %all-to-all-done.4.refs_0_ = bf16[8,12,8,128]{3,2,1,0:T(8,128)(2,1)S(1)} async-done(((bf16[8,12,8,128]{3,2,1,0:T(8,128)(2,1)}), bf16[8,12,8,128]{3,2,1,0:T(8,128)(2,1)S(1)}, u32[]{:S(2)}, u32[]{:S(2)}) %all-to-all-start.4) | async-done | bytes 196640 | tf_op jit(solution)/shard_map/all_to_all | solution.py:135
  135.2 2.5 %parity_sums.11 = bf16[96,8,128]{2,1,0:T(8,128)(2,1)} custom-call(s32[4]{0:T(128)S(1)} %iota_xor_fusion.order, s32[40]{0:T(128)S(1)} %get-tuple-element.162.first, s32[40]{0:T(128)S(1)} %get-tuple-element.161.total, bf16[176,384]{1,0:T(8,128)(2,1)S(1)} %copy-done.9, bf16[176,384]{1,0:T(8,128)(2,1)} %collective-permute-done.6.refs_1_, ...), custom_call_target="tpu_custom_call" | custom-call | flops 399999991808 | bytes 419430400 | tf_op jit(solution)/shard_map/parity_sums/pallas_call | solution.py:55
  137.6 3.9 %all-to-all-start.5 = ((bf16[8,12,8,128]{3,2,1,0:T(8,128)(2,1)}), bf16[8,12,8,128]{3,2,1,0:T(8,128)(2,1)S(1)}, u32[]{:S(2)}, u32[]{:S(2)}) async-start(bf16[8,12,8,128]{3,2,1,0:T(8,128)(2,1)} %bitcast.18), calls=%async_computation.5 | async-start | bytes 393216 | tf_op jit(solution)/shard_map/all_to_all | solution.py:135
  141.9 5.9 %all-to-all-done.5.refs_1_ = bf16[8,12,8,128]{3,2,1,0:T(8,128)(2,1)S(1)} async-done(((bf16[8,12,8,128]{3,2,1,0:T(8,128)(2,1)}), bf16[8,12,8,128]{3,2,1,0:T(8,128)(2,1)S(1)}, u32[]{:S(2)}, u32[]{:S(2)}) %all-to-all-start.5) | async-done | bytes 196640 | tf_op jit(solution)/shard_map/all_to_all | solution.py:135
  148.0 2.3 %finish.4.refs_4_ = bf16[12,640,128]{2,1,0:T(8,128)(2,1)} custom-call(s32[1]{0:T(128)} %bitcast.parity, s32[1]{0:T(128)S(6)} %copy.9.lat_count, bf16[8,12,16,128]{3,2,1,0:T(8,128)(2,1)} %all-to-all-done.2.refs_0_, bf16[8,12,16,128]{3,2,1,0:T(8,128)(2,1)} %all-to-all-done.3.refs_1_, ...), custom_call_target="tpu_custom_call", output_to_operand_aliasing={{}: (6, {})} | custom-call | tf_op jit(solution)/shard_map/finish/pallas_call | solution.py:99
  150.4 3.7 %collective-permute-done.17.refs_3_ = bf16[8,12,8,128]{3,2,1,0:T(8,128)(2,1)S(1)} collective-permute-done((bf16[8,12,8,128]{3,2,1,0:T(8,128)(2,1)S(1)}, bf16[8,12,8,128]{3,2,1,0:T(8,128)(2,1)S(1)}, u32[]{:S(2)}, u32[]{:S(2)}) %collective-permute-start.17) | collective-permute-done | bytes 196640 | tf_op jit(solution)/shard_map/ppermute | solution.py:127
  (77 shorter events, 28.9 us)
Async XLA Ops:
  1.1 27.2 %collective-permute-start.1 = (bf16[176,768]{1,0:T(8,128)(2,1)S(1)}, bf16[176,768]{1,0:T(8,128)(2,1)S(1)}, u32[]{:S(2)}, u32[]{:S(2)}) collective-permute-start(bf16[176,768]{1,0:T(8,128)(2,1)S(1)} %get-tuple-element.86), channel_id=1, source_target_pairs={{0,1},{1,0},{2,3},{3,2},{4,5},{5,4},{6,7},{7,6},{8,9},{9,8},{10,11... | collective-permute-start | bytes 811016 | tf_op jit(solution)/shard_map/ppermute | solution.py:127
  4.2 24.1 %collective-permute-start.3 = (bf16[176,768]{1,0:T(8,128)(2,1)S(1)}, bf16[176,768]{1,0:T(8,128)(2,1)S(1)}, u32[]{:S(2)}, u32[]{:S(2)}) collective-permute-start(bf16[176,768]{1,0:T(8,128)(2,1)S(1)} %get-tuple-element.86), channel_id=1, source_target_pairs={{0,3},{1,2},{2,1},{3,0},{4,7},{5,6},{6,5},{7,4},{8,11},{9,10},{10,... | collective-permute-start | bytes 811016 | tf_op jit(solution)/shard_map/ppermute | solution.py:127
  8.9 19.3 %copy-start.4 = (bf16[176,768]{1,0:T(8,128)(2,1)}, bf16[176,768]{1,0:T(8,128)(2,1)S(1)}, u32[]{:S(2)}) copy-start(bf16[176,768]{1,0:T(8,128)(2,1)S(1)} %get-tuple-element.108.refs_0_) | copy-start | bytes 811012
  9.0 19.3 %copy-start.18 = (s32[40]{0:T(128)S(1)}, s32[40]{0:T(128)}, u32[]{:S(2)}) copy-start(s32[40]{0:T(128)} %param.6) | copy-start | bytes 484
  9.0 19.3 %collective-permute-start = (bf16[176,768]{1,0:T(8,128)(2,1)S(1)}, bf16[176,768]{1,0:T(8,128)(2,1)S(1)}, u32[]{:S(2)}, u32[]{:S(2)}) collective-permute-start(bf16[176,768]{1,0:T(8,128)(2,1)S(1)} %get-tuple-element.172), channel_id=1, source_target_pairs={{0,1},{1,0},{2,3},{3,2},{4,5},{5,4},{6,7},{7,6},{8,9},{9,8},{10,11... | collective-permute-start | bytes 811016 | tf_op jit(solution)/shard_map/ppermute | solution.py:127
  9.6 18.6 %collective-permute-start.2 = (bf16[176,768]{1,0:T(8,128)(2,1)S(1)}, bf16[176,768]{1,0:T(8,128)(2,1)S(1)}, u32[]{:S(2)}, u32[]{:S(2)}) collective-permute-start(bf16[176,768]{1,0:T(8,128)(2,1)S(1)} %get-tuple-element.93.refs_0_), channel_id=1, source_target_pairs={{0,2},{1,3},{2,0},{3,1},{4,6},{5,7},{6,4},{7,5},{8,10},{9,11},{10,... | collective-permute-start | bytes 811016 | tf_op jit(solution)/shard_map/ppermute | solution.py:127
  28.2 14.3 %copy-start.16 = (bf16[176,768]{1,0:T(8,128)(2,1)}, bf16[176,768]{1,0:T(8,128)(2,1)S(1)}, u32[]{:S(2)}) copy-start(bf16[176,768]{1,0:T(8,128)(2,1)S(1)} %collective-permute-done.refs_1_) | copy-start | bytes 811012
  28.2 11.6 %collective-permute-start.4 = (bf16[176,768]{1,0:T(8,128)(2,1)S(1)}, bf16[176,768]{1,0:T(8,128)(2,1)S(1)}, u32[]{:S(2)}, u32[]{:S(2)}) collective-permute-start(bf16[176,768]{1,0:T(8,128)(2,1)S(1)} %get-tuple-element.91), channel_id=1, source_target_pairs={{0,1},{1,0},{2,3},{3,2},{4,5},{5,4},{6,7},{7,6},{8,9},{9,8},{10,11... | collective-permute-start | bytes 811016 | tf_op jit(solution)/shard_map/ppermute | solution.py:127
  29.1 26.0 %collective-permute-start.8 = (bf16[352,768]{1,0:T(8,128)(2,1)}, bf16[352,768]{1,0:T(8,128)(2,1)}, u32[]{:S(2)}, u32[]{:S(2)}) collective-permute-start(bf16[352,768]{1,0:T(8,128)(2,1)} %pad_maximum_fusion.1), channel_id=1, source_target_pairs={{0,2},{1,3},{2,0},{3,1},{4,6},{5,7},{6,4},{7,5},{8,10},{9,11},{10,... | collective-permute-start | bytes 1622024 | tf_op jit(solution)/shard_map/ppermute | solution.py:127
  43.3 12.6 %copy-start.5 = (bf16[176,768]{1,0:T(8,128)(2,1)S(1)}, bf16[176,768]{1,0:T(8,128)(2,1)}, u32[]{:S(2)}) copy-start(bf16[176,768]{1,0:T(8,128)(2,1)} %copy-done.4) | copy-start | bytes 811012
  43.3 12.6 %all-to-all-start = ((bf16[8,12,16,128]{3,2,1,0:T(8,128)(2,1)}), bf16[8,12,16,128]{3,2,1,0:T(8,128)(2,1)}, u32[]{:S(2)}, u32[]{:S(2)}) async-start(bf16[8,12,16,128]{3,2,1,0:T(8,128)(2,1)} %bitcast.31), calls=%async_computation | async-start | bytes 786432 | tf_op jit(solution)/shard_map/all_to_all | solution.py:135
  49.5 15.2 %collective-permute-start.7 = (bf16[176,768]{1,0:T(8,128)(2,1)}, bf16[176,768]{1,0:T(8,128)(2,1)}, u32[]{:S(2)}, u32[]{:S(2)}) collective-permute-start(bf16[176,768]{1,0:T(8,128)(2,1)} %get-tuple-element.102), channel_id=1, source_target_pairs={{0,1},{1,0},{2,3},{3,2},{4,5},{5,4},{6,7},{7,6},{8,9},{9,8},{10,11... | collective-permute-start | bytes 811016 | tf_op jit(solution)/shard_map/ppermute | solution.py:127
  51.3 28.0 %collective-permute-start.5 = (bf16[352,768]{1,0:T(8,128)(2,1)}, bf16[352,768]{1,0:T(8,128)(2,1)}, u32[]{:S(2)}, u32[]{:S(2)}) collective-permute-start(bf16[352,768]{1,0:T(8,128)(2,1)} %pad_maximum_fusion), channel_id=1, source_target_pairs={{0,2},{1,3},{2,0},{3,1},{4,6},{5,7},{6,4},{7,5},{8,10},{9,11},{10,... | collective-permute-start | bytes 1622024 | tf_op jit(solution)/shard_map/ppermute | solution.py:127
  55.9 28.6 %collective-permute-start.11 = (bf16[8,12,16,128]{3,2,1,0:T(8,128)(2,1)}, bf16[8,12,16,128]{3,2,1,0:T(8,128)(2,1)}, u32[]{:S(2)}, u32[]{:S(2)}) collective-permute-start(bf16[8,12,16,128]{3,2,1,0:T(8,128)(2,1)} %all-to-all-done.refs_0_), channel_id=1, source_target_pairs={{0,1},{1,0},{2,3},{3,2},{4,5},{5,4},{6,7},{7,6},{8,9},{9,8},{10,11... | collective-permute-start | bytes 1179656 | tf_op jit(solution)/shard_map/ppermute | solution.py:127
  58.2 10.7 %copy-start.1 = (bf16[176,768]{1,0:T(8,128)(2,1)S(1)}, bf16[176,768]{1,0:T(8,128)(2,1)}, u32[]{:S(2)}) copy-start(bf16[176,768]{1,0:T(8,128)(2,1)} %get-tuple-element.131.refs_0_) | copy-start | bytes 811012
  61.4 23.0 %copy-start.3 = (bf16[176,768]{1,0:T(8,128)(2,1)S(1)}, bf16[176,768]{1,0:T(8,128)(2,1)}, u32[]{:S(2)}) copy-start(bf16[176,768]{1,0:T(8,128)(2,1)} %get-tuple-element.123.refs_0_) | copy-start | bytes 811012
  64.7 14.6 %all-to-all-start.1 = ((bf16[8,12,16,128]{3,2,1,0:T(8,128)(2,1)}), bf16[8,12,16,128]{3,2,1,0:T(8,128)(2,1)}, u32[]{:S(2)}, u32[]{:S(2)}) async-start(bf16[8,12,16,128]{3,2,1,0:T(8,128)(2,1)} %bitcast.32), calls=%async_computation.1 | async-start | bytes 786432 | tf_op jit(solution)/shard_map/all_to_all | solution.py:135
  68.8 19.8 %collective-permute-start.10 = (bf16[176,384]{1,0:T(8,128)(2,1)}, bf16[176,384]{1,0:T(8,128)(2,1)}, u32[]{:S(2)}, u32[]{:S(2)}) collective-permute-start(bf16[176,384]{1,0:T(8,128)(2,1)} %get-tuple-element.114), channel_id=1, source_target_pairs={{0,1},{1,0},{2,3},{3,2},{4,5},{5,4},{6,7},{7,6},{8,9},{9,8},{10,11... | collective-permute-start | bytes 405512 | tf_op jit(solution)/shard_map/ppermute | solution.py:127
  70.7 31.8 %collective-permute-start.9 = (bf16[352,768]{1,0:T(8,128)(2,1)}, bf16[352,768]{1,0:T(8,128)(2,1)}, u32[]{:S(2)}, u32[]{:S(2)}) collective-permute-start(bf16[352,768]{1,0:T(8,128)(2,1)} %pad_maximum_fusion.2), channel_id=1, source_target_pairs={{0,2},{1,3},{2,0},{3,1},{4,6},{5,7},{6,4},{7,5},{8,10},{9,11},{10,... | collective-permute-start | bytes 1622024 | tf_op jit(solution)/shard_map/ppermute | solution.py:127
  79.3 27.8 %collective-permute-start.12 = (bf16[8,12,16,128]{3,2,1,0:T(8,128)(2,1)}, bf16[8,12,16,128]{3,2,1,0:T(8,128)(2,1)}, u32[]{:S(2)}, u32[]{:S(2)}) collective-permute-start(bf16[8,12,16,128]{3,2,1,0:T(8,128)(2,1)} %all-to-all-done.1.refs_1_), channel_id=1, source_target_pairs={{0,1},{1,0},{2,3},{3,2},{4,5},{5,4},{6,7},{7,6},{8,9},{9,8},{10,11... | collective-permute-start | bytes 1179656 | tf_op jit(solution)/shard_map/ppermute | solution.py:127
  88.6 13.9 %all-to-all-start.2 = ((bf16[8,12,16,128]{3,2,1,0:T(8,128)(2,1)}), bf16[8,12,16,128]{3,2,1,0:T(8,128)(2,1)}, u32[]{:S(2)}, u32[]{:S(2)}) async-start(bf16[8,12,16,128]{3,2,1,0:T(8,128)(2,1)} %bitcast.33), calls=%async_computation.2 | async-start | bytes 786432 | tf_op jit(solution)/shard_map/all_to_all | solution.py:135
  92.7 17.7 %collective-permute-start.6 = (bf16[176,384]{1,0:T(8,128)(2,1)}, bf16[176,384]{1,0:T(8,128)(2,1)}, u32[]{:S(2)}, u32[]{:S(2)}) collective-permute-start(bf16[176,384]{1,0:T(8,128)(2,1)} %get-tuple-element.100), channel_id=1, source_target_pairs={{0,1},{1,0},{2,3},{3,2},{4,5},{5,4},{6,7},{7,6},{8,9},{9,8},{10,11... | collective-permute-start | bytes 405512 | tf_op jit(solution)/shard_map/ppermute | solution.py:127
  94.5 25.2 %collective-permute-start.14 = (bf16[352,384]{1,0:T(8,128)(2,1)}, bf16[352,384]{1,0:T(8,128)(2,1)}, u32[]{:S(2)}, u32[]{:S(2)}) collective-permute-start(bf16[352,384]{1,0:T(8,128)(2,1)} %pad_maximum_fusion.4), channel_id=1, source_target_pairs={{0,2},{1,3},{2,0},{3,1},{4,6},{5,7},{6,4},{7,5},{8,10},{9,11},{10,... | collective-permute-start | bytes 811016 | tf_op jit(solution)/shard_map/ppermute | solution.py:127
  110.4 12.4 %all-to-all-start.3 = ((bf16[8,12,16,128]{3,2,1,0:T(8,128)(2,1)}), bf16[8,12,16,128]{3,2,1,0:T(8,128)(2,1)}, u32[]{:S(2)}, u32[]{:S(2)}) async-start(bf16[8,12,16,128]{3,2,1,0:T(8,128)(2,1)} %bitcast.16), calls=%async_computation.3 | async-start | bytes 786432 | tf_op jit(solution)/shard_map/all_to_all | solution.py:135
  117.6 14.8 %collective-permute-start.13 = (bf16[352,384]{1,0:T(8,128)(2,1)}, bf16[352,384]{1,0:T(8,128)(2,1)}, u32[]{:S(2)}, u32[]{:S(2)}) collective-permute-start(bf16[352,384]{1,0:T(8,128)(2,1)} %pad_maximum_fusion.3), channel_id=1, source_target_pairs={{0,2},{1,3},{2,0},{3,1},{4,6},{5,7},{6,4},{7,5},{8,10},{9,11},{10,... | collective-permute-start | bytes 811016 | tf_op jit(solution)/shard_map/ppermute | solution.py:127
  117.6 17.5 %collective-permute-start.15 = (bf16[8,12,16,128]{3,2,1,0:T(8,128)(2,1)}, bf16[8,12,16,128]{3,2,1,0:T(8,128)(2,1)}, u32[]{:S(2)}, u32[]{:S(2)}) collective-permute-start(bf16[8,12,16,128]{3,2,1,0:T(8,128)(2,1)} %all-to-all-done.2.refs_0_), channel_id=1, source_target_pairs={{0,1},{1,0},{2,3},{3,2},{4,5},{5,4},{6,7},{7,6},{8,9},{9,8},{10,11... | collective-permute-start | bytes 1179656 | tf_op jit(solution)/shard_map/ppermute | solution.py:127
  125.3 9.6 %all-to-all-start.4 = ((bf16[8,12,8,128]{3,2,1,0:T(8,128)(2,1)}), bf16[8,12,8,128]{3,2,1,0:T(8,128)(2,1)S(1)}, u32[]{:S(2)}, u32[]{:S(2)}) async-start(bf16[8,12,8,128]{3,2,1,0:T(8,128)(2,1)} %bitcast.17), calls=%async_computation.4 | async-start | bytes 393216 | tf_op jit(solution)/shard_map/all_to_all | solution.py:135
  131.7 16.3 %collective-permute-start.18 = (bf16[8,12,16,128]{3,2,1,0:T(8,128)(2,1)}, bf16[8,12,16,128]{3,2,1,0:T(8,128)(2,1)}, u32[]{:S(2)}, u32[]{:S(2)}) collective-permute-start(bf16[8,12,16,128]{3,2,1,0:T(8,128)(2,1)} %all-to-all-done.3.refs_1_), channel_id=1, source_target_pairs={{0,1},{1,0},{2,3},{3,2},{4,5},{5,4},{6,7},{7,6},{8,9},{9,8},{10,11... | collective-permute-start | bytes 1179656 | tf_op jit(solution)/shard_map/ppermute | solution.py:127
  137.6 10.1 %all-to-all-start.5 = ((bf16[8,12,8,128]{3,2,1,0:T(8,128)(2,1)}), bf16[8,12,8,128]{3,2,1,0:T(8,128)(2,1)S(1)}, u32[]{:S(2)}, u32[]{:S(2)}) async-start(bf16[8,12,8,128]{3,2,1,0:T(8,128)(2,1)} %bitcast.18), calls=%async_computation.5 | async-start | bytes 393216 | tf_op jit(solution)/shard_map/all_to_all | solution.py:135
  141.5 12.6 %copy-start.7 = (bf16[8,12,8,128]{3,2,1,0:T(8,128)(2,1)S(1)}, bf16[8,12,8,128]{3,2,1,0:T(8,128)(2,1)}, u32[]{:S(2)}) copy-start(bf16[8,12,8,128]{3,2,1,0:T(8,128)(2,1)} %copy-done.6) | copy-start | bytes 589828
  141.5 8.9 %collective-permute-start.16 = (bf16[8,12,8,128]{3,2,1,0:T(8,128)(2,1)}, bf16[8,12,8,128]{3,2,1,0:T(8,128)(2,1)S(1)}, u32[]{:S(2)}, u32[]{:S(2)}) collective-permute-start(bf16[8,12,8,128]{3,2,1,0:T(8,128)(2,1)} %copy-done.6), channel_id=1, source_target_pairs={{0,1},{1,0},{2,3},{3,2},{4,5},{5,4},{6,7},{7,6},{8,9},{9,8},{10,11... | collective-permute-start | bytes 589832 | tf_op jit(solution)/shard_map/ppermute | solution.py:127
  147.8 6.3 %collective-permute-start.17 = (bf16[8,12,8,128]{3,2,1,0:T(8,128)(2,1)S(1)}, bf16[8,12,8,128]{3,2,1,0:T(8,128)(2,1)S(1)}, u32[]{:S(2)}, u32[]{:S(2)}) collective-permute-start(bf16[8,12,8,128]{3,2,1,0:T(8,128)(2,1)S(1)} %all-to-all-done.5.refs_1_), channel_id=1, source_target_pairs={{0,1},{1,0},{2,3},{3,2},{4,5},{5,4},{6,7},{7,6},{8,9},{9,8},{10,11... | collective-permute-start | bytes 589832 | tf_op jit(solution)/shard_map/ppermute | solution.py:127
  (12 other events, 30.9 us)
